TPU v7x, 32 devices: a whole 2x2x4 slice. The times are simulated.
32 devices in a mesh: dp: 2 (over y), ctx: 4 (over z), tensor: 4 (over x, core).
Axes of the slice: x: 2, y: 2, z: 4, core: 2. Of those that a mesh axis runs over, the one named last changes fastest.
Arguments:
- hidden: bfloat16 [2, 2048, 2048], P('dp', 'ctx'), may hold values from -17 to 17
- cotangent: bfloat16 [2, 2048, 2048], P('dp', 'ctx'), may hold values from -6 to 6
- norm1_gain: float32 [2048], replicated, may hold values from 0.5 to 1.5
- ssm_in: bfloat16 [2048, 2, 3072], P(None, None, 'tensor'), may hold values from -0.125 to 0.125
- ssm_bc: bfloat16 [2048, 2, 256], replicated, may hold values from -0.125 to 0.125
- ssm_dt: bfloat16 [2048, 48], P(None, 'tensor'), may hold values from -0.125 to 0.125
- dt_bias: float32 [48], P('tensor'), may hold values from -7 to -5
- a_log: float32 [48], P('tensor'), may hold values from -4.6 to 2.3
- d_skip: float32 [48], P('tensor'), may hold values from 0.5 to 2
- ssm_out: bfloat16 [3072, 2048], P('tensor'), may hold values from -0.109375 to 0.109375
- attn_q: bfloat16 [2048, 1024], P(None, 'tensor'), may hold values from -0.125 to 0.125
- attn_kv: bfloat16 [2048, 2, 256], replicated, may hold values from -0.125 to 0.125
- attn_out: bfloat16 [1024, 2048], P('tensor'), may hold values from -4 to 4
- norm2_gain: float32 [2048], replicated, may hold values from 0.5 to 1.5
- mlp_gate_up: bfloat16 [2048, 2, 4096], P(None, None, 'tensor'), may hold values from -0.125 to 0.125
- mlp_down: bfloat16 [4096, 2048], P('tensor'), may hold values from -0.09375 to 0.09375
Outputs:
- output: bfloat16 [2, 2048, 2048], P('dp', 'ctx')
- grad_hidden: bfloat16 [2, 2048, 2048], P('dp', 'ctx')
- grad_norm1_gain: float32 [2048], P(('dp', 'ctx'))
- grad_ssm_in: float32 [2048, 2, 3072], P(('dp', 'ctx'), None, 'tensor')
- grad_ssm_bc: float32 [2048, 2, 256], P(('dp', 'ctx'))
- grad_ssm_dt: float32 [2048, 48], P(('dp', 'ctx'), 'tensor')
- grad_dt_bias: float32 [48], P('tensor')
- grad_a_log: float32 [48], P('tensor')
- grad_d_skip: float32 [48], P('tensor')
- grad_ssm_out: float32 [3072, 2048], P('tensor', ('dp', 'ctx'))
- grad_attn_q: float32 [2048, 1024], P(('dp', 'ctx'), 'tensor')
- grad_attn_kv: float32 [2048, 2, 256], P(('dp', 'ctx', 'tensor'))
- grad_attn_out: float32 [1024, 2048], P('tensor', ('dp', 'ctx'))
- grad_norm2_gain: float32 [2048], P(('dp', 'ctx'))
- grad_mlp_gate_up: float32 [2048, 2, 4096], P(('dp', 'ctx'), None, 'tensor')
- grad_mlp_down: float32 [4096, 2048], P('tensor', ('dp', 'ctx'))
- branch_rms: float32 [3], replicated
All inputs are finite; a program needn't handle non-finite values.
Results may differ from a plain program's by a relative error of at most 0.013.
The roundings to bfloat16 on the way count: a program that leaves them out, or rounds other values in their place, can miss the bound.
Values may be sent and summed in bfloat16 or wider, within the bound.
No kernel may reach another device: no remote copies, remote signals or barrier semaphores. Data moves between devices by JAX's collectives and lax.ppermute only.
A program may use at most 320 MiB of HBM per device.

v0:
```python
from functools import partial
import math

import jax
import jax.numpy as jnp
from jax import lax
from jax.sharding import PartitionSpec as P

KVHEADS = 2
AHEAD_DIM = 128
SCAN_BLOCK = 256
QBLOCK = 512


EPSILON = 1e-05
NEG_FILL = -1e30
PRECISE = lax.Precision.HIGHEST


def prefix(value, axis, join, neutral, backward):
    count, mine = (lax.axis_size(axis), lax.axis_index(axis))
    pieces = jax.tree.map(lambda part: lax.all_gather(part, axis), value)
    if backward:
        pieces = jax.tree.map(lambda part: part[::-1], pieces)
        mine = count - 1 - mine
    running = jax.tree.map(
        lambda part, zero: jnp.full_like(part, 0) + jnp.asarray(zero, part.dtype), value, neutral
    )

    def hop(position, running):
        longer = join(running, jax.tree.map(lambda part: part[position], pieces))
        return jax.tree.map(lambda new, old: jnp.where(position < mine, new, old), longer, running)

    return lax.fori_loop(0, count - 1, hop, running)


def swapped(value, axis, stride):
    mask = 2**stride
    pairs = [(source, source ^ mask) for source in range(lax.axis_size(axis))]
    return lax.ppermute(value, axis, pairs)


def matmul_low(former, latter):
    return jnp.dot(former, latter, preferred_element_type=jnp.float32)


def inner_rows(former, latter):
    return lax.dot_general(
        former, latter, (((0,), (0,)), ((), ())), preferred_element_type=jnp.float32
    )


def times_back(former, latter):
    return lax.dot_general(
        former, latter, (((1,), (1,)), ((), ())), preferred_element_type=jnp.float32
    )


def round_keep(values):
    return lax.optimization_barrier(values.astype(jnp.bfloat16)).astype(jnp.float32)


def silu_slope(values):
    logistic = jax.nn.sigmoid(values)
    return logistic * (1.0 + values * (1.0 - logistic))


def norm_back(grad_normed, source, scale_rows, gain):
    weighted = grad_normed * gain
    cubed = scale_rows * scale_rows * scale_rows
    grad_source = scale_rows * weighted - source * cubed * jnp.mean(
        weighted * source, axis=-1, keepdims=True
    )
    grad_gain = jnp.sum(grad_normed * source * scale_rows, axis=0)
    return (grad_source, grad_gain)


def ssd_block(states, pieces, decay_rate, skip_gain):
    source_block, write_block, read_block, step_block = pieces
    increments = step_block * decay_rate
    running = jnp.cumsum(increments, axis=0)
    block_len = increments.shape[0]
    lower_mask = (
        jnp.arange(block_len, dtype=jnp.int32)[:, None]
        >= jnp.arange(block_len, dtype=jnp.int32)[None, :]
    )
    differences = running[:, None, :] - running[None, :, :]
    decays = jnp.exp(jnp.where(lower_mask[:, :, None], differences, NEG_FILL))
    intersection = jnp.dot(read_block, write_block.T, precision=PRECISE)
    mixing = decays * intersection[:, :, None] * step_block[None, :, :]
    within = jnp.einsum("tsh,shp->thp", mixing, source_block, precision=PRECISE)
    carried = (
        jnp.einsum("tn,hpn->thp", read_block, states, precision=PRECISE)
        * jnp.exp(running)[:, :, None]
    )
    result = within + carried + skip_gain[None, :, None] * source_block
    tailing = jnp.exp(running[-1][None, :] - running) * step_block
    incoming = jnp.einsum("sh,shp,sn->hpn", tailing, source_block, write_block, precision=PRECISE)
    states = states * jnp.exp(running[-1])[:, None, None] + incoming
    return (states, result)


def run_ssd(source_heads, write_rows, read_rows, step_rows, a_log, d_skip, entering, block_len):
    row_total = source_heads.shape[0]
    block_count = row_total // block_len
    decay_rate = -jnp.exp(a_log)

    def blocked(source):
        return source.reshape((block_count, block_len) + source.shape[1:])

    def stepper(states, pieces):
        return ssd_block(states, pieces, decay_rate, d_skip)

    closing, outputs = lax.scan(
        jax.checkpoint(stepper),
        entering,
        (blocked(source_heads), blocked(write_rows), blocked(read_rows), blocked(step_rows)),
    )
    return (outputs.reshape(source_heads.shape), closing)


def chain_states(earlier, later):
    return (earlier[0] * later[0], earlier[1] * later[0][:, None, None] + later[1])


def body(
    hidden,
    cotangent,
    norm1_gain,
    ssm_in,
    ssm_bc,
    ssm_dt,
    dt_bias,
    a_log,
    d_skip,
    ssm_out,
    attn_q,
    attn_kv,
    attn_out,
    norm2_gain,
    mlp_gate_up,
    mlp_down,
):
    ctx_rank = lax.axis_index("ctx")
    tensor_rank = lax.axis_index("tensor")
    tensor_count = lax.axis_size("tensor")
    source = hidden[0].astype(jnp.float32)
    tokens = source.shape[0]
    model_width = source.shape[1]
    scale_one = lax.rsqrt(jnp.mean(source * source, axis=-1, keepdims=True) + EPSILON)
    input_one = (source * scale_one * norm1_gain).astype(jnp.bfloat16)
    inner_local = ssm_in.shape[2]
    heads_local = ssm_dt.shape[1]
    head_width = inner_local // heads_local
    state_width = ssm_bc.shape[2]
    in_matrix = ssm_in.reshape(model_width, 2 * inner_local)
    bc_matrix = ssm_bc.reshape(model_width, 2 * state_width)
    zx_proj = matmul_low(input_one, in_matrix)
    gate_ssm = zx_proj[:, :inner_local]
    source_heads = round_keep(zx_proj[:, inner_local:]).reshape(tokens, heads_local, head_width)
    bc_rows = round_keep(matmul_low(input_one, bc_matrix))
    write_rows = bc_rows[:, :state_width]
    read_rows = bc_rows[:, state_width:]
    dt_pre = matmul_low(input_one, ssm_dt) + dt_bias
    dt_rows = jax.nn.softplus(dt_pre)
    decay_rate = -jnp.exp(a_log)
    running = jnp.cumsum(dt_rows * decay_rate, axis=0)
    whole_decay = jnp.exp(running[-1])
    to_end = jnp.exp(running[-1][None, :] - running) * dt_rows
    own_state = jnp.einsum("th,thp,tn->hpn", to_end, source_heads, write_rows, precision=PRECISE)
    neutral = (jnp.ones_like(whole_decay), jnp.zeros_like(own_state))
    entering = prefix((whole_decay, own_state), "ctx", chain_states, neutral, False)[1]
    ssm_pair, ssm_back = jax.vjp(
        partial(run_ssd, block_len=SCAN_BLOCK),
        source_heads,
        write_rows,
        read_rows,
        dt_rows,
        a_log,
        d_skip,
        entering,
    )
    ssm_values = ssm_pair[0].reshape(tokens, inner_local)
    gate_act = jax.nn.silu(gate_ssm)
    gated_rows = (ssm_values * gate_act).astype(jnp.bfloat16)
    ssm_part = matmul_low(gated_rows, ssm_out)
    kv_index = tensor_rank * KVHEADS // tensor_count
    kv_matrix = lax.dynamic_slice_in_dim(attn_kv, kv_index * AHEAD_DIM, AHEAD_DIM, 2).reshape(
        model_width, 2 * AHEAD_DIM
    )
    queries = matmul_low(input_one, attn_q).astype(jnp.bfloat16)
    heads_query = attn_q.shape[1] // AHEAD_DIM
    key_value = matmul_low(input_one, kv_matrix).astype(jnp.bfloat16)
    whole_kv = lax.all_gather(key_value, "ctx", axis=0, tiled=True)
    key_rows = whole_kv[:, :AHEAD_DIM]
    value_rows = whole_kv[:, AHEAD_DIM:]
    length = whole_kv.shape[0]
    block_rows = min(QBLOCK, tokens)
    starts = jnp.arange(tokens // block_rows, dtype=jnp.int32) * block_rows
    key_place = jnp.arange(length, dtype=jnp.int32)
    factor = 1.0 / math.sqrt(AHEAD_DIM)

    def block_scores(offset):
        query_rows = queries.reshape(block_rows, heads_query, AHEAD_DIM)
        scores = (
            jnp.einsum("qhd,kd->hqk", query_rows, key_rows, preferred_element_type=jnp.float32)
            * factor
        )
        positions = ctx_rank * tokens + offset + jnp.arange(block_rows, dtype=jnp.int32)
        allowed = key_place[None, :] <= positions[:, None]
        return (query_rows, jnp.where(allowed[None], scores, NEG_FILL))

    def attend(offset):
        query_rows, masked = block_scores(offset)
        maxima = jnp.max(masked, axis=-1, keepdims=True)
        weights = jnp.exp(masked - maxima)
        totals = jnp.sum(weights, axis=-1, keepdims=True)
        probability = (weights / totals).astype(jnp.bfloat16)
        mixed_rows = jnp.einsum(
            "hqk,kd->qhd", probability, value_rows, preferred_element_type=jnp.float32
        )
        return (
            mixed_rows.reshape(block_rows, heads_query * AHEAD_DIM).astype(jnp.bfloat16),
            maxima + jnp.log(totals),
        )

    attended, log_totals = lax.map(attend, starts)
    attended = attended.reshape(tokens, heads_query * AHEAD_DIM)
    attn_part = matmul_low(attended, attn_out)
    mixer_total = lax.psum(ssm_part + attn_part, "tensor")
    middle = source + mixer_total
    scale_two = lax.rsqrt(jnp.mean(middle * middle, axis=-1, keepdims=True) + EPSILON)
    input_two = (middle * scale_two * norm2_gain).astype(jnp.bfloat16)
    ff_local = mlp_down.shape[0]
    gu_matrix = mlp_gate_up.reshape(model_width, 2 * ff_local)
    gate_up = matmul_low(input_two, gu_matrix)
    gate_rows = gate_up[:, :ff_local]
    up_rows = gate_up[:, ff_local:]
    gate_silu = jax.nn.silu(gate_rows)
    activated = (gate_silu * up_rows).astype(jnp.bfloat16)
    mlp_total = lax.psum(matmul_low(activated, mlp_down), "tensor")
    block_out = middle + mlp_total
    squares = jnp.stack(
        [
            jnp.sum(mixer_total * mixer_total),
            jnp.sum(mlp_total * mlp_total),
            jnp.sum(block_out * block_out),
        ]
    )
    grad_low = cotangent[0]
    grad_out = grad_low.astype(jnp.float32)
    grad_down = inner_rows(activated, grad_low)
    grad_act = times_back(grad_low, mlp_down)
    grad_gu = jnp.concatenate(
        [grad_act * up_rows * silu_slope(gate_rows), grad_act * gate_silu], axis=1
    ).astype(jnp.bfloat16)
    grad_gate_up = inner_rows(input_two, grad_gu).reshape(model_width, 2, ff_local)
    grad_normed_two = lax.psum(times_back(grad_gu, gu_matrix), "tensor")
    grad_middle, grad_gain_two = norm_back(grad_normed_two, middle, scale_two, norm2_gain)
    grad_middle = grad_out + grad_middle
    grad_mix = grad_middle.astype(jnp.bfloat16)
    grad_ssm_out = inner_rows(gated_rows, grad_mix)
    grad_gated = times_back(grad_mix, ssm_out)
    grad_values = round_keep(grad_gated * gate_act).reshape(tokens, heads_local, head_width)
    grad_gate_ssm = grad_gated * ssm_values * silu_slope(gate_ssm)
    grad_attn_out = inner_rows(attended, grad_mix)
    grad_attended = times_back(grad_mix, attn_out).astype(jnp.bfloat16)
    from_start = jnp.exp(running)
    own_grad = jnp.einsum("th,thp,tn->hpn", from_start, grad_values, read_rows, precision=PRECISE)
    leaving = prefix((whole_decay, own_grad), "ctx", chain_states, neutral, True)[1]
    ssm_grads = ssm_back((grad_values, leaving))
    grad_dt_pre = ssm_grads[3] * jax.nn.sigmoid(dt_pre)
    grad_dt_bias = jnp.sum(grad_dt_pre, axis=0)
    grad_dt_low = grad_dt_pre.astype(jnp.bfloat16)
    grad_zx = jnp.concatenate(
        [grad_gate_ssm, ssm_grads[0].reshape(tokens, inner_local)], axis=1
    ).astype(jnp.bfloat16)
    grad_ssm_in = inner_rows(input_one, grad_zx).reshape(model_width, 2, inner_local)
    grad_ssm_dt = inner_rows(input_one, grad_dt_low)
    input_terms = times_back(grad_zx, in_matrix) + times_back(grad_dt_low, ssm_dt)

    def attend_back(carried, pieces):
        offset, log_rows, grad_rows = pieces
        query_rows, masked = block_scores(offset)
        probability = jnp.exp(masked - log_rows)
        prob_low = probability.astype(jnp.bfloat16)
        grad_key, grad_value = carried
        grad_value = grad_value + jnp.einsum(
            "hqk,qhd->kd", prob_low, grad_rows, preferred_element_type=jnp.float32
        )
        grad_prob = jnp.einsum(
            "qhd,kd->hqk", grad_rows, value_rows, preferred_element_type=jnp.float32
        )
        centre = jnp.sum(probability * grad_prob, axis=-1, keepdims=True)
        grad_score = (probability * (grad_prob - centre)).astype(jnp.bfloat16)
        grad_query = (
            jnp.einsum("hqk,kd->qhd", grad_score, key_rows, preferred_element_type=jnp.float32)
            * factor
        )
        grad_key = (
            grad_key
            + jnp.einsum("hqk,qhd->kd", grad_score, query_rows, preferred_element_type=jnp.float32)
            * factor
        )
        return (
            (grad_key, grad_value),
            grad_query.reshape(block_rows, heads_query * AHEAD_DIM).astype(jnp.bfloat16),
        )

    zero_kv = jnp.zeros((length, AHEAD_DIM), jnp.float32)
    grad_blocks = grad_attended.reshape(tokens // block_rows, block_rows, heads_query, AHEAD_DIM)
    kv_sums, grad_query_blocks = lax.scan(
        attend_back, (zero_kv, zero_kv), (starts, log_totals, grad_blocks)
    )
    grad_query_low = grad_query_blocks.reshape(tokens, heads_query * AHEAD_DIM)
    own_kv = lax.psum_scatter(
        jnp.concatenate([kv_sums[0], kv_sums[1]], axis=1), "ctx", scatter_dimension=0, tiled=True
    )
    grad_kv_low = (own_kv + swapped(own_kv, "tensor", 0)).astype(jnp.bfloat16)
    pair_share = KVHEADS / tensor_count
    grad_kv_local = pair_share * inner_rows(input_one, grad_kv_low)
    grad_attn_kv = lax.dynamic_update_slice_in_dim(
        jnp.zeros((model_width, 2, attn_kv.shape[2]), jnp.float32),
        grad_kv_local.reshape(model_width, 2, AHEAD_DIM),
        kv_index * AHEAD_DIM,
        2,
    )
    grad_attn_q = inner_rows(input_one, grad_query_low)
    input_terms = (
        input_terms
        + times_back(grad_query_low, attn_q)
        + pair_share * times_back(grad_kv_low, kv_matrix)
    )
    summed = lax.psum(
        (input_terms, jnp.concatenate([ssm_grads[1], ssm_grads[2]], axis=1)), "tensor"
    )
    grad_bc_low = summed[1].astype(jnp.bfloat16)
    grad_ssm_bc = inner_rows(input_one, grad_bc_low).reshape(model_width, 2, state_width)
    grad_normed_one = summed[0] + times_back(grad_bc_low, bc_matrix)
    grad_source, grad_gain_one = norm_back(grad_normed_one, source, scale_one, norm1_gain)
    grad_hidden = (grad_middle + grad_source).astype(jnp.bfloat16)[None]
    everything = (
        lax.psum_scatter(grad_gain_one, ("dp", "ctx"), scatter_dimension=0, tiled=True),
        lax.psum_scatter(grad_ssm_in, ("dp", "ctx"), scatter_dimension=0, tiled=True),
        lax.psum_scatter(grad_ssm_bc, ("dp", "ctx"), scatter_dimension=0, tiled=True),
        lax.psum_scatter(grad_ssm_dt, ("dp", "ctx"), scatter_dimension=0, tiled=True),
        lax.psum_scatter(grad_ssm_out, ("dp", "ctx"), scatter_dimension=1, tiled=True),
        lax.psum_scatter(grad_attn_q, ("dp", "ctx"), scatter_dimension=0, tiled=True),
        lax.psum_scatter(grad_attn_out, ("dp", "ctx"), scatter_dimension=1, tiled=True),
        lax.psum_scatter(grad_gain_two, ("dp", "ctx"), scatter_dimension=0, tiled=True),
        lax.psum_scatter(grad_gate_up, ("dp", "ctx"), scatter_dimension=0, tiled=True),
        lax.psum_scatter(grad_down, ("dp", "ctx"), scatter_dimension=1, tiled=True),
    )
    shared = lax.psum_scatter(
        grad_attn_kv, ("dp", "ctx", "tensor"), scatter_dimension=0, tiled=True
    )
    small_sums = lax.psum((grad_dt_bias, ssm_grads[4], ssm_grads[5], squares), ("dp", "ctx"))
    counted = tokens * model_width * lax.axis_size("dp") * lax.axis_size("ctx")
    branch_rms = jnp.sqrt(small_sums[3] / counted)
    output = block_out.astype(jnp.bfloat16)[None]
    return (
        output,
        grad_hidden,
        everything[0],
        everything[1],
        everything[2],
        everything[3],
        small_sums[0],
        small_sums[1],
        small_sums[2],
        everything[4],
        everything[5],
        shared,
        everything[6],
        everything[7],
        everything[8],
        everything[9],
        branch_rms,
    )


def solution(mesh):
    return jax.shard_map(
        body,
        mesh=mesh,
        in_specs=(
            P("dp", "ctx", None),
            P("dp", "ctx", None),
            P(),
            P(None, None, "tensor"),
            P(),
            P(None, "tensor"),
            P("tensor"),
            P("tensor"),
            P("tensor"),
            P("tensor", None),
            P(None, "tensor"),
            P(),
            P("tensor", None),
            P(),
            P(None, None, "tensor"),
            P("tensor", None),
        ),
        out_specs=(
            P("dp", "ctx", None),
            P("dp", "ctx", None),
            P(("dp", "ctx")),
            P(("dp", "ctx"), None, "tensor"),
            P(("dp", "ctx"), None, None),
            P(("dp", "ctx"), "tensor"),
            P("tensor"),
            P("tensor"),
            P("tensor"),
            P("tensor", ("dp", "ctx")),
            P(("dp", "ctx"), "tensor"),
            P(("dp", "ctx", "tensor"), None, None),
            P("tensor", ("dp", "ctx")),
            P(("dp", "ctx")),
            P(("dp", "ctx"), None, "tensor"),
            P("tensor", ("dp", "ctx")),
            P(),
        ),
        check_vma=False,
    )
```

profile of v0, /device:TPU:0, one launch (start us, length us, event | category | flops | bytes accessed | tf_op | source)
XLA Modules:
  0.0 2148.7 jit_solution(451032201537482246)
XLA Ops:
  12.8 3.1 fusion.155
  22.4 4.3 copy.295
  26.7 3.4 fusion.142
  41.6 3.0 reshape.465
  47.4 13.0 all-gather.2
  67.6 3.2 fusion.194
  75.9 35.4 %all-gather.9.cloned.1.call-done = f32[48,64,256]{2,1,0:T(8,128)} async-done(((f32[12,64,256]{2,1,0:T(8,128)}), f32[48,64,256]{2,1,0:T(8,128)}) %all-gather.9.cloned.1.call-update) | async-done | bytes 3145744 | tf_op jit(solution)/shard_map/all_gather | solution.py:22
  111.3 7.0 while.83
  118.9 64.0 %while.82 = (s32[]{:T(128)}, f32[12,64,256]{2,1,0:T(8,128)}, f32[2,256,12,64]{1,0,3,2:T(2,128)}, f32[2,12,64,256]{3,2,1,0:T(8,128)}, f32[2,256,12]{1,2,0:T(8,128...) while((s32[]{:T(128)}, f32[12,64,256]{2,1,0:T(8,128)}, ...), condition=%wide.region_8.9_spmd.clone, body=%wide.region_5.8_spmd.clone.sunk | while | flops 2018190336 | bytes 24531304 | solution.py:114
  124.5 3.1 convolution_add_fusion.8
  128.1 4.3 fusion.305
  134.2 16.8 dynamic_update_slice.80
  156.6 3.1 convolution_add_fusion.8
  160.1 4.3 fusion.305
  166.2 16.8 dynamic_update_slice.80
  185.6 3.1 copy.226
  196.2 10.1 copy.299
  206.4 73.7 %all-reduce.15.cloned.1.call-done = f32[512,2048]{1,0:T(8,128)} async-done(((f32[512,2048]{1,0:T(8,128)}), f32[512,2048]{1,0:T(8,128)}) %all-reduce.15.cloned.1.call-update) | async-done | bytes 4194320 | tf_op jit(solution)/shard_map/psum | solution.py:230
  280.1 5.2 multiply_reduce_fusion.9
  287.4 4.6 fusion.182
  292.0 3.1 multiply_convert_fusion.2
  295.2 4.7 fusion.197
  299.8 6.2 fusion.151
  306.1 153.5 %all-reduce.23.cloned.1.call-done = (f32[512,2048]{1,0:T(8,128)}, f32[512,2048]{1,0:T(8,128)}) async-done(((f32[512,2048]{1,0:T(8,128)}, f32[512,2048]{1,0:T(8,128)}), (f32[512,2048]{1,0:T(8,128)}, f32[512,2048]{1,0:T(8,128)})) %all-reduce.23.cloned.1.call-update) | async-done | bytes 8388624 | tf_op jit(solution)/shard_map/psum | solution.py:258
  459.6 7.6 multiply_reduce_fusion.5
  468.1 2.9 fusion.191
  482.4 5.9 multiply_convert_fusion.5
  494.8 3.2 fusion.158
  500.9 25.6 %reduce-scatter.9.cloned.1.call-done = f32[512,256]{0,1:T(8,128)} async-done(((f32[2048,256]{0,1:T(8,128)}), f32[512,256]{0,1:T(8,128)}) %reduce-scatter.9.cloned.1.call-update) | async-done | bytes 524304 | tf_op jit(solution)/shard_map/reduce_scatter | solution.py:316
  526.5 64.3 %all-gather.11.cloned.1.call-done = f32[48,64,256]{2,1,0:T(8,128)} async-done(((f32[12,64,256]{2,1,0:T(8,128)}), f32[48,64,256]{2,1,0:T(8,128)}) %all-gather.11.cloned.1.call-update) | async-done | bytes 3145744 | tf_op jit(solution)/shard_map/all_gather | solution.py:22
  590.7 3.9 rev.7
  594.6 4.2 while.84
  605.0 2.9 broadcast_in_dim.225
  612.8 75.2 %while.85 = (s32[]{:T(128)}, f32[12]{0:T(128)}, f32[12]{0:T(128)}, f32[12,64,256]{2,1,0:T(8,128)S(1)}, bf16[2,256,12,64]{1,3,2,0:T(8,128)(2,1)}, /*index=5*/f32[...) while((s32[]{:T(128)}, f32[12]{0:T(128)}, f32[12]{0:T(128)}, ...), condition=%wide.region_32.33_spmd.clone, body=%wide.region_18.32_spmd.clone.sunk | while | flops 4849516544 | bytes 62877340 | solution.py:114
  620.9 5.5 fusion.327
  628.3 3.2 multiply_reduce_fusion.13
  642.0 4.1 fusion.333
  657.8 5.5 fusion.327
  665.3 3.2 multiply_reduce_fusion.13
  679.7 4.1 fusion.333
  691.4 5.7 fusion.163
  697.2 3.1 multiply_add_fusion
  701.9 10.7 fusion.150
  712.6 25.6 %copy.250 = f32[2048,2,1024]{2,1,0:T(2,128)} copy(f32[2048,2,1024]{0,2,1:T(8,128)} %bitcast.537) | data formatting | bytes 33554432 | tf_op jit(solution)/shard_map/reshape | solution.py:257
  742.5 34.1 %all-reduce.24 = bf16[512,512]{0,1:T(8,128)(2,1)} all-reduce(f32[512,512]{0,1:T(8,128)S(1)} %pad_maximum_fusion.5), channel_id=1, replica_groups=mesh['dp'=2,'ctx'=4,'tensor'=4] {'tensor'}, use_global_device_ids=true, to_apply=%region_36.37 | all-reduce | flops 262144 | bytes 1572864 | tf_op jit(solution)/shard_map/psum | solution.py:334
  776.6 4.7 fusion.128
  787.4 8.1 fusion.130
  798.9 3.7 fusion.200
  805.5 7.4 fusion.132
  814.0 6.1 fusion.199
  825.6 18.6 all-reduce.17.cloned.1.call-done
  844.2 6.8 fusion.116
  851.0 39.9 %all-reduce.6 = (f32[2048]{0:T(1024)S(1)}, f32[12]{0:T(128)}, f32[12]{0:T(128)}, f32[12]{0:T(128)}, f32[2048]{0:T(1024)S(1)}, /*index=5*/f32[3]{0:T(128)S(1)}) all-reduce(f32[2048]{0:T(1024)S(1)} %get-tuple-element.1041, f32[12]{0:T(128)S(1)} %get-tuple-element.1137, ...), channel_id=5, replica_groups=mesh['dp'=2,'ctx'=4,'tensor'=4] {'dp','ctx'}, use_global_device_ids=true, to_apply=%region_39.40.clone | all-reduce | flops 4135 | bytes 33080
  892.7 6.9 fusion.127
  899.6 459.9 %all-reduce.21.cloned.1.call-done = f32[2048,2,1024]{2,1,0:T(2,128)} async-done(((f32[2048,2,1024]{2,1,0:T(2,128)}), f32[2048,2,1024]{2,1,0:T(2,128)}) %all-reduce.21.cloned.1.call-update) | async-done | bytes 16777232
  1359.4 3.8 constant_dynamic-slice_fusion.1
  1363.2 87.1 %reduce-scatter.13.cloned.1.call-done = f32[256,2,256]{2,0,1:T(8,128)} async-done(((f32[2048,2,256]{2,0,1:T(8,128)}), f32[256,2,256]{2,0,1:T(8,128)}) %reduce-scatter.13.cloned.1.call-update) | async-done | bytes 524304 | tf_op jit(solution)/shard_map/reduce_scatter | solution.py:345
  1452.6 208.4 %reduce-scatter.11.cloned.1.call-done = f32[256,2,768]{2,0,1:T(8,128)} async-done(((f32[2048,2,768]{2,0,1:T(8,128)}), f32[256,2,768]{2,0,1:T(8,128)}) %reduce-scatter.11.cloned.1.call-update) | async-done | bytes 1572880 | tf_op jit(solution)/shard_map/reduce_scatter | solution.py:344
  1661.0 3.8 copy.251
  1664.8 67.2 %reduce-scatter.19.cloned.1.call-done = f32[256,256]{1,0:T(8,128)} async-done(((f32[2048,256]{1,0:T(8,128)}), f32[256,256]{1,0:T(8,128)}) %reduce-scatter.19.cloned.1.call-update) | async-done | bytes 262160 | tf_op jit(solution)/shard_map/reduce_scatter | solution.py:348
  1731.9 71.4 %reduce-scatter.21.cloned.1.call-done = f32[256,256]{1,0:T(8,128)} async-done(((f32[256,2048]{1,0:T(8,128)}), f32[256,256]{1,0:T(8,128)}) %reduce-scatter.21.cloned.1.call-update) | async-done | bytes 262160 | tf_op jit(solution)/shard_map/reduce_scatter | solution.py:349
  1803.3 64.1 %reduce-scatter.15.cloned.1.call-done = f32[256,12]{0,1:T(8,128)} async-done(((f32[2048,12]{0,1:T(8,128)}), f32[256,12]{0,1:T(8,128)}) %reduce-scatter.15.cloned.1.call-update) | async-done | bytes 12304 | tf_op jit(solution)/shard_map/reduce_scatter | solution.py:346
  1867.5 152.5 %reduce-scatter.23.cloned.1.call-done = f32[1024,256]{1,0:T(8,128)} async-done(((f32[1024,2048]{1,0:T(8,128)}), f32[1024,256]{1,0:T(8,128)}) %reduce-scatter.23.cloned.1.call-update) | async-done | bytes 1048592 | tf_op jit(solution)/shard_map/reduce_scatter | solution.py:352
  2020.0 121.9 %reduce-scatter.17.cloned.1.call-done = f32[768,256]{1,0:T(8,128)} async-done(((f32[768,2048]{1,0:T(8,128)}), f32[768,256]{1,0:T(8,128)}) %reduce-scatter.17.cloned.1.call-update) | async-done | bytes 786448 | tf_op jit(solution)/shard_map/reduce_scatter | solution.py:347
  (507 shorter events, 189.8 us)
Async XLA Ops:
  7.2 183.8 %copy-start = (bf16[768,2048]{1,0:T(8,128)(2,1)S(1)}, bf16[768,2048]{1,0:T(8,128)(2,1)}, u32[]{:S(2)}) copy-start(bf16[768,2048]{1,0:T(8,128)(2,1)} %param.33) | copy-start | bytes 9437188
  7.2 5.6 copy-start.71
  7.2 60.4 %all-gather.7.cloned.1.call-start = ((), (), s32[]{:S(2)}) async-start(), calls=%async_computation.8 | async-start | bytes 1310720 | tf_op jit(solution)/shard_map/all_gather | solution.py:194
  10.0 27.4 %copy-start.77 = (f32[512]{0:T(512)}, f32[512]{0:T(512)S(1)}, u32[]{:S(2)}) copy-start(f32[512]{0:T(512)S(1)} %get-tuple-element.1169) | copy-start | bytes 6148
  15.9 95.4 %all-gather.9.cloned.1.call-start = ((), (), s32[]{:S(2)}) async-start(), calls=%async_computation.19 | async-start | bytes 3932160 | tf_op jit(solution)/shard_map/all_gather | solution.py:22
  20.8 18.2 copy-start.61
  41.5 238.6 %all-reduce.15.cloned.1.call-start = ((), (), s32[]{:S(2)}) async-start(), calls=%async_computation.9 | async-start | bytes 8388608 | tf_op jit(solution)/shard_map/psum | solution.py:230
  75.9 117.0 %copy-start.57 = (bf16[128,2,512]{2,0,1:T(8,128)(2,1)}, bf16[128,2,512]{2,0,1:T(8,128)(2,1)S(1)}, u32[]{:S(2)}) copy-start(bf16[128,2,512]{2,0,1:T(8,128)(2,1)S(1)} %fusion.159) | copy-start | bytes 786436
  121.9 5.8 copy-start.10
  121.9 5.8 copy-start.12
  121.9 6.2 copy-start.4
  121.9 6.2 copy-start.73
  153.9 5.8 copy-start.10
  153.9 5.8 copy-start.12
  153.9 6.2 copy-start.4
  153.9 6.2 copy-start.73
  195.8 263.8 %all-reduce.23.cloned.1.call-start = ((), (), s32[]{:S(2)}) async-start(), calls=%async_computation.23 | async-start | bytes 16777216 | tf_op jit(solution)/shard_map/psum | solution.py:258
  206.4 81.0 %copy-start.74 = (f32[2048]{0:T(1024)S(1)}, f32[2048]{0:T(1024)}, u32[]{:S(2)}) copy-start(f32[2048]{0:T(1024)} %param.37) | copy-start | bytes 24580
  280.1 7.3 copy-start.24
  285.3 181.9 %copy-start.79 = (f32[512]{0:T(512)}, f32[512]{0:T(512)S(1)}, u32[]{:S(2)}) copy-start(f32[512]{0:T(512)S(1)} %get-tuple-element.1171) | copy-start | bytes 6148
  306.1 220.4 %reduce-scatter.9.cloned.1.call-start = ((), (), s32[]{:S(2)}) async-start(), calls=%async_computation.10 | async-start | bytes 2621440 | tf_op jit(solution)/shard_map/reduce_scatter | solution.py:316
  459.6 7.6 copy-start.15
  459.6 7.9 copy-start.22
  459.6 8.5 copy-start.43
  459.6 12.2 slice-start
  468.1 5.1 slice-start.1
  482.3 108.4 %all-gather.11.cloned.1.call-start = ((), (), s32[]{:S(2)}) async-start(), calls=%async_computation.20 | async-start | bytes 3932160 | tf_op jit(solution)/shard_map/all_gather | solution.py:22
  492.6 331.5 %all-reduce.19.cloned.1.call-start = ((), (), s32[]{:S(2)}) async-start(), calls=%async_computation.21 | async-start | bytes 8388608
  526.5 72.3 %collective-permute-start = (f32[512,256]{0,1:T(8,128)}, f32[512,256]{0,1:T(8,128)}, u32[]{:S(2)}, u32[]{:S(2)}) collective-permute-start(f32[512,256]{0,1:T(8,128)} %reduce-scatter.9.cloned.1.call-done), channel_id=1, source_target_pairs={{0,1},{1,0},{2,3},{3,2},{4,5},{5,4},{6,7},{7,6},{8,9},{9,8},{10,11... | collective-permute-start | bytes 1572872 | tf_op jit(solution)/shard_map/ppermute | solution.py:40
  594.6 5.5 copy-start.17
  609.4 234.8 %all-reduce.17.cloned.1.call-start = ((), (), s32[]{:S(2)}) async-start(), calls=%async_computation.11 | async-start | bytes 8388608 | tf_op jit(solution)/shard_map/psum | solution.py:334
  620.8 5.6 copy-start.26
  620.8 5.6 copy-start.52
  637.0 5.0 copy-start.20
  637.0 5.0 copy-start.27
  642.0 6.2 copy-start.3
  642.0 6.2 copy-start.48
  657.7 5.6 copy-start.26
  657.8 5.6 copy-start.52
  673.9 5.7 copy-start.20
  673.9 5.7 copy-start.27
  673.9 5.7 copy-start.34
  679.6 6.2 copy-start.3
  679.6 6.2 copy-start.48
  690.4 6.7 copy-start.36
  691.4 5.8 copy-start.18
  691.4 5.8 copy-start.31
  691.4 5.8 copy-start.41
  700.3 659.1 %all-reduce.21.cloned.1.call-start = ((), (), s32[]{:S(2)}) async-start(), calls=%async_computation.22 | async-start | bytes 33554432
  738.2 38.3 %copy-start.8 = (bf16[1,512,2048]{2,1,0:T(8,128)(2,1)S(1)}, bf16[1,512,2048]{2,1,0:T(8,128)(2,1)}, u32[]{:S(2)}) copy-start(bf16[1,512,2048]{2,1,0:T(8,128)(2,1)} %param.24) | copy-start | bytes 6291460
  738.2 38.3 %copy-start.72 = (f32[2048]{0:T(1024)S(1)}, f32[2048]{0:T(1024)}, u32[]{:S(2)}) copy-start(f32[2048]{0:T(1024)} %param.26) | copy-start | bytes 24580
  738.2 38.3 %copy-start.78 = (f32[512]{0:T(512)S(1)}, f32[512]{0:T(512)}, u32[]{:S(2)}) copy-start(f32[512]{0:T(512)} %copy-done.77) | copy-start | bytes 6148
  738.2 712.1 %reduce-scatter.13.cloned.1.call-start = ((), (), s32[]{:S(2)}) async-start(), calls=%async_computation.13 | async-start | bytes 4718592 | tf_op jit(solution)/shard_map/reduce_scatter | solution.py:345
  781.3 879.7 %reduce-scatter.11.cloned.1.call-start = ((), (), s32[]{:S(2)}) async-start(), calls=%async_computation.12 | async-start | bytes 14155776 | tf_op jit(solution)/shard_map/reduce_scatter | solution.py:344
  795.6 936.3 %reduce-scatter.19.cloned.1.call-start = ((), (), s32[]{:S(2)}) async-start(), calls=%async_computation.16 | async-start | bytes 2359296 | tf_op jit(solution)/shard_map/reduce_scatter | solution.py:348
  798.9 1004.5 %reduce-scatter.21.cloned.1.call-start = ((), (), s32[]{:S(2)}) async-start(), calls=%async_computation.17 | async-start | bytes 2359296 | tf_op jit(solution)/shard_map/reduce_scatter | solution.py:349
  802.7 1064.8 %reduce-scatter.15.cloned.1.call-start = ((), (), s32[]{:S(2)}) async-start(), calls=%async_computation.14 | async-start | bytes 147456 | tf_op jit(solution)/shard_map/reduce_scatter | solution.py:346
  805.5 1214.6 %reduce-scatter.23.cloned.1.call-start = ((), (), s32[]{:S(2)}) async-start(), calls=%async_computation.18 | async-start | bytes 9437184 | tf_op jit(solution)/shard_map/reduce_scatter | solution.py:352
  812.9 1329.0 %reduce-scatter.17.cloned.1.call-start = ((), (), s32[]{:S(2)}) async-start(), calls=%async_computation.15 | async-start | bytes 7077888 | tf_op jit(solution)/shard_map/reduce_scatter | solution.py:347
  820.1 24.1 %copy-start.44 = (bf16[512,512]{0,1:T(8,128)(2,1)S(1)}, bf16[512,512]{0,1:T(8,128)(2,1)}, u32[]{:S(2)}) copy-start(bf16[512,512]{0,1:T(8,128)(2,1)} %all-reduce.24) | copy-start | bytes 1572868
  825.6 25.4 %copy-start.76 = (f32[2048]{0:T(1024)S(1)}, f32[2048]{0:T(1024)}, u32[]{:S(2)}) copy-start(f32[2048]{0:T(1024)} %get-tuple-element.1048) | copy-start | bytes 24580
  825.6 25.4 %copy-start.81 = (f32[12]{0:T(128)S(1)}, f32[12]{0:T(128)}, u32[]{:S(2)}) copy-start(f32[12]{0:T(128)} %get-tuple-element.693) | copy-start | bytes 148
  825.6 67.1 %copy-start.83 = (f32[512]{0:T(512)S(1)}, f32[512]{0:T(512)}, u32[]{:S(2)}) copy-start(f32[512]{0:T(512)} %get-tuple-element.1168) | copy-start | bytes 6148
  1359.4 782.4 %copy-start.1 = (bf16[768,2048]{1,0:T(8,128)(2,1)S(1)}, bf16[768,2048]{1,0:T(8,128)(2,1)}, u32[]{:S(2)}) copy-start(bf16[768,2048]{1,0:T(8,128)(2,1)} %param.33) | copy-start | bytes 9437188
  (74 other events, 202.1 us)
Sparse Core Ops, SparseCore 0:
  16.1 30.6 all-gather.6
  48.3 62.9 all-gather.8
  195.9 84.1 all-reduce.14
  306.2 153.3 all-reduce.22
  482.4 44.0 reduce-scatter.8
  527.9 62.8 all-gather.10
  609.5 140.4 all-reduce.18
  752.3 91.8 all-reduce.16
  848.9 510.5 all-reduce.20
  1363.4 86.9 reduce-scatter.12
  1454.0 206.9 reduce-scatter.10
  1664.9 66.9 reduce-scatter.18
  1736.0 67.2 reduce-scatter.20
  1807.1 60.3 reduce-scatter.14
  1871.5 148.4 reduce-scatter.22
  2024.5 117.3 reduce-scatter.16
where the time goes:
time: 2160 us; the launch traced here: 2150 us
  waiting for transfers between devices  1600 us (74%)
  matrix products  186 us (9%)
  local copies, waits for them, and re-layouts  175 us (8%)
  blocking collectives  87 us (4%)
  other arithmetic  77.7 us (4%)
    unnamed x18, waiting for transfers between devices  460 us
    reduce_scatter x1, waiting for transfers between devices, body(): lax.psum_scatter(grad_ssm_in, ('dp', 'ctx'), scatter_dimension=0, tiled=T...  208 us
    psum x1, waiting for transfers between devices, body(): grad_normed_two = lax.psum(times_back(grad_gu, gu_matrix), 'tensor')  153 us
    reduce_scatter x1, waiting for transfers between devices, body(): lax.psum_scatter(grad_down, ('dp', 'ctx'), scatter_dimension=1, tiled=True)  153 us
    reduce_scatter x1, waiting for transfers between devices, body(): lax.psum_scatter(grad_ssm_out, ('dp', 'ctx'), scatter_dimension=1, tiled=...  122 us
    all_gather x2, waiting for transfers between devices, prefix(): pieces = jax.tree.map(lambda part: lax.all_gather(part, axis), value)  99.7 us
    reduce_scatter x1, waiting for transfers between devices, body(): lax.psum_scatter(grad_ssm_bc, ('dp', 'ctx'), scatter_dimension=0, tiled=T...  87.1 us
    psum x1, waiting for transfers between devices, body(): mixer_total = lax.psum(ssm_part + attn_part, 'tensor')  73.7 us
  transfers between devices with their start and end apart: 17, of which 14 were waited for; matrix products, arithmetic and copies ran while one was open for 13% of the time, Pallas kernels for 0%

commit v1 on v0

v1 whole, which is shorter than its diff:
```python
from functools import partial
import math

import jax
import jax.numpy as jnp
from jax import lax
from jax.sharding import PartitionSpec as P

KVHEADS = 2
AHEAD_DIM = 128
SCAN_BLOCK = 256
QBLOCK = 512


EPSILON = 1e-05
NEG_FILL = -1e30
PRECISE = lax.Precision.HIGHEST

CORE, CHIP = (1, 2)


def pairs_of(stride):
    return [(source, source ^ stride) for source in range(4)]


def partner(value, stride):
    return lax.ppermute(value, "tensor", pairs_of(stride))


def shifted(value, axis, shift):
    count = lax.axis_size(axis)
    return lax.ppermute(value, axis, [(i, (i + shift) % count) for i in range(count)])


def moved(value, axis, shift):
    count = lax.axis_size(axis)
    pairs = [(i, i + shift) for i in range(count) if 0 <= i + shift < count]
    return lax.ppermute(value, axis, pairs)


def cut(value, index, size, axis):
    return lax.dynamic_slice_in_dim(value, index * size, size, axis)


def paired_rows(mine, other, core):
    first = jnp.where(core == 0, mine, other)
    second = jnp.where(core == 0, other, mine)
    return jnp.concatenate([first, second], axis=0)


def gather_rows(mine, core):
    return paired_rows(mine, partner(mine, CORE), core)


def sum_rows(make, core):
    sent = partner(make(1 - core).astype(jnp.bfloat16), CORE)
    mine = (make(core) + sent.astype(jnp.float32)).astype(jnp.bfloat16)
    return mine.astype(jnp.float32) + partner(mine, CHIP).astype(jnp.float32)


def dp_columns(value, core):
    count, mine = (lax.axis_size("dp"), lax.axis_index("dp"))
    share = value.shape[1] // count
    half = value.shape[0] // 2
    pieces = [cut(value, mine, share, 1)]
    rows = cut(value, core, half, 0)
    for shift in range(1, count):
        sent = shifted(cut(rows, (mine + shift) % count, share, 1), "dp", shift)
        pieces.append(gather_rows(sent, core))
    return jnp.concatenate(pieces, axis=0)


def dp_rows(value):
    pieces = [value] + [shifted(value, "dp", shift) for shift in range(1, lax.axis_size("dp"))]
    return jnp.concatenate(pieces, axis=0)


def weight_grad(former, latter):
    local = inner_rows(former, latter).astype(jnp.bfloat16)
    return lax.psum_scatter(local, "ctx", scatter_dimension=0, tiled=True).astype(jnp.float32)


def all_sum(value, axis):
    count, mine = (lax.axis_size(axis), lax.axis_index(axis))
    pieces = jnp.stack([value] + [shifted(value, axis, shift) for shift in range(1, count)])
    total = jnp.zeros_like(value)
    for rank in range(count):
        total = total + lax.dynamic_index_in_dim(pieces, (mine - rank) % count, 0, keepdims=False)
    return total


def scatter_sum(value, axis):
    count, mine = (lax.axis_size(axis), lax.axis_index(axis))
    share = value.shape[0] // count
    total = cut(value, mine, share, 0)
    for shift in range(1, count):
        total = total + shifted(cut(value, (mine + shift) % count, share, 0), axis, shift)
    return total


def chained(state, log_decay, axis, direction):
    count = lax.axis_size(axis)
    total = jnp.zeros_like(state)
    between = jnp.zeros_like(log_decay)
    for shift in range(1, count):
        arrived = moved(state.astype(jnp.bfloat16), axis, direction * shift).astype(jnp.float32)
        total = total + arrived * jnp.exp(between)[:, None, None]
        between = between + moved(log_decay, axis, direction * shift)
    return total


def matmul_low(former, latter):
    return jnp.dot(former, latter, preferred_element_type=jnp.float32)


def inner_rows(former, latter):
    return lax.dot_general(
        former, latter, (((0,), (0,)), ((), ())), preferred_element_type=jnp.float32
    )


def times_back(former, latter):
    return lax.dot_general(
        former, latter, (((1,), (1,)), ((), ())), preferred_element_type=jnp.float32
    )


def round_keep(values):
    return lax.optimization_barrier(values.astype(jnp.bfloat16)).astype(jnp.float32)


def silu_slope(values):
    logistic = jax.nn.sigmoid(values)
    return logistic * (1.0 + values * (1.0 - logistic))


def norm_back(grad_normed, source, scale_rows, gain):
    weighted = grad_normed * gain
    cubed = scale_rows * scale_rows * scale_rows
    grad_source = scale_rows * weighted - source * cubed * jnp.mean(
        weighted * source, axis=-1, keepdims=True
    )
    grad_gain = jnp.sum(grad_normed * source * scale_rows, axis=0)
    return (grad_source, grad_gain)


def ssd_block(states, pieces, decay_rate, skip_gain):
    source_block, write_block, read_block, step_block = pieces
    increments = step_block * decay_rate
    running = jnp.cumsum(increments, axis=0)
    block_len = increments.shape[0]
    lower_mask = (
        jnp.arange(block_len, dtype=jnp.int32)[:, None]
        >= jnp.arange(block_len, dtype=jnp.int32)[None, :]
    )
    differences = running[:, None, :] - running[None, :, :]
    decays = jnp.exp(jnp.where(lower_mask[:, :, None], differences, NEG_FILL))
    intersection = jnp.dot(read_block, write_block.T, precision=PRECISE)
    mixing = decays * intersection[:, :, None] * step_block[None, :, :]
    within = jnp.einsum("tsh,shp->thp", mixing, source_block, precision=PRECISE)
    carried = (
        jnp.einsum("tn,hpn->thp", read_block, states, precision=PRECISE)
        * jnp.exp(running)[:, :, None]
    )
    result = within + carried + skip_gain[None, :, None] * source_block
    tailing = jnp.exp(running[-1][None, :] - running) * step_block
    incoming = jnp.einsum("sh,shp,sn->hpn", tailing, source_block, write_block, precision=PRECISE)
    states = states * jnp.exp(running[-1])[:, None, None] + incoming
    return (states, result)


def run_ssd(source_heads, write_rows, read_rows, step_rows, a_log, d_skip, entering, block_len):
    row_total = source_heads.shape[0]
    block_count = row_total // block_len
    decay_rate = -jnp.exp(a_log)

    def blocked(source):
        return source.reshape((block_count, block_len) + source.shape[1:])

    def stepper(states, pieces):
        return ssd_block(states, pieces, decay_rate, d_skip)

    closing, outputs = lax.scan(
        jax.checkpoint(stepper),
        entering,
        (blocked(source_heads), blocked(write_rows), blocked(read_rows), blocked(step_rows)),
    )
    return (outputs.reshape(source_heads.shape), closing)


def body(
    hidden,
    cotangent,
    norm1_gain,
    ssm_in,
    ssm_bc,
    ssm_dt,
    dt_bias,
    a_log,
    d_skip,
    ssm_out,
    attn_q,
    attn_kv,
    attn_out,
    norm2_gain,
    mlp_gate_up,
    mlp_down,
):
    ctx_rank = lax.axis_index("ctx")
    ctx_count = lax.axis_size("ctx")
    tensor_rank = lax.axis_index("tensor")
    core = tensor_rank % 2
    chip = tensor_rank // 2
    hidden_rows = hidden[0]
    grad_low = cotangent[0]
    source = hidden_rows.astype(jnp.float32)
    tokens = source.shape[0]
    half = tokens // 2
    model_width = source.shape[1]
    inner_local = ssm_in.shape[2]
    heads_local = ssm_dt.shape[1]
    head_width = inner_local // heads_local
    state_width = ssm_bc.shape[2]
    in_matrix = ssm_in.reshape(model_width, 2 * inner_local)
    bc_matrix = ssm_bc.reshape(model_width, 2 * state_width)
    bc_share = 2 * state_width // 4
    bc_columns = cut(bc_matrix, tensor_rank, bc_share, 1)
    heads_query = attn_q.shape[1] // AHEAD_DIM
    kv_pair = cut(attn_kv, chip, AHEAD_DIM, 2)
    kv_matrix = kv_pair.reshape(model_width, 2 * AHEAD_DIM)
    kv_columns = lax.dynamic_index_in_dim(kv_pair, core, 1, keepdims=False)
    ff_local = mlp_down.shape[0]
    gu_matrix = mlp_gate_up.reshape(model_width, 2 * ff_local)
    factor = 1.0 / math.sqrt(AHEAD_DIM)

    scale_one = lax.rsqrt(jnp.mean(source * source, axis=-1, keepdims=True) + EPSILON)
    input_one = (source * scale_one * norm1_gain).astype(jnp.bfloat16)

    key_value = matmul_low(input_one, kv_matrix).astype(jnp.bfloat16)
    kv_sent = cut(key_value, core, AHEAD_DIM, 1)
    kv_got = [kv_sent] + [moved(kv_sent, "ctx", shift) for shift in range(1, ctx_count)]
    kv_mine = jnp.concatenate(kv_got, axis=0)
    kv_other = partner(kv_mine, CORE)
    key_rows = jnp.where(core == 0, kv_mine, kv_other)
    value_rows = jnp.where(core == 0, kv_other, kv_mine)

    cot_columns = dp_columns(grad_low, core)
    one_columns = dp_columns(input_one, core)

    zx_proj = matmul_low(input_one, in_matrix)
    gate_ssm = zx_proj[:, :inner_local]
    source_heads = round_keep(zx_proj[:, inner_local:]).reshape(tokens, heads_local, head_width)
    bc_rows = round_keep(matmul_low(input_one, bc_matrix))
    write_rows = bc_rows[:, :state_width]
    read_rows = bc_rows[:, state_width:]
    dt_pre = matmul_low(input_one, ssm_dt) + dt_bias
    dt_rows = jax.nn.softplus(dt_pre)
    decay_rate = -jnp.exp(a_log)
    running = jnp.cumsum(dt_rows * decay_rate, axis=0)
    to_end = jnp.exp(running[-1][None, :] - running) * dt_rows
    own_state = jnp.einsum("th,thp,tn->hpn", to_end, source_heads, write_rows, precision=PRECISE)
    entering = chained(own_state, running[-1], "ctx", 1)
    ssm_pair, ssm_back = jax.vjp(
        partial(run_ssd, block_len=SCAN_BLOCK),
        source_heads,
        write_rows,
        read_rows,
        dt_rows,
        a_log,
        d_skip,
        entering,
    )
    ssm_values = ssm_pair[0].reshape(tokens, inner_local)
    gate_act = jax.nn.silu(gate_ssm)
    gated_rows = (ssm_values * gate_act).astype(jnp.bfloat16)

    queries = matmul_low(input_one, attn_q).astype(jnp.bfloat16)
    query_rows = queries.reshape(tokens, heads_query, AHEAD_DIM)
    row_place = jnp.arange(tokens, dtype=jnp.int32)
    key_block = jnp.arange(ctx_count * tokens, dtype=jnp.int32) // tokens
    key_place = jnp.arange(ctx_count * tokens, dtype=jnp.int32) % tokens
    allowed = jnp.where(
        key_block[None, :] == 0,
        key_place[None, :] <= row_place[:, None],
        key_block[None, :] <= ctx_rank,
    )
    scores = (
        jnp.einsum("qhd,kd->hqk", query_rows, key_rows, preferred_element_type=jnp.float32) * factor
    )
    masked = jnp.where(allowed[None], scores, NEG_FILL)
    maxima = jnp.max(masked, axis=-1, keepdims=True)
    weights = jnp.exp(masked - maxima)
    probability = weights / jnp.sum(weights, axis=-1, keepdims=True)
    prob_low = probability.astype(jnp.bfloat16)
    mixed_rows = jnp.einsum("hqk,kd->qhd", prob_low, value_rows, preferred_element_type=jnp.float32)
    attended = mixed_rows.reshape(tokens, heads_query * AHEAD_DIM).astype(jnp.bfloat16)

    def mixer_share(index):
        return matmul_low(cut(gated_rows, index, half, 0), ssm_out) + matmul_low(
            cut(attended, index, half, 0), attn_out
        )

    mixer_total = sum_rows(mixer_share, core)
    middle = cut(hidden_rows, core, half, 0).astype(jnp.float32) + mixer_total
    scale_two = lax.rsqrt(jnp.mean(middle * middle, axis=-1, keepdims=True) + EPSILON)
    two_mine = (middle * scale_two * norm2_gain).astype(jnp.bfloat16)
    input_two = gather_rows(two_mine, core)
    gate_up = matmul_low(input_two, gu_matrix)
    gate_rows = gate_up[:, :ff_local]
    up_rows = gate_up[:, ff_local:]
    gate_silu = jax.nn.silu(gate_rows)
    activated = (gate_silu * up_rows).astype(jnp.bfloat16)
    grad_act = times_back(grad_low, mlp_down)
    grad_gu = jnp.concatenate(
        [grad_act * up_rows * silu_slope(gate_rows), grad_act * gate_silu], axis=1
    ).astype(jnp.bfloat16)
    grad_normed_two = sum_rows(lambda index: times_back(cut(grad_gu, index, half, 0), gu_matrix), core)

    mlp_total = sum_rows(lambda index: matmul_low(cut(activated, index, half, 0), mlp_down), core)
    block_out = middle + mlp_total
    output = gather_rows(block_out.astype(jnp.bfloat16), core)
    squares = jnp.stack(
        [
            jnp.sum(mixer_total * mixer_total),
            jnp.sum(mlp_total * mlp_total),
            jnp.sum(block_out * block_out),
        ]
    )
    two_columns = dp_columns(input_two, core)
    grad_gate_up = weight_grad(two_columns, dp_rows(grad_gu))
    grad_down = weight_grad(cot_columns, dp_rows(activated))

    grad_middle, grad_gain_two = norm_back(grad_normed_two, middle, scale_two, norm2_gain)
    grad_middle = cut(grad_low, core, half, 0).astype(jnp.float32) + grad_middle
    grad_mix = gather_rows(grad_middle.astype(jnp.bfloat16), core)
    mix_columns = dp_columns(grad_mix, core)
    grad_outs = weight_grad(
        mix_columns, dp_rows(jnp.concatenate([gated_rows, attended], axis=1))
    )
    grad_gated = times_back(grad_mix, ssm_out)
    grad_values = round_keep(grad_gated * gate_act).reshape(tokens, heads_local, head_width)
    grad_gate_ssm = (grad_gated * ssm_values * silu_slope(gate_ssm)).astype(jnp.bfloat16)
    grad_attended = times_back(grad_mix, attn_out).astype(jnp.bfloat16)
    from_start = jnp.exp(running)
    own_grad = jnp.einsum("th,thp,tn->hpn", from_start, grad_values, read_rows, precision=PRECISE)
    leaving = chained(own_grad, running[-1], "ctx", -1)

    grad_rows = grad_attended.reshape(tokens, heads_query, AHEAD_DIM)
    grad_value = jnp.einsum("hqk,qhd->kd", prob_low, grad_rows, preferred_element_type=jnp.float32)
    grad_prob = jnp.einsum("qhd,kd->hqk", grad_rows, value_rows, preferred_element_type=jnp.float32)
    centre = jnp.sum(probability * grad_prob, axis=-1, keepdims=True)
    grad_score = (probability * (grad_prob - centre)).astype(jnp.bfloat16)
    grad_query = (
        jnp.einsum("hqk,kd->qhd", grad_score, key_rows, preferred_element_type=jnp.float32) * factor
    )
    grad_query_low = grad_query.reshape(tokens, heads_query * AHEAD_DIM).astype(jnp.bfloat16)
    grad_key = (
        jnp.einsum("hqk,qhd->kd", grad_score, query_rows, preferred_element_type=jnp.float32) * factor
    )
    kv_kept = jnp.where(core == 0, grad_key, grad_value)
    kv_given = jnp.where(core == 0, grad_value, grad_key).astype(jnp.bfloat16)
    kv_paired = (kv_kept + partner(kv_given, CORE).astype(jnp.float32)).reshape(
        ctx_count, tokens, AHEAD_DIM
    )
    kv_sum = kv_paired[0]
    for shift in range(1, ctx_count):
        kv_sum = kv_sum + moved(kv_paired[shift].astype(jnp.bfloat16), "ctx", -shift).astype(
            jnp.float32
        )
    grad_kv_low = kv_sum.astype(jnp.bfloat16)

    ssm_grads = ssm_back((grad_values, leaving))
    grad_dt_pre = ssm_grads[3] * jax.nn.sigmoid(dt_pre)
    grad_dt_bias = jnp.sum(grad_dt_pre, axis=0)
    grad_dt_low = grad_dt_pre.astype(jnp.bfloat16)
    grad_source_low = ssm_grads[0].reshape(tokens, inner_local).astype(jnp.bfloat16)
    grad_bc = jnp.concatenate([ssm_grads[1], ssm_grads[2]], axis=1)
    bc_pair = 2 * bc_share
    bc_sent = partner(cut(grad_bc, 1 - chip, bc_pair, 1).astype(jnp.bfloat16), CHIP)
    bc_mine = cut(grad_bc, chip, bc_pair, 1) + bc_sent.astype(jnp.float32)
    bc_given = partner(cut(bc_mine, 1 - core, bc_share, 1).astype(jnp.bfloat16), CORE)
    grad_bc_low = (cut(bc_mine, core, bc_share, 1) + bc_given.astype(jnp.float32)).astype(jnp.bfloat16)

    pad = -heads_local % AHEAD_DIM
    grad_all = jnp.concatenate(
        [
            grad_gate_ssm,
            grad_source_low,
            grad_query_low,
            grad_kv_low,
            grad_bc_low,
            jnp.pad(grad_dt_low, ((0, 0), (0, pad))),
        ],
        axis=1,
    )
    weight_all = jnp.concatenate(
        [in_matrix, attn_q, kv_columns, bc_columns, jnp.pad(ssm_dt, ((0, 0), (0, pad)))], axis=1
    )
    grad_normed_one = sum_rows(lambda index: times_back(cut(grad_all, index, half, 0), weight_all), core)
    source_mine = cut(hidden_rows, core, half, 0).astype(jnp.float32)
    grad_source, grad_gain_one = norm_back(
        grad_normed_one, source_mine, cut(scale_one, core, half, 0), norm1_gain
    )
    grad_hidden = gather_rows((grad_middle + grad_source).astype(jnp.bfloat16), core)
    grad_ins = weight_grad(one_columns, dp_rows(grad_all))

    at = 2 * inner_local
    grad_ssm_in = grad_ins[:, :at].reshape(-1, 2, inner_local)
    grad_attn_q = grad_ins[:, at : at + heads_query * AHEAD_DIM]
    at = at + heads_query * AHEAD_DIM
    kv_part = grad_ins[:, at : at + AHEAD_DIM]
    at = at + AHEAD_DIM
    bc_part = grad_ins[:, at : at + bc_share]
    at = at + bc_share
    grad_ssm_dt = grad_ins[:, at : at + heads_local]

    share = kv_part.shape[0] // 4
    blocks = [cut(kv_part, tensor_rank, share, 0)]
    for stride in range(1, 4):
        blocks.append(partner(cut(kv_part, tensor_rank ^ stride, share, 0), stride))
    blocks = jnp.stack(blocks)

    def of_rank(pieces, rank):
        return lax.dynamic_index_in_dim(pieces, tensor_rank ^ rank, 0, keepdims=False)

    grad_attn_kv = jnp.stack(
        [
            jnp.concatenate([of_rank(blocks, kind), of_rank(blocks, 2 + kind)], axis=1)
            for kind in range(2)
        ],
        axis=1,
    )
    bc_blocks = jnp.stack([bc_part] + [partner(bc_part, stride) for stride in range(1, 4)])
    grad_ssm_bc = jnp.concatenate([of_rank(bc_blocks, rank) for rank in range(4)], axis=1).reshape(
        -1, 2, state_width
    )

    both = jnp.concatenate([grad_gain_one, grad_gain_two, jnp.pad(squares, (0, 125))])
    both = both + partner(both, CORE)
    gains = scatter_sum(
        scatter_sum(jnp.stack([both[:model_width], both[model_width : 2 * model_width]], axis=1), "dp"),
        "ctx",
    )
    small = jnp.concatenate(
        [
            grad_dt_bias,
            ssm_grads[4],
            ssm_grads[5],
            both[2 * model_width : 2 * model_width + 3],
        ]
    )
    small = all_sum(all_sum(small, "dp"), "ctx")
    counted = tokens * model_width * lax.axis_size("dp") * ctx_count
    branch_rms = jnp.sqrt(small[3 * heads_local :] / counted)
    return (
        output[None],
        grad_hidden[None],
        gains[:, 0],
        grad_ssm_in,
        grad_ssm_bc,
        grad_ssm_dt,
        small[:heads_local],
        small[heads_local : 2 * heads_local],
        small[2 * heads_local : 3 * heads_local],
        grad_outs[:, :inner_local].T,
        grad_attn_q,
        grad_attn_kv,
        grad_outs[:, inner_local:].T,
        gains[:, 1],
        grad_gate_up.reshape(-1, 2, ff_local),
        grad_down.T,
        branch_rms,
    )


def solution(mesh):
    return jax.shard_map(
        body,
        mesh=mesh,
        in_specs=(
            P("dp", "ctx", None),
            P("dp", "ctx", None),
            P(),
            P(None, None, "tensor"),
            P(),
            P(None, "tensor"),
            P("tensor"),
            P("tensor"),
            P("tensor"),
            P("tensor", None),
            P(None, "tensor"),
            P(),
            P("tensor", None),
            P(),
            P(None, None, "tensor"),
            P("tensor", None),
        ),
        out_specs=(
            P("dp", "ctx", None),
            P("dp", "ctx", None),
            P(("dp", "ctx")),
            P(("dp", "ctx"), None, "tensor"),
            P(("dp", "ctx"), None, None),
            P(("dp", "ctx"), "tensor"),
            P("tensor"),
            P("tensor"),
            P("tensor"),
            P("tensor", ("dp", "ctx")),
            P(("dp", "ctx"), "tensor"),
            P(("dp", "ctx", "tensor"), None, None),
            P("tensor", ("dp", "ctx")),
            P(("dp", "ctx")),
            P(("dp", "ctx"), None, "tensor"),
            P("tensor", ("dp", "ctx")),
            P(),
        ),
        check_vma=False,
    )
```

time: 2160 us -> 854 us (0.40)
  waiting for transfers between devices: 1600 us -> 342 us
  blocking collectives: 87 us -> 0 us
  starting transfers between devices: 1.29 us -> 63.6 us
    reduce_scatter x8 -> x4, waiting for transfers between devices: 798 us -> 1.04 us  [weight_grad(): lax.psum_scatter(local, 'ctx', scatter_dimension=0, tiled=True)]
    unnamed x18 -> x4, waiting for transfers between devices: 460 us -> 0.07 us
    ppermute x1 -> x59, waiting for transfers between devices: 0.01 us -> 341 us  [the longest x16 167 us: shifted(): lax.ppermute(value, axis, [(i, (i + shift) % count) for i in range(count)])]
    psum x3 -> x0, waiting for transfers between devices: 246 us -> none  [the longest x1 153 us: body(): grad_normed_two = lax.psum(times_back(grad_gu, gu_matrix), 'tensor')]
    all_gather x3 -> x0, waiting for transfers between devices: 99.7 us -> none  [the longest x2 99.7 us: prefix(): pieces = jax.tree.map(lambda part: lax.all_gather(part, axis), value)]
    ppermute x1 -> x59, starting transfers between devices: 0.01 us -> 63.4 us  [the longest x16 31.4 us: moved(): return lax.ppermute(value, axis, pairs)]
    unnamed x1 -> x0, blocking collectives: 39.9 us -> none
    psum x1 -> x0, blocking collectives: 34.1 us -> none  [body(): lax.psum((input_terms, jnp.concatenate([ssm_grads[1], ssm_grads[2]], axis...]
  transfers between devices with their start and end apart: 17 -> 63, of which waited for: 14 -> 31; matrix products, arithmetic and copies ran while one was open for 13% -> 42% of each run, Pallas kernels for 0% -> 0%
where the time goes in v1:
time: 854 us; the launch traced here: 846 us
  waiting for transfers between devices  342 us (40%)
  matrix products  175 us (20%)
  local copies, waits for them, and re-layouts  154 us (18%)
  other arithmetic  93.2 us (11%)
  starting transfers between devices  63.6 us (7%)
  between operations  15.7 us (2%)
    ppermute x16, waiting for transfers between devices, shifted(): lax.ppermute(value, axis, [(i, (i + shift) % count) for i in range(count)])  167 us
    ppermute x16, waiting for transfers between devices, moved(): return lax.ppermute(value, axis, pairs)  101 us
    ppermute x27, waiting for transfers between devices, partner(): return lax.ppermute(value, 'tensor', pairs_of(stride))  73.1 us
    unnamed x180, local copies, waits for them, and re-layouts  45.6 us
    dynamic_update_slice x10, local copies, waits for them, and re-layouts, run_ssd(): lax.scan(jax.checkpoint(stepper), entering, (blocked(source_heads), block...  41.5 us
    dot_general x12, matrix products, matmul_low(): return jnp.dot(former, latter, preferred_element_type=jnp.float32)  33.8 us
    ppermute x16, starting transfers between devices, moved(): return lax.ppermute(value, axis, pairs)  31.4 us
    dot_general x7, matrix products, times_back(): lax.dot_general(former, latter, (((1,), (1,)), ((), ())), preferred_eleme...  30.6 us
  transfers between devices with their start and end apart: 63, of which 31 were waited for; matrix products, arithmetic and copies ran while one was open for 42% of the time, Pallas kernels for 0%

profile of v1, /device:TPU:0, one launch (start us, length us, event | category | flops | bytes accessed | tf_op | source)
XLA Modules:
  0.0 846.0 jit_solution(14171580559591078586)
XLA Ops:
  15.0 5.1 collective-permute-start.5
  20.0 5.2 collective-permute-start.6
  37.4 3.3 convolution_convert_fusion.5
  40.7 4.3 copy.319
  45.0 3.4 fusion.310
  63.5 3.1 reshape.502
  67.2 2.8 copy.238
  76.8 4.4 collective-permute-done
  81.2 8.5 %collective-permute-done.1 = bf16[12,64,256]{2,1,0:T(8,128)(2,1)S(1)} collective-permute-done((bf16[12,64,256]{2,1,0:T(8,128)(2,1)}, bf16[12,64,256]{2,1,0:T(8,128)(2,1)S(1)}, u32[]{:S(2)}, u32[]{:S(2)}) %collective-permute-start.1) | collective-permute-done | bytes 393248 | tf_op jit(solution)/shard_map/ppermute | solution.py:38
  89.7 7.0 collective-permute-done.3
  97.8 66.0 %while.43 = (s32[]{:T(128)}, f32[12,64,256]{2,1,0:T(8,128)}, f32[2,256,12,64]{1,0,3,2:T(2,128)}, f32[2,12,64,256]{3,2,1,0:T(8,128)}, f32[2,256,12]{1,2,0:T(8,128...) while((s32[]{:T(128)}, f32[12,64,256]{2,1,0:T(8,128)}, ...), condition=%wide.region_6.7_spmd.clone, body=%wide.region_3.6_spmd.clone.sunk | while | flops 2018190336 | bytes 26372288 | solution.py:183
  103.4 3.7 fusion.413
  108.7 16.8 %dynamic_update_slice.67 = f32[2,256,12,64]{1,0,3,2:T(2,128)} dynamic-update-slice(f32[2,256,12,64]{1,0,3,2:T(2,128)} %get-tuple-element.1160, f32[1,256,12,64]{1,0,3,2:T(1,128)} %copy.351, s32[]{:T(128)} %get-tuple-element.1158, s32[]{:T(128)} %constant.357.clone.1..sunk, s32[]{:T(128)} %constant.357.clone.1..sunk, s32[]{:T(128)} %constant.357.clone.1..sunk) | dynamic-update-slice | bytes 1572868 | tf_op jit(solution)/shard_map/jvp()/while/body/jit(dynamic_update_index_in_dim)/dynamic_update_slice | solution.py:183
  127.7 2.9 convolution_add_fusion.9
  136.2 3.7 fusion.413
  141.5 16.8 %dynamic_update_slice.67 = f32[2,256,12,64]{1,0,3,2:T(2,128)} dynamic-update-slice(f32[2,256,12,64]{1,0,3,2:T(2,128)} %get-tuple-element.1160, f32[1,256,12,64]{1,0,3,2:T(1,128)} %copy.351, s32[]{:T(128)} %get-tuple-element.1158, s32[]{:T(128)} %constant.357.clone.1..sunk, s32[]{:T(128)} %constant.357.clone.1..sunk, s32[]{:T(128)} %constant.357.clone.1..sunk) | dynamic-update-slice | bytes 1572868 | tf_op jit(solution)/shard_map/jvp()/while/body/jit(dynamic_update_index_in_dim)/dynamic_update_slice | solution.py:183
  160.5 2.9 convolution_add_fusion.9
  166.5 3.0 copy.240
  169.5 3.2 multiply_convert_fusion.6
  174.6 8.1 fusion.322
  182.8 5.1 fusion.195
  199.8 23.7 %collective-permute-done.10 = bf16[256,2048]{1,0:T(8,128)(2,1)S(1)} collective-permute-done((bf16[256,2048]{1,0:T(8,128)(2,1)S(1)}, bf16[256,2048]{1,0:T(8,128)(2,1)S(1)}, u32[]{:S(2)}, u32[]{:S(2)}) %collective-permute-start.10) | collective-permute-done | bytes 1048608 | tf_op jit(solution)/shard_map/ppermute | solution.py:27
  229.3 10.4 %copy.323 = bf16[256,8,2,1024]{3,1,2,0:T(8,128)(2,1)} copy(bf16[256,8,2,1024]{3,2,1,0:T(2,128)(2,1)} %bitcast.543) | data formatting | bytes 16777216
  243.5 7.1 fusion.124
  250.6 4.1 multiply_convert_fusion
  262.4 12.9 %collective-permute-done.56 = bf16[256,1024]{1,0:T(8,128)(2,1)} collective-permute-done((bf16[256,1024]{1,0:T(8,128)(2,1)S(1)}, bf16[256,1024]{1,0:T(8,128)(2,1)}, u32[]{:S(2)}, u32[]{:S(2)}) %collective-permute-start.56) | collective-permute-done | bytes 524320 | tf_op jit(solution)/shard_map/ppermute | solution.py:32
  276.8 3.3 add_convert_fusion.2
  281.7 3.4 add_convert_fusion.1
  288.2 12.9 %collective-permute-done.58 = bf16[512,1024]{1,0:T(8,128)(2,1)} collective-permute-done((bf16[512,1024]{1,0:T(8,128)(2,1)}, bf16[512,1024]{1,0:T(8,128)(2,1)}, u32[]{:S(2)}, u32[]{:S(2)}) %collective-permute-start.58) | collective-permute-done | bytes 1048608 | tf_op jit(solution)/shard_map/ppermute | solution.py:32
  301.2 5.5 fusion.172
  306.8 21.5 %collective-permute-done.16 = bf16[256,2048]{1,0:T(8,128)(2,1)} collective-permute-done((bf16[256,2048]{1,0:T(8,128)(2,1)}, bf16[256,2048]{1,0:T(8,128)(2,1)}, u32[]{:S(2)}, u32[]{:S(2)}) %collective-permute-start.16) | collective-permute-done | bytes 1048608 | tf_op jit(solution)/shard_map/ppermute | solution.py:27
  328.2 5.6 multiply_reduce_fusion.7
  333.8 4.3 fusion.314
  344.3 12.5 %collective-permute-done.47 = bf16[256,1024]{1,0:T(8,128)(2,1)S(1)} collective-permute-done((bf16[256,1024]{1,0:T(8,128)(2,1)S(1)}, bf16[256,1024]{1,0:T(8,128)(2,1)S(1)}, u32[]{:S(2)}, u32[]{:S(2)}) %collective-permute-start.47) | collective-permute-done | bytes 524320 | tf_op jit(solution)/shard_map/ppermute | solution.py:32
  358.8 19.7 %collective-permute-done.49 = bf16[512,1024]{1,0:T(8,128)(2,1)S(1)} collective-permute-done((bf16[512,1024]{1,0:T(8,128)(2,1)S(1)}, bf16[512,1024]{1,0:T(8,128)(2,1)S(1)}, u32[]{:S(2)}, u32[]{:S(2)}) %collective-permute-start.49) | collective-permute-done | bytes 1048608 | tf_op jit(solution)/shard_map/ppermute | solution.py:32
  378.5 3.8 fusion.177
  382.4 3.3 pad_maximum_fusion.1
  388.7 55.3 %collective-permute-done.53 = bf16[256,1024]{1,0:T(8,128)(2,1)} collective-permute-done((bf16[256,1024]{1,0:T(8,128)(2,1)S(1)}, bf16[256,1024]{1,0:T(8,128)(2,1)}, u32[]{:S(2)}, u32[]{:S(2)}) %collective-permute-start.53) | collective-permute-done | bytes 524320 | tf_op jit(solution)/shard_map/ppermute | solution.py:32
  447.1 8.6 %collective-permute-done.20 = f32[12]{0:T(128)S(1)} collective-permute-done((f32[12]{0:T(128)S(1)}, f32[12]{0:T(128)S(1)}, u32[]{:S(2)}, u32[]{:S(2)}) %collective-permute-start.20) | collective-permute-done | bytes 80 | tf_op jit(solution)/shard_map/ppermute | solution.py:38
  461.2 8.2 fusion.119
  469.4 5.7 fusion.222
  484.7 5.0 fusion.95
  500.8 3.0 fusion.198
  504.7 2.9 collective-permute-done.18
  507.6 56.2 %collective-permute-done.19 = bf16[12,64,256]{2,1,0:T(8,128)(2,1)} collective-permute-done((bf16[12,64,256]{2,1,0:T(8,128)(2,1)}, bf16[12,64,256]{2,1,0:T(8,128)(2,1)}, u32[]{:S(2)}, u32[]{:S(2)}) %collective-permute-start.19) | collective-permute-done | bytes 393248 | tf_op jit(solution)/shard_map/ppermute | solution.py:38
  568.4 77.4 %while.44 = (s32[]{:T(128)}, f32[12]{0:T(128)}, f32[12]{0:T(128)}, f32[12,64,256]{2,1,0:T(8,128)S(1)}, bf16[2,256,12,64]{1,3,2,0:T(8,128)(2,1)}, /*index=5*/f32[...) while((s32[]{:T(128)}, f32[12]{0:T(128)}, f32[12]{0:T(128)}, ...), condition=%wide.region_25.26_spmd.clone, body=%wide.region_11.25_spmd.clone.sunk | while | flops 4849516544 | bytes 70007096 | solution.py:183
  582.3 5.5 fusion.433
  589.9 3.2 reduce-window.90
  602.1 3.1 fusion.439
  620.7 5.5 fusion.433
  628.3 3.2 reduce-window.90
  640.5 3.1 fusion.439
  658.7 4.3 collective-permute-done.24
  663.1 6.2 collective-permute-done.25
  674.6 3.2 constant_dynamic-update-slice_fusion.3
  677.8 3.9 constant_dynamic-slice_fusion.15
  682.8 47.2 %collective-permute-done.37 = bf16[256,1024]{1,0:T(8,128)(2,1)} collective-permute-done((bf16[256,1024]{1,0:T(8,128)(2,1)}, bf16[256,1024]{1,0:T(8,128)(2,1)}, u32[]{:S(2)}, u32[]{:S(2)}) %collective-permute-start.37) | collective-permute-done | bytes 524320 | tf_op jit(solution)/shard_map/ppermute | solution.py:32
  734.7 8.4 convolution_convert_fusion
  744.1 7.4 convolution_convert_fusion.2
  754.5 6.8 add_convert_fusion
  768.6 18.3 %collective-permute-done.30 = bf16[256,2048]{1,0:T(8,128)(2,1)} collective-permute-done((bf16[256,2048]{1,0:T(8,128)(2,1)S(1)}, bf16[256,2048]{1,0:T(8,128)(2,1)}, u32[]{:S(2)}, u32[]{:S(2)}) %collective-permute-start.30) | collective-permute-done | bytes 1048608 | tf_op jit(solution)/shard_map/ppermute | solution.py:27
  795.4 3.7 collective-permute-start.46
  815.9 4.1 reshape.507
  832.2 3.8 collective-permute-done.42
  (682 shorter events, 275.3 us)
Async XLA Ops:
  7.2 183.6 %copy-start = (bf16[768,2048]{1,0:T(8,128)(2,1)S(1)}, bf16[768,2048]{1,0:T(8,128)(2,1)}, u32[]{:S(2)}) copy-start(bf16[768,2048]{1,0:T(8,128)(2,1)} %param.29) | copy-start | bytes 9437188
  7.2 756.6 %reduce-scatter.11.cloned.1.call-start = ((), (), s32[]{:S(2)}) async-start(), calls=%async_computation.7 | async-start | bytes 2621440 | tf_op jit(solution)/shard_map/reduce_scatter | solution.py:80
  15.0 57.7 %collective-permute-start.5 = (bf16[512,128]{1,0:T(8,128)(2,1)S(1)}, bf16[512,128]{1,0:T(8,128)(2,1)S(1)}, u32[]{:S(2)}, u32[]{:S(2)}) collective-permute-start(bf16[512,128]{1,0:T(8,128)(2,1)S(1)} %dynamic-slice_convert_fusion), channel_id=1, source_target_pairs={{0,4},{4,8},{8,12},{1,5},{5,9},{9,13},{2,6},{6,10},{10,14},{3,7},{... | collective-permute-start | bytes 393224 | tf_op jit(solution)/shard_map/ppermute | solution.py:38
  20.0 54.9 %collective-permute-start.6 = (bf16[512,128]{1,0:T(8,128)(2,1)S(1)}, bf16[512,128]{1,0:T(8,128)(2,1)}, u32[]{:S(2)}, u32[]{:S(2)}) collective-permute-start(bf16[512,128]{1,0:T(8,128)(2,1)S(1)} %dynamic-slice_convert_fusion), channel_id=1, source_target_pairs={{0,8},{4,12},{1,9},{5,13},{2,10},{6,14},{3,11},{7,15},{16,24},{20,... | collective-permute-start | bytes 393224 | tf_op jit(solution)/shard_map/ppermute | solution.py:38
  25.2 49.8 %collective-permute-start.7 = (bf16[512,128]{1,0:T(8,128)(2,1)S(1)}, bf16[512,128]{1,0:T(8,128)(2,1)}, u32[]{:S(2)}, u32[]{:S(2)}) collective-permute-start(bf16[512,128]{1,0:T(8,128)(2,1)S(1)} %dynamic-slice_convert_fusion), channel_id=1, source_target_pairs={{0,12},{1,13},{2,14},{3,15},{16,28},{17,29},{18,30},{19,31}} | collective-permute-start | bytes 393224 | tf_op jit(solution)/shard_map/ppermute | solution.py:38
  33.5 36.6 %collective-permute-start.2 = (f32[12]{0:T(128)S(1)}, f32[12]{0:T(128)}, u32[]{:S(2)}, u32[]{:S(2)}) collective-permute-start(f32[12]{0:T(128)S(1)} %slice_reduce_fusion.6), channel_id=1, source_target_pairs={{0,4},{4,8},{8,12},{1,5},{5,9},{9,13},{2,6},{6,10},{10,14},{3,7},{... | collective-permute-start | bytes 152 | tf_op jit(solution)/shard_map/ppermute | solution.py:38
  35.3 36.0 %collective-permute-start.4 = (f32[12]{0:T(128)S(1)}, f32[12]{0:T(128)}, u32[]{:S(2)}, u32[]{:S(2)}) collective-permute-start(f32[12]{0:T(128)S(1)} %slice_reduce_fusion.6), channel_id=1, source_target_pairs={{0,8},{4,12},{1,9},{5,13},{2,10},{6,14},{3,11},{7,15},{16,24},{20,... | collective-permute-start | bytes 152 | tf_op jit(solution)/shard_map/ppermute | solution.py:38
  70.0 11.2 %collective-permute-start = (bf16[12,64,256]{2,1,0:T(8,128)(2,1)}, bf16[12,64,256]{2,1,0:T(8,128)(2,1)S(1)}, u32[]{:S(2)}, u32[]{:S(2)}) collective-permute-start(bf16[12,64,256]{2,1,0:T(8,128)(2,1)} %fusion.189), channel_id=1, source_target_pairs={{0,4},{4,8},{8,12},{1,5},{5,9},{9,13},{2,6},{6,10},{10,14},{3,7},{... | collective-permute-start | bytes 1179656 | tf_op jit(solution)/shard_map/ppermute | solution.py:38
  71.4 18.3 %collective-permute-start.1 = (bf16[12,64,256]{2,1,0:T(8,128)(2,1)}, bf16[12,64,256]{2,1,0:T(8,128)(2,1)S(1)}, u32[]{:S(2)}, u32[]{:S(2)}) collective-permute-start(bf16[12,64,256]{2,1,0:T(8,128)(2,1)} %fusion.189), channel_id=1, source_target_pairs={{0,8},{4,12},{1,9},{5,13},{2,10},{6,14},{3,11},{7,15},{16,24},{20,... | collective-permute-start | bytes 1179656 | tf_op jit(solution)/shard_map/ppermute | solution.py:38
  72.7 23.9 %collective-permute-start.3 = (bf16[12,64,256]{2,1,0:T(8,128)(2,1)}, bf16[12,64,256]{2,1,0:T(8,128)(2,1)S(1)}, u32[]{:S(2)}, u32[]{:S(2)}) collective-permute-start(bf16[12,64,256]{2,1,0:T(8,128)(2,1)} %fusion.189), channel_id=1, source_target_pairs={{0,12},{1,13},{2,14},{3,15},{16,28},{17,29},{18,30},{19,31}} | collective-permute-start | bytes 1179656 | tf_op jit(solution)/shard_map/ppermute | solution.py:38
  76.8 96.0 %collective-permute-start.8 = (bf16[2048,128]{1,0:T(8,128)(2,1)}, bf16[2048,128]{1,0:T(8,128)(2,1)}, u32[]{:S(2)}, u32[]{:S(2)}) collective-permute-start(bf16[2048,128]{1,0:T(8,128)(2,1)} %pad_maximum_fusion.9), channel_id=1, source_target_pairs={{0,1},{1,0},{2,3},{3,2},{4,5},{5,4},{6,7},{7,6},{8,9},{9,8},{10,11... | collective-permute-start | bytes 1572872 | tf_op jit(solution)/shard_map/ppermute | solution.py:27
  192.8 3.0 collective-permute-start.9
  198.2 25.3 %collective-permute-start.10 = (bf16[256,2048]{1,0:T(8,128)(2,1)S(1)}, bf16[256,2048]{1,0:T(8,128)(2,1)S(1)}, u32[]{:S(2)}, u32[]{:S(2)}) collective-permute-start(bf16[256,2048]{1,0:T(8,128)(2,1)S(1)} %add_convert_fusion.3), channel_id=1, source_target_pairs={{0,2},{1,3},{2,0},{3,1},{4,6},{5,7},{6,4},{7,5},{8,10},{9,11},{10,... | collective-permute-start | bytes 3145736 | tf_op jit(solution)/shard_map/ppermute | solution.py:27
  229.3 10.4 %collective-permute-start.11 = (bf16[256,2048]{1,0:T(8,128)(2,1)}, bf16[256,2048]{1,0:T(8,128)(2,1)}, u32[]{:S(2)}, u32[]{:S(2)}) collective-permute-start(bf16[256,2048]{1,0:T(8,128)(2,1)} %multiply_convert_fusion.3), channel_id=1, source_target_pairs={{0,1},{1,0},{2,3},{3,2},{4,5},{5,4},{6,7},{7,6},{8,9},{9,8},{10,11... | collective-permute-start | bytes 3145736 | tf_op jit(solution)/shard_map/ppermute | solution.py:27
  257.4 19.4 %collective-permute-start.12 = (bf16[256,2048]{1,0:T(8,128)(2,1)S(1)}, bf16[256,2048]{1,0:T(8,128)(2,1)S(1)}, u32[]{:S(2)}, u32[]{:S(2)}) collective-permute-start(bf16[256,2048]{1,0:T(8,128)(2,1)S(1)} %convolution_convert_fusion.1), channel_id=1, source_target_pairs={{0,1},{1,0},{2,3},{3,2},{4,5},{5,4},{6,7},{7,6},{8,9},{9,8},{10,11... | collective-permute-start | bytes 3145736 | tf_op jit(solution)/shard_map/ppermute | solution.py:27
  260.4 21.2 %collective-permute-start.15 = (bf16[256,2048]{1,0:T(8,128)(2,1)S(1)}, bf16[256,2048]{1,0:T(8,128)(2,1)S(1)}, u32[]{:S(2)}, u32[]{:S(2)}) collective-permute-start(bf16[256,2048]{1,0:T(8,128)(2,1)S(1)} %convolution_convert_fusion.3), channel_id=1, source_target_pairs={{0,1},{1,0},{2,3},{3,2},{4,5},{5,4},{6,7},{7,6},{8,9},{9,8},{10,11... | collective-permute-start | bytes 3145736 | tf_op jit(solution)/shard_map/ppermute | solution.py:27
  260.8 14.5 %collective-permute-start.56 = (bf16[256,1024]{1,0:T(8,128)(2,1)S(1)}, bf16[256,1024]{1,0:T(8,128)(2,1)}, u32[]{:S(2)}, u32[]{:S(2)}) collective-permute-start(bf16[256,1024]{1,0:T(8,128)(2,1)S(1)} %dynamic-slice_bitcast_fusion.7), channel_id=1, source_target_pairs={{0,16},{16,0},{1,17},{17,1},{2,18},{18,2},{3,19},{19,3},{4,20},{20... | collective-permute-start | bytes 1572872 | tf_op jit(solution)/shard_map/ppermute | solution.py:32
  275.3 11.7 %collective-permute-start.57 = (bf16[256,1024]{1,0:T(8,128)(2,1)}, bf16[256,1024]{1,0:T(8,128)(2,1)}, u32[]{:S(2)}, u32[]{:S(2)}) collective-permute-start(bf16[256,1024]{1,0:T(8,128)(2,1)} %collective-permute-done.56), channel_id=1, source_target_pairs={{0,1},{1,0},{2,3},{3,2},{4,5},{5,4},{6,7},{7,6},{8,9},{9,8},{10,11... | collective-permute-start | bytes 1572872 | tf_op jit(solution)/shard_map/ppermute | solution.py:27
  275.3 25.9 %collective-permute-start.58 = (bf16[512,1024]{1,0:T(8,128)(2,1)}, bf16[512,1024]{1,0:T(8,128)(2,1)}, u32[]{:S(2)}, u32[]{:S(2)}) collective-permute-start(bf16[512,1024]{1,0:T(8,128)(2,1)} %get-tuple-element.844), channel_id=1, source_target_pairs={{0,16},{16,0},{1,17},{17,1},{2,18},{18,2},{3,19},{19,3},{4,20},{20... | collective-permute-start | bytes 3145736 | tf_op jit(solution)/shard_map/ppermute | solution.py:32
  280.2 26.6 %collective-permute-start.13 = (bf16[256,2048]{1,0:T(8,128)(2,1)}, bf16[256,2048]{1,0:T(8,128)(2,1)}, u32[]{:S(2)}, u32[]{:S(2)}) collective-permute-start(bf16[256,2048]{1,0:T(8,128)(2,1)} %add_convert_fusion.2), channel_id=1, source_target_pairs={{0,2},{1,3},{2,0},{3,1},{4,6},{5,7},{6,4},{7,5},{8,10},{9,11},{10,... | collective-permute-start | bytes 3145736 | tf_op jit(solution)/shard_map/ppermute | solution.py:27
  285.1 43.1 %collective-permute-start.16 = (bf16[256,2048]{1,0:T(8,128)(2,1)}, bf16[256,2048]{1,0:T(8,128)(2,1)}, u32[]{:S(2)}, u32[]{:S(2)}) collective-permute-start(bf16[256,2048]{1,0:T(8,128)(2,1)} %add_convert_fusion.1), channel_id=1, source_target_pairs={{0,2},{1,3},{2,0},{3,1},{4,6},{5,7},{6,4},{7,5},{8,10},{9,11},{10,... | collective-permute-start | bytes 3145736 | tf_op jit(solution)/shard_map/ppermute | solution.py:27
  306.7 506.0 %reduce-scatter.7.cloned.1.call-start = ((), (), s32[]{:S(2)}) async-start(), calls=%async_computation.5 | async-start | bytes 2621440 | tf_op jit(solution)/shard_map/reduce_scatter | solution.py:80
  338.1 2.7 collective-permute-start.17
  342.0 14.8 %collective-permute-start.47 = (bf16[256,1024]{1,0:T(8,128)(2,1)S(1)}, bf16[256,1024]{1,0:T(8,128)(2,1)S(1)}, u32[]{:S(2)}, u32[]{:S(2)}) collective-permute-start(bf16[256,1024]{1,0:T(8,128)(2,1)S(1)} %fusion.227), channel_id=1, source_target_pairs={{0,16},{16,0},{1,17},{17,1},{2,18},{18,2},{3,19},{19,3},{4,20},{20... | collective-permute-start | bytes 1572872 | tf_op jit(solution)/shard_map/ppermute | solution.py:32
  342.8 35.6 %collective-permute-start.49 = (bf16[512,1024]{1,0:T(8,128)(2,1)S(1)}, bf16[512,1024]{1,0:T(8,128)(2,1)S(1)}, u32[]{:S(2)}, u32[]{:S(2)}) collective-permute-start(bf16[512,1024]{1,0:T(8,128)(2,1)S(1)} %pad_maximum_fusion.8), channel_id=1, source_target_pairs={{0,16},{16,0},{1,17},{17,1},{2,18},{18,2},{3,19},{19,3},{4,20},{20... | collective-permute-start | bytes 3145736 | tf_op jit(solution)/shard_map/ppermute | solution.py:32
  356.8 1.9 collective-permute-start.48
  382.3 433.6 %reduce-scatter.9.cloned.1.call-start = ((), (), s32[]{:S(2)}) async-start(), calls=%async_computation.6 | async-start | bytes 5242880 | tf_op jit(solution)/shard_map/reduce_scatter | solution.py:80
  385.6 75.5 %collective-permute-start.55 = (bf16[512,2048]{1,0:T(8,128)(2,1)}, bf16[512,2048]{1,0:T(8,128)(2,1)}, u32[]{:S(2)}, u32[]{:S(2)}) collective-permute-start(bf16[512,2048]{1,0:T(8,128)(2,1)} %pad_maximum_fusion.1), channel_id=1, source_target_pairs={{0,16},{16,0},{1,17},{17,1},{2,18},{18,2},{3,19},{19,3},{4,20},{20... | collective-permute-start | bytes 6291464 | tf_op jit(solution)/shard_map/ppermute | solution.py:32
  387.3 56.8 %collective-permute-start.53 = (bf16[256,1024]{1,0:T(8,128)(2,1)S(1)}, bf16[256,1024]{1,0:T(8,128)(2,1)}, u32[]{:S(2)}, u32[]{:S(2)}) collective-permute-start(bf16[256,1024]{1,0:T(8,128)(2,1)S(1)} %fusion.228), channel_id=1, source_target_pairs={{0,16},{16,0},{1,17},{17,1},{2,18},{18,2},{3,19},{19,3},{4,20},{20... | collective-permute-start | bytes 1572872 | tf_op jit(solution)/shard_map/ppermute | solution.py:32
  444.0 15.8 %collective-permute-start.54 = (bf16[256,1024]{1,0:T(8,128)(2,1)}, bf16[256,1024]{1,0:T(8,128)(2,1)}, u32[]{:S(2)}, u32[]{:S(2)}) collective-permute-start(bf16[256,1024]{1,0:T(8,128)(2,1)} %collective-permute-done.53), channel_id=1, source_target_pairs={{0,1},{1,0},{2,3},{3,2},{4,5},{5,4},{6,7},{7,6},{8,9},{9,8},{10,11... | collective-permute-start | bytes 1572872 | tf_op jit(solution)/shard_map/ppermute | solution.py:27
  444.0 11.6 %collective-permute-start.20 = (f32[12]{0:T(128)S(1)}, f32[12]{0:T(128)S(1)}, u32[]{:S(2)}, u32[]{:S(2)}) collective-permute-start(f32[12]{0:T(128)S(1)} %copy-done.96), channel_id=1, source_target_pairs={{4,0},{8,4},{12,8},{5,1},{9,5},{13,9},{6,2},{10,6},{14,10},{7,3},{... | collective-permute-start | bytes 152 | tf_op jit(solution)/shard_map/ppermute | solution.py:38
  445.3 13.1 %collective-permute-start.22 = (f32[12]{0:T(128)S(1)}, f32[12]{0:T(128)S(1)}, u32[]{:S(2)}, u32[]{:S(2)}) collective-permute-start(f32[12]{0:T(128)S(1)} %copy-done.96), channel_id=1, source_target_pairs={{8,0},{12,4},{9,1},{13,5},{10,2},{14,6},{11,3},{15,7},{24,16},{28,... | collective-permute-start | bytes 152 | tf_op jit(solution)/shard_map/ppermute | solution.py:38
  469.4 351.6 %reduce-scatter.5.cloned.1.call-start = ((), (), s32[]{:S(2)}) async-start(), calls=%async_computation.4 | async-start | bytes 5570560 | tf_op jit(solution)/shard_map/reduce_scatter | solution.py:80
  479.7 27.9 %collective-permute-start.18 = (bf16[12,64,256]{2,1,0:T(8,128)(2,1)}, bf16[12,64,256]{2,1,0:T(8,128)(2,1)S(1)}, u32[]{:S(2)}, u32[]{:S(2)}) collective-permute-start(bf16[12,64,256]{2,1,0:T(8,128)(2,1)} %fusion.192), channel_id=1, source_target_pairs={{4,0},{8,4},{12,8},{5,1},{9,5},{13,9},{6,2},{10,6},{14,10},{7,3},{... | collective-permute-start | bytes 1179656 | tf_op jit(solution)/shard_map/ppermute | solution.py:38
  481.1 82.6 %collective-permute-start.19 = (bf16[12,64,256]{2,1,0:T(8,128)(2,1)}, bf16[12,64,256]{2,1,0:T(8,128)(2,1)}, u32[]{:S(2)}, u32[]{:S(2)}) collective-permute-start(bf16[12,64,256]{2,1,0:T(8,128)(2,1)} %fusion.192), channel_id=1, source_target_pairs={{8,0},{12,4},{9,1},{13,5},{10,2},{14,6},{11,3},{15,7},{24,16},{28,... | collective-permute-start | bytes 1179656 | tf_op jit(solution)/shard_map/ppermute | solution.py:38
  482.4 81.3 %collective-permute-start.21 = (bf16[12,64,256]{2,1,0:T(8,128)(2,1)}, bf16[12,64,256]{2,1,0:T(8,128)(2,1)}, u32[]{:S(2)}, u32[]{:S(2)}) collective-permute-start(bf16[12,64,256]{2,1,0:T(8,128)(2,1)} %fusion.192), channel_id=1, source_target_pairs={{12,0},{13,1},{14,2},{15,3},{28,16},{29,17},{30,18},{31,19}} | collective-permute-start | bytes 1179656 | tf_op jit(solution)/shard_map/ppermute | solution.py:38
  500.8 152.2 %collective-permute-start.23 = (bf16[2048,128]{1,0:T(8,128)(2,1)}, bf16[2048,128]{1,0:T(8,128)(2,1)}, u32[]{:S(2)}, u32[]{:S(2)}) collective-permute-start(bf16[2048,128]{1,0:T(8,128)(2,1)} %get-tuple-element.912), channel_id=1, source_target_pairs={{0,1},{1,0},{2,3},{3,2},{4,5},{5,4},{6,7},{7,6},{8,9},{9,8},{10,11... | collective-permute-start | bytes 1572872 | tf_op jit(solution)/shard_map/ppermute | solution.py:27
  646.9 11.5 %collective-permute-start.27 = (bf16[512,256]{1,0:T(8,128)(2,1)S(1)}, bf16[512,256]{1,0:T(8,128)(2,1)S(1)}, u32[]{:S(2)}, u32[]{:S(2)}) collective-permute-start(bf16[512,256]{1,0:T(8,128)(2,1)S(1)} %fusion.224), channel_id=1, source_target_pairs={{0,2},{1,3},{2,0},{3,1},{4,6},{5,7},{6,4},{7,5},{8,10},{9,11},{10,... | collective-permute-start | bytes 786440 | tf_op jit(solution)/shard_map/ppermute | solution.py:27
  654.4 8.6 %collective-permute-start.24 = (bf16[512,128]{1,0:T(8,128)(2,1)S(1)}, bf16[512,128]{1,0:T(8,128)(2,1)S(1)}, u32[]{:S(2)}, u32[]{:S(2)}) collective-permute-start(bf16[512,128]{1,0:T(8,128)(2,1)S(1)} %get-tuple-element.868), channel_id=1, source_target_pairs={{4,0},{8,4},{12,8},{5,1},{9,5},{13,9},{6,2},{10,6},{14,10},{7,3},{... | collective-permute-start | bytes 393224 | tf_op jit(solution)/shard_map/ppermute | solution.py:38
  655.9 13.4 %collective-permute-start.25 = (bf16[512,128]{1,0:T(8,128)(2,1)S(1)}, bf16[512,128]{1,0:T(8,128)(2,1)S(1)}, u32[]{:S(2)}, u32[]{:S(2)}) collective-permute-start(bf16[512,128]{1,0:T(8,128)(2,1)S(1)} %get-tuple-element.870), channel_id=1, source_target_pairs={{8,0},{12,4},{9,1},{13,5},{10,2},{14,6},{11,3},{15,7},{24,16},{28,... | collective-permute-start | bytes 393224 | tf_op jit(solution)/shard_map/ppermute | solution.py:38
  657.2 12.1 %collective-permute-start.26 = (bf16[512,128]{1,0:T(8,128)(2,1)S(1)}, bf16[512,128]{1,0:T(8,128)(2,1)S(1)}, u32[]{:S(2)}, u32[]{:S(2)}) collective-permute-start(bf16[512,128]{1,0:T(8,128)(2,1)S(1)} %get-tuple-element.869), channel_id=1, source_target_pairs={{12,0},{13,1},{14,2},{15,3},{28,16},{29,17},{30,18},{31,19}} | collective-permute-start | bytes 393224 | tf_op jit(solution)/shard_map/ppermute | solution.py:38
  658.6 11.4 %collective-permute-start.28 = (bf16[512,128]{1,0:T(8,128)(2,1)S(1)}, bf16[512,128]{1,0:T(8,128)(2,1)S(1)}, u32[]{:S(2)}, u32[]{:S(2)}) collective-permute-start(bf16[512,128]{1,0:T(8,128)(2,1)S(1)} %dynamic-slice_convert_fusion.1), channel_id=1, source_target_pairs={{0,1},{1,0},{2,3},{3,2},{4,5},{5,4},{6,7},{7,6},{8,9},{9,8},{10,11... | collective-permute-start | bytes 393224 | tf_op jit(solution)/shard_map/ppermute | solution.py:27
  671.5 63.2 %collective-permute-start.39 = (bf16[512,2176]{1,0:T(8,128)(2,1)}, bf16[512,2176]{1,0:T(8,128)(2,1)}, u32[]{:S(2)}, u32[]{:S(2)}) collective-permute-start(bf16[512,2176]{1,0:T(8,128)(2,1)} %pad_dynamic-update-slice_fusion.1), channel_id=1, source_target_pairs={{0,16},{16,0},{1,17},{17,1},{2,18},{18,2},{3,19},{19,3},{4,20},{20... | collective-permute-start | bytes 6684680 | tf_op jit(solution)/shard_map/ppermute | solution.py:32
  672.6 57.5 %collective-permute-start.37 = (bf16[256,1024]{1,0:T(8,128)(2,1)}, bf16[256,1024]{1,0:T(8,128)(2,1)}, u32[]{:S(2)}, u32[]{:S(2)}) collective-permute-start(bf16[256,1024]{1,0:T(8,128)(2,1)} %dynamic_slice.280), channel_id=1, source_target_pairs={{0,16},{16,0},{1,17},{17,1},{2,18},{18,2},{3,19},{19,3},{4,20},{20... | collective-permute-start | bytes 1572872 | tf_op jit(solution)/shard_map/ppermute | solution.py:32
  730.1 3.5 collective-permute-start.38
  751.5 3.0 collective-permute-start.29
  752.3 9.7 %collective-permute-start.14 = (bf16[256,2048]{1,0:T(8,128)(2,1)S(1)}, bf16[256,2048]{1,0:T(8,128)(2,1)S(1)}, u32[]{:S(2)}, u32[]{:S(2)}) collective-permute-start(bf16[256,2048]{1,0:T(8,128)(2,1)S(1)} %copy-done.50), channel_id=1, source_target_pairs={{0,1},{1,0},{2,3},{3,2},{4,5},{5,4},{6,7},{7,6},{8,9},{9,8},{10,11... | collective-permute-start | bytes 3145736 | tf_op jit(solution)/shard_map/ppermute | solution.py:27
  761.4 25.5 %collective-permute-start.30 = (bf16[256,2048]{1,0:T(8,128)(2,1)S(1)}, bf16[256,2048]{1,0:T(8,128)(2,1)}, u32[]{:S(2)}, u32[]{:S(2)}) collective-permute-start(bf16[256,2048]{1,0:T(8,128)(2,1)S(1)} %add_convert_fusion), channel_id=1, source_target_pairs={{0,2},{1,3},{2,0},{3,1},{4,6},{5,7},{6,4},{7,5},{8,10},{9,11},{10,... | collective-permute-start | bytes 3145736 | tf_op jit(solution)/shard_map/ppermute | solution.py:27
  789.0 2.7 collective-permute-start.32
  791.1 19.7 %collective-permute-start.31 = (bf16[256,2048]{1,0:T(8,128)(2,1)S(1)}, bf16[256,2048]{1,0:T(8,128)(2,1)S(1)}, u32[]{:S(2)}, u32[]{:S(2)}) collective-permute-start(bf16[256,2048]{1,0:T(8,128)(2,1)S(1)} %fusion.128), channel_id=1, source_target_pairs={{0,1},{1,0},{2,3},{3,2},{4,5},{5,4},{6,7},{7,6},{8,9},{9,8},{10,11... | collective-permute-start | bytes 3145736 | tf_op jit(solution)/shard_map/ppermute | solution.py:27
  791.7 3.5 collective-permute-start.43
  792.2 9.9 %collective-permute-start.33 = (f32[1024,2]{0,1:T(2,128)S(1)}, f32[1024,2]{0,1:T(2,128)S(1)}, u32[]{:S(2)}, u32[]{:S(2)}) collective-permute-start(f32[1024,2]{0,1:T(2,128)S(1)} %fusion.283), channel_id=1, source_target_pairs={{0,16},{16,0},{1,17},{17,1},{2,18},{18,2},{3,19},{19,3},{4,20},{20... | collective-permute-start | bytes 24584 | tf_op jit(solution)/shard_map/ppermute | solution.py:32
  795.3 5.6 collective-permute-start.44
  795.4 5.7 collective-permute-start.45
  795.4 6.0 collective-permute-start.46
  802.2 5.7 collective-permute-start.34
  804.4 4.7 collective-permute-start.35
  806.3 4.0 collective-permute-start.36
  822.0 10.2 %collective-permute-start.40 = (f32[256,128]{1,0:T(8,128)S(1)}, f32[256,128]{1,0:T(8,128)S(1)}, u32[]{:S(2)}, u32[]{:S(2)}) collective-permute-start(f32[256,128]{1,0:T(8,128)S(1)} %get-tuple-element.855), channel_id=1, source_target_pairs={{0,1},{1,0},{2,3},{3,2},{4,5},{5,4},{6,7},{7,6},{8,9},{9,8},{10,11... | collective-permute-start | bytes 393224 | tf_op jit(solution)/shard_map/ppermute | solution.py:27
  822.0 10.2 %collective-permute-start.41 = (f32[256,128]{1,0:T(8,128)S(1)}, f32[256,128]{1,0:T(8,128)S(1)}, u32[]{:S(2)}, u32[]{:S(2)}) collective-permute-start(f32[256,128]{1,0:T(8,128)S(1)} %get-tuple-element.855), channel_id=1, source_target_pairs={{0,2},{1,3},{2,0},{3,1},{4,6},{5,7},{6,4},{7,5},{8,10},{9,11},{10,... | collective-permute-start | bytes 393224 | tf_op jit(solution)/shard_map/ppermute | solution.py:27
  823.6 7.1 collective-permute-start.50
  823.8 7.5 collective-permute-start.51
  824.4 7.0 collective-permute-start.52
  830.8 5.2 collective-permute-start.42
  (141 other events, 1134.1 us)
Sparse Core Ops, SparseCore 0:
  306.8 52.3 reduce-scatter.10
  382.4 51.4 reduce-scatter.6
  469.5 103.0 reduce-scatter.8
  743.3 77.6 reduce-scatter.4

commit v2 on v1

--- a/solution.py
+++ b/solution.py
@@ -4,17 +4,16 @@
 import jax
 import jax.numpy as jnp
 from jax import lax
+from jax.experimental import pallas as pl
+from jax.experimental.pallas import tpu as pltpu
 from jax.sharding import PartitionSpec as P
 
-KVHEADS = 2
 AHEAD_DIM = 128
 SCAN_BLOCK = 256
-QBLOCK = 512
 
 
 EPSILON = 1e-05
 NEG_FILL = -1e30
-PRECISE = lax.Precision.HIGHEST
 
 CORE, CHIP = (1, 2)
 
@@ -100,13 +99,14 @@
 
 def chained(state, log_decay, axis, direction):
     count = lax.axis_size(axis)
-    total = jnp.zeros_like(state)
+    width = state.shape[1]
+    total = jnp.zeros((log_decay.shape[0], state.shape[0] // log_decay.shape[0], width), jnp.float32)
     between = jnp.zeros_like(log_decay)
     for shift in range(1, count):
-        arrived = moved(state.astype(jnp.bfloat16), axis, direction * shift).astype(jnp.float32)
+        arrived = moved(state, axis, direction * shift).astype(jnp.float32).reshape(total.shape)
         total = total + arrived * jnp.exp(between)[:, None, None]
         between = between + moved(log_decay, axis, direction * shift)
-    return total
+    return total.astype(jnp.bfloat16).reshape(state.shape)
 
 
 def matmul_low(former, latter):
@@ -123,10 +123,6 @@
     return lax.dot_general(
         former, latter, (((1,), (1,)), ((), ())), preferred_element_type=jnp.float32
     )
-
-
-def round_keep(values):
-    return lax.optimization_barrier(values.astype(jnp.bfloat16)).astype(jnp.float32)
 
 
 def silu_slope(values):
@@ -144,48 +140,403 @@
     return (grad_source, grad_gain)
 
 
-def ssd_block(states, pieces, decay_rate, skip_gain):
-    source_block, write_block, read_block, step_block = pieces
-    increments = step_block * decay_rate
-    running = jnp.cumsum(increments, axis=0)
-    block_len = increments.shape[0]
-    lower_mask = (
-        jnp.arange(block_len, dtype=jnp.int32)[:, None]
-        >= jnp.arange(block_len, dtype=jnp.int32)[None, :]
-    )
-    differences = running[:, None, :] - running[None, :, :]
-    decays = jnp.exp(jnp.where(lower_mask[:, :, None], differences, NEG_FILL))
-    intersection = jnp.dot(read_block, write_block.T, precision=PRECISE)
-    mixing = decays * intersection[:, :, None] * step_block[None, :, :]
-    within = jnp.einsum("tsh,shp->thp", mixing, source_block, precision=PRECISE)
-    carried = (
-        jnp.einsum("tn,hpn->thp", read_block, states, precision=PRECISE)
-        * jnp.exp(running)[:, :, None]
-    )
-    result = within + carried + skip_gain[None, :, None] * source_block
-    tailing = jnp.exp(running[-1][None, :] - running) * step_block
-    incoming = jnp.einsum("sh,shp,sn->hpn", tailing, source_block, write_block, precision=PRECISE)
-    states = states * jnp.exp(running[-1])[:, None, None] + incoming
-    return (states, result)
-
-
-def run_ssd(source_heads, write_rows, read_rows, step_rows, a_log, d_skip, entering, block_len):
-    row_total = source_heads.shape[0]
-    block_count = row_total // block_len
-    decay_rate = -jnp.exp(a_log)
-
-    def blocked(source):
-        return source.reshape((block_count, block_len) + source.shape[1:])
-
-    def stepper(states, pieces):
-        return ssd_block(states, pieces, decay_rate, d_skip)
-
-    closing, outputs = lax.scan(
-        jax.checkpoint(stepper),
-        entering,
-        (blocked(source_heads), blocked(write_rows), blocked(read_rows), blocked(step_rows)),
-    )
-    return (outputs.reshape(source_heads.shape), closing)
+def split_lanes(first, second, shape):
+    lane = lax.broadcasted_iota(jnp.int32, shape, 1)
+    return jnp.where(lane < shape[1] // 2, first, second)
+
+
+def lane_sums(values):
+    width = values.shape[1] // 2
+    lane = lax.broadcasted_iota(jnp.int32, values.shape, 1)
+    first = jnp.sum(jnp.where(lane < width, values, 0.0), axis=1, keepdims=True)
+    second = jnp.sum(jnp.where(lane < width, 0.0, values), axis=1, keepdims=True)
+    return (first, second)
+
+
+def wide(values):
+    return values.astype(jnp.float32)
+
+
+def narrow(values):
+    return values.astype(jnp.bfloat16)
+
+
+def state_kernel(u_ref, small_ref, b_ref, state_ref, *, to_end):
+    rows = small_ref[0]
+    if to_end:
+        last = rows[0:2, rows.shape[1] - 1 :]
+        weights = jnp.exp(last - rows[0:2]) * rows[2:4]
+    else:
+        weights = jnp.exp(rows[0:2])
+    cols = jnp.concatenate([weights, rows[2:8]], axis=0).T
+    u = wide(u_ref[...])
+    weighted = narrow(u * split_lanes(cols[:, 0:1], cols[:, 1:2], u.shape))
+    state_ref[...] = narrow(inner_rows(weighted, b_ref[...]))
+
+
+def scan_kernel(u_ref, small_ref, b_ref, c_ref, y_ref, cb_ref):
+    size = SCAN_BLOCK
+    count = u_ref.shape[0] // size
+    block = [slice(i * size, (i + 1) * size) for i in range(count)]
+
+    @pl.when(pl.program_id(0) == 0)
+    def _():
+        for i in range(count):
+            for j in range(i + 1):
+                cb_ref[block[i], block[j]] = times_back(c_ref[block[i], :], b_ref[block[j], :])
+
+    rows = small_ref[0]
+    cols = rows.T
+    lower = lax.broadcasted_iota(jnp.int32, (size, size), 0) >= lax.broadcasted_iota(
+        jnp.int32, (size, size), 1
+    )
+    for i in range(count):
+        parts = []
+        for h in range(2):
+            total = jnp.zeros((size, u_ref.shape[1]), jnp.float32)
+            for j in range(i + 1):
+                difference = cols[block[i], h : h + 1] - rows[h : h + 1, block[j]]
+                if i == j:
+                    difference = jnp.where(lower, difference, NEG_FILL)
+                mixing = jnp.exp(difference) * cb_ref[block[i], block[j]] * rows[2 + h : 3 + h, block[j]]
+                total = total + matmul_low(narrow(mixing), u_ref[block[j], :])
+            parts.append(total)
+        skip = split_lanes(cols[block[i], 4:5], cols[block[i], 5:6], parts[0].shape)
+        y_ref[block[i], :] = split_lanes(*parts, parts[0].shape) + skip * wide(u_ref[block[i], :])
+
+
+def carry_kernel(y_ref, z_ref, small_ref, c_ref, state_ref, out_ref, gated_ref):
+    cols = jnp.exp(small_ref[0][0:8]).T
+    carried = times_back(c_ref[...], state_ref[...])
+    values = y_ref[...] + carried * split_lanes(cols[:, 0:1], cols[:, 1:2], carried.shape)
+    out_ref[...] = values
+    gate = z_ref[...]
+    gated_ref[...] = narrow(values * (gate * jax.nn.sigmoid(gate)))
+
+
+def scan_back_kernel(u_ref, dy_ref, small_ref, b_ref, c_ref, dw_ref, sums_ref, db_ref, dc_ref, cb_ref, mix_ref):
+    size = SCAN_BLOCK
+    count = u_ref.shape[0] // size
+    width = u_ref.shape[1]
+    block = [slice(i * size, (i + 1) * size) for i in range(count)]
+
+    @pl.when(pl.program_id(0) == 0)
+    def _():
+        mix_ref[...] = jnp.zeros_like(mix_ref)
+        for i in range(count):
+            for j in range(i, count):
+                cb_ref[block[i], block[j]] = times_back(b_ref[block[i], :], c_ref[block[j], :])
+
+    rows = small_ref[0]
+    cols = rows.T
+    upper = lax.broadcasted_iota(jnp.int32, (size, size), 0) <= lax.broadcasted_iota(
+        jnp.int32, (size, size), 1
+    )
+    lane = lax.broadcasted_iota(jnp.int32, (size, width), 1)
+    read_sums = [[jnp.zeros((1, size), jnp.float32) for _ in range(count)] for _ in range(2)]
+    write_sums = [[], []]
+    for i in range(count):
+        parts = []
+        for h in range(2):
+            total = jnp.zeros((size, width), jnp.float32)
+            write_sum = jnp.zeros((size, 1), jnp.float32)
+            step = cols[block[i], 2 + h : 3 + h]
+            for j in range(i, count):
+                difference = rows[h : h + 1, block[j]] - cols[block[i], h : h + 1]
+                if i == j:
+                    difference = jnp.where(upper, difference, NEG_FILL)
+                decay = jnp.exp(difference)
+                dy = dy_ref[block[j], :]
+                dy_head = jnp.where((lane < width // 2) == (h == 0), dy, jnp.zeros_like(dy))
+                product = decay * times_back(u_ref[block[i], :], dy_head)
+                crossing = cb_ref[block[i], block[j]]
+                total = total + matmul_low(narrow(decay * crossing), dy)
+                weighted = product * step
+                mix_ref[block[i], block[j]] += weighted
+                write_sum = write_sum + jnp.sum(product * crossing, axis=1, keepdims=True)
+                read_sums[h][j] = read_sums[h][j] + jnp.sum(weighted * crossing, axis=0, keepdims=True)
+            parts.append(total)
+            write_sums[h].append(write_sum)
+        dw_ref[block[i], :] = split_lanes(*parts, parts[0].shape)
+    both = [jnp.concatenate(write_sums[h], axis=0) for h in range(2)]
+    column = lax.broadcasted_iota(jnp.int32, (u_ref.shape[0], 8), 1)
+    packed = jnp.where(column == 0, both[0], jnp.where(column == 1, both[1], 0.0)).T
+    skip = jnp.sum(wide(u_ref[...]) * wide(dy_ref[...]), axis=0, keepdims=True)
+    skip = jnp.concatenate([skip, jnp.zeros((1, u_ref.shape[0] - width), jnp.float32)], axis=1)
+    reads = [jnp.concatenate(read_sums[h], axis=1) for h in range(2)]
+    sums_ref[0] = jnp.concatenate([reads[0], reads[1], packed[0:2], skip, packed[2:5]], axis=0)
+
+    @pl.when(pl.program_id(0) == pl.num_programs(0) - 1)
+    def _():
+        for i in range(count):
+            total = jnp.zeros((size, b_ref.shape[1]), jnp.float32)
+            for j in range(i, count):
+                total = total + matmul_low(narrow(mix_ref[block[i], block[j]]), c_ref[block[j], :])
+            db_ref[block[i], :] = total
+        for j in range(count):
+            total = jnp.zeros((size, b_ref.shape[1]), jnp.float32)
+            for i in range(j + 1):
+                total = total + inner_rows(narrow(mix_ref[block[i], block[j]]), b_ref[block[i], :])
+            dc_ref[block[j], :] = total
+
+
+def carry_back_kernel(
+    u_ref, dy_ref, small_ref, sums_ref, dw_ref, b_ref, c_ref, state_ref, grad_ref, db_in_ref, dc_in_ref,
+    du_ref, steps_ref, db_ref, dc_ref,
+):
+    rows = small_ref[0]
+    tokens = rows.shape[1]
+    last = rows[0:2, tokens - 1 :]
+    from_start = jnp.exp(rows[0:2])
+    to_end = jnp.exp(last - rows[0:2])
+    cols = jnp.concatenate([from_start, to_end, rows[2:6]], axis=0).T
+    u = wide(u_ref[...])
+    dy = wide(dy_ref[...])
+
+    def spread(at):
+        return split_lanes(cols[:, at : at + 1], cols[:, at + 1 : at + 2], u.shape)
+
+    @pl.when(pl.program_id(0) == 0)
+    def _():
+        db_ref[...] = db_in_ref[...]
+        dc_ref[...] = dc_in_ref[...]
+
+    state = state_ref[...]
+    grad = grad_ref[...]
+    started = spread(0) * dy
+    ended = spread(2) * u
+    step = spread(4)
+    dw = dw_ref[...] + spread(2) * times_back(b_ref[...], grad)
+    du_ref[...] = narrow(step * dw + spread(6) * dy)
+    dc_ref[...] += matmul_low(narrow(started), state)
+    db_ref[...] += matmul_low(narrow(ended * step), grad)
+    reads = lane_sums(started * times_back(c_ref[...], state))
+    writes = lane_sums(ended * times_back(b_ref[...], grad))
+    column = lax.broadcasted_iota(jnp.int32, (tokens, 8), 1)
+    packed = jnp.zeros((tokens, 8), jnp.float32)
+    for at, values in enumerate(reads + writes):
+        packed = jnp.where(column == at, values, packed)
+    packed = packed.T
+    sums = sums_ref[0]
+    written = sums[2:4] + packed[2:4]
+    slope = sums[0:2] + packed[0:2] - rows[2:4] * written
+    products = jnp.sum(wide(state) * wide(grad), axis=1, keepdims=True)
+    height = products.shape[0] // 2
+    across = jnp.concatenate(
+        [
+            jnp.sum(products[:height], axis=0, keepdims=True),
+            jnp.sum(products[height:], axis=0, keepdims=True),
+        ],
+        axis=0,
+    ) * jnp.exp(last)
+    across = across + jnp.sum(rows[2:4] * packed[2:4], axis=1, keepdims=True)
+    held = jnp.concatenate([slope, jnp.zeros((6, tokens), jnp.float32)], axis=0)
+    place = lax.broadcasted_iota(jnp.int32, held.shape, 1)
+    reach = 1
+    while reach < tokens:
+        held = held + jnp.where(place < tokens - reach, pltpu.roll(held, tokens - reach, 1), 0.0)
+        reach = 2 * reach
+    flow = held[0:2] + across
+    steps_ref[0] = jnp.concatenate([written + rows[6:8] * flow, flow, held[2:6]], axis=0)
+
+
+def attend_scores(rank_ref, k_ref, q_ref, own, factor):
+    scores = times_back(k_ref[...], q_ref[...]) * factor
+    keys, queries = scores.shape
+    row = lax.broadcasted_iota(jnp.int32, (own, queries), 0)
+    column = lax.broadcasted_iota(jnp.int32, (own, queries), 1) + pl.program_id(1) * queries
+    near = jnp.where(row <= column, scores[:own], NEG_FILL)
+    if keys == own:
+        return near
+    far_row = lax.broadcasted_iota(jnp.int32, (keys - own, queries), 0)
+    far = jnp.where(far_row < rank_ref[0] * own, scores[own:], NEG_FILL)
+    return jnp.concatenate([near, far], axis=0)
+
+
+def attend_kernel(rank_ref, q_ref, k_ref, v_ref, out_ref, log_ref, flat_ref, *, own, factor):
+    @pl.when((pl.program_id(0) == 0) & (pl.program_id(1) == 0))
+    def _():
+        flat_ref[...] = v_ref[...].T
+
+    scores = attend_scores(rank_ref, k_ref, q_ref, own, factor)
+    maxima = jnp.max(scores, axis=0, keepdims=True)
+    weights = jnp.exp(scores - maxima)
+    totals = jnp.sum(weights, axis=0, keepdims=True)
+    probability = narrow(weights * (1.0 / totals))
+    out_ref[...] = narrow(matmul_low(flat_ref[...], probability).T)
+    log_ref[0] = jnp.broadcast_to(maxima + jnp.log(totals), log_ref.shape[1:])
+
+
+def attend_back_kernel(
+    rank_ref, q_ref, do_ref, log_ref, k_ref, v_ref, dq_ref, dk_ref, dv_ref, flat_ref, *, own, factor
+):
+    @pl.when((pl.program_id(0) == 0) & (pl.program_id(1) == 0))
+    def _():
+        flat_ref[...] = k_ref[...].T
+        dk_ref[...] = jnp.zeros_like(dk_ref)
+        dv_ref[...] = jnp.zeros_like(dv_ref)
+
+    scores = attend_scores(rank_ref, k_ref, q_ref, own, factor)
+    probability = jnp.exp(scores - log_ref[0][0:1])
+    dv_ref[...] += matmul_low(narrow(probability), do_ref[...])
+    grad_prob = times_back(v_ref[...], do_ref[...])
+    centre = jnp.sum(probability * grad_prob, axis=0, keepdims=True)
+    grad_score = narrow(probability * (grad_prob - centre))
+    dk_ref[...] += matmul_low(grad_score, q_ref[...]) * factor
+    dq_ref[...] = narrow((matmul_low(flat_ref[...], grad_score) * factor).T)
+
+
+def sizes(*values):
+    return sum(v.size * v.dtype.itemsize for v in values)
+
+
+def call(name, kernel, grid, specs, args, outs, scratch=(), flops=0):
+    cost = pl.CostEstimate(
+        flops=int(flops),
+        bytes_accessed=int(sizes(*args) + sizes(*[out for out, _ in outs])),
+        transcendentals=0,
+    )
+    return pl.pallas_call(
+        kernel,
+        name=name,
+        grid=grid,
+        in_specs=specs,
+        out_specs=[spec for _, spec in outs],
+        out_shape=[out for out, _ in outs],
+        scratch_shapes=list(scratch),
+        cost_estimate=cost,
+        compiler_params=pltpu.CompilerParams(vmem_limit_bytes=48 * 1024 * 1024),
+    )(*args)
+
+
+def like(shape, kind):
+    return jax.ShapeDtypeStruct(shape, kind)
+
+
+class Scan:
+    def __init__(self, tokens, inner, state):
+        self.tokens, self.inner, self.state = (tokens, inner, state)
+        self.pairs = inner // 128
+        self.tile = pl.BlockSpec((tokens, 128), lambda p: (0, p))
+        self.small = pl.BlockSpec((1, 8, tokens), lambda p: (p, 0, 0))
+        self.shared = pl.BlockSpec((tokens, state), lambda p: (0, 0))
+        self.states = pl.BlockSpec((128, state), lambda p: (p, 0))
+        self.small_like = like((self.pairs, 8, tokens), jnp.float32)
+        self.work = 2 * tokens * inner * state
+
+    def rows_like(self, kind):
+        return like((self.tokens, self.inner), kind)
+
+    def own_state(self, u, small, b, to_end):
+        return call(
+            "own_state",
+            partial(state_kernel, to_end=to_end),
+            (self.pairs,),
+            [self.tile, self.small, self.shared],
+            (u, small, b),
+            [(like((self.inner, self.state), jnp.bfloat16), self.states)],
+            flops=self.work,
+        )[0]
+
+    def within(self, u, small, b, c):
+        return call(
+            "scan",
+            scan_kernel,
+            (self.pairs,),
+            [self.tile, self.small, self.shared, self.shared],
+            (u, small, b, c),
+            [(self.rows_like(jnp.float32), self.tile)],
+            [pltpu.VMEM((self.tokens, self.tokens), jnp.float32)],
+            flops=8 * self.work,
+        )[0]
+
+    def carried(self, y, z, small, c, state):
+        return call(
+            "carry",
+            carry_kernel,
+            (self.pairs,),
+            [self.tile, self.tile, self.small, self.shared, self.states],
+            (y, z, small, c, state),
+            [(self.rows_like(jnp.float32), self.tile), (self.rows_like(jnp.bfloat16), self.tile)],
+            flops=self.work,
+        )
+
+    def within_back(self, u, dy, small, b, c):
+        shared = like((self.tokens, self.state), jnp.float32)
+        square = pltpu.VMEM((self.tokens, self.tokens), jnp.float32)
+        return call(
+            "scan_back",
+            scan_back_kernel,
+            (self.pairs,),
+            [self.tile, self.tile, self.small, self.shared, self.shared],
+            (u, dy, small, b, c),
+            [
+                (self.rows_like(jnp.float32), self.tile),
+                (self.small_like, self.small),
+                (shared, self.shared),
+                (shared, self.shared),
+            ],
+            [square, square],
+            flops=20 * self.work,
+        )
+
+    def carried_back(self, u, dy, small, sums, dw, b, c, state, grad, db, dc):
+        shared = like((self.tokens, self.state), jnp.float32)
+        return call(
+            "carry_back",
+            carry_back_kernel,
+            (self.pairs,),
+            [self.tile, self.tile, self.small, self.small, self.tile]
+            + [self.shared, self.shared, self.states, self.states, self.shared, self.shared],
+            (u, dy, small, sums, dw, b, c, state, grad, db, dc),
+            [
+                (self.rows_like(jnp.bfloat16), self.tile),
+                (self.small_like, self.small),
+                (shared, self.shared),
+                (shared, self.shared),
+            ],
+            flops=6 * self.work,
+        )
+
+
+class Attend:
+    def __init__(self, tokens, keys, heads):
+        self.tokens, self.keys, self.heads = (tokens, keys, heads)
+        size = min(256, tokens)
+        self.grid = (heads, tokens // size)
+        self.factor = 1.0 / math.sqrt(AHEAD_DIM)
+        self.rank = pl.BlockSpec(memory_space=pltpu.SMEM)
+        self.tile = pl.BlockSpec((size, AHEAD_DIM), lambda h, q: (q, h))
+        self.log = pl.BlockSpec((1, 8, size), lambda h, q: (h, 0, q))
+        self.whole = pl.BlockSpec((keys, AHEAD_DIM), lambda h, q: (0, 0))
+        self.rows_like = like((tokens, heads * AHEAD_DIM), jnp.bfloat16)
+        self.flat = pltpu.VMEM((AHEAD_DIM, keys), jnp.bfloat16)
+        self.work = 2 * tokens * heads * AHEAD_DIM * keys
+
+    def forward(self, rank, q, k, v):
+        return call(
+            "attend",
+            partial(attend_kernel, own=self.tokens, factor=self.factor),
+            self.grid,
+            [self.rank, self.tile, self.whole, self.whole],
+            (rank, q, k, v),
+            [(self.rows_like, self.tile), (like((self.heads, 8, self.tokens), jnp.float32), self.log)],
+            [self.flat],
+            flops=4 * self.work,
+        )
+
+    def back(self, rank, q, do, log, k, v):
+        whole = like((self.keys, AHEAD_DIM), jnp.float32)
+        return call(
+            "attend_back",
+            partial(attend_back_kernel, own=self.tokens, factor=self.factor),
+            self.grid,
+            [self.rank, self.tile, self.tile, self.log, self.whole, self.whole],
+            (rank, q, do, log, k, v),
+            [(self.rows_like, self.tile), (whole, self.whole), (whole, self.whole)],
+            [self.flat],
+            flops=10 * self.work,
+        )
 
 
 def body(
@@ -249,51 +600,33 @@
 
     zx_proj = matmul_low(input_one, in_matrix)
     gate_ssm = zx_proj[:, :inner_local]
-    source_heads = round_keep(zx_proj[:, inner_local:]).reshape(tokens, heads_local, head_width)
-    bc_rows = round_keep(matmul_low(input_one, bc_matrix))
+    source_rows = zx_proj[:, inner_local:].astype(jnp.bfloat16)
+    bc_rows = matmul_low(input_one, bc_matrix).astype(jnp.bfloat16)
     write_rows = bc_rows[:, :state_width]
     read_rows = bc_rows[:, state_width:]
-    dt_pre = matmul_low(input_one, ssm_dt) + dt_bias
+    dt_pre = lax.dot_general(
+        ssm_dt, input_one, (((0,), (1,)), ((), ())), preferred_element_type=jnp.float32
+    ) + dt_bias[:, None]
     dt_rows = jax.nn.softplus(dt_pre)
     decay_rate = -jnp.exp(a_log)
-    running = jnp.cumsum(dt_rows * decay_rate, axis=0)
-    to_end = jnp.exp(running[-1][None, :] - running) * dt_rows
-    own_state = jnp.einsum("th,thp,tn->hpn", to_end, source_heads, write_rows, precision=PRECISE)
-    entering = chained(own_state, running[-1], "ctx", 1)
-    ssm_pair, ssm_back = jax.vjp(
-        partial(run_ssd, block_len=SCAN_BLOCK),
-        source_heads,
-        write_rows,
-        read_rows,
-        dt_rows,
-        a_log,
-        d_skip,
-        entering,
-    )
-    ssm_values = ssm_pair[0].reshape(tokens, inner_local)
-    gate_act = jax.nn.silu(gate_ssm)
-    gated_rows = (ssm_values * gate_act).astype(jnp.bfloat16)
-
+    running = jnp.cumsum(dt_rows * decay_rate[:, None], axis=1)
+    head_pairs = heads_local // 2
+
+    def by_head(value):
+        return jnp.broadcast_to(value[:, None], (heads_local, tokens))
+
+    small_rows = jnp.stack([running, dt_rows, by_head(d_skip), by_head(decay_rate)], axis=1)
+    small_rows = small_rows.reshape(head_pairs, 2, 4, tokens).transpose(0, 2, 1, 3)
+    small_rows = small_rows.reshape(head_pairs, 8, tokens)
+    scan = Scan(tokens, inner_local, state_width)
+    own_state = scan.own_state(source_rows, small_rows, write_rows, True)
+    entering = chained(own_state, running[:, -1], "ctx", 1)
+    within_rows = scan.within(source_rows, small_rows, write_rows, read_rows)
     queries = matmul_low(input_one, attn_q).astype(jnp.bfloat16)
-    query_rows = queries.reshape(tokens, heads_query, AHEAD_DIM)
-    row_place = jnp.arange(tokens, dtype=jnp.int32)
-    key_block = jnp.arange(ctx_count * tokens, dtype=jnp.int32) // tokens
-    key_place = jnp.arange(ctx_count * tokens, dtype=jnp.int32) % tokens
-    allowed = jnp.where(
-        key_block[None, :] == 0,
-        key_place[None, :] <= row_place[:, None],
-        key_block[None, :] <= ctx_rank,
-    )
-    scores = (
-        jnp.einsum("qhd,kd->hqk", query_rows, key_rows, preferred_element_type=jnp.float32) * factor
-    )
-    masked = jnp.where(allowed[None], scores, NEG_FILL)
-    maxima = jnp.max(masked, axis=-1, keepdims=True)
-    weights = jnp.exp(masked - maxima)
-    probability = weights / jnp.sum(weights, axis=-1, keepdims=True)
-    prob_low = probability.astype(jnp.bfloat16)
-    mixed_rows = jnp.einsum("hqk,kd->qhd", prob_low, value_rows, preferred_element_type=jnp.float32)
-    attended = mixed_rows.reshape(tokens, heads_query * AHEAD_DIM).astype(jnp.bfloat16)
+    attend = Attend(tokens, ctx_count * tokens, heads_query)
+    rank = ctx_rank.astype(jnp.int32)[None]
+    attended, log_rows = attend.forward(rank, queries, key_rows, value_rows)
+    ssm_values, gated_rows = scan.carried(within_rows, gate_ssm, small_rows, read_rows, entering)
 
     def mixer_share(index):
         return matmul_low(cut(gated_rows, index, half, 0), ssm_out) + matmul_low(
@@ -338,24 +671,13 @@
         mix_columns, dp_rows(jnp.concatenate([gated_rows, attended], axis=1))
     )
     grad_gated = times_back(grad_mix, ssm_out)
-    grad_values = round_keep(grad_gated * gate_act).reshape(tokens, heads_local, head_width)
+    grad_values = (grad_gated * jax.nn.silu(gate_ssm)).astype(jnp.bfloat16)
     grad_gate_ssm = (grad_gated * ssm_values * silu_slope(gate_ssm)).astype(jnp.bfloat16)
     grad_attended = times_back(grad_mix, attn_out).astype(jnp.bfloat16)
-    from_start = jnp.exp(running)
-    own_grad = jnp.einsum("th,thp,tn->hpn", from_start, grad_values, read_rows, precision=PRECISE)
-    leaving = chained(own_grad, running[-1], "ctx", -1)
-
-    grad_rows = grad_attended.reshape(tokens, heads_query, AHEAD_DIM)
-    grad_value = jnp.einsum("hqk,qhd->kd", prob_low, grad_rows, preferred_element_type=jnp.float32)
-    grad_prob = jnp.einsum("qhd,kd->hqk", grad_rows, value_rows, preferred_element_type=jnp.float32)
-    centre = jnp.sum(probability * grad_prob, axis=-1, keepdims=True)
-    grad_score = (probability * (grad_prob - centre)).astype(jnp.bfloat16)
-    grad_query = (
-        jnp.einsum("hqk,kd->qhd", grad_score, key_rows, preferred_element_type=jnp.float32) * factor
-    )
-    grad_query_low = grad_query.reshape(tokens, heads_query * AHEAD_DIM).astype(jnp.bfloat16)
-    grad_key = (
-        jnp.einsum("hqk,qhd->kd", grad_score, query_rows, preferred_element_type=jnp.float32) * factor
+    own_grad = scan.own_state(grad_values, small_rows, read_rows, False)
+    leaving = chained(own_grad, running[:, -1], "ctx", -1)
+    grad_query_low, grad_key, grad_value = attend.back(
+        rank, queries, grad_attended, log_rows, key_rows, value_rows
     )
     kv_kept = jnp.where(core == 0, grad_key, grad_value)
     kv_given = jnp.where(core == 0, grad_value, grad_key).astype(jnp.bfloat16)
@@ -369,12 +691,20 @@
         )
     grad_kv_low = kv_sum.astype(jnp.bfloat16)
 
-    ssm_grads = ssm_back((grad_values, leaving))
-    grad_dt_pre = ssm_grads[3] * jax.nn.sigmoid(dt_pre)
-    grad_dt_bias = jnp.sum(grad_dt_pre, axis=0)
-    grad_dt_low = grad_dt_pre.astype(jnp.bfloat16)
-    grad_source_low = ssm_grads[0].reshape(tokens, inner_local).astype(jnp.bfloat16)
-    grad_bc = jnp.concatenate([ssm_grads[1], ssm_grads[2]], axis=1)
+    grad_written, scan_sums, grad_b, grad_c = scan.within_back(
+        source_rows, grad_values, small_rows, write_rows, read_rows
+    )
+    grad_source_low, steps, grad_b, grad_c = scan.carried_back(
+        source_rows, grad_values, small_rows, scan_sums, grad_written,
+        write_rows, read_rows, entering, leaving, grad_b, grad_c,
+    )
+    grad_dt_pre = steps[:, 0:2].reshape(heads_local, tokens) * jax.nn.sigmoid(dt_pre)
+    flow_rows = steps[:, 2:4].reshape(heads_local, tokens)
+    grad_dt_bias = jnp.sum(grad_dt_pre, axis=1)
+    grad_a_log = decay_rate * jnp.sum(dt_rows * flow_rows, axis=1)
+    grad_d_skip = jnp.sum(scan_sums[:, 4, : 2 * head_width].reshape(heads_local, head_width), axis=1)
+    grad_dt_low = grad_dt_pre.astype(jnp.bfloat16).T
+    grad_bc = jnp.concatenate([grad_b, grad_c], axis=1)
     bc_pair = 2 * bc_share
     bc_sent = partner(cut(grad_bc, 1 - chip, bc_pair, 1).astype(jnp.bfloat16), CHIP)
     bc_mine = cut(grad_bc, chip, bc_pair, 1) + bc_sent.astype(jnp.float32)
@@ -444,8 +774,8 @@
     small = jnp.concatenate(
         [
             grad_dt_bias,
-            ssm_grads[4],
-            ssm_grads[5],
+            grad_a_log,
+            grad_d_skip,
             both[2 * model_width : 2 * model_width + 3],
         ]
     )

time: 854 us -> 730 us (0.85)
  matrix products: 175 us -> 97.8 us
  local copies, waits for them, and re-layouts: 154 us -> 96.4 us
  Pallas kernels: 0 us -> 55.7 us
  other arithmetic: 93.2 us -> 63.1 us
  waiting for transfers between devices: 342 us -> 328 us
    dot_general x35 -> x1, matrix products: 76.8 us -> 1.51 us  [body(): lax.dot_general(ssm_dt, input_one, (((0,), (1,)), ((), ())), preferred_el...]
    pallas_call x0 -> x8, Pallas kernels: none -> 55.7 us  [call(): pl.pallas_call(kernel, name=name, grid=grid, in_specs=specs, out_specs=[s...]
    dynamic_update_slice x10 -> x0, local copies, waits for them, and re-layouts: 41.5 us -> none  [run_ssd(): lax.scan(jax.checkpoint(stepper), entering, (blocked(source_heads), block...]
    another operation x41 -> x10, local copies, waits for them, and re-layouts: 16.3 us -> 0.53 us  [the longest x5 0.32 us: body(): jnp.stack([running, dt_rows, by_head(d_skip), by_head(decay_rate)], axis=1)]
    another operation x29 -> x4, other arithmetic: 17.7 us -> 2.58 us
    unnamed x180 -> x197, local copies, waits for them, and re-layouts: 45.6 us -> 52.5 us
    dot_general x12 -> x11, matrix products: 33.8 us -> 38.8 us  [matmul_low(): return jnp.dot(former, latter, preferred_element_type=jnp.float32)]
  transfers between devices with their start and end apart: 63 -> 63, of which waited for: 31 -> 27; matrix products, arithmetic and copies ran while one was open for 42% -> 27% of each run, Pallas kernels for 0% -> 7%
where the time goes in v2:
time: 730 us; the launch traced here: 720 us
  waiting for transfers between devices  328 us (45%)
  matrix products  97.8 us (13%)
  local copies, waits for them, and re-layouts  96.4 us (13%)
  starting transfers between devices  63.2 us (9%)
  other arithmetic  63.1 us (9%)
  Pallas kernels  55.7 us (8%)
  between operations  16 us (2%)
    ppermute x16, waiting for transfers between devices, shifted(): lax.ppermute(value, axis, [(i, (i + shift) % count) for i in range(count)])  163 us
    ppermute x16, waiting for transfers between devices, moved(): return lax.ppermute(value, axis, pairs)  93.9 us
    ppermute x27, waiting for transfers between devices, partner(): return lax.ppermute(value, 'tensor', pairs_of(stride))  70.8 us
    pallas_call x8, Pallas kernels, call(): pl.pallas_call(kernel, name=name, grid=grid, in_specs=specs, out_specs=[s...  55.7 us
    unnamed x197, local copies, waits for them, and re-layouts  52.5 us
    dot_general x11, matrix products, matmul_low(): return jnp.dot(former, latter, preferred_element_type=jnp.float32)  38.8 us
    ppermute x16, starting transfers between devices, moved(): return lax.ppermute(value, axis, pairs)  31.7 us
    dot_general x7, matrix products, times_back(): lax.dot_general(former, latter, (((1,), (1,)), ((), ())), preferred_eleme...  30.8 us
  transfers between devices with their start and end apart: 63, of which 27 were waited for; matrix products, arithmetic and copies ran while one was open for 27% of the time, Pallas kernels for 7%

profile of v2, /device:TPU:0, one launch (start us, length us, event | category | flops | bytes accessed | tf_op | source)
XLA Modules:
  0.0 719.9 jit_solution(9186862002781007465)
XLA Ops:
  7.3 2.2 fusion.5
  9.5 2.6 constant_dynamic-slice_fusion.15
  12.1 2.8 fusion.93
  15.6 5.7 collective-permute-start.5
  21.3 4.5 collective-permute-start.6
  36.6 4.3 copy.94
  40.9 3.4 fusion.151
  47.5 3.3 convolution_convert_fusion.5.q_ref
  51.3 2.2 copy.95
  57.7 4.7 own_state.2
  63.4 4.5 scan.1.y_ref
  73.1 2.3 collective-permute-start.3
  77.0 3.1 collective-permute-done
  80.2 8.5 %collective-permute-done.1 = bf16[768,256]{1,0:T(8,128)(2,1)} collective-permute-done((bf16[768,256]{1,0:T(8,128)(2,1)}, bf16[768,256]{1,0:T(8,128)(2,1)}, u32[]{:S(2)}, u32[]{:S(2)}) %collective-permute-start.1) | collective-permute-done | bytes 393248 | tf_op jit(solution)/shard_map/ppermute | solution.py:37
  88.6 7.0 collective-permute-done.3
  97.1 4.8 carry.1
  104.7 6.7 attend.1
  119.2 23.8 %collective-permute-done.10 = bf16[256,2048]{1,0:T(8,128)(2,1)S(1)} collective-permute-done((bf16[256,2048]{1,0:T(8,128)(2,1)S(1)}, bf16[256,2048]{1,0:T(8,128)(2,1)S(1)}, u32[]{:S(2)}, u32[]{:S(2)}) %collective-permute-start.10) | collective-permute-done | bytes 1048608 | tf_op jit(solution)/shard_map/ppermute | solution.py:26
  147.3 10.4 %copy.98 = bf16[256,8,2,1024]{3,1,2,0:T(8,128)(2,1)} copy(bf16[256,8,2,1024]{3,2,1,0:T(2,128)(2,1)} %bitcast.148) | data formatting | bytes 16777216
  160.5 15.8 %fusion.22 = f32[512,2048]{1,0:T(8,128)S(1)} fusion(bf16[2048,2048]{1,0:T(8,128)(2,1)} %bitcast.149, bf16[256,2048]{1,0:T(8,128)(2,1)S(1)} %get-tuple-element.141, bf16[256,2048]{1,0:T(8,128)(2,1)S(1)} %get-tuple-element.140), kind=kOutput, calls=%fused_computation.47 | convolution fusion | flops 4299161600 | bytes 14680064 | tf_op jit(solution)/shard_map/dot_general | solution.py:113
  176.4 4.1 multiply_convert_fusion
  180.5 2.7 convolution_convert_fusion.1
  183.8 2.4 convolution_convert_fusion.3
  188.1 12.9 %collective-permute-done.56 = bf16[256,1024]{1,0:T(8,128)(2,1)} collective-permute-done((bf16[256,1024]{1,0:T(8,128)(2,1)S(1)}, bf16[256,1024]{1,0:T(8,128)(2,1)}, u32[]{:S(2)}, u32[]{:S(2)}) %collective-permute-start.56) | collective-permute-done | bytes 524320 | tf_op jit(solution)/shard_map/ppermute | solution.py:31
  202.6 3.3 add_convert_fusion.2
  207.4 3.4 add_convert_fusion.1
  213.9 13.0 %collective-permute-done.58 = bf16[512,1024]{1,0:T(8,128)(2,1)} collective-permute-done((bf16[512,1024]{1,0:T(8,128)(2,1)}, bf16[512,1024]{1,0:T(8,128)(2,1)}, u32[]{:S(2)}, u32[]{:S(2)}) %collective-permute-start.58) | collective-permute-done | bytes 1048608 | tf_op jit(solution)/shard_map/ppermute | solution.py:31
  226.9 5.7 fusion.65
  232.7 21.2 %collective-permute-done.16 = bf16[256,2048]{1,0:T(8,128)(2,1)} collective-permute-done((bf16[256,2048]{1,0:T(8,128)(2,1)}, bf16[256,2048]{1,0:T(8,128)(2,1)}, u32[]{:S(2)}, u32[]{:S(2)}) %collective-permute-start.16) | collective-permute-done | bytes 1048608 | tf_op jit(solution)/shard_map/ppermute | solution.py:26
  254.0 5.6 multiply_reduce_fusion.3
  259.6 3.7 fusion.154
  263.3 2.7 collective-permute-done.17
  269.5 12.5 %collective-permute-done.47 = bf16[256,1024]{1,0:T(8,128)(2,1)S(1)} collective-permute-done((bf16[256,1024]{1,0:T(8,128)(2,1)S(1)}, bf16[256,1024]{1,0:T(8,128)(2,1)S(1)}, u32[]{:S(2)}, u32[]{:S(2)}) %collective-permute-start.47) | collective-permute-done | bytes 524320 | tf_op jit(solution)/shard_map/ppermute | solution.py:31
  284.0 19.7 %collective-permute-done.49 = bf16[512,1024]{1,0:T(8,128)(2,1)S(1)} collective-permute-done((bf16[512,1024]{1,0:T(8,128)(2,1)S(1)}, bf16[512,1024]{1,0:T(8,128)(2,1)S(1)}, u32[]{:S(2)}, u32[]{:S(2)}) %collective-permute-start.49) | collective-permute-done | bytes 1048608 | tf_op jit(solution)/shard_map/ppermute | solution.py:31
  303.7 3.8 fusion.70
  307.6 3.3 pad_maximum_fusion.1
  314.0 55.3 %collective-permute-done.53 = bf16[256,1024]{1,0:T(8,128)(2,1)} collective-permute-done((bf16[256,1024]{1,0:T(8,128)(2,1)S(1)}, bf16[256,1024]{1,0:T(8,128)(2,1)}, u32[]{:S(2)}, u32[]{:S(2)}) %collective-permute-start.53) | collective-permute-done | bytes 524320 | tf_op jit(solution)/shard_map/ppermute | solution.py:31
  371.9 9.5 %collective-permute-done.20 = f32[12]{0:T(128)S(1)} collective-permute-done((f32[12]{0:T(128)S(1)}, f32[12]{0:T(128)S(1)}, u32[]{:S(2)}, u32[]{:S(2)}) %collective-permute-start.20) | collective-permute-done | bytes 80 | tf_op jit(solution)/shard_map/ppermute | solution.py:37
  381.3 2.7 collective-permute-done.22
  390.1 8.1 %fusion.16 = bf16[1024,2048]{1,0:T(8,128)(2,1)} fusion(bf16[512,2048]{1,0:T(8,128)(2,1)} %collective-permute-done.55, bf16[512,1024]{1,0:T(8,128)(2,1)S(1)} %copy-done.64, bf16[512,1024]{1,0:T(8,128)(2,1)S(1)} %copy-done.66, bf16[256,1024]{1,0:T(8,128)(2,1)S(1)} %get-tuple-element.147, bf16[256,1024]{1,0:T(8,128)(2,1)S(1)} %get-tuple-element.146, ...), kind=kOutput, calls=%fused_computation.19 | convolution fusion | flops 4315938816 | bytes 10485760 | tf_op jit(solution)/shard_map/dot_general | solution.py:117
  398.3 4.1 multiply_convert_fusion.4
  402.4 3.6 own_state.3
  411.1 8.8 %attend_back.1 = (bf16[512,256]{1,0:T(8,128)(2,1)S(1)}, f32[2048,128]{1,0:T(8,128)S(1)}, f32[2048,128]{1,0:T(8,128)S(1)}) custom-call(s32[1]{0:T(128)} %bitcast.6.rank_ref, bf16[512,256]{1,0:T(8,128)(2,1)S(1)} %copy-done.31, bf16[512,256]{1,0:T(8,128)(2,1)S(1)} %fusion.77.do_ref, f32[2,8,512]{2,1,0:T(8,128)S(1)} %get-tuple-element.40.log_ref, ...), custom_call_target="tpu_custom_call" | custom-call | flops 5368709120 | bytes 3964932 | tf_op jit(solution)/shard_map/attend_back/pallas_call | solution.py:399
  424.0 10.0 %scan_back.1 = (f32[512,768]{1,0:T(8,128)S(1)}, f32[6,8,512]{2,1,0:T(8,128)S(1)}, f32[512,256]{1,0:T(8,128)S(1)}, f32[512,256]{1,0:T(8,128)S(1)}) custom-call(bf16[512,768]{1,0:T(8,128)(2,1)S(1)} %copy-done.2, bf16[512,768]{1,0:T(8,128)(2,1)S(1)} %get-tuple-element.193.dy_ref.u_ref, f32[6,8,512]{2,1,0:T(8,128)S(1)} %reshape.244.small_ref, ...), custom_call_target="tpu_custom_call" | custom-call | flops 4026531840 | bytes 4915200 | tf_op jit(solution)/shard_map/scan_back/pallas_call | solution.py:399
  435.1 53.5 %collective-permute-done.19 = bf16[768,256]{1,0:T(8,128)(2,1)S(1)} collective-permute-done((bf16[768,256]{1,0:T(8,128)(2,1)S(1)}, bf16[768,256]{1,0:T(8,128)(2,1)S(1)}, u32[]{:S(2)}, u32[]{:S(2)}) %collective-permute-start.19) | collective-permute-done | bytes 393248 | tf_op jit(solution)/shard_map/ppermute | solution.py:37
  488.9 12.7 %carry_back.1 = (bf16[512,768]{1,0:T(8,128)(2,1)S(1)}, f32[6,8,512]{2,1,0:T(8,128)S(1)}, f32[512,256]{1,0:T(8,128)S(1)}, f32[512,256]{1,0:T(8,128)S(1)}) custom-call(bf16[512,768]{1,0:T(8,128)(2,1)S(1)} %copy-done.2, bf16[512,768]{1,0:T(8,128)(2,1)S(1)} %get-tuple-element.193.dy_ref.u_ref, f32[6,8,512]{2,1,0:T(8,128)S(1)} %reshape.244.small_ref, ...), custom_call_target="tpu_custom_call" | custom-call | flops 1207959552 | bytes 7634944 | tf_op jit(solution)/shard_map/carry_back/pallas_call | solution.py:399
  517.4 3.7 collective-permute-done.24
  521.1 6.0 collective-permute-done.25
  533.4 6.0 constant_dynamic-update-slice_fusion.5
  539.4 4.1 constant_dynamic-slice_fusion.14
  544.6 42.2 %collective-permute-done.37 = bf16[256,1024]{1,0:T(8,128)(2,1)} collective-permute-done((bf16[256,1024]{1,0:T(8,128)(2,1)}, bf16[256,1024]{1,0:T(8,128)(2,1)}, u32[]{:S(2)}, u32[]{:S(2)}) %collective-permute-start.37) | collective-permute-done | bytes 524320 | tf_op jit(solution)/shard_map/ppermute | solution.py:31
  593.4 9.1 %convolution_convert_fusion = bf16[1024,2176]{1,0:T(8,128)(2,1)} fusion(bf16[512,2176]{1,0:T(8,128)(2,1)} %collective-permute-done.39, bf16[512,2176]{1,0:T(8,128)(2,1)} %pad_dynamic-update-slice_fusion.1, bf16[256,1024]{1,0:T(8,128)(2,1)S(1)} %get-tuple-element.151, bf16[256,1024]{1,0:T(8,128)(2,1)S(1)} %get-tuple-element.150, ...), kind=kOutput, calls=%fused_computation | convolution fusion | flops 4580835328 | bytes 11010048 | tf_op jit(solution)/shard_map/dot_general | solution.py:117
  604.6 8.3 %convolution_convert_fusion.2 = bf16[256,2048]{1,0:T(8,128)(2,1)} fusion(bf16[2048,2176]{1,0:T(8,128)(2,1)} %pad_dynamic-update-slice_fusion, bf16[512,2176]{1,0:T(8,128)(2,1)} %pad_dynamic-update-slice_fusion.1, s32[]{:T(128)S(6)} %select_n.296), kind=kOutput, calls=%fused_computation.45 | convolution fusion | flops 2282225664 | bytes 11075588 | tf_op jit(solution)/shard_map/dot_general | solution.py:123
  616.6 7.8 %add_convert_fusion = bf16[256,2048]{1,0:T(8,128)(2,1)} fusion(bf16[256,2048]{1,0:T(8,128)(2,1)} %collective-permute-done.29, bf16[2048,2176]{1,0:T(8,128)(2,1)} %pad_dynamic-update-slice_fusion, bf16[512,2176]{1,0:T(8,128)(2,1)} %pad_dynamic-update-slice_fusion.1, s32[]{:T(128)S(6)} %select_n.288), kind=kOutput, calls=%fused_computation.94 | convolution fusion | flops 2283274240 | bytes 12124164 | tf_op jit(solution)/shard_map/dot_general | solution.py:123
  630.5 2.5 copy.90
  633.1 17.2 %collective-permute-done.30 = bf16[256,2048]{1,0:T(8,128)(2,1)} collective-permute-done((bf16[256,2048]{1,0:T(8,128)(2,1)}, bf16[256,2048]{1,0:T(8,128)(2,1)}, u32[]{:S(2)}, u32[]{:S(2)}) %collective-permute-start.30) | collective-permute-done | bytes 1048608 | tf_op jit(solution)/shard_map/ppermute | solution.py:26
  650.2 2.7 fusion.29
  653.0 3.0 fusion.26
  661.5 2.7 collective-permute-start.46
  669.5 2.2 collective-permute-start.35
  681.0 2.3 copy.87
  685.1 4.1 reshape.258
  697.4 3.1 reshape.249
  705.6 3.2 collective-permute-done.42
  (429 shorter events, 163.1 us)
Async XLA Ops:
  7.2 94.7 %copy-start = (bf16[768,2048]{1,0:T(8,128)(2,1)S(1)}, bf16[768,2048]{1,0:T(8,128)(2,1)}, u32[]{:S(2)}) copy-start(bf16[768,2048]{1,0:T(8,128)(2,1)} %param.25) | copy-start | bytes 9437188
  7.2 621.2 %reduce-scatter.11.cloned.1.call-start = ((), (), s32[]{:S(2)}) async-start(), calls=%async_computation.7 | async-start | bytes 2621440 | tf_op jit(solution)/shard_map/reduce_scatter | solution.py:79
  15.6 57.5 %collective-permute-start.5 = (bf16[512,128]{1,0:T(8,128)(2,1)}, bf16[512,128]{1,0:T(8,128)(2,1)}, u32[]{:S(2)}, u32[]{:S(2)}) collective-permute-start(bf16[512,128]{1,0:T(8,128)(2,1)} %dynamic-slice_convert_fusion.1), channel_id=1, source_target_pairs={{0,4},{4,8},{8,12},{1,5},{5,9},{9,13},{2,6},{6,10},{10,14},{3,7},{... | collective-permute-start | bytes 393224 | tf_op jit(solution)/shard_map/ppermute | solution.py:37
  21.3 54.4 %collective-permute-start.6 = (bf16[512,128]{1,0:T(8,128)(2,1)}, bf16[512,128]{1,0:T(8,128)(2,1)}, u32[]{:S(2)}, u32[]{:S(2)}) collective-permute-start(bf16[512,128]{1,0:T(8,128)(2,1)} %dynamic-slice_convert_fusion.1), channel_id=1, source_target_pairs={{0,8},{4,12},{1,9},{5,13},{2,10},{6,14},{3,11},{7,15},{16,24},{20,... | collective-permute-start | bytes 393224 | tf_op jit(solution)/shard_map/ppermute | solution.py:37
  25.8 49.9 %collective-permute-start.7 = (bf16[512,128]{1,0:T(8,128)(2,1)}, bf16[512,128]{1,0:T(8,128)(2,1)}, u32[]{:S(2)}, u32[]{:S(2)}) collective-permute-start(bf16[512,128]{1,0:T(8,128)(2,1)} %dynamic-slice_convert_fusion.1), channel_id=1, source_target_pairs={{0,12},{1,13},{2,14},{3,15},{16,28},{17,29},{18,30},{19,31}} | collective-permute-start | bytes 393224 | tf_op jit(solution)/shard_map/ppermute | solution.py:37
  33.9 35.1 %collective-permute-start.2 = (f32[12]{0:T(128)S(1)}, f32[12]{0:T(128)S(1)}, u32[]{:S(2)}, u32[]{:S(2)}) collective-permute-start(f32[12]{0:T(128)S(1)} %slice_reduce_fusion.1), channel_id=1, source_target_pairs={{0,4},{4,8},{8,12},{1,5},{5,9},{9,13},{2,6},{6,10},{10,14},{3,7},{... | collective-permute-start | bytes 152 | tf_op jit(solution)/shard_map/ppermute | solution.py:37
  35.2 35.9 %collective-permute-start.4 = (f32[12]{0:T(128)S(1)}, f32[12]{0:T(128)S(1)}, u32[]{:S(2)}, u32[]{:S(2)}) collective-permute-start(f32[12]{0:T(128)S(1)} %slice_reduce_fusion.1), channel_id=1, source_target_pairs={{0,8},{4,12},{1,9},{5,13},{2,10},{6,14},{3,11},{7,15},{16,24},{20,... | collective-permute-start | bytes 152 | tf_op jit(solution)/shard_map/ppermute | solution.py:37
  69.0 11.2 %collective-permute-start = (bf16[768,256]{1,0:T(8,128)(2,1)}, bf16[768,256]{1,0:T(8,128)(2,1)}, u32[]{:S(2)}, u32[]{:S(2)}) collective-permute-start(bf16[768,256]{1,0:T(8,128)(2,1)} %own_state.2), channel_id=1, source_target_pairs={{0,4},{4,8},{8,12},{1,5},{5,9},{9,13},{2,6},{6,10},{10,14},{3,7},{... | collective-permute-start | bytes 1179656 | tf_op jit(solution)/shard_map/ppermute | solution.py:37
  71.1 17.6 %collective-permute-start.1 = (bf16[768,256]{1,0:T(8,128)(2,1)}, bf16[768,256]{1,0:T(8,128)(2,1)}, u32[]{:S(2)}, u32[]{:S(2)}) collective-permute-start(bf16[768,256]{1,0:T(8,128)(2,1)} %own_state.2), channel_id=1, source_target_pairs={{0,8},{4,12},{1,9},{5,13},{2,10},{6,14},{3,11},{7,15},{16,24},{20,... | collective-permute-start | bytes 1179656 | tf_op jit(solution)/shard_map/ppermute | solution.py:37
  73.1 22.5 %collective-permute-start.3 = (bf16[768,256]{1,0:T(8,128)(2,1)}, bf16[768,256]{1,0:T(8,128)(2,1)}, u32[]{:S(2)}, u32[]{:S(2)}) collective-permute-start(bf16[768,256]{1,0:T(8,128)(2,1)} %own_state.2), channel_id=1, source_target_pairs={{0,12},{1,13},{2,14},{3,15},{16,28},{17,29},{18,30},{19,31}} | collective-permute-start | bytes 1179656 | tf_op jit(solution)/shard_map/ppermute | solution.py:37
  76.9 26.4 %collective-permute-start.8 = (bf16[2048,128]{1,0:T(8,128)(2,1)S(1)}, bf16[2048,128]{1,0:T(8,128)(2,1)S(1)}, u32[]{:S(2)}, u32[]{:S(2)}) collective-permute-start(bf16[2048,128]{1,0:T(8,128)(2,1)S(1)} %pad_maximum_fusion.8), channel_id=1, source_target_pairs={{0,1},{1,0},{2,3},{3,2},{4,5},{5,4},{6,7},{7,6},{8,9},{9,8},{10,11... | collective-permute-start | bytes 1572872 | tf_op jit(solution)/shard_map/ppermute | solution.py:26
  112.9 3.0 collective-permute-start.9
  117.6 25.4 %collective-permute-start.10 = (bf16[256,2048]{1,0:T(8,128)(2,1)S(1)}, bf16[256,2048]{1,0:T(8,128)(2,1)S(1)}, u32[]{:S(2)}, u32[]{:S(2)}) collective-permute-start(bf16[256,2048]{1,0:T(8,128)(2,1)S(1)} %fusion.20), channel_id=1, source_target_pairs={{0,2},{1,3},{2,0},{3,1},{4,6},{5,7},{6,4},{7,5},{8,10},{9,11},{10,... | collective-permute-start | bytes 3145736 | tf_op jit(solution)/shard_map/ppermute | solution.py:26
  147.2 10.4 %collective-permute-start.11 = (bf16[256,2048]{1,0:T(8,128)(2,1)}, bf16[256,2048]{1,0:T(8,128)(2,1)}, u32[]{:S(2)}, u32[]{:S(2)}) collective-permute-start(bf16[256,2048]{1,0:T(8,128)(2,1)} %multiply_convert_fusion.3), channel_id=1, source_target_pairs={{0,1},{1,0},{2,3},{3,2},{4,5},{5,4},{6,7},{7,6},{8,9},{9,8},{10,11... | collective-permute-start | bytes 3145736 | tf_op jit(solution)/shard_map/ppermute | solution.py:26
  183.2 19.4 %collective-permute-start.12 = (bf16[256,2048]{1,0:T(8,128)(2,1)S(1)}, bf16[256,2048]{1,0:T(8,128)(2,1)S(1)}, u32[]{:S(2)}, u32[]{:S(2)}) collective-permute-start(bf16[256,2048]{1,0:T(8,128)(2,1)S(1)} %convolution_convert_fusion.1), channel_id=1, source_target_pairs={{0,1},{1,0},{2,3},{3,2},{4,5},{5,4},{6,7},{7,6},{8,9},{9,8},{10,11... | collective-permute-start | bytes 3145736 | tf_op jit(solution)/shard_map/ppermute | solution.py:26
  186.2 21.2 %collective-permute-start.15 = (bf16[256,2048]{1,0:T(8,128)(2,1)S(1)}, bf16[256,2048]{1,0:T(8,128)(2,1)S(1)}, u32[]{:S(2)}, u32[]{:S(2)}) collective-permute-start(bf16[256,2048]{1,0:T(8,128)(2,1)S(1)} %convolution_convert_fusion.3), channel_id=1, source_target_pairs={{0,1},{1,0},{2,3},{3,2},{4,5},{5,4},{6,7},{7,6},{8,9},{9,8},{10,11... | collective-permute-start | bytes 3145736 | tf_op jit(solution)/shard_map/ppermute | solution.py:26
  186.6 14.5 %collective-permute-start.56 = (bf16[256,1024]{1,0:T(8,128)(2,1)S(1)}, bf16[256,1024]{1,0:T(8,128)(2,1)}, u32[]{:S(2)}, u32[]{:S(2)}) collective-permute-start(bf16[256,1024]{1,0:T(8,128)(2,1)S(1)} %dynamic-slice_bitcast_fusion.1), channel_id=1, source_target_pairs={{0,16},{16,0},{1,17},{17,1},{2,18},{18,2},{3,19},{19,3},{4,20},{20... | collective-permute-start | bytes 1572872 | tf_op jit(solution)/shard_map/ppermute | solution.py:31
  201.0 11.6 %collective-permute-start.57 = (bf16[256,1024]{1,0:T(8,128)(2,1)}, bf16[256,1024]{1,0:T(8,128)(2,1)}, u32[]{:S(2)}, u32[]{:S(2)}) collective-permute-start(bf16[256,1024]{1,0:T(8,128)(2,1)} %collective-permute-done.56), channel_id=1, source_target_pairs={{0,1},{1,0},{2,3},{3,2},{4,5},{5,4},{6,7},{7,6},{8,9},{9,8},{10,11... | collective-permute-start | bytes 1572872 | tf_op jit(solution)/shard_map/ppermute | solution.py:26
  201.0 25.9 %collective-permute-start.58 = (bf16[512,1024]{1,0:T(8,128)(2,1)}, bf16[512,1024]{1,0:T(8,128)(2,1)}, u32[]{:S(2)}, u32[]{:S(2)}) collective-permute-start(bf16[512,1024]{1,0:T(8,128)(2,1)} %get-tuple-element.132), channel_id=1, source_target_pairs={{0,16},{16,0},{1,17},{17,1},{2,18},{18,2},{3,19},{19,3},{4,20},{20... | collective-permute-start | bytes 3145736 | tf_op jit(solution)/shard_map/ppermute | solution.py:31
  205.9 26.9 %collective-permute-start.13 = (bf16[256,2048]{1,0:T(8,128)(2,1)}, bf16[256,2048]{1,0:T(8,128)(2,1)}, u32[]{:S(2)}, u32[]{:S(2)}) collective-permute-start(bf16[256,2048]{1,0:T(8,128)(2,1)} %add_convert_fusion.2), channel_id=1, source_target_pairs={{0,2},{1,3},{2,0},{3,1},{4,6},{5,7},{6,4},{7,5},{8,10},{9,11},{10,... | collective-permute-start | bytes 3145736 | tf_op jit(solution)/shard_map/ppermute | solution.py:26
  210.8 43.2 %collective-permute-start.16 = (bf16[256,2048]{1,0:T(8,128)(2,1)}, bf16[256,2048]{1,0:T(8,128)(2,1)}, u32[]{:S(2)}, u32[]{:S(2)}) collective-permute-start(bf16[256,2048]{1,0:T(8,128)(2,1)} %add_convert_fusion.1), channel_id=1, source_target_pairs={{0,2},{1,3},{2,0},{3,1},{4,6},{5,7},{6,4},{7,5},{8,10},{9,11},{10,... | collective-permute-start | bytes 3145736 | tf_op jit(solution)/shard_map/ppermute | solution.py:26
  232.6 445.3 %reduce-scatter.7.cloned.1.call-start = ((), (), s32[]{:S(2)}) async-start(), calls=%async_computation.5 | async-start | bytes 2621440 | tf_op jit(solution)/shard_map/reduce_scatter | solution.py:79
  263.3 2.7 collective-permute-start.17
  267.2 14.8 %collective-permute-start.47 = (bf16[256,1024]{1,0:T(8,128)(2,1)S(1)}, bf16[256,1024]{1,0:T(8,128)(2,1)S(1)}, u32[]{:S(2)}, u32[]{:S(2)}) collective-permute-start(bf16[256,1024]{1,0:T(8,128)(2,1)S(1)} %fusion.98), channel_id=1, source_target_pairs={{0,16},{16,0},{1,17},{17,1},{2,18},{18,2},{3,19},{19,3},{4,20},{20... | collective-permute-start | bytes 1572872 | tf_op jit(solution)/shard_map/ppermute | solution.py:31
  268.1 35.6 %collective-permute-start.49 = (bf16[512,1024]{1,0:T(8,128)(2,1)S(1)}, bf16[512,1024]{1,0:T(8,128)(2,1)S(1)}, u32[]{:S(2)}, u32[]{:S(2)}) collective-permute-start(bf16[512,1024]{1,0:T(8,128)(2,1)S(1)} %constant_dynamic-update-slice_fusion.6), channel_id=1, source_target_pairs={{0,16},{16,0},{1,17},{17,1},{2,18},{18,2},{3,19},{19,3},{4,20},{20... | collective-permute-start | bytes 3145736 | tf_op jit(solution)/shard_map/ppermute | solution.py:31
  282.0 1.9 collective-permute-start.48
  307.5 377.6 %reduce-scatter.9.cloned.1.call-start = ((), (), s32[]{:S(2)}) async-start(), calls=%async_computation.6 | async-start | bytes 5242880 | tf_op jit(solution)/shard_map/reduce_scatter | solution.py:79
  310.9 79.2 %collective-permute-start.55 = (bf16[512,2048]{1,0:T(8,128)(2,1)}, bf16[512,2048]{1,0:T(8,128)(2,1)}, u32[]{:S(2)}, u32[]{:S(2)}) collective-permute-start(bf16[512,2048]{1,0:T(8,128)(2,1)} %pad_maximum_fusion.1), channel_id=1, source_target_pairs={{0,16},{16,0},{1,17},{17,1},{2,18},{18,2},{3,19},{19,3},{4,20},{20... | collective-permute-start | bytes 6291464 | tf_op jit(solution)/shard_map/ppermute | solution.py:31
  312.4 56.9 %collective-permute-start.53 = (bf16[256,1024]{1,0:T(8,128)(2,1)S(1)}, bf16[256,1024]{1,0:T(8,128)(2,1)}, u32[]{:S(2)}, u32[]{:S(2)}) collective-permute-start(bf16[256,1024]{1,0:T(8,128)(2,1)S(1)} %fusion.99), channel_id=1, source_target_pairs={{0,16},{16,0},{1,17},{17,1},{2,18},{18,2},{3,19},{19,3},{4,20},{20... | collective-permute-start | bytes 1572872 | tf_op jit(solution)/shard_map/ppermute | solution.py:31
  369.3 19.5 %collective-permute-start.54 = (bf16[256,1024]{1,0:T(8,128)(2,1)}, bf16[256,1024]{1,0:T(8,128)(2,1)}, u32[]{:S(2)}, u32[]{:S(2)}) collective-permute-start(bf16[256,1024]{1,0:T(8,128)(2,1)} %collective-permute-done.53), channel_id=1, source_target_pairs={{0,1},{1,0},{2,3},{3,2},{4,5},{5,4},{6,7},{7,6},{8,9},{9,8},{10,11... | collective-permute-start | bytes 1572872 | tf_op jit(solution)/shard_map/ppermute | solution.py:26
  369.3 12.1 %collective-permute-start.20 = (f32[12]{0:T(128)S(1)}, f32[12]{0:T(128)S(1)}, u32[]{:S(2)}, u32[]{:S(2)}) collective-permute-start(f32[12]{0:T(128)S(1)} %copy-done.82), channel_id=1, source_target_pairs={{4,0},{8,4},{12,8},{5,1},{9,5},{13,9},{6,2},{10,6},{14,10},{7,3},{... | collective-permute-start | bytes 152 | tf_op jit(solution)/shard_map/ppermute | solution.py:37
  370.6 13.5 %collective-permute-start.22 = (f32[12]{0:T(128)S(1)}, f32[12]{0:T(128)}, u32[]{:S(2)}, u32[]{:S(2)}) collective-permute-start(f32[12]{0:T(128)S(1)} %copy-done.82), channel_id=1, source_target_pairs={{8,0},{12,4},{9,1},{13,5},{10,2},{14,6},{11,3},{15,7},{24,16},{28,... | collective-permute-start | bytes 152 | tf_op jit(solution)/shard_map/ppermute | solution.py:37
  398.3 290.9 %reduce-scatter.5.cloned.1.call-start = ((), (), s32[]{:S(2)}) async-start(), calls=%async_computation.4 | async-start | bytes 5570560 | tf_op jit(solution)/shard_map/reduce_scatter | solution.py:79
  406.1 29.0 %collective-permute-start.18 = (bf16[768,256]{1,0:T(8,128)(2,1)S(1)}, bf16[768,256]{1,0:T(8,128)(2,1)S(1)}, u32[]{:S(2)}, u32[]{:S(2)}) collective-permute-start(bf16[768,256]{1,0:T(8,128)(2,1)S(1)} %own_state.3), channel_id=1, source_target_pairs={{4,0},{8,4},{12,8},{5,1},{9,5},{13,9},{6,2},{10,6},{14,10},{7,3},{... | collective-permute-start | bytes 1179656 | tf_op jit(solution)/shard_map/ppermute | solution.py:37
  407.5 81.1 %collective-permute-start.19 = (bf16[768,256]{1,0:T(8,128)(2,1)S(1)}, bf16[768,256]{1,0:T(8,128)(2,1)S(1)}, u32[]{:S(2)}, u32[]{:S(2)}) collective-permute-start(bf16[768,256]{1,0:T(8,128)(2,1)S(1)} %own_state.3), channel_id=1, source_target_pairs={{8,0},{12,4},{9,1},{13,5},{10,2},{14,6},{11,3},{15,7},{24,16},{28,... | collective-permute-start | bytes 1179656 | tf_op jit(solution)/shard_map/ppermute | solution.py:37
  408.8 79.8 %collective-permute-start.21 = (bf16[768,256]{1,0:T(8,128)(2,1)S(1)}, bf16[768,256]{1,0:T(8,128)(2,1)S(1)}, u32[]{:S(2)}, u32[]{:S(2)}) collective-permute-start(bf16[768,256]{1,0:T(8,128)(2,1)S(1)} %own_state.3), channel_id=1, source_target_pairs={{12,0},{13,1},{14,2},{15,3},{28,16},{29,17},{30,18},{31,19}} | collective-permute-start | bytes 1179656 | tf_op jit(solution)/shard_map/ppermute | solution.py:37
  420.8 91.1 %collective-permute-start.23 = (bf16[2048,128]{1,0:T(8,128)(2,1)}, bf16[2048,128]{1,0:T(8,128)(2,1)}, u32[]{:S(2)}, u32[]{:S(2)}) collective-permute-start(bf16[2048,128]{1,0:T(8,128)(2,1)} %select_convert_fusion), channel_id=1, source_target_pairs={{0,1},{1,0},{2,3},{3,2},{4,5},{5,4},{6,7},{7,6},{8,9},{9,8},{10,11... | collective-permute-start | bytes 1572872 | tf_op jit(solution)/shard_map/ppermute | solution.py:26
  506.1 11.1 %collective-permute-start.27 = (bf16[512,256]{1,0:T(8,128)(2,1)}, bf16[512,256]{1,0:T(8,128)(2,1)S(1)}, u32[]{:S(2)}, u32[]{:S(2)}) collective-permute-start(bf16[512,256]{1,0:T(8,128)(2,1)} %dynamic-slice_convert_fusion), channel_id=1, source_target_pairs={{0,2},{1,3},{2,0},{3,1},{4,6},{5,7},{6,4},{7,5},{8,10},{9,11},{10,... | collective-permute-start | bytes 786440 | tf_op jit(solution)/shard_map/ppermute | solution.py:26
  513.3 7.8 %collective-permute-start.24 = (bf16[512,128]{1,0:T(8,128)(2,1)S(1)}, bf16[512,128]{1,0:T(8,128)(2,1)S(1)}, u32[]{:S(2)}, u32[]{:S(2)}) collective-permute-start(bf16[512,128]{1,0:T(8,128)(2,1)S(1)} %get-tuple-element.159), channel_id=1, source_target_pairs={{4,0},{8,4},{12,8},{5,1},{9,5},{13,9},{6,2},{10,6},{14,10},{7,3},{... | collective-permute-start | bytes 393224 | tf_op jit(solution)/shard_map/ppermute | solution.py:37
  514.6 12.5 %collective-permute-start.25 = (bf16[512,128]{1,0:T(8,128)(2,1)S(1)}, bf16[512,128]{1,0:T(8,128)(2,1)S(1)}, u32[]{:S(2)}, u32[]{:S(2)}) collective-permute-start(bf16[512,128]{1,0:T(8,128)(2,1)S(1)} %get-tuple-element.161), channel_id=1, source_target_pairs={{8,0},{12,4},{9,1},{13,5},{10,2},{14,6},{11,3},{15,7},{24,16},{28,... | collective-permute-start | bytes 393224 | tf_op jit(solution)/shard_map/ppermute | solution.py:37
  515.9 11.2 %collective-permute-start.26 = (bf16[512,128]{1,0:T(8,128)(2,1)S(1)}, bf16[512,128]{1,0:T(8,128)(2,1)S(1)}, u32[]{:S(2)}, u32[]{:S(2)}) collective-permute-start(bf16[512,128]{1,0:T(8,128)(2,1)S(1)} %get-tuple-element.160), channel_id=1, source_target_pairs={{12,0},{13,1},{14,2},{15,3},{28,16},{29,17},{30,18},{31,19}} | collective-permute-start | bytes 393224 | tf_op jit(solution)/shard_map/ppermute | solution.py:37
  517.3 10.5 %collective-permute-start.28 = (bf16[512,128]{1,0:T(8,128)(2,1)S(1)}, bf16[512,128]{1,0:T(8,128)(2,1)S(1)}, u32[]{:S(2)}, u32[]{:S(2)}) collective-permute-start(bf16[512,128]{1,0:T(8,128)(2,1)S(1)} %dynamic-slice_convert_fusion.2), channel_id=1, source_target_pairs={{0,1},{1,0},{2,3},{3,2},{4,5},{5,4},{6,7},{7,6},{8,9},{9,8},{10,11... | collective-permute-start | bytes 393224 | tf_op jit(solution)/shard_map/ppermute | solution.py:26
  529.3 64.2 %collective-permute-start.39 = (bf16[512,2176]{1,0:T(8,128)(2,1)}, bf16[512,2176]{1,0:T(8,128)(2,1)}, u32[]{:S(2)}, u32[]{:S(2)}) collective-permute-start(bf16[512,2176]{1,0:T(8,128)(2,1)} %pad_dynamic-update-slice_fusion.1), channel_id=1, source_target_pairs={{0,16},{16,0},{1,17},{17,1},{2,18},{18,2},{3,19},{19,3},{4,20},{20... | collective-permute-start | bytes 6684680 | tf_op jit(solution)/shard_map/ppermute | solution.py:31
  532.0 54.8 %collective-permute-start.37 = (bf16[256,1024]{1,0:T(8,128)(2,1)}, bf16[256,1024]{1,0:T(8,128)(2,1)}, u32[]{:S(2)}, u32[]{:S(2)}) collective-permute-start(bf16[256,1024]{1,0:T(8,128)(2,1)} %dynamic_slice.202), channel_id=1, source_target_pairs={{0,16},{16,0},{1,17},{17,1},{2,18},{18,2},{3,19},{19,3},{4,20},{20... | collective-permute-start | bytes 1572872 | tf_op jit(solution)/shard_map/ppermute | solution.py:31
  586.9 5.3 collective-permute-start.38
  612.8 3.7 collective-permute-start.29
  613.4 11.7 %collective-permute-start.14 = (bf16[256,2048]{1,0:T(8,128)(2,1)}, bf16[256,2048]{1,0:T(8,128)(2,1)}, u32[]{:S(2)}, u32[]{:S(2)}) collective-permute-start(bf16[256,2048]{1,0:T(8,128)(2,1)} %get-tuple-element.131), channel_id=1, source_target_pairs={{0,1},{1,0},{2,3},{3,2},{4,5},{5,4},{6,7},{7,6},{8,9},{9,8},{10,11... | collective-permute-start | bytes 3145736 | tf_op jit(solution)/shard_map/ppermute | solution.py:26
  624.4 25.9 %collective-permute-start.30 = (bf16[256,2048]{1,0:T(8,128)(2,1)}, bf16[256,2048]{1,0:T(8,128)(2,1)}, u32[]{:S(2)}, u32[]{:S(2)}) collective-permute-start(bf16[256,2048]{1,0:T(8,128)(2,1)} %add_convert_fusion), channel_id=1, source_target_pairs={{0,2},{1,3},{2,0},{3,1},{4,6},{5,7},{6,4},{7,5},{8,10},{9,11},{10,... | collective-permute-start | bytes 3145736 | tf_op jit(solution)/shard_map/ppermute | solution.py:26
  652.9 3.7 collective-permute-start.32
  656.0 20.0 %collective-permute-start.31 = (bf16[256,2048]{1,0:T(8,128)(2,1)S(1)}, bf16[256,2048]{1,0:T(8,128)(2,1)S(1)}, u32[]{:S(2)}, u32[]{:S(2)}) collective-permute-start(bf16[256,2048]{1,0:T(8,128)(2,1)S(1)} %fusion.26), channel_id=1, source_target_pairs={{0,1},{1,0},{2,3},{3,2},{4,5},{5,4},{6,7},{7,6},{8,9},{9,8},{10,11... | collective-permute-start | bytes 3145736 | tf_op jit(solution)/shard_map/ppermute | solution.py:26
  656.7 3.5 collective-permute-start.43
  657.6 9.9 %collective-permute-start.33 = (f32[1024,2]{0,1:T(2,128)S(1)}, f32[1024,2]{0,1:T(2,128)S(1)}, u32[]{:S(2)}, u32[]{:S(2)}) collective-permute-start(f32[1024,2]{0,1:T(2,128)S(1)} %fusion.127), channel_id=1, source_target_pairs={{0,16},{16,0},{1,17},{17,1},{2,18},{18,2},{3,19},{19,3},{4,20},{20... | collective-permute-start | bytes 24584 | tf_op jit(solution)/shard_map/ppermute | solution.py:31
  660.3 5.7 collective-permute-start.44
  660.3 6.5 collective-permute-start.45
  661.5 5.4 collective-permute-start.46
  667.6 5.7 collective-permute-start.34
  669.5 4.7 collective-permute-start.35
  671.7 3.8 collective-permute-start.36
  690.2 15.5 %collective-permute-start.40 = (f32[256,128]{1,0:T(8,128)S(1)}, f32[256,128]{1,0:T(8,128)}, u32[]{:S(2)}, u32[]{:S(2)}) collective-permute-start(f32[256,128]{1,0:T(8,128)S(1)} %get-tuple-element.143), channel_id=1, source_target_pairs={{0,1},{1,0},{2,3},{3,2},{4,5},{5,4},{6,7},{7,6},{8,9},{9,8},{10,11... | collective-permute-start | bytes 393224 | tf_op jit(solution)/shard_map/ppermute | solution.py:26
  690.3 15.4 %collective-permute-start.41 = (f32[256,128]{1,0:T(8,128)S(1)}, f32[256,128]{1,0:T(8,128)}, u32[]{:S(2)}, u32[]{:S(2)}) collective-permute-start(f32[256,128]{1,0:T(8,128)S(1)} %get-tuple-element.143), channel_id=1, source_target_pairs={{0,2},{1,3},{2,0},{3,1},{4,6},{5,7},{6,4},{7,5},{8,10},{9,11},{10,... | collective-permute-start | bytes 393224 | tf_op jit(solution)/shard_map/ppermute | solution.py:26
  692.8 10.9 %collective-permute-start.50 = (f32[64,128]{1,0:T(8,128)}, f32[64,128]{1,0:T(8,128)}, u32[]{:S(2)}, u32[]{:S(2)}) collective-permute-start(f32[64,128]{1,0:T(8,128)} %get-tuple-element.173), channel_id=1, source_target_pairs={{0,1},{1,0},{2,3},{3,2},{4,5},{5,4},{6,7},{7,6},{8,9},{9,8},{10,11... | collective-permute-start | bytes 98312 | tf_op jit(solution)/shard_map/ppermute | solution.py:26
  692.9 11.0 %collective-permute-start.51 = (f32[64,128]{1,0:T(8,128)}, f32[64,128]{1,0:T(8,128)}, u32[]{:S(2)}, u32[]{:S(2)}) collective-permute-start(f32[64,128]{1,0:T(8,128)} %get-tuple-element.172), channel_id=1, source_target_pairs={{0,2},{1,3},{2,0},{3,1},{4,6},{5,7},{6,4},{7,5},{8,10},{9,11},{10,... | collective-permute-start | bytes 98312 | tf_op jit(solution)/shard_map/ppermute | solution.py:26
  693.2 10.8 %collective-permute-start.52 = (f32[64,128]{1,0:T(8,128)}, f32[64,128]{1,0:T(8,128)}, u32[]{:S(2)}, u32[]{:S(2)}) collective-permute-start(f32[64,128]{1,0:T(8,128)} %get-tuple-element.171), channel_id=1, source_target_pairs={{0,3},{1,2},{2,1},{3,0},{4,7},{5,6},{6,5},{7,4},{8,11},{9,10},{10,... | collective-permute-start | bytes 98312 | tf_op jit(solution)/shard_map/ppermute | solution.py:26
  703.7 5.2 collective-permute-start.42
  (88 other events, 1090.1 us)
Sparse Core Ops, SparseCore 0:
  232.7 52.9 reduce-scatter.10
  307.7 52.0 reduce-scatter.6
  398.4 103.0 reduce-scatter.8
  602.7 78.1 reduce-scatter.4

commit v3 on v2

v3 whole, which is shorter than its diff:
```python
from functools import partial
import math

import jax
import jax.numpy as jnp
from jax import lax
from jax.experimental import pallas as pl
from jax.experimental.pallas import tpu as pltpu
from jax.sharding import PartitionSpec as P

AHEAD_DIM = 128
SCAN_BLOCK = 256


EPSILON = 1e-05
NEG_FILL = -1e30

CORE, CHIP = (1, 2)


def partner(value, stride):
    return lax.ppermute(value, "tensor", [(rank, rank ^ stride) for rank in range(4)])


def shifted(value, axis, shift):
    count = lax.axis_size(axis)
    return lax.ppermute(value, axis, [(i, (i + shift) % count) for i in range(count)])


def moved(value, axis, shift):
    count = lax.axis_size(axis)
    pairs = [(i, i + shift) for i in range(count) if 0 <= i + shift < count]
    return lax.ppermute(value, axis, pairs)


def after(value, *others):
    return lax.optimization_barrier((value,) + others)[0]


def cut(value, index, size, axis):
    return lax.dynamic_slice_in_dim(value, index * size, size, axis)


def paired_rows(mine, other, core):
    first = jnp.where(core == 0, mine, other)
    second = jnp.where(core == 0, other, mine)
    return jnp.concatenate([first, second], axis=0)


def gather_rows(mine, core):
    return paired_rows(mine, partner(mine, CORE), core)


def send_columns(rows):
    count, mine = (lax.axis_size("dp"), lax.axis_index("dp"))
    share = rows.shape[1] // count
    return [
        shifted(cut(rows, (mine + shift) % count, share, 1), "dp", shift) for shift in range(1, count)
    ]


def both_halves(arrived):
    return [(part, partner(part, CORE)) for part in arrived]


def send_rows(value):
    return [shifted(value, "dp", shift) for shift in range(1, lax.axis_size("dp"))]


def ctx_sum(value):
    return lax.psum_scatter(value, "ctx", scatter_dimension=0, tiled=True).astype(jnp.float32)


def all_sum(value, axis):
    count, mine = (lax.axis_size(axis), lax.axis_index(axis))
    pieces = jnp.stack([value] + [shifted(value, axis, shift) for shift in range(1, count)])
    total = jnp.zeros_like(value)
    for rank in range(count):
        total = total + lax.dynamic_index_in_dim(pieces, (mine - rank) % count, 0, keepdims=False)
    return total


def scatter_sum(value, axis):
    count, mine = (lax.axis_size(axis), lax.axis_index(axis))
    share = value.shape[0] // count
    total = cut(value, mine, share, 0)
    for shift in range(1, count):
        total = total + shifted(cut(value, (mine + shift) % count, share, 0), axis, shift)
    return total


def chained(state, log_decay, forward, fillers):
    count = lax.axis_size("ctx")
    decay = jnp.exp(log_decay)[:, None, None]
    per_head = (decay.shape[0], state.shape[0] // decay.shape[0], state.shape[1])
    own = state.reshape(per_head)
    sent = state
    entering = None
    for step in range(1, count):
        pair = (step - 1, step) if forward else (count - step, count - step - 1)
        arrived = lax.ppermute(sent, "ctx", [pair])
        if step <= len(fillers):
            arrived = after(arrived, *fillers[step - 1](sent))
        entering = arrived if entering is None else entering + arrived
        if step < count - 1:
            total = own.astype(jnp.float32) + decay * arrived.reshape(per_head).astype(jnp.float32)
            sent = total.astype(jnp.bfloat16).reshape(state.shape)
    return entering


def matmul_low(former, latter):
    return jnp.dot(former, latter, preferred_element_type=jnp.float32)


def inner_rows(former, latter):
    return lax.dot_general(
        former, latter, (((0,), (0,)), ((), ())), preferred_element_type=jnp.float32
    )


def times_back(former, latter):
    return lax.dot_general(
        former, latter, (((1,), (1,)), ((), ())), preferred_element_type=jnp.float32
    )


def silu_slope(values):
    logistic = jax.nn.sigmoid(values)
    return logistic * (1.0 + values * (1.0 - logistic))


def split_lanes(first, second, shape):
    lane = lax.broadcasted_iota(jnp.int32, shape, 1)
    return jnp.where(lane < shape[1] // 2, first, second)


def wide(values):
    return values.astype(jnp.float32)


def narrow(values):
    return values.astype(jnp.bfloat16)


def in_two(values):
    high = narrow(values)
    return (high, narrow(values - wide(high)))


def spread(rows, shape):
    rows = jnp.concatenate([rows, jnp.zeros((6, rows.shape[1]), jnp.float32)], axis=0)
    place = lax.broadcasted_iota(jnp.int32, (8, shape[1]), 0)
    lane = lax.broadcasted_iota(jnp.int32, (8, shape[1]), 1)
    chosen = narrow(jnp.where(place == lane // (shape[1] // 2), 1.0, 0.0))
    high, low = in_two(rows.T)
    return matmul_low(high, chosen) + matmul_low(low, chosen)


def lane_sums(values):
    place = lax.broadcasted_iota(jnp.int32, (8, values.shape[1]), 0)
    lane = lax.broadcasted_iota(jnp.int32, (8, values.shape[1]), 1)
    chosen = narrow(jnp.where(place == lane // (values.shape[1] // 2), 1.0, 0.0))
    high, low = in_two(values)
    return times_back(chosen, high) + times_back(chosen, low)


def lanes_of(ref):
    return [slice(at, at + 128) for at in range(0, ref.shape[1], 128)]


def state_kernel(u_ref, small_ref, b_ref, state_ref, *, to_end):
    for pair, lanes in enumerate(lanes_of(u_ref)):
        rows = small_ref[pair]
        if to_end:
            last = rows[0:2, rows.shape[1] - 1 :]
            weights = jnp.exp(last - rows[0:2]) * rows[2:4]
        else:
            weights = jnp.exp(rows[0:2])
        u = wide(u_ref[:, lanes])
        weighted = narrow(u * spread(weights, u.shape))
        state_ref[lanes, :] = narrow(inner_rows(weighted, b_ref[...]))


def scan_kernel(u_ref, small_ref, b_ref, c_ref, y_ref, cb_ref):
    size = SCAN_BLOCK
    count = u_ref.shape[0] // size
    block = [slice(i * size, (i + 1) * size) for i in range(count)]

    @pl.when(pl.program_id(0) == 0)
    def _():
        for i in range(count):
            for j in range(i + 1):
                cb_ref[block[i], block[j]] = times_back(c_ref[block[i], :], b_ref[block[j], :])

    lower = lax.broadcasted_iota(jnp.int32, (size, size), 0) >= lax.broadcasted_iota(
        jnp.int32, (size, size), 1
    )
    for pair, lanes in enumerate(lanes_of(u_ref)):
        rows = small_ref[pair]
        cols = rows.T
        for i in range(count):
            parts = []
            for h in range(2):
                total = jnp.zeros((size, 128), jnp.float32)
                for j in range(i + 1):
                    difference = cols[block[i], h : h + 1] - rows[h : h + 1, block[j]]
                    if i == j:
                        difference = jnp.where(lower, difference, NEG_FILL)
                    weights = cb_ref[block[i], block[j]] * rows[2 + h : 3 + h, block[j]]
                    mixing = narrow(jnp.exp(difference) * weights)
                    total = total + matmul_low(mixing, u_ref[block[j], lanes])
                parts.append(total)
            skip = split_lanes(cols[block[i], 4:5], cols[block[i], 5:6], parts[0].shape)
            values = split_lanes(*parts, parts[0].shape) + skip * wide(u_ref[block[i], lanes])
            y_ref[block[i], lanes] = values


def carry_kernel(y_ref, z_ref, small_ref, c_ref, state_ref, out_ref, gated_ref):
    for pair, lanes in enumerate(lanes_of(y_ref)):
        carried = times_back(c_ref[...], state_ref[lanes, :])
        decay = spread(jnp.exp(small_ref[pair][0:2]), carried.shape)
        values = y_ref[:, lanes] + carried * decay
        out_ref[:, lanes] = values
        gate = z_ref[:, lanes]
        gated_ref[:, lanes] = narrow(values * (gate * jax.nn.sigmoid(gate)))


def scan_back_kernel(u_ref, dy_ref, small_ref, b_ref, c_ref, dw_ref, sums_ref, db_ref, dc_ref, cb_ref, mix_ref):
    size = SCAN_BLOCK
    count = u_ref.shape[0] // size
    width = u_ref.shape[1]
    block = [slice(i * size, (i + 1) * size) for i in range(count)]

    @pl.when(pl.program_id(0) == 0)
    def _():
        mix_ref[...] = jnp.zeros_like(mix_ref)
        for i in range(count):
            for j in range(i, count):
                cb_ref[block[i], block[j]] = times_back(b_ref[block[i], :], c_ref[block[j], :])

    rows = small_ref[0]
    cols = rows.T
    upper = lax.broadcasted_iota(jnp.int32, (size, size), 0) <= lax.broadcasted_iota(
        jnp.int32, (size, size), 1
    )
    lane = lax.broadcasted_iota(jnp.int32, (size, width), 1)
    read_sums = [[jnp.zeros((1, size), jnp.float32) for _ in range(count)] for _ in range(2)]
    write_sums = [[], []]
    ones = jnp.ones((8, size), jnp.bfloat16)
    for i in range(count):
        parts = []
        for h in range(2):
            total = jnp.zeros((size, width), jnp.float32)
            write_sum = jnp.zeros((8, size), jnp.float32)
            step = cols[block[i], 2 + h : 3 + h]
            for j in range(i, count):
                difference = rows[h : h + 1, block[j]] - cols[block[i], h : h + 1]
                if i == j:
                    difference = jnp.where(upper, difference, NEG_FILL)
                decay = jnp.exp(difference)
                dy = dy_ref[block[j], :]
                dy_head = jnp.where((lane < width // 2) == (h == 0), dy, jnp.zeros_like(dy))
                product = decay * times_back(u_ref[block[i], :], dy_head)
                crossing = cb_ref[block[i], block[j]]
                total = total + matmul_low(narrow(decay * crossing), dy)
                weighted = product * step
                mix_ref[block[i], block[j]] += weighted
                high, low = in_two(product * crossing)
                write_sum = write_sum + times_back(ones, high) + times_back(ones, low)
                read_sums[h][j] = read_sums[h][j] + jnp.sum(weighted * crossing, axis=0, keepdims=True)
            parts.append(total)
            write_sums[h].append(write_sum)
        dw_ref[block[i], :] = split_lanes(*parts, parts[0].shape)
    writes = [jnp.concatenate(write_sums[h], axis=1)[0:1] for h in range(2)]
    skip = jnp.sum(wide(u_ref[...]) * wide(dy_ref[...]), axis=0, keepdims=True)
    skip = jnp.concatenate([skip, jnp.zeros((1, u_ref.shape[0] - width), jnp.float32)], axis=1)
    reads = [jnp.concatenate(read_sums[h], axis=1) for h in range(2)]
    sums_ref[0] = jnp.concatenate(reads + writes + [skip, jnp.zeros_like(skip)] + reads, axis=0)

    @pl.when(pl.program_id(0) == pl.num_programs(0) - 1)
    def _():
        for i in range(count):
            total = jnp.zeros((size, b_ref.shape[1]), jnp.float32)
            for j in range(i, count):
                total = total + matmul_low(narrow(mix_ref[block[i], block[j]]), c_ref[block[j], :])
            db_ref[block[i], :] = total
        for j in range(count):
            total = jnp.zeros((size, b_ref.shape[1]), jnp.float32)
            for i in range(j + 1):
                total = total + inner_rows(narrow(mix_ref[block[i], block[j]]), b_ref[block[i], :])
            dc_ref[block[j], :] = total


def carry_back_kernel(
    u_ref, dy_ref, small_ref, sums_ref, dw_ref, b_ref, c_ref, state_ref, grad_ref, db_in_ref, dc_in_ref,
    du_ref, steps_ref, db_ref, dc_ref,
):
    tokens = u_ref.shape[0]

    @pl.when(pl.program_id(0) == 0)
    def _():
        db_ref[...] = db_in_ref[...]
        dc_ref[...] = dc_in_ref[...]

    all_started, all_ended = ([], [])
    for pair, lanes in enumerate(lanes_of(u_ref)):
        rows = small_ref[pair]
        last = rows[0:2, tokens - 1 :]
        u = wide(u_ref[:, lanes])
        dy = wide(dy_ref[:, lanes])
        state = state_ref[lanes, :]
        grad = grad_ref[lanes, :]
        started = spread(jnp.exp(rows[0:2]), u.shape) * dy
        tail = spread(jnp.exp(last - rows[0:2]), u.shape)
        ended = tail * u
        step = spread(rows[2:4], u.shape)
        left = times_back(b_ref[...], grad)
        dw = dw_ref[:, lanes] + tail * left
        du_ref[:, lanes] = narrow(step * dw + spread(rows[4:6], u.shape) * dy)
        all_started.append(narrow(started))
        all_ended.append(narrow(ended * step))
        reads = lane_sums(started * times_back(c_ref[...], state))[0:2]
        writes = lane_sums(ended * left)[0:2]
        sums = sums_ref[pair]
        written = sums[2:4] + writes
        slope = sums[0:2] + reads - rows[2:4] * written
        products = jnp.sum(wide(state) * wide(grad), axis=1, keepdims=True)
        height = products.shape[0] // 2
        across = jnp.concatenate(
            [
                jnp.sum(products[:height], axis=0, keepdims=True),
                jnp.sum(products[height:], axis=0, keepdims=True),
            ],
            axis=0,
        ) * jnp.exp(last)
        across = across + jnp.sum(rows[2:4] * writes, axis=1, keepdims=True)
        held = jnp.concatenate([slope, jnp.zeros((6, tokens), jnp.float32)], axis=0)
        place = lax.broadcasted_iota(jnp.int32, held.shape, 1)
        reach = 1
        while reach < tokens:
            held = held + jnp.where(place < tokens - reach, pltpu.roll(held, tokens - reach, 1), 0.0)
            reach = 2 * reach
        flow = held[0:2] + across
        steps_ref[pair] = jnp.concatenate([written + rows[6:8] * flow, flow, held[2:6]], axis=0)
    dc_ref[...] += matmul_low(jnp.concatenate(all_started, axis=1), state_ref[...])
    db_ref[...] += matmul_low(jnp.concatenate(all_ended, axis=1), grad_ref[...])


def attend_scores(rank_ref, k_ref, q_ref, own, factor):
    scores = times_back(k_ref[...], q_ref[...]) * factor
    keys, queries = scores.shape
    row = lax.broadcasted_iota(jnp.int32, (own, queries), 0)
    column = lax.broadcasted_iota(jnp.int32, (own, queries), 1) + pl.program_id(1) * queries
    near = jnp.where(row <= column, scores[:own], NEG_FILL)
    if keys == own:
        return near
    far_row = lax.broadcasted_iota(jnp.int32, (keys - own, queries), 0)
    far = jnp.where(far_row < rank_ref[0] * own, scores[own:], NEG_FILL)
    return jnp.concatenate([near, far], axis=0)


def attend_kernel(rank_ref, q_ref, k_ref, v_ref, out_ref, log_ref, flat_ref, *, own, factor):
    @pl.when((pl.program_id(0) == 0) & (pl.program_id(1) == 0))
    def _():
        flat_ref[...] = v_ref[...].T

    scores = attend_scores(rank_ref, k_ref, q_ref, own, factor)
    maxima = jnp.max(scores, axis=0, keepdims=True)
    weights = jnp.exp(scores - maxima)
    totals = jnp.sum(weights, axis=0, keepdims=True)
    probability = narrow(weights * (1.0 / totals))
    out_ref[...] = narrow(matmul_low(flat_ref[...], probability).T)
    log_ref[0] = jnp.broadcast_to(maxima + jnp.log(totals), log_ref.shape[1:])


def attend_back_kernel(
    rank_ref, q_ref, do_ref, log_ref, k_ref, v_ref, dq_ref, dk_ref, dv_ref, flat_ref, *, own, factor
):
    @pl.when((pl.program_id(0) == 0) & (pl.program_id(1) == 0))
    def _():
        flat_ref[...] = k_ref[...].T
        dk_ref[...] = jnp.zeros_like(dk_ref)
        dv_ref[...] = jnp.zeros_like(dv_ref)

    scores = attend_scores(rank_ref, k_ref, q_ref, own, factor)
    probability = jnp.exp(scores - log_ref[0][0:1])
    dv_ref[...] += matmul_low(narrow(probability), do_ref[...])
    grad_prob = times_back(v_ref[...], do_ref[...])
    centre = jnp.sum(probability * grad_prob, axis=0, keepdims=True)
    grad_score = narrow(probability * (grad_prob - centre))
    dk_ref[...] += matmul_low(grad_score, q_ref[...]) * factor
    dq_ref[...] = narrow((matmul_low(flat_ref[...], grad_score) * factor).T)


def call(name, kernel, grid, specs, args, outs, scratch=()):
    return pl.pallas_call(
        kernel,
        name=name,
        grid=grid,
        in_specs=specs,
        out_specs=[spec for _, spec in outs],
        out_shape=[out for out, _ in outs],
        scratch_shapes=list(scratch),
        cost_estimate=pl.CostEstimate(flops=0, bytes_accessed=0, transcendentals=0),
        compiler_params=pltpu.CompilerParams(vmem_limit_bytes=48 * 1024 * 1024),
    )(*args)


def like(shape, kind):
    return jax.ShapeDtypeStruct(shape, kind)


class Scan:
    def __init__(self, tokens, inner, state):
        self.tokens, self.inner, self.state = (tokens, inner, state)
        self.pairs = inner // 128
        self.shared = pl.BlockSpec((tokens, state), lambda p: (0, 0))
        self.small_like = like((self.pairs, 8, tokens), jnp.float32)
        self.square = pltpu.VMEM((tokens, tokens), jnp.float32)

    def specs(self, group):
        group = math.gcd(group, self.pairs)
        return (
            (self.pairs // group,),
            pl.BlockSpec((self.tokens, 128 * group), lambda p: (0, p)),
            pl.BlockSpec((group, 8, self.tokens), lambda p: (p, 0, 0)),
            pl.BlockSpec((128 * group, self.state), lambda p: (p, 0)),
        )

    def rows_like(self, kind):
        return like((self.tokens, self.inner), kind)

    def own_state(self, u, small, b, to_end):
        grid, tile, row, states = self.specs(6)
        return call(
            "own_state",
            partial(state_kernel, to_end=to_end),
            grid,
            [tile, row, self.shared],
            (u, small, b),
            [(like((self.inner, self.state), jnp.bfloat16), states)],
        )[0]

    def within(self, u, small, b, c):
        grid, tile, row, states = self.specs(6)
        return call(
            "scan",
            scan_kernel,
            grid,
            [tile, row, self.shared, self.shared],
            (u, small, b, c),
            [(self.rows_like(jnp.float32), tile)],
            [self.square],
        )[0]

    def carried(self, y, z, small, c, state):
        grid, tile, row, states = self.specs(6)
        return call(
            "carry",
            carry_kernel,
            grid,
            [tile, tile, row, self.shared, states],
            (y, z, small, c, state),
            [(self.rows_like(jnp.float32), tile), (self.rows_like(jnp.bfloat16), tile)],
        )

    def within_back(self, u, dy, small, b, c):
        shared = like((self.tokens, self.state), jnp.float32)
        grid, tile, row, states = self.specs(1)
        return call(
            "scan_back",
            scan_back_kernel,
            grid,
            [tile, tile, row, self.shared, self.shared],
            (u, dy, small, b, c),
            [(self.rows_like(jnp.float32), tile), (self.small_like, row)] + 2 * [(shared, self.shared)],
            [self.square, self.square],
        )

    def carried_back(self, u, dy, small, sums, dw, b, c, state, grad, db, dc):
        shared = like((self.tokens, self.state), jnp.float32)
        grid, tile, row, states = self.specs(6)
        return call(
            "carry_back",
            carry_back_kernel,
            grid,
            [tile, tile, row, row, tile] + 2 * [self.shared] + 2 * [states] + 2 * [self.shared],
            (u, dy, small, sums, dw, b, c, state, grad, db, dc),
            [(self.rows_like(jnp.bfloat16), tile), (self.small_like, row)] + 2 * [(shared, self.shared)],
        )


class Attend:
    def __init__(self, tokens, keys, heads):
        self.tokens, self.keys, self.heads = (tokens, keys, heads)
        size = min(256, tokens)
        self.grid = (heads, tokens // size)
        self.factor = 1.0 / math.sqrt(AHEAD_DIM)
        self.rank = pl.BlockSpec(memory_space=pltpu.SMEM)
        self.tile = pl.BlockSpec((size, AHEAD_DIM), lambda h, q: (q, h))
        self.log = pl.BlockSpec((1, 8, size), lambda h, q: (h, 0, q))
        self.whole = pl.BlockSpec((keys, AHEAD_DIM), lambda h, q: (0, 0))
        self.rows_like = like((tokens, heads * AHEAD_DIM), jnp.bfloat16)
        self.flat = pltpu.VMEM((AHEAD_DIM, keys), jnp.bfloat16)

    def forward(self, rank, q, k, v):
        return call(
            "attend",
            partial(attend_kernel, own=self.tokens, factor=self.factor),
            self.grid,
            [self.rank, self.tile, self.whole, self.whole],
            (rank, q, k, v),
            [(self.rows_like, self.tile), (like((self.heads, 8, self.tokens), jnp.float32), self.log)],
            [self.flat],
        )

    def back(self, rank, q, do, log, k, v):
        whole = like((self.keys, AHEAD_DIM), jnp.float32)
        return call(
            "attend_back",
            partial(attend_back_kernel, own=self.tokens, factor=self.factor),
            self.grid,
            [self.rank, self.tile, self.tile, self.log, self.whole, self.whole],
            (rank, q, do, log, k, v),
            [(self.rows_like, self.tile), (whole, self.whole), (whole, self.whole)],
            [self.flat],
        )


def call_at(name, kernel, scalars, grid, specs, args, outs):
    return pl.pallas_call(
        kernel,
        name=name,
        grid_spec=pltpu.PrefetchScalarGridSpec(
            num_scalar_prefetch=1,
            grid=grid,
            in_specs=specs,
            out_specs=[spec for _, spec in outs],
        ),
        out_shape=[out for out, _ in outs],
        cost_estimate=pl.CostEstimate(flops=0, bytes_accessed=0, transcendentals=0),
        compiler_params=pltpu.CompilerParams(vmem_limit_bytes=48 * 1024 * 1024),
    )(scalars, *args)


def mean_scale(values):
    return lax.rsqrt(jnp.mean(values * values, axis=-1, keepdims=True) + EPSILON)


def norm_kernel(x_ref, gain_ref, out_ref):
    x = wide(x_ref[...])
    out_ref[...] = narrow(x * mean_scale(x) * gain_ref[...])


def normed(x, gain):
    rows, width = x.shape
    size = min(128, rows)
    tile = pl.BlockSpec((size, width), lambda i: (i, 0))
    line = pl.BlockSpec((1, width), lambda i: (0, 0))
    return call(
        "norm_one", norm_kernel, (rows // size,), [tile, line], (x, gain), [(like(x.shape, x.dtype), tile)]
    )[0]


def middle_kernel(at_ref, x_ref, mine_ref, theirs_ref, gain_ref, middle_ref, out_ref, sum_ref):
    @pl.when(pl.program_id(0) == 0)
    def _():
        sum_ref[...] = jnp.zeros_like(sum_ref)

    mixed = wide(mine_ref[...]) + wide(theirs_ref[...])
    middle = wide(x_ref[...]) + mixed
    middle_ref[...] = middle
    out_ref[...] = narrow(middle * mean_scale(middle) * gain_ref[...])
    sum_ref[...] += jnp.sum(mixed * mixed, axis=0, keepdims=True)


def middle_norm(at, x, mine, theirs, gain):
    rows, width = mine.shape
    size = min(128, rows)
    steps = rows // size
    tile = pl.BlockSpec((size, width), lambda i, at: (i, 0))
    half = pl.BlockSpec((size, width), lambda i, at: (at[0] * steps + i, 0))
    line = pl.BlockSpec((1, width), lambda i, at: (0, 0))
    return call_at(
        "norm_two",
        middle_kernel,
        at,
        (steps,),
        [half, tile, tile, line],
        (x, mine, theirs, gain),
        [
            (like(mine.shape, jnp.float32), tile),
            (like(mine.shape, jnp.bfloat16), tile),
            (like((1, width), jnp.float32), line),
        ],
    )


def norm_back_kernel(at_ref, x_ref, base_ref, mine_ref, theirs_ref, gain_ref, *outs):
    sum_ref = outs[-1]

    @pl.when(pl.program_id(0) == 0)
    def _():
        sum_ref[...] = jnp.zeros_like(sum_ref)

    grad = wide(mine_ref[...]) + wide(theirs_ref[...])
    x = wide(x_ref[...])
    scale = mean_scale(x)
    weighted = grad * gain_ref[...]
    inner = jnp.mean(weighted * x, axis=-1, keepdims=True)
    total = wide(base_ref[...]) + (scale * weighted - x * (scale * scale * scale * inner))
    for out_ref in outs[:-1]:
        out_ref[...] = total.astype(out_ref.dtype)
    sum_ref[...] += jnp.sum(grad * x * scale, axis=0, keepdims=True)


def norm_grad(name, at, x, base, mine, theirs, gain, kinds):
    rows, width = mine.shape
    size = min(128, rows)
    steps = rows // size
    tile = pl.BlockSpec((size, width), lambda i, at: (i, 0))
    half = pl.BlockSpec((size, width), lambda i, at: (at[0] * steps + i, 0))
    line = pl.BlockSpec((1, width), lambda i, at: (0, 0))
    return call_at(
        name,
        norm_back_kernel,
        at,
        (steps,),
        [half if x.shape[0] > rows else tile, half if base.shape[0] > rows else tile, tile, tile, line],
        (x, base, mine, theirs, gain),
        [(like(mine.shape, kind), tile) for kind in kinds] + [(like((1, width), jnp.float32), line)],
    )


def expand_kernel(x_ref, gate_ref, up_ref, dact_ref, act_ref, grad_ref):
    gate = matmul_low(x_ref[...], gate_ref[...])
    up = matmul_low(x_ref[...], up_ref[...])
    dact = dact_ref[...]
    logistic = jax.nn.sigmoid(gate)
    silu = gate * logistic
    act_ref[...] = narrow(silu * up)
    grad_ref[0] = narrow(dact * up * (logistic * (1.0 + gate * (1.0 - logistic))))
    grad_ref[1] = narrow(dact * silu)


def expand(x, weight, dact):
    rows, depth = x.shape
    width = dact.shape[1]
    size = min(256, width)
    steps = width // size
    return call(
        "expand",
        expand_kernel,
        (steps,),
        [
            pl.BlockSpec((rows, depth), lambda j: (0, 0)),
            pl.BlockSpec((depth, size), lambda j: (0, j)),
            pl.BlockSpec((depth, size), lambda j: (0, steps + j)),
            pl.BlockSpec((rows, size), lambda j: (0, j)),
        ],
        (x, weight, weight, dact),
        [
            (like((rows, width), jnp.bfloat16), pl.BlockSpec((rows, size), lambda j: (0, j))),
            (like((2, rows, width), jnp.bfloat16), pl.BlockSpec((2, rows, size), lambda j: (0, 0, j))),
        ],
    )


def share_kernel(at_ref, *refs, count, back, added):
    total = jnp.zeros(refs[-1].shape, jnp.float32)
    for former, latter in zip(refs[:count], refs[count : 2 * count], strict=True):
        rows = former[...].reshape(former.shape[-2:])
        total = total + (times_back(rows, latter[...]) if back else matmul_low(rows, latter[...]))
    if added:
        total = total + wide(refs[2 * count][...])
    refs[-1][...] = narrow(total)


def half_share(name, at, terms, back, added=None):
    rows = terms[0][0].shape[-2] // 2
    width = terms[0][2].shape[0 if back else 1]
    size = min(512, width)
    specs = []
    for former, plane, _, _ in terms:
        if former.ndim == 3:
            specs.append(
                pl.BlockSpec((1, rows, former.shape[2]), lambda j, at, plane=plane: (plane, at[0], 0))
            )
        else:
            specs.append(pl.BlockSpec((rows, former.shape[1]), lambda j, at: (at[0], 0)))
    for former, _, latter, columns in terms:
        if back:
            specs.append(pl.BlockSpec((size, former.shape[-1]), lambda j, at, c=columns: (j, c)))
        else:
            specs.append(pl.BlockSpec((former.shape[-1], size), lambda j, at: (0, j)))
    args = [term[0] for term in terms] + [term[2] for term in terms]
    tile = pl.BlockSpec((rows, size), lambda j, at: (0, j))
    if added is not None:
        specs.append(tile)
        args.append(added)
    kernel = partial(share_kernel, count=len(terms), back=back, added=added is not None)
    return call_at(
        name, kernel, at, (width // size,), specs, args, [(like((rows, width), jnp.bfloat16), tile)]
    )[0]


def weight_kernel(at_ref, own_ref, *refs, shifts, count):
    out_ref = refs[-1]
    half = own_ref.shape[0] // 2
    pairs = refs[: 2 * shifts]
    seconds = refs[2 * shifts : -1]
    own = own_ref[...].T
    flat = [ref[...].T for ref in pairs]
    places = [pl.ds(pl.multiple_of(which * half, half), half) for which in (at_ref[0], 1 - at_ref[0])]
    at = 0
    for index in range(count):
        planes = seconds[index].shape[0] if seconds[index].ndim == 3 else 1
        for plane in range(planes):
            width = seconds[index].shape[-1]
            for start in range(0, width, 512):
                stop = min(width, start + 512)

                def rows(ref, place):
                    if planes > 1:
                        return ref[plane, place, start:stop]
                    return ref[place, start:stop]

                total = matmul_low(own, rows(seconds[index], slice(None)))
                for shift in range(shifts):
                    ref = seconds[count * (shift + 1) + index]
                    for which in range(2):
                        total = total + matmul_low(flat[2 * shift + which], rows(ref, places[which]))
                out_ref[:, at + start : at + stop] = narrow(total)
            at = at + width


def weight_part(name, at, own, others, seconds, arrived):
    shifts = len(others)
    tokens = own.shape[0]
    share = own.shape[1] // (shifts + 1)
    size = min(256, share)
    specs = [pl.BlockSpec((tokens, size), lambda m, at: (0, at[1] * (share // size) + m))]
    args = [own]
    for pair in others:
        for part in pair:
            specs.append(pl.BlockSpec((tokens // 2, size), lambda m, at: (0, m)))
            args.append(part)
    width = 0
    for group in [seconds] + list(arrived):
        for part in group:
            specs.append(pl.BlockSpec(part.shape, lambda m, at, nd=part.ndim: (0,) * nd))
            args.append(part)
    for part in seconds:
        width = width + part.shape[-1] * (part.shape[0] if part.ndim == 3 else 1)
    kernel = partial(weight_kernel, shifts=shifts, count=len(seconds))
    tile = pl.BlockSpec((size, width), lambda m, at: (m, 0))
    return call_at(
        name, kernel, at, (share // size,), specs, args, [(like((share, width), jnp.bfloat16), tile)]
    )[0]


def body(
    hidden,
    cotangent,
    norm1_gain,
    ssm_in,
    ssm_bc,
    ssm_dt,
    dt_bias,
    a_log,
    d_skip,
    ssm_out,
    attn_q,
    attn_kv,
    attn_out,
    norm2_gain,
    mlp_gate_up,
    mlp_down,
):
    ctx_rank = lax.axis_index("ctx")
    ctx_count = lax.axis_size("ctx")
    tensor_rank = lax.axis_index("tensor")
    core = tensor_rank % 2
    chip = tensor_rank // 2
    hidden_rows = hidden[0]
    grad_low = cotangent[0]
    tokens, model_width = hidden_rows.shape
    half = tokens // 2
    inner_local = ssm_in.shape[2]
    heads_local = ssm_dt.shape[1]
    head_width = inner_local // heads_local
    head_pairs = heads_local // 2
    state_width = ssm_bc.shape[2]
    bc_share = 2 * state_width // 4
    heads_query = attn_q.shape[1] // AHEAD_DIM
    ff_local = mlp_down.shape[0]
    here = jnp.stack([core, lax.axis_index("dp")]).astype(jnp.int32)
    there = jnp.stack([1 - core, lax.axis_index("dp")]).astype(jnp.int32)
    gain_one = norm1_gain[None]
    gain_two = norm2_gain[None]

    input_one = normed(hidden_rows, gain_one)
    u_matrix = ssm_in[:, 1]
    bc_matrix = ssm_bc.reshape(model_width, 2 * state_width)
    source_rows = matmul_low(input_one, u_matrix).astype(jnp.bfloat16)
    bc_rows = matmul_low(input_one, bc_matrix).astype(jnp.bfloat16)
    write_rows = bc_rows[:, :state_width]
    read_rows = bc_rows[:, state_width:]
    dt_pre = lax.dot_general(
        ssm_dt, input_one, (((0,), (1,)), ((), ())), preferred_element_type=jnp.float32
    ) + dt_bias[:, None]
    dt_rows = jax.nn.softplus(dt_pre)
    decay_rate = -jnp.exp(a_log)
    running = jnp.cumsum(dt_rows * decay_rate[:, None], axis=1)

    def by_head(value):
        return jnp.broadcast_to(value[:, None], (heads_local, tokens))

    small_rows = jnp.stack([running, dt_rows, by_head(d_skip), by_head(decay_rate)], axis=1)
    small_rows = small_rows.reshape(head_pairs, 2, 4, tokens).transpose(0, 2, 1, 3)
    small_rows = small_rows.reshape(head_pairs, 8, tokens)
    scan = Scan(tokens, inner_local, state_width)
    own_state = scan.own_state(source_rows, small_rows, write_rows, True)

    one_late = after(input_one, own_state)
    kv_pair = cut(attn_kv, chip, AHEAD_DIM, 2)
    key_value = matmul_low(one_late, kv_pair.reshape(model_width, 2 * AHEAD_DIM)).astype(jnp.bfloat16)
    kv_sent = cut(key_value, core, AHEAD_DIM, 1)
    kv_got = [kv_sent] + [moved(kv_sent, "ctx", shift) for shift in range(1, ctx_count)]
    cot_sent = send_columns(cut(after(grad_low, own_state), core, half, 0))
    one_sent = send_columns(cut(one_late, core, half, 0))
    z_matrix = after(ssm_in, own_state)[:, 0]
    queries = matmul_low(one_late, attn_q).astype(jnp.bfloat16)
    gate_ssm = matmul_low(one_late, z_matrix)
    attend = Attend(tokens, ctx_count * tokens, heads_query)
    rank = ctx_rank.astype(jnp.int32)[None]
    kept = {}

    def fill_within(sent):
        kept["within"] = scan.within(source_rows, after(small_rows, own_state), write_rows, read_rows)
        return (kept["within"], gate_ssm, queries)

    def fill_attend(sent):
        mine = jnp.concatenate(kv_got, axis=0)
        other = partner(mine, CORE)
        kept["key"] = jnp.where(core == 0, mine, other)
        kept["value"] = jnp.where(core == 0, other, mine)
        kept["attended"], kept["log"] = attend.forward(
            after(rank, sent), queries, kept["key"], kept["value"]
        )
        kept["attended_sent"] = send_rows(kept["attended"])
        return (kept["attended"],)

    def fill_act(sent):
        kept["act"] = times_back(after(grad_low, sent), mlp_down)
        return (kept["act"],)

    entering = chained(own_state, running[:, -1], True, [fill_within, fill_attend, fill_act])
    key_rows, value_rows, attended = (kept["key"], kept["value"], kept["attended"])
    ssm_values, gated_rows = scan.carried(kept["within"], gate_ssm, small_rows, read_rows, entering)
    outs_sent = [
        [gated, att] for gated, att in zip(send_rows(gated_rows), kept["attended_sent"], strict=True)
    ]

    terms = [(gated_rows, 0, ssm_out, 0), (attended, 0, attn_out, 0)]
    given = partner(half_share("mix_other", there, terms, False), CORE)
    mix_mine = half_share("mix_own", here, terms, False, given)
    mix_theirs = partner(mix_mine, CHIP)
    gu_matrix = after(mlp_gate_up, mix_mine).reshape(model_width, 2 * ff_local)
    cot_columns = both_halves([after(part, mix_mine) for part in cot_sent])
    one_columns = both_halves([after(part, mix_mine) for part in one_sent])
    mix_theirs = after(mix_theirs, gu_matrix)
    middle, two_mine, mix_squares = middle_norm(here, hidden_rows, mix_mine, mix_theirs, gain_two)

    input_two = gather_rows(two_mine, core)
    activated, grad_gu = expand(input_two, gu_matrix, kept["act"])
    act_sent = send_rows(activated)
    two_sent = send_columns(two_mine)
    gu_sent = send_rows(grad_gu)
    terms = [(grad_gu, 0, gu_matrix, 0), (grad_gu, 1, gu_matrix, 1)]
    given = partner(half_share("two_other", there, terms, True), CORE)
    two_back = half_share("two_own", here, terms, True, given)
    two_theirs = partner(two_back, CHIP)
    terms = [(after(activated, two_back), 0, mlp_down, 0)]
    given = partner(half_share("mlp_other", there, terms, False), CORE)
    mlp_mine = half_share("mlp_own", here, terms, False, given)
    down_part = weight_part(
        "grad_down", after(here, mlp_mine), grad_low, cot_columns, [activated], [[part] for part in act_sent]
    )
    grad_down = ctx_sum(down_part)
    two_theirs = after(two_theirs, down_part)
    grad_middle, mix_grad_mine, gain_two_sum = norm_grad(
        "norm_two_back", here, middle, grad_low, two_back, two_theirs, gain_two, (jnp.float32, jnp.bfloat16)
    )

    grad_mix = gather_rows(mix_grad_mine, core)
    mix_sent = send_columns(mix_grad_mine)
    grad_gated = times_back(grad_mix, ssm_out)
    grad_values = (grad_gated * jax.nn.silu(gate_ssm)).astype(jnp.bfloat16)
    own_grad = scan.own_state(grad_values, small_rows, read_rows, False)
    mlp_theirs = partner(after(mlp_mine, own_grad), CHIP)
    grad_gate_ssm = (grad_gated * ssm_values * silu_slope(gate_ssm)).astype(jnp.bfloat16)
    grad_attended = times_back(after(grad_mix, own_grad), attn_out).astype(jnp.bfloat16)
    gate_sent = send_rows(grad_gate_ssm)

    def fill_attend_back(sent):
        grad_query, grad_key, grad_value = attend.back(
            after(rank, own_grad), queries, grad_attended, kept["log"], key_rows, value_rows
        )
        kept["grad_query"] = grad_query
        kept["query_sent"] = send_rows(grad_query)
        own_part = jnp.where(core == 0, grad_key, grad_value)
        given = partner(jnp.where(core == 0, grad_value, grad_key).astype(jnp.bfloat16), CORE)
        paired = (own_part + given.astype(jnp.float32)).reshape(ctx_count, tokens, AHEAD_DIM)
        kept["kv"] = paired[0]
        kept["kv_sent"] = [
            moved(paired[shift].astype(jnp.bfloat16), "ctx", -shift) for shift in range(1, ctx_count)
        ]
        return (grad_query,)

    def fill_scan_back(sent):
        kept["scan"] = scan.within_back(
            source_rows, after(grad_values, sent), small_rows, write_rows, read_rows
        )
        return (kept["scan"][0],)

    def fill_weights(sent):
        kept["gate_up"] = weight_part(
            "grad_gate_up",
            after(here, sent),
            input_two,
            both_halves(two_sent),
            [grad_gu],
            [[part] for part in gu_sent],
        )
        kept["outs"] = weight_part(
            "grad_outs", after(here, sent), grad_mix, both_halves(mix_sent), [gated_rows, attended], outs_sent
        )
        return (kept["gate_up"], kept["outs"])

    leaving = chained(own_grad, running[:, -1], False, [fill_attend_back, fill_scan_back, fill_weights])
    grad_gate_up = ctx_sum(kept["gate_up"])
    grad_outs = ctx_sum(kept["outs"])
    grad_written, scan_sums, grad_b, grad_c = kept["scan"]
    grad_source, steps, grad_b, grad_c = scan.carried_back(
        source_rows, grad_values, small_rows, scan_sums, grad_written,
        write_rows, read_rows, entering, leaving, grad_b, grad_c,
    )
    source_sent = send_rows(grad_source)
    grad_bc = jnp.concatenate([grad_b, grad_c], axis=1)
    bc_sent = partner(cut(grad_bc, 1 - core, 2 * bc_share, 1).astype(jnp.bfloat16), CORE)
    bc_mine = cut(grad_bc, core, 2 * bc_share, 1) + bc_sent.astype(jnp.float32)
    bc_given = partner(cut(bc_mine, 1 - chip, bc_share, 1).astype(jnp.bfloat16), CHIP)
    grad_bc_low = (cut(bc_mine, chip, bc_share, 1) + bc_given.astype(jnp.float32)).astype(jnp.bfloat16)
    kv_sum = kept["kv"]
    for part in kept["kv_sent"]:
        kv_sum = kv_sum + part.astype(jnp.float32)
    grad_kv_low = kv_sum.astype(jnp.bfloat16)
    grad_query = kept["grad_query"]
    kv_columns = cut(attn_kv, chip, AHEAD_DIM, 2)
    kv_columns = lax.dynamic_index_in_dim(kv_columns, core, 1, keepdims=False)
    ins_first = weight_part(
        "grad_ins_first",
        here,
        input_one,
        one_columns,
        [grad_gate_ssm, grad_query],
        [[gate, query] for gate, query in zip(gate_sent, kept["query_sent"], strict=True)],
    )
    grad_ins_first = ctx_sum(ins_first)

    grad_dt_pre = steps[:, 0:2].reshape(heads_local, tokens) * jax.nn.sigmoid(dt_pre)
    flow_rows = steps[:, 2:4].reshape(heads_local, tokens)
    grad_dt_bias = jnp.sum(grad_dt_pre, axis=1)
    grad_a_log = decay_rate * jnp.sum(dt_rows * flow_rows, axis=1)
    grad_d_skip = jnp.sum(scan_sums[:, 4, : 2 * head_width].reshape(heads_local, head_width), axis=1)
    pad = -heads_local % AHEAD_DIM
    grad_dt_low = jnp.pad(grad_dt_pre.astype(jnp.bfloat16).T, ((0, 0), (0, pad)))
    grad_small = jnp.concatenate([grad_kv_low, grad_bc_low, grad_dt_low], axis=1)
    small_sent = send_rows(grad_small)
    weight_small = jnp.concatenate(
        [
            kv_columns,
            cut(bc_matrix, 2 * core + chip, bc_share, 1),
            jnp.pad(ssm_dt, ((0, 0), (0, pad))),
        ],
        axis=1,
    )
    terms = [
        (grad_gate_ssm, 0, z_matrix, 0),
        (grad_source, 0, u_matrix, 0),
        (grad_query, 0, attn_q, 0),
        (grad_small, 0, weight_small, 0),
    ]
    given = partner(half_share("one_other", there, terms, True), CORE)
    one_back = half_share("one_own", here, terms, True, given)
    one_theirs = partner(one_back, CHIP)
    ins_small = weight_part(
        "grad_ins_small", after(here, one_back), input_one, one_columns, [grad_small], [[p] for p in small_sent]
    )
    grad_ins_small = ctx_sum(ins_small)
    ins_source = weight_part(
        "grad_ins_source", after(here, ins_small), input_one, one_columns, [grad_source], [[p] for p in source_sent]
    )
    grad_ins_source = ctx_sum(ins_source)
    one_theirs = after(one_theirs, ins_source)
    hidden_mine, gain_one_sum = norm_grad(
        "norm_one_back", here, hidden_rows, grad_middle, one_back, one_theirs, gain_one, (jnp.bfloat16,)
    )
    grad_hidden = gather_rows(hidden_mine, core)

    mlp_total = mlp_mine.astype(jnp.float32) + mlp_theirs.astype(jnp.float32)
    block_out = middle + mlp_total
    output = gather_rows(block_out.astype(jnp.bfloat16), core)

    kv_part = grad_ins_small[:, :AHEAD_DIM]
    bc_part = grad_ins_small[:, AHEAD_DIM : AHEAD_DIM + bc_share]
    grad_ssm_dt = grad_ins_small[:, AHEAD_DIM + bc_share : AHEAD_DIM + bc_share + heads_local]
    share = kv_part.shape[0] // 4
    blocks = [cut(kv_part, tensor_rank, share, 0)]
    for stride in range(1, 4):
        blocks.append(partner(cut(kv_part, tensor_rank ^ stride, share, 0), stride))
    blocks = jnp.stack(blocks)
    bc_blocks = jnp.stack([bc_part] + [partner(bc_part, stride) for stride in range(1, 4)])

    def of_rank(pieces, rank):
        return lax.dynamic_index_in_dim(pieces, tensor_rank ^ rank, 0, keepdims=False)

    grad_attn_kv = jnp.stack(
        [
            jnp.concatenate([of_rank(blocks, kind), of_rank(blocks, 2 + kind)], axis=1)
            for kind in range(2)
        ],
        axis=1,
    )
    grad_ssm_bc = jnp.concatenate(
        [of_rank(bc_blocks, 2 * (place % 2) + place // 2) for place in range(4)], axis=1
    ).reshape(-1, 2, state_width)

    gains = jnp.concatenate([gain_one_sum, gain_two_sum], axis=0).T
    gains = gains + partner(gains, CORE)
    gains = scatter_sum(scatter_sum(gains, "dp"), "ctx")
    squares = jnp.stack([jnp.sum(mix_squares), jnp.sum(mlp_total * mlp_total), jnp.sum(block_out * block_out)])
    squares = squares + partner(squares, CORE)
    small = jnp.concatenate([grad_dt_bias, grad_a_log, grad_d_skip, squares])
    small = all_sum(all_sum(small, "dp"), "ctx")
    counted = tokens * model_width * lax.axis_size("dp") * ctx_count
    branch_rms = jnp.sqrt(small[3 * heads_local :] / counted)
    return (
        output[None],
        grad_hidden[None],
        gains[:, 0],
        jnp.stack([grad_ins_first[:, :inner_local], grad_ins_source], axis=1),
        grad_ssm_bc,
        grad_ssm_dt,
        small[:heads_local],
        small[heads_local : 2 * heads_local],
        small[2 * heads_local : 3 * heads_local],
        grad_outs[:, :inner_local].T,
        grad_ins_first[:, inner_local:],
        grad_attn_kv,
        grad_outs[:, inner_local:].T,
        gains[:, 1],
        grad_gate_up.reshape(-1, 2, ff_local),
        grad_down.T,
        branch_rms,
    )


def solution(mesh):
    return jax.shard_map(
        body,
        mesh=mesh,
        in_specs=(
            P("dp", "ctx", None),
            P("dp", "ctx", None),
            P(),
            P(None, None, "tensor"),
            P(),
            P(None, "tensor"),
            P("tensor"),
            P("tensor"),
            P("tensor"),
            P("tensor", None),
            P(None, "tensor"),
            P(),
            P("tensor", None),
            P(),
            P(None, None, "tensor"),
            P("tensor", None),
        ),
        out_specs=(
            P("dp", "ctx", None),
            P("dp", "ctx", None),
            P(("dp", "ctx")),
            P(("dp", "ctx"), None, "tensor"),
            P(("dp", "ctx"), None, None),
            P(("dp", "ctx"), "tensor"),
            P("tensor"),
            P("tensor"),
            P("tensor"),
            P("tensor", ("dp", "ctx")),
            P(("dp", "ctx"), "tensor"),
            P(("dp", "ctx", "tensor"), None, None),
            P("tensor", ("dp", "ctx")),
            P(("dp", "ctx")),
            P(("dp", "ctx"), None, "tensor"),
            P("tensor", ("dp", "ctx")),
            P(),
        ),
        check_vma=False,
    )
```

time: 730 us -> 614 us (0.84)
  waiting for transfers between devices: 328 us -> 205 us
  Pallas kernels: 55.7 us -> 146 us
  matrix products: 97.8 us -> 18.3 us
  other arithmetic: 63.1 us -> 47.5 us
  starting transfers between devices: 63.2 us -> 70.6 us
    ppermute x16 -> x6, waiting for transfers between devices: 93.9 us -> 0.02 us  [moved(): return lax.ppermute(value, axis, pairs)]
    pallas_call x0 -> x17, Pallas kernels: none -> 91.1 us  [call_at(): pl.pallas_call(kernel, name=name, grid_spec=pltpu.PrefetchScalarGridSpec(...]
    ppermute x16 -> x20, waiting for transfers between devices: 163 us -> 84.2 us  [shifted(): lax.ppermute(value, axis, [(i, (i + shift) % count) for i in range(count)])]
    reduce_scatter x4 -> x6, waiting for transfers between devices: 0.02 us -> 64.3 us  [ctx_sum(): lax.psum_scatter(value, 'ctx', scatter_dimension=0, tiled=True)]
    dot_general x11 -> x5, matrix products: 38.8 us -> 7.68 us  [matmul_low(): return jnp.dot(former, latter, preferred_element_type=jnp.float32)]
    dot_general x4 -> x0, matrix products: 26.7 us -> none  [inner_rows(): lax.dot_general(former, latter, (((0,), (0,)), ((), ())), preferred_eleme...]
    dot_general x7 -> x3, matrix products: 30.8 us -> 9.19 us  [times_back(): lax.dot_general(former, latter, (((1,), (1,)), ((), ())), preferred_eleme...]
    ppermute x16 -> x6, starting transfers between devices: 31.7 us -> 15.9 us  [moved(): return lax.ppermute(value, axis, pairs)]
  transfers between devices with their start and end apart: 63 -> 66, of which waited for: 27 -> 25; matrix products, arithmetic and copies ran while one was open for 27% -> 18% of each run, Pallas kernels for 7% -> 17%
where the time goes in v3:
time: 614 us; the launch traced here: 605 us
  waiting for transfers between devices  205 us (33%)
  Pallas kernels  146 us (24%)
  local copies, waits for them, and re-layouts  101 us (16%)
  starting transfers between devices  70.6 us (11%)
  other arithmetic  47.5 us (8%)
  matrix products  18.3 us (3%)
  between operations  16.3 us (3%)
    pallas_call x17, Pallas kernels, call_at(): pl.pallas_call(kernel, name=name, grid_spec=pltpu.PrefetchScalarGridSpec(...  91.1 us
    ppermute x20, waiting for transfers between devices, shifted(): lax.ppermute(value, axis, [(i, (i + shift) % count) for i in range(count)])  84.2 us
    reduce_scatter x6, waiting for transfers between devices, ctx_sum(): lax.psum_scatter(value, 'ctx', scatter_dimension=0, tiled=True)  64.3 us
    unnamed x188, local copies, waits for them, and re-layouts  57.2 us
    ppermute x28, waiting for transfers between devices, partner(): lax.ppermute(value, 'tensor', [(rank, rank ^ stride) for rank in range(4)])  55.9 us
    pallas_call x10, Pallas kernels, call(): pl.pallas_call(kernel, name=name, grid=grid, in_specs=specs, out_specs=[s...  54.4 us
    ppermute x20, starting transfers between devices, shifted(): lax.ppermute(value, axis, [(i, (i + shift) % count) for i in range(count)])  34.2 us
    ppermute x6, starting transfers between devices, moved(): return lax.ppermute(value, axis, pairs)  15.9 us
  transfers between devices with their start and end apart: 66, of which 25 were waited for; matrix products, arithmetic and copies ran while one was open for 18% of the time, Pallas kernels for 17%

profile of v3, /device:TPU:0, one launch (start us, length us, event | category | flops | bytes accessed | tf_op | source)
XLA Modules:
  0.0 604.8 jit_solution(18332278320163680782)
XLA Ops:
  16.9 2.2 copy.106
  20.5 8.0 %slice.99 = bf16[2048,1,768]{2,1,0:T(2,128)(2,1)S(1)} slice(bf16[2048,2,768]{2,1,0:T(2,128)(2,1)} %param.19), slice={[0:2048], [1:2], [0:768]} | slice | bytes 6291456 | tf_op jit(solution)/shard_map/slice | solution.py:803
  30.8 3.3 own_state.2
  37.1 7.6 %collective-permute-start.4 = (bf16[512,128]{1,0:T(8,128)(2,1)}, bf16[512,128]{1,0:T(8,128)(2,1)}, u32[]{:S(2)}, u32[]{:S(2)}) collective-permute-start(bf16[512,128]{1,0:T(8,128)(2,1)} %dynamic-slice_convert_fusion.1), channel_id=1, source_target_pairs={{0,12},{1,13},{2,14},{3,15},{16,28},{17,29},{18,30},{19,31}} | collective-permute-start | bytes 393224 | tf_op jit(solution)/shard_map/ppermute | solution.py:33
  46.6 2.5 collective-permute-start.2
  49.1 2.2 collective-permute-start
  51.4 3.6 copy.89
  55.0 3.2 fusion.29.z_ref
  58.5 3.2 scan.1.y_ref
  67.4 6.7 %attend.1 = (bf16[512,256]{1,0:T(8,128)(2,1)S(1)}, f32[2,8,512]{2,1,0:T(8,128)S(1)}) custom-call(s32[1]{0:T(128)} %bitcast.9.rank_ref, bf16[512,256]{1,0:T(8,128)(2,1)S(1)} %convolution_convert_fusion.3.q_ref, bf16[2048,128]{1,0:T(8,128)(2,1)S(1)} %get-tuple-element.207.k_ref, bf16[2048,128]{1,0:T(8,128)(2,1)S(1)} %get-tuple-element.206.v_ref), custom_call_target="tpu_custom_call" | custom-call | tf_op jit(solution)/shard_map/attend/pallas_call | solution.py:396
  76.2 5.3 fusion.37.dact_ref
  82.6 3.5 carry.1
  86.1 4.8 mix_other.1
  91.5 2.2 collective-permute-done.7.refs_4_
  93.8 4.4 mix_own.1.mine_ref
  99.8 10.4 %copy.109 = bf16[256,8,2,1024]{3,1,2,0:T(8,128)(2,1)} copy(bf16[256,8,2,1024]{3,2,1,0:T(2,128)(2,1)} %bitcast.139) | data formatting | bytes 16777216
  110.1 13.6 %collective-permute-done.8.theirs_ref = bf16[256,2048]{1,0:T(8,128)(2,1)S(1)} collective-permute-done((bf16[256,2048]{1,0:T(8,128)(2,1)S(1)}, bf16[256,2048]{1,0:T(8,128)(2,1)S(1)}, u32[]{:S(2)}, u32[]{:S(2)}) %collective-permute-start.8) | collective-permute-done | bytes 1048608 | tf_op jit(solution)/shard_map/ppermute | solution.py:22
  123.7 2.7 norm_two.1
  126.5 2.6 collective-permute-done.9
  129.6 9.6 %expand.1 = (bf16[512,1024]{1,0:T(8,128)(2,1)}, bf16[2,512,1024]{2,1,0:T(8,128)(2,1)}) custom-call(bf16[512,2048]{1,0:T(8,128)(2,1)S(1)} %pad_maximum_fusion.x_ref.own_ref, bf16[2048,2048]{1,0:T(8,128)(2,1)} %bitcast.126, bf16[2048,2048]{1,0:T(8,128)(2,1)} %bitcast.127, f32[512,1024]{1,0:T(8,128)} %fusion.37.dact_ref), custom_call_target="tpu_custom_call" | custom-call | tf_op jit(solution)/shard_map/expand/pallas_call | solution.py:396
  139.2 7.2 %two_other.1 = bf16[256,2048]{1,0:T(8,128)(2,1)} custom-call(s32[2]{0:T(128)S(1)} %pad_add_fusion.1.at_ref, bf16[2,512,1024]{2,1,0:T(8,128)(2,1)} %get-tuple-element.84.refs_0_.refs_1_.refs_2_, bf16[2,512,1024]{2,1,0:T(8,128)(2,1)} %get-tuple-element.84.refs_0_.refs_1_.refs_2_, bf16[2048,2048]{1,0:T(8,128)(2,1)} %bitcast.128, bf16[2048,2048]{1,0:T(8,128)(2,1)} %bitcast.129), custom_call_target="tpu_custom_call" | custom-call | tf_op jit(solution)/shard_map/two_other/pallas_call | solution.py:531
  149.4 7.7 %two_own.1.mine_ref = bf16[256,2048]{1,0:T(8,128)(2,1)} custom-call(s32[2]{0:T(128)S(1)} %pad_add_fusion.at_ref, bf16[2,512,1024]{2,1,0:T(8,128)(2,1)} %get-tuple-element.84.refs_0_.refs_1_.refs_2_, bf16[2,512,1024]{2,1,0:T(8,128)(2,1)} %get-tuple-element.84.refs_0_.refs_1_.refs_2_, bf16[2048,2048]{1,0:T(8,128)(2,1)} %bitcast.130, ...), custom_call_target="tpu_custom_call" | custom-call | tf_op jit(solution)/shard_map/two_own/pallas_call | solution.py:531
  157.1 5.5 mlp_other.1
  165.7 4.8 mlp_own.1
  171.4 17.1 %collective-permute-done.15.refs_3_ = bf16[512,1024]{1,0:T(8,128)(2,1)} collective-permute-done((bf16[512,1024]{1,0:T(8,128)(2,1)}, bf16[512,1024]{1,0:T(8,128)(2,1)}, u32[]{:S(2)}, u32[]{:S(2)}) %collective-permute-start.15) | collective-permute-done | bytes 1048608 | tf_op jit(solution)/shard_map/ppermute | solution.py:27
  188.5 5.7 grad_down.1
  195.6 4.3 norm_two_back.1
  199.9 2.4 constant_dynamic-slice_fusion.15
  203.8 3.8 slice_bitcast_fusion.refs_4_
  207.6 8.7 %collective-permute-done.22.refs_0_ = bf16[256,1024]{1,0:T(8,128)(2,1)} collective-permute-done((bf16[256,1024]{1,0:T(8,128)(2,1)S(1)}, bf16[256,1024]{1,0:T(8,128)(2,1)}, u32[]{:S(2)}, u32[]{:S(2)}) %collective-permute-start.22) | collective-permute-done | bytes 524320 | tf_op jit(solution)/shard_map/ppermute | solution.py:27
  219.7 2.2 copy-done.75
  222.9 3.2 multiply_convert_fusion
  226.1 2.3 own_state.3
  230.1 8.8 %attend_back.1 = (bf16[512,256]{1,0:T(8,128)(2,1)S(1)}, f32[2048,128]{1,0:T(8,128)S(1)}, f32[2048,128]{1,0:T(8,128)S(1)}) custom-call(s32[1]{0:T(128)} %bitcast.9.rank_ref, bf16[512,256]{1,0:T(8,128)(2,1)S(1)} %copy-done.56, bf16[512,256]{1,0:T(8,128)(2,1)S(1)} %convolution_convert_fusion.2.do_ref, f32[2,8,512]{2,1,0:T(8,128)S(1)} %get-tuple-element.96.log_ref, ...), custom_call_target="tpu_custom_call" | custom-call | tf_op jit(solution)/shard_map/attend_back/pallas_call | solution.py:396
  243.2 3.3 constant_dynamic-slice_fusion.16
  250.6 2.8 fusion.2.refs_7_
  256.6 9.7 %scan_back.1 = (f32[512,768]{1,0:T(8,128)S(1)}, f32[6,8,512]{2,1,0:T(8,128)S(1)}, f32[512,256]{1,0:T(8,128)S(1)}, f32[512,256]{1,0:T(8,128)S(1)}) custom-call(bf16[512,768]{1,0:T(8,128)(2,1)S(1)} %convolution_convert_fusion.u_ref, bf16[512,768]{1,0:T(8,128)(2,1)S(1)} %copy-done.20, f32[6,8,512]{2,1,0:T(8,128)S(1)} %reshape.144.small_ref, ...), custom_call_target="tpu_custom_call" | custom-call | tf_op jit(solution)/shard_map/scan_back/pallas_call | solution.py:396
  271.7 4.7 collective-permute-done.25.refs_0_
  277.7 2.2 fusion.31
  282.1 9.3 %grad_gate_up.1 = bf16[1024,2048]{1,0:T(8,128)(2,1)} custom-call(s32[2]{0:T(128)S(1)} %pad_add_fusion.at_ref, bf16[512,2048]{1,0:T(8,128)(2,1)S(1)} %copy-done.9, bf16[256,1024]{1,0:T(8,128)(2,1)} %collective-permute-done.22.refs_0_, bf16[256,1024]{1,0:T(8,128)(2,1)} %collective-permute-done.23.refs_1_, ...), custom_call_target="tpu_custom_call" | custom-call | tf_op jit(solution)/shard_map/grad_gate_up/pallas_call | solution.py:531
  292.7 6.2 %collective-permute-done.27.refs_4_ = bf16[512,768]{1,0:T(8,128)(2,1)} collective-permute-done((bf16[512,768]{1,0:T(8,128)(2,1)}, bf16[512,768]{1,0:T(8,128)(2,1)}, u32[]{:S(2)}, u32[]{:S(2)}) %collective-permute-start.27) | collective-permute-done | bytes 786464 | tf_op jit(solution)/shard_map/ppermute | solution.py:27
  302.4 5.7 grad_outs.1
  314.8 6.3 %carry_back.1 = (bf16[512,768]{1,0:T(8,128)(2,1)S(1)}, f32[6,8,512]{2,1,0:T(8,128)S(1)}, f32[512,256]{1,0:T(8,128)S(1)}, f32[512,256]{1,0:T(8,128)S(1)}) custom-call(bf16[512,768]{1,0:T(8,128)(2,1)S(1)} %convolution_convert_fusion.u_ref, bf16[512,768]{1,0:T(8,128)(2,1)S(1)} %copy-done.21, f32[6,8,512]{2,1,0:T(8,128)S(1)} %reshape.144.small_ref, ...), custom_call_target="tpu_custom_call" | custom-call | tf_op jit(solution)/shard_map/carry_back/pallas_call | solution.py:396
  330.2 3.1 collective-permute-done.34
  335.6 5.9 one_other.1
  344.8 6.2 %one_own.1.mine_ref = bf16[256,2048]{1,0:T(8,128)(2,1)S(1)} custom-call(s32[2]{0:T(128)S(1)} %pad_add_fusion.at_ref, bf16[512,768]{1,0:T(8,128)(2,1)S(1)} %copy-done.17, bf16[512,768]{1,0:T(8,128)(2,1)S(1)} %copy-done.16, bf16[512,256]{1,0:T(8,128)(2,1)S(1)} %copy-done.47, bf16[512,384]{1,0:T(8,128)(2,1)S(1)} %fusion.13.refs_3_.refs_2_, ...), custom_call_target="tpu_custom_call" | custom-call | tf_op jit(solution)/shard_map/one_own/pallas_call | solution.py:531
  353.2 4.0 grad_ins_small.1
  361.2 22.5 %collective-permute-done.48.refs_5_ = bf16[512,256]{1,0:T(8,128)(2,1)S(1)} collective-permute-done((bf16[512,256]{1,0:T(8,128)(2,1)}, bf16[512,256]{1,0:T(8,128)(2,1)S(1)}, u32[]{:S(2)}, u32[]{:S(2)}) %collective-permute-start.48) | collective-permute-done | bytes 262176 | tf_op jit(solution)/shard_map/ppermute | solution.py:27
  385.8 4.9 grad_ins_first.1
  393.6 16.4 %collective-permute-done.40.refs_3_ = bf16[512,768]{1,0:T(8,128)(2,1)S(1)} collective-permute-done((bf16[512,768]{1,0:T(8,128)(2,1)S(1)}, bf16[512,768]{1,0:T(8,128)(2,1)S(1)}, u32[]{:S(2)}, u32[]{:S(2)}) %collective-permute-start.40) | collective-permute-done | bytes 786464 | tf_op jit(solution)/shard_map/ppermute | solution.py:27
  410.1 4.5 grad_ins_source.1
  419.1 19.8 %collective-permute-done.17 = bf16[256,2048]{1,0:T(8,128)(2,1)} collective-permute-done((bf16[256,2048]{1,0:T(8,128)(2,1)}, bf16[256,2048]{1,0:T(8,128)(2,1)}, u32[]{:S(2)}, u32[]{:S(2)}) %collective-permute-start.17) | collective-permute-done | bytes 1048608 | tf_op jit(solution)/shard_map/ppermute | solution.py:22
  438.9 4.8 multiply_reduce_fusion.1
  453.8 7.4 %collective-permute-start.56 = (f32[39]{0:T(128)S(1)}, f32[39]{0:T(128)S(1)}, u32[]{:S(2)}, u32[]{:S(2)}) collective-permute-start(f32[39]{0:T(128)S(1)} %fusion.53), channel_id=1, source_target_pairs={{0,12},{4,0},{8,4},{12,8},{1,13},{5,1},{9,5},{13,9},{2,14},{6,2},{... | collective-permute-start | bytes 476 | tf_op jit(solution)/shard_map/ppermute | solution.py:27
  462.5 3.3 collective-permute-done.55
  467.9 6.3 %collective-permute-done.36.theirs_ref = bf16[256,2048]{1,0:T(8,128)(2,1)} collective-permute-done((bf16[256,2048]{1,0:T(8,128)(2,1)S(1)}, bf16[256,2048]{1,0:T(8,128)(2,1)}, u32[]{:S(2)}, u32[]{:S(2)}) %collective-permute-start.36) | collective-permute-done | bytes 1048608 | tf_op jit(solution)/shard_map/ppermute | solution.py:22
  475.9 3.7 norm_one_back.1
  484.8 7.2 %collective-permute-start.46 = (f32[256,2]{0,1:T(2,128)S(1)}, f32[256,2]{0,1:T(2,128)S(1)}, u32[]{:S(2)}, u32[]{:S(2)}) collective-permute-start(f32[256,2]{0,1:T(2,128)S(1)} %get-tuple-element.233), channel_id=1, source_target_pairs={{0,12},{4,0},{8,4},{12,8},{1,13},{5,1},{9,5},{13,9},{2,14},{6,2},{... | collective-permute-start | bytes 6152 | tf_op jit(solution)/shard_map/ppermute | solution.py:27
  494.7 2.5 copy.102
  508.6 2.8 collective-permute-done.51
  519.5 2.3 copy.99
  526.8 2.4 copy.97
  529.1 64.3 %reduce-scatter.15.cloned.1.call-done = bf16[256,2048]{1,0:T(8,128)(2,1)} async-done(((bf16[1024,2048]{1,0:T(8,128)(2,1)}), bf16[256,2048]{1,0:T(8,128)(2,1)}) %reduce-scatter.15.cloned.1.call-update) | async-done | bytes 1048592 | tf_op jit(solution)/shard_map/reduce_scatter | solution.py:71
  593.4 4.1 reshape.155
  (412 shorter events, 154.7 us)
Async XLA Ops:
  7.2 485.3 %reduce-scatter.17.cloned.1.call-start = ((), (), s32[]{:S(2)}) async-start(), calls=%async_computation.11 | async-start | bytes 2621440 | tf_op jit(solution)/shard_map/reduce_scatter | solution.py:71
  37.1 24.7 %collective-permute-start.4 = (bf16[512,128]{1,0:T(8,128)(2,1)}, bf16[512,128]{1,0:T(8,128)(2,1)}, u32[]{:S(2)}, u32[]{:S(2)}) collective-permute-start(bf16[512,128]{1,0:T(8,128)(2,1)} %dynamic-slice_convert_fusion.1), channel_id=1, source_target_pairs={{0,12},{1,13},{2,14},{3,15},{16,28},{17,29},{18,30},{19,31}} | collective-permute-start | bytes 393224 | tf_op jit(solution)/shard_map/ppermute | solution.py:33
  44.7 17.1 %collective-permute-start.3 = (bf16[512,128]{1,0:T(8,128)(2,1)}, bf16[512,128]{1,0:T(8,128)(2,1)}, u32[]{:S(2)}, u32[]{:S(2)}) collective-permute-start(bf16[512,128]{1,0:T(8,128)(2,1)} %dynamic-slice_convert_fusion.1), channel_id=1, source_target_pairs={{0,8},{4,12},{1,9},{5,13},{2,10},{6,14},{3,11},{7,15},{16,24},{20,... | collective-permute-start | bytes 393224 | tf_op jit(solution)/shard_map/ppermute | solution.py:33
  46.6 15.2 %collective-permute-start.2 = (bf16[512,128]{1,0:T(8,128)(2,1)}, bf16[512,128]{1,0:T(8,128)(2,1)}, u32[]{:S(2)}, u32[]{:S(2)}) collective-permute-start(bf16[512,128]{1,0:T(8,128)(2,1)} %dynamic-slice_convert_fusion.1), channel_id=1, source_target_pairs={{0,4},{4,8},{8,12},{1,5},{5,9},{9,13},{2,6},{6,10},{10,14},{3,7},{... | collective-permute-start | bytes 393224 | tf_op jit(solution)/shard_map/ppermute | solution.py:33
  49.1 14.7 %collective-permute-start = (bf16[768,256]{1,0:T(8,128)(2,1)}, bf16[768,256]{1,0:T(8,128)(2,1)}, u32[]{:S(2)}, u32[]{:S(2)}) collective-permute-start(bf16[768,256]{1,0:T(8,128)(2,1)} %own_state.2), channel_id=1, source_target_pairs={{0,4},{1,5},{2,6},{3,7},{16,20},{17,21},{18,22},{19,23}} | collective-permute-start | bytes 1179656 | tf_op jit(solution)/shard_map/ppermute | solution.py:101
  63.0 3.0 collective-permute-start.5
  65.3 8.9 %collective-permute-start.1 = (bf16[768,256]{1,0:T(8,128)(2,1)S(1)}, bf16[768,256]{1,0:T(8,128)(2,1)S(1)}, u32[]{:S(2)}, u32[]{:S(2)}) collective-permute-start(bf16[768,256]{1,0:T(8,128)(2,1)S(1)} %fusion.8), channel_id=1, source_target_pairs={{4,8},{5,9},{6,10},{7,11},{20,24},{21,25},{22,26},{23,27}} | collective-permute-start | bytes 1179656 | tf_op jit(solution)/shard_map/ppermute | solution.py:101
  75.5 6.0 collective-permute-start.6
  90.9 2.8 collective-permute-start.7
  98.2 25.5 %collective-permute-start.8 = (bf16[256,2048]{1,0:T(8,128)(2,1)S(1)}, bf16[256,2048]{1,0:T(8,128)(2,1)S(1)}, u32[]{:S(2)}, u32[]{:S(2)}) collective-permute-start(bf16[256,2048]{1,0:T(8,128)(2,1)S(1)} %mix_own.1.mine_ref), channel_id=1, source_target_pairs={{0,2},{1,3},{2,0},{3,1},{4,6},{5,7},{6,4},{7,5},{8,10},{9,11},{10,... | collective-permute-start | bytes 3145736 | tf_op jit(solution)/shard_map/ppermute | solution.py:22
  126.4 2.7 collective-permute-start.9
  146.3 3.1 collective-permute-start.10
  147.8 17.9 %collective-permute-start.13 = (bf16[256,1024]{1,0:T(8,128)(2,1)S(1)}, bf16[256,1024]{1,0:T(8,128)(2,1)}, u32[]{:S(2)}, u32[]{:S(2)}) collective-permute-start(bf16[256,1024]{1,0:T(8,128)(2,1)S(1)} %dynamic_slice.119), channel_id=1, source_target_pairs={{0,16},{16,0},{1,17},{17,1},{2,18},{18,2},{3,19},{19,3},{4,20},{20... | collective-permute-start | bytes 1572872 | tf_op jit(solution)/shard_map/ppermute | solution.py:27
  162.6 3.1 collective-permute-start.11
  162.7 25.8 %collective-permute-start.15 = (bf16[512,1024]{1,0:T(8,128)(2,1)}, bf16[512,1024]{1,0:T(8,128)(2,1)}, u32[]{:S(2)}, u32[]{:S(2)}) collective-permute-start(bf16[512,1024]{1,0:T(8,128)(2,1)} %get-tuple-element.85.refs_0_.refs_2_), channel_id=1, source_target_pairs={{0,16},{16,0},{1,17},{17,1},{2,18},{18,2},{3,19},{19,3},{4,20},{20... | collective-permute-start | bytes 3145736 | tf_op jit(solution)/shard_map/ppermute | solution.py:27
  164.2 31.4 %collective-permute-start.12 = (bf16[256,2048]{1,0:T(8,128)(2,1)}, bf16[256,2048]{1,0:T(8,128)(2,1)}, u32[]{:S(2)}, u32[]{:S(2)}) collective-permute-start(bf16[256,2048]{1,0:T(8,128)(2,1)} %two_own.1.mine_ref), channel_id=1, source_target_pairs={{0,2},{1,3},{2,0},{3,1},{4,6},{5,7},{6,4},{7,5},{8,10},{9,11},{10,... | collective-permute-start | bytes 3145736 | tf_op jit(solution)/shard_map/ppermute | solution.py:22
  165.7 5.8 collective-permute-start.14
  199.9 19.4 %collective-permute-start.16 = (bf16[256,2048]{1,0:T(8,128)(2,1)S(1)}, bf16[256,2048]{1,0:T(8,128)(2,1)S(1)}, u32[]{:S(2)}, u32[]{:S(2)}) collective-permute-start(bf16[256,2048]{1,0:T(8,128)(2,1)S(1)} %get-tuple-element.90), channel_id=1, source_target_pairs={{0,1},{1,0},{2,3},{3,2},{4,5},{5,4},{6,7},{7,6},{8,9},{9,8},{10,11... | collective-permute-start | bytes 3145736 | tf_op jit(solution)/shard_map/ppermute | solution.py:22
  202.3 14.0 %collective-permute-start.22 = (bf16[256,1024]{1,0:T(8,128)(2,1)S(1)}, bf16[256,1024]{1,0:T(8,128)(2,1)}, u32[]{:S(2)}, u32[]{:S(2)}) collective-permute-start(bf16[256,1024]{1,0:T(8,128)(2,1)S(1)} %constant_dynamic-slice_fusion.18), channel_id=1, source_target_pairs={{0,16},{16,0},{1,17},{17,1},{2,18},{18,2},{3,19},{19,3},{4,20},{20... | collective-permute-start | bytes 1572872 | tf_op jit(solution)/shard_map/ppermute | solution.py:27
  216.4 54.7 %collective-permute-start.23 = (bf16[256,1024]{1,0:T(8,128)(2,1)}, bf16[256,1024]{1,0:T(8,128)(2,1)}, u32[]{:S(2)}, u32[]{:S(2)}) collective-permute-start(bf16[256,1024]{1,0:T(8,128)(2,1)} %collective-permute-done.22.refs_0_), channel_id=1, source_target_pairs={{0,1},{1,0},{2,3},{3,2},{4,5},{5,4},{6,7},{7,6},{8,9},{9,8},{10,11... | collective-permute-start | bytes 1572872 | tf_op jit(solution)/shard_map/ppermute | solution.py:22
  216.4 64.3 %collective-permute-start.24 = (bf16[2,512,1024]{2,1,0:T(8,128)(2,1)}, bf16[2,512,1024]{2,1,0:T(8,128)(2,1)}, u32[]{:S(2)}, u32[]{:S(2)}) collective-permute-start(bf16[2,512,1024]{2,1,0:T(8,128)(2,1)} %get-tuple-element.84.refs_0_.refs_1_.refs_2_), channel_id=1, source_target_pairs={{0,16},{16,0},{1,17},{17,1},{2,18},{18,2},{3,19},{19,3},{4,20},{20... | collective-permute-start | bytes 6291464 | tf_op jit(solution)/shard_map/ppermute | solution.py:27
  218.7 57.7 %collective-permute-start.25 = (bf16[256,1024]{1,0:T(8,128)(2,1)}, bf16[256,1024]{1,0:T(8,128)(2,1)}, u32[]{:S(2)}, u32[]{:S(2)}) collective-permute-start(bf16[256,1024]{1,0:T(8,128)(2,1)} %constant_dynamic-slice_fusion.17), channel_id=1, source_target_pairs={{0,16},{16,0},{1,17},{17,1},{2,18},{18,2},{3,19},{19,3},{4,20},{20... | collective-permute-start | bytes 1572872 | tf_op jit(solution)/shard_map/ppermute | solution.py:27
  228.4 12.3 %collective-permute-start.19 = (bf16[768,256]{1,0:T(8,128)(2,1)S(1)}, bf16[768,256]{1,0:T(8,128)(2,1)S(1)}, u32[]{:S(2)}, u32[]{:S(2)}) collective-permute-start(bf16[768,256]{1,0:T(8,128)(2,1)S(1)} %own_state.3), channel_id=1, source_target_pairs={{12,8},{13,9},{14,10},{15,11},{28,24},{29,25},{30,26},{31,27}} | collective-permute-start | bytes 1179656 | tf_op jit(solution)/shard_map/ppermute | solution.py:101
  240.8 35.6 %collective-permute-start.29 = (bf16[2048,128]{1,0:T(8,128)(2,1)}, bf16[2048,128]{1,0:T(8,128)(2,1)}, u32[]{:S(2)}, u32[]{:S(2)}) collective-permute-start(bf16[2048,128]{1,0:T(8,128)(2,1)} %select_convert_fusion), channel_id=1, source_target_pairs={{0,1},{1,0},{2,3},{3,2},{4,5},{5,4},{6,7},{7,6},{8,9},{9,8},{10,11... | collective-permute-start | bytes 1572872 | tf_op jit(solution)/shard_map/ppermute | solution.py:22
  241.8 25.7 %collective-permute-start.20 = (bf16[768,256]{1,0:T(8,128)(2,1)}, bf16[768,256]{1,0:T(8,128)(2,1)}, u32[]{:S(2)}, u32[]{:S(2)}) collective-permute-start(bf16[768,256]{1,0:T(8,128)(2,1)} %fusion.10), channel_id=1, source_target_pairs={{8,4},{9,5},{10,6},{11,7},{24,20},{25,21},{26,22},{27,23}} | collective-permute-start | bytes 1179656 | tf_op jit(solution)/shard_map/ppermute | solution.py:101
  250.5 247.3 %reduce-scatter.11.cloned.1.call-start = ((), (), s32[]{:S(2)}) async-start(), calls=%async_computation.8 | async-start | bytes 983040 | tf_op jit(solution)/shard_map/reduce_scatter | solution.py:71
  267.5 23.9 %collective-permute-start.28 = (bf16[512,256]{1,0:T(8,128)(2,1)}, bf16[512,256]{1,0:T(8,128)(2,1)}, u32[]{:S(2)}, u32[]{:S(2)}) collective-permute-start(bf16[512,256]{1,0:T(8,128)(2,1)} %copy-done.49), channel_id=1, source_target_pairs={{0,16},{16,0},{1,17},{17,1},{2,18},{18,2},{3,19},{19,3},{4,20},{20... | collective-permute-start | bytes 786440 | tf_op jit(solution)/shard_map/ppermute | solution.py:27
  271.1 27.7 %collective-permute-start.27 = (bf16[512,768]{1,0:T(8,128)(2,1)}, bf16[512,768]{1,0:T(8,128)(2,1)}, u32[]{:S(2)}, u32[]{:S(2)}) collective-permute-start(bf16[512,768]{1,0:T(8,128)(2,1)} %get-tuple-element.78.refs_0_.refs_2_), channel_id=1, source_target_pairs={{0,16},{16,0},{1,17},{17,1},{2,18},{18,2},{3,19},{19,3},{4,20},{20... | collective-permute-start | bytes 2359304 | tf_op jit(solution)/shard_map/ppermute | solution.py:27
  276.4 23.8 %collective-permute-start.26 = (bf16[256,1024]{1,0:T(8,128)(2,1)}, bf16[256,1024]{1,0:T(8,128)(2,1)}, u32[]{:S(2)}, u32[]{:S(2)}) collective-permute-start(bf16[256,1024]{1,0:T(8,128)(2,1)} %collective-permute-done.25.refs_0_), channel_id=1, source_target_pairs={{0,1},{1,0},{2,3},{3,2},{4,5},{5,4},{6,7},{7,6},{8,9},{9,8},{10,11... | collective-permute-start | bytes 1572872 | tf_op jit(solution)/shard_map/ppermute | solution.py:22
  276.4 33.0 %collective-permute-start.21 = (bf16[768,256]{1,0:T(8,128)(2,1)}, bf16[768,256]{1,0:T(8,128)(2,1)}, u32[]{:S(2)}, u32[]{:S(2)}) collective-permute-start(bf16[768,256]{1,0:T(8,128)(2,1)} %fusion.11), channel_id=1, source_target_pairs={{4,0},{5,1},{6,2},{7,3},{20,16},{21,17},{22,18},{23,19}} | collective-permute-start | bytes 1179656 | tf_op jit(solution)/shard_map/ppermute | solution.py:101
  280.6 60.9 %collective-permute-start.37 = (bf16[256,1024]{1,0:T(8,128)(2,1)}, bf16[256,1024]{1,0:T(8,128)(2,1)}, u32[]{:S(2)}, u32[]{:S(2)}) collective-permute-start(bf16[256,1024]{1,0:T(8,128)(2,1)} %dynamic_slice.128), channel_id=1, source_target_pairs={{0,16},{16,0},{1,17},{17,1},{2,18},{18,2},{3,19},{19,3},{4,20},{20... | collective-permute-start | bytes 1572872 | tf_op jit(solution)/shard_map/ppermute | solution.py:27
  291.4 31.7 %collective-permute-start.30 = (bf16[512,128]{1,0:T(8,128)(2,1)}, bf16[512,128]{1,0:T(8,128)(2,1)}, u32[]{:S(2)}, u32[]{:S(2)}) collective-permute-start(bf16[512,128]{1,0:T(8,128)(2,1)} %get-tuple-element.213), channel_id=1, source_target_pairs={{4,0},{8,4},{12,8},{5,1},{9,5},{13,9},{6,2},{10,6},{14,10},{7,3},{... | collective-permute-start | bytes 393224 | tf_op jit(solution)/shard_map/ppermute | solution.py:33
  298.8 24.2 %collective-permute-start.32 = (bf16[512,128]{1,0:T(8,128)(2,1)}, bf16[512,128]{1,0:T(8,128)(2,1)}, u32[]{:S(2)}, u32[]{:S(2)}) collective-permute-start(bf16[512,128]{1,0:T(8,128)(2,1)} %get-tuple-element.214), channel_id=1, source_target_pairs={{12,0},{13,1},{14,2},{15,3},{28,16},{29,17},{30,18},{31,19}} | collective-permute-start | bytes 393224 | tf_op jit(solution)/shard_map/ppermute | solution.py:33
  300.1 22.9 %collective-permute-start.31 = (bf16[512,128]{1,0:T(8,128)(2,1)}, bf16[512,128]{1,0:T(8,128)(2,1)}, u32[]{:S(2)}, u32[]{:S(2)}) collective-permute-start(bf16[512,128]{1,0:T(8,128)(2,1)} %get-tuple-element.215), channel_id=1, source_target_pairs={{8,0},{12,4},{9,1},{13,5},{10,2},{14,6},{11,3},{15,7},{24,16},{28,... | collective-permute-start | bytes 393224 | tf_op jit(solution)/shard_map/ppermute | solution.py:33
  323.0 3.0 collective-permute-start.33
  327.4 6.0 collective-permute-start.34
  341.5 3.3 collective-permute-start.35
  341.6 10.4 %collective-permute-start.38 = (bf16[256,1024]{1,0:T(8,128)(2,1)}, bf16[256,1024]{1,0:T(8,128)(2,1)S(1)}, u32[]{:S(2)}, u32[]{:S(2)}) collective-permute-start(bf16[256,1024]{1,0:T(8,128)(2,1)} %collective-permute-done.37.refs_0_), channel_id=1, source_target_pairs={{0,1},{1,0},{2,3},{3,2},{4,5},{5,4},{6,7},{7,6},{8,9},{9,8},{10,11... | collective-permute-start | bytes 1572872 | tf_op jit(solution)/shard_map/ppermute | solution.py:22
  342.1 11.1 %collective-permute-start.39 = (bf16[512,384]{1,0:T(8,128)(2,1)S(1)}, bf16[512,384]{1,0:T(8,128)(2,1)S(1)}, u32[]{:S(2)}, u32[]{:S(2)}) collective-permute-start(bf16[512,384]{1,0:T(8,128)(2,1)S(1)} %fusion.13.refs_3_.refs_2_), channel_id=1, source_target_pairs={{0,16},{16,0},{1,17},{17,1},{2,18},{18,2},{3,19},{19,3},{4,20},{20... | collective-permute-start | bytes 1179656 | tf_op jit(solution)/shard_map/ppermute | solution.py:27
  358.1 159.4 %reduce-scatter.13.cloned.1.call-start = ((), (), s32[]{:S(2)}) async-start(), calls=%async_computation.9 | async-start | bytes 2621440 | tf_op jit(solution)/shard_map/reduce_scatter | solution.py:71
  358.8 163.9 %reduce-scatter.7.cloned.1.call-start = ((), (), s32[]{:S(2)}) async-start(), calls=%async_computation.6 | async-start | bytes 2621440 | tf_op jit(solution)/shard_map/reduce_scatter | solution.py:71
  359.1 24.6 %collective-permute-start.47 = (bf16[512,768]{1,0:T(8,128)(2,1)}, bf16[512,768]{1,0:T(8,128)(2,1)S(1)}, u32[]{:S(2)}, u32[]{:S(2)}) collective-permute-start(bf16[512,768]{1,0:T(8,128)(2,1)} %get-tuple-element.196.refs_0_.refs_2_), channel_id=1, source_target_pairs={{0,16},{16,0},{1,17},{17,1},{2,18},{18,2},{3,19},{19,3},{4,20},{20... | collective-permute-start | bytes 2359304 | tf_op jit(solution)/shard_map/ppermute | solution.py:27
  360.6 23.1 %collective-permute-start.48 = (bf16[512,256]{1,0:T(8,128)(2,1)}, bf16[512,256]{1,0:T(8,128)(2,1)S(1)}, u32[]{:S(2)}, u32[]{:S(2)}) collective-permute-start(bf16[512,256]{1,0:T(8,128)(2,1)} %copy-done.45), channel_id=1, source_target_pairs={{0,16},{16,0},{1,17},{17,1},{2,18},{18,2},{3,19},{19,3},{4,20},{20... | collective-permute-start | bytes 786440 | tf_op jit(solution)/shard_map/ppermute | solution.py:27
  392.1 133.5 %reduce-scatter.9.cloned.1.call-start = ((), (), s32[]{:S(2)}) async-start(), calls=%async_computation.7 | async-start | bytes 1966080 | tf_op jit(solution)/shard_map/reduce_scatter | solution.py:71
  392.1 17.9 %collective-permute-start.40 = (bf16[512,768]{1,0:T(8,128)(2,1)S(1)}, bf16[512,768]{1,0:T(8,128)(2,1)S(1)}, u32[]{:S(2)}, u32[]{:S(2)}) collective-permute-start(bf16[512,768]{1,0:T(8,128)(2,1)S(1)} %copy-done.16), channel_id=1, source_target_pairs={{0,16},{16,0},{1,17},{17,1},{2,18},{18,2},{3,19},{19,3},{4,20},{20... | collective-permute-start | bytes 2359304 | tf_op jit(solution)/shard_map/ppermute | solution.py:27
  415.8 177.7 %reduce-scatter.15.cloned.1.call-start = ((), (), s32[]{:S(2)}) async-start(), calls=%async_computation.10 | async-start | bytes 5242880 | tf_op jit(solution)/shard_map/reduce_scatter | solution.py:71
  415.8 23.1 %collective-permute-start.17 = (bf16[256,2048]{1,0:T(8,128)(2,1)}, bf16[256,2048]{1,0:T(8,128)(2,1)}, u32[]{:S(2)}, u32[]{:S(2)}) collective-permute-start(bf16[256,2048]{1,0:T(8,128)(2,1)} %copy-done.38), channel_id=1, source_target_pairs={{0,2},{1,3},{2,0},{3,1},{4,6},{5,7},{6,4},{7,5},{8,10},{9,11},{10,... | collective-permute-start | bytes 3145736 | tf_op jit(solution)/shard_map/ppermute | solution.py:22
  448.8 25.4 %collective-permute-start.36 = (bf16[256,2048]{1,0:T(8,128)(2,1)S(1)}, bf16[256,2048]{1,0:T(8,128)(2,1)}, u32[]{:S(2)}, u32[]{:S(2)}) collective-permute-start(bf16[256,2048]{1,0:T(8,128)(2,1)S(1)} %copy-done.31), channel_id=1, source_target_pairs={{0,2},{1,3},{2,0},{3,1},{4,6},{5,7},{6,4},{7,5},{8,10},{9,11},{10,... | collective-permute-start | bytes 3145736 | tf_op jit(solution)/shard_map/ppermute | solution.py:22
  450.2 3.5 collective-permute-start.53
  451.9 27.9 %collective-permute-start.18 = (bf16[256,2048]{1,0:T(8,128)(2,1)}, bf16[256,2048]{1,0:T(8,128)(2,1)S(1)}, u32[]{:S(2)}, u32[]{:S(2)}) collective-permute-start(bf16[256,2048]{1,0:T(8,128)(2,1)} %get-tuple-element.195), channel_id=1, source_target_pairs={{0,1},{1,0},{2,3},{3,2},{4,5},{5,4},{6,7},{7,6},{8,9},{9,8},{10,11... | collective-permute-start | bytes 3145736 | tf_op jit(solution)/shard_map/ppermute | solution.py:22
  453.8 8.7 %collective-permute-start.56 = (f32[39]{0:T(128)S(1)}, f32[39]{0:T(128)S(1)}, u32[]{:S(2)}, u32[]{:S(2)}) collective-permute-start(f32[39]{0:T(128)S(1)} %fusion.53), channel_id=1, source_target_pairs={{0,12},{4,0},{8,4},{12,8},{1,13},{5,1},{9,5},{13,9},{2,14},{6,2},{... | collective-permute-start | bytes 476 | tf_op jit(solution)/shard_map/ppermute | solution.py:27
  461.2 4.6 collective-permute-start.55
  461.2 5.5 collective-permute-start.54
  481.0 3.7 collective-permute-start.43
  484.7 12.5 %collective-permute-start.44 = (f32[256,2]{0,1:T(2,128)S(1)}, f32[256,2]{0,1:T(2,128)S(1)}, u32[]{:S(2)}, u32[]{:S(2)}) collective-permute-start(f32[256,2]{0,1:T(2,128)S(1)} %get-tuple-element.232), channel_id=1, source_target_pairs={{0,4},{4,8},{8,12},{12,0},{1,5},{5,9},{9,13},{13,1},{2,6},{6,10},{... | collective-permute-start | bytes 6152 | tf_op jit(solution)/shard_map/ppermute | solution.py:27
  484.8 12.4 %collective-permute-start.46 = (f32[256,2]{0,1:T(2,128)S(1)}, f32[256,2]{0,1:T(2,128)S(1)}, u32[]{:S(2)}, u32[]{:S(2)}) collective-permute-start(f32[256,2]{0,1:T(2,128)S(1)} %get-tuple-element.233), channel_id=1, source_target_pairs={{0,12},{4,0},{8,4},{12,8},{1,13},{5,1},{9,5},{13,9},{2,14},{6,2},{... | collective-permute-start | bytes 6152 | tf_op jit(solution)/shard_map/ppermute | solution.py:27
  492.0 5.2 collective-permute-start.45
  497.2 17.3 %collective-permute-start.41 = (bf16[256,2048]{1,0:T(8,128)(2,1)S(1)}, bf16[256,2048]{1,0:T(8,128)(2,1)}, u32[]{:S(2)}, u32[]{:S(2)}) collective-permute-start(bf16[256,2048]{1,0:T(8,128)(2,1)S(1)} %copy-done.54), channel_id=1, source_target_pairs={{0,1},{1,0},{2,3},{3,2},{4,5},{5,4},{6,7},{7,6},{8,9},{9,8},{10,11... | collective-permute-start | bytes 3145736 | tf_op jit(solution)/shard_map/ppermute | solution.py:22
  500.3 4.6 collective-permute-start.59
  501.8 4.1 collective-permute-start.58
  502.5 3.5 collective-permute-start.57
  502.5 6.1 %collective-permute-start.50 = (f32[256,128]{1,0:T(8,128)S(1)}, f32[256,128]{1,0:T(8,128)S(1)}, u32[]{:S(2)}, u32[]{:S(2)}) collective-permute-start(f32[256,128]{1,0:T(8,128)S(1)} %get-tuple-element.221), channel_id=1, source_target_pairs={{0,2},{1,3},{2,0},{3,1},{4,6},{5,7},{6,4},{7,5},{8,10},{9,11},{10,... | collective-permute-start | bytes 393224 | tf_op jit(solution)/shard_map/ppermute | solution.py:22
  504.9 3.7 collective-permute-start.49
  505.9 5.5 collective-permute-start.51
  (89 other events, 606.2 us)
Sparse Core Ops, SparseCore 0:
  250.7 55.0 reduce-scatter.16
  358.2 28.6 reduce-scatter.10
  389.3 43.1 reduce-scatter.12
  434.6 43.1 reduce-scatter.6
  480.7 34.7 reduce-scatter.8
  517.7 75.6 reduce-scatter.14

commit v4 on v3

--- a/solution.py
+++ b/solution.py
@@ -14,6 +14,7 @@
 
 EPSILON = 1e-05
 NEG_FILL = -1e30
+VMEM_GRANT = 28 * 1024 * 1024
 
 CORE, CHIP = (1, 2)
 
@@ -67,8 +68,8 @@
     return [shifted(value, "dp", shift) for shift in range(1, lax.axis_size("dp"))]
 
 
-def ctx_sum(value):
-    return lax.psum_scatter(value, "ctx", scatter_dimension=0, tiled=True).astype(jnp.float32)
+def ctx_partner(value, stride):
+    return lax.ppermute(value, "ctx", [(rank, rank ^ stride) for rank in range(4)])
 
 
 def all_sum(value, axis):
@@ -77,15 +78,6 @@
     total = jnp.zeros_like(value)
     for rank in range(count):
         total = total + lax.dynamic_index_in_dim(pieces, (mine - rank) % count, 0, keepdims=False)
-    return total
-
-
-def scatter_sum(value, axis):
-    count, mine = (lax.axis_size(axis), lax.axis_index(axis))
-    share = value.shape[0] // count
-    total = cut(value, mine, share, 0)
-    for shift in range(1, count):
-        total = total + shifted(cut(value, (mine + shift) % count, share, 0), axis, shift)
     return total
 
 
@@ -122,11 +114,6 @@
     return lax.dot_general(
         former, latter, (((1,), (1,)), ((), ())), preferred_element_type=jnp.float32
     )
-
-
-def silu_slope(values):
-    logistic = jax.nn.sigmoid(values)
-    return logistic * (1.0 + values * (1.0 - logistic))
 
 
 def split_lanes(first, second, shape):
@@ -401,8 +388,8 @@
         out_specs=[spec for _, spec in outs],
         out_shape=[out for out, _ in outs],
         scratch_shapes=list(scratch),
-        cost_estimate=pl.CostEstimate(flops=0, bytes_accessed=0, transcendentals=0),
-        compiler_params=pltpu.CompilerParams(vmem_limit_bytes=48 * 1024 * 1024),
+        cost_estimate=pl.CostEstimate(flops=1, bytes_accessed=1, transcendentals=0),
+        compiler_params=pltpu.CompilerParams(vmem_limit_bytes=VMEM_GRANT),
     )(*args)
 
 
@@ -538,8 +525,8 @@
             out_specs=[spec for _, spec in outs],
         ),
         out_shape=[out for out, _ in outs],
-        cost_estimate=pl.CostEstimate(flops=0, bytes_accessed=0, transcendentals=0),
-        compiler_params=pltpu.CompilerParams(vmem_limit_bytes=48 * 1024 * 1024),
+        cost_estimate=pl.CostEstimate(flops=1, bytes_accessed=1, transcendentals=0),
+        compiler_params=pltpu.CompilerParams(vmem_limit_bytes=VMEM_GRANT),
     )(scalars, *args)
 
 
@@ -632,68 +619,138 @@
     )
 
 
-def expand_kernel(x_ref, gate_ref, up_ref, dact_ref, act_ref, grad_ref):
-    gate = matmul_low(x_ref[...], gate_ref[...])
-    up = matmul_low(x_ref[...], up_ref[...])
-    dact = dact_ref[...]
-    logistic = jax.nn.sigmoid(gate)
-    silu = gate * logistic
-    act_ref[...] = narrow(silu * up)
-    grad_ref[0] = narrow(dact * up * (logistic * (1.0 + gate * (1.0 - logistic))))
-    grad_ref[1] = narrow(dact * silu)
-
-
-def expand(x, weight, dact):
+def half_places(at_ref, rows):
+    half = rows // 2
+    return [pl.ds(pl.multiple_of(which * half, half), half) for which in (at_ref[0], 1 - at_ref[0])]
+
+
+def project_kernel(x_ref, weight_ref, out_ref):
+    out_ref[...] = matmul_low(x_ref[...], weight_ref[...]).astype(out_ref.dtype)
+
+
+def project(name, x, weight, start, width, kind):
     rows, depth = x.shape
-    width = dact.shape[1]
+    size = math.gcd(256, width)
+    return call(
+        name,
+        project_kernel,
+        (width // size,),
+        [
+            pl.BlockSpec((rows, depth), lambda j: (0, 0)),
+            pl.BlockSpec((depth, size), lambda j: (0, start // size + j)),
+        ],
+        (x, weight),
+        [(like((rows, width), kind), pl.BlockSpec((rows, size), lambda j: (0, j)))],
+    )[0]
+
+
+def expand_kernel(at_ref, mine_ref, other_ref, gate_ref, up_ref, dact_ref, act_ref, dgate_ref, dup_ref):
+    for place, x_ref in zip(half_places(at_ref, dact_ref.shape[0]), (mine_ref, other_ref), strict=True):
+        gate = matmul_low(x_ref[...], gate_ref[...])
+        up = matmul_low(x_ref[...], up_ref[...])
+        dact = dact_ref[place, :]
+        logistic = jax.nn.sigmoid(gate)
+        silu = gate * logistic
+        act_ref[place, :] = narrow(silu * up)
+        dgate_ref[place, :] = narrow(dact * up * (logistic * (1.0 + gate * (1.0 - logistic))))
+        dup_ref[place, :] = narrow(dact * silu)
+
+
+def expand(at, mine, other, weight, dact):
+    half, depth = mine.shape
+    rows, width = dact.shape
     size = min(256, width)
     steps = width // size
-    return call(
+    tile = pl.BlockSpec((rows, size), lambda j, at: (0, j))
+    return call_at(
         "expand",
         expand_kernel,
+        at,
         (steps,),
         [
-            pl.BlockSpec((rows, depth), lambda j: (0, 0)),
-            pl.BlockSpec((depth, size), lambda j: (0, j)),
-            pl.BlockSpec((depth, size), lambda j: (0, steps + j)),
-            pl.BlockSpec((rows, size), lambda j: (0, j)),
+            pl.BlockSpec((half, depth), lambda j, at: (0, 0)),
+            pl.BlockSpec((half, depth), lambda j, at: (0, 0)),
+            pl.BlockSpec((depth, size), lambda j, at: (0, j)),
+            pl.BlockSpec((depth, size), lambda j, at: (0, steps + j)),
+            tile,
         ],
-        (x, weight, weight, dact),
-        [
-            (like((rows, width), jnp.bfloat16), pl.BlockSpec((rows, size), lambda j: (0, j))),
-            (like((2, rows, width), jnp.bfloat16), pl.BlockSpec((2, rows, size), lambda j: (0, 0, j))),
-        ],
-    )
+        (mine, other, weight, weight, dact),
+        [(like((rows, width), jnp.bfloat16), tile)] * 3,
+    )
+
+
+def gated_back_kernel(
+    at_ref, mine_ref, other_ref, weight_ref, gate_ref, y_ref, dy_ref, dgate_ref
+):
+    for place, x_ref in zip(half_places(at_ref, gate_ref.shape[0]), (mine_ref, other_ref), strict=True):
+        dgated = times_back(x_ref[...], weight_ref[...])
+        gate = gate_ref[place, :]
+        logistic = jax.nn.sigmoid(gate)
+        dy_ref[place, :] = narrow(dgated * (gate * logistic))
+        dgate_ref[place, :] = narrow(
+            dgated * y_ref[place, :] * (logistic * (1.0 + gate * (1.0 - logistic)))
+        )
+
+
+def gated_back(at, mine, other, weight, gate, y):
+    half, depth = mine.shape
+    rows, width = gate.shape
+    size = min(256, width)
+    tile = pl.BlockSpec((rows, size), lambda j, at: (0, j))
+    whole = pl.BlockSpec((half, depth), lambda j, at: (0, 0))
+    return call_at(
+        "gated_back",
+        gated_back_kernel,
+        at,
+        (width // size,),
+        [whole, whole, pl.BlockSpec((size, depth), lambda j, at: (j, 0)), tile, tile],
+        (mine, other, weight, gate, y),
+        [(like((rows, width), jnp.bfloat16), tile)] * 2,
+    )
+
+
+def rows_back_kernel(at_ref, mine_ref, other_ref, weight_ref, out_ref):
+    for place, x_ref in zip(half_places(at_ref, out_ref.shape[0]), (mine_ref, other_ref), strict=True):
+        out_ref[place, :] = narrow(times_back(x_ref[...], weight_ref[...]))
+
+
+def rows_back(at, mine, other, weight):
+    half, depth = mine.shape
+    width = weight.shape[0]
+    size = min(256, width)
+    whole = pl.BlockSpec((half, depth), lambda j, at: (0, 0))
+    return call_at(
+        "attended_back",
+        rows_back_kernel,
+        at,
+        (width // size,),
+        [whole, whole, pl.BlockSpec((size, depth), lambda j, at: (j, 0))],
+        (mine, other, weight),
+        [(like((2 * half, width), jnp.bfloat16), pl.BlockSpec((2 * half, size), lambda j, at: (0, j)))],
+    )[0]
 
 
 def share_kernel(at_ref, *refs, count, back, added):
     total = jnp.zeros(refs[-1].shape, jnp.float32)
     for former, latter in zip(refs[:count], refs[count : 2 * count], strict=True):
-        rows = former[...].reshape(former.shape[-2:])
-        total = total + (times_back(rows, latter[...]) if back else matmul_low(rows, latter[...]))
+        product = times_back if back else matmul_low
+        total = total + product(former[...], latter[...])
     if added:
         total = total + wide(refs[2 * count][...])
     refs[-1][...] = narrow(total)
 
 
 def half_share(name, at, terms, back, added=None):
-    rows = terms[0][0].shape[-2] // 2
-    width = terms[0][2].shape[0 if back else 1]
-    size = min(512, width)
-    specs = []
-    for former, plane, _, _ in terms:
-        if former.ndim == 3:
-            specs.append(
-                pl.BlockSpec((1, rows, former.shape[2]), lambda j, at, plane=plane: (plane, at[0], 0))
-            )
+    rows = terms[0][0].shape[0] // 2
+    width = terms[0][1].shape[0 if back else 1]
+    size = min(1024, width)
+    specs = [pl.BlockSpec((rows, former.shape[1]), lambda j, at: (at[0], 0)) for former, _, _ in terms]
+    for former, latter, columns in terms:
+        if back:
+            specs.append(pl.BlockSpec((size, former.shape[1]), lambda j, at, c=columns: (j, c)))
         else:
-            specs.append(pl.BlockSpec((rows, former.shape[1]), lambda j, at: (at[0], 0)))
-    for former, _, latter, columns in terms:
-        if back:
-            specs.append(pl.BlockSpec((size, former.shape[-1]), lambda j, at, c=columns: (j, c)))
-        else:
-            specs.append(pl.BlockSpec((former.shape[-1], size), lambda j, at: (0, j)))
-    args = [term[0] for term in terms] + [term[2] for term in terms]
+            specs.append(pl.BlockSpec((former.shape[1], size), lambda j, at: (0, j)))
+    args = [term[0] for term in terms] + [term[1] for term in terms]
     tile = pl.BlockSpec((rows, size), lambda j, at: (0, j))
     if added is not None:
         specs.append(tile)
@@ -704,59 +761,105 @@
     )[0]
 
 
-def weight_kernel(at_ref, own_ref, *refs, shifts, count):
+def weight_kernel(at_ref, *refs, ranks, count, added):
     out_ref = refs[-1]
-    half = own_ref.shape[0] // 2
-    pairs = refs[: 2 * shifts]
-    seconds = refs[2 * shifts : -1]
-    own = own_ref[...].T
-    flat = [ref[...].T for ref in pairs]
-    places = [pl.ds(pl.multiple_of(which * half, half), half) for which in (at_ref[0], 1 - at_ref[0])]
+    firsts = [ref[...].T for ref in refs[: 2 * ranks]]
+    seconds = refs[2 * ranks : 2 * ranks + ranks * count]
+    places = half_places(at_ref, seconds[0].shape[0])
     at = 0
     for index in range(count):
-        planes = seconds[index].shape[0] if seconds[index].ndim == 3 else 1
-        for plane in range(planes):
-            width = seconds[index].shape[-1]
-            for start in range(0, width, 512):
-                stop = min(width, start + 512)
-
-                def rows(ref, place):
-                    if planes > 1:
-                        return ref[plane, place, start:stop]
-                    return ref[place, start:stop]
-
-                total = matmul_low(own, rows(seconds[index], slice(None)))
-                for shift in range(shifts):
-                    ref = seconds[count * (shift + 1) + index]
-                    for which in range(2):
-                        total = total + matmul_low(flat[2 * shift + which], rows(ref, places[which]))
-                out_ref[:, at + start : at + stop] = narrow(total)
-            at = at + width
-
-
-def weight_part(name, at, own, others, seconds, arrived):
-    shifts = len(others)
-    tokens = own.shape[0]
-    share = own.shape[1] // (shifts + 1)
-    size = min(256, share)
-    specs = [pl.BlockSpec((tokens, size), lambda m, at: (0, at[1] * (share // size) + m))]
-    args = [own]
-    for pair in others:
-        for part in pair:
-            specs.append(pl.BlockSpec((tokens // 2, size), lambda m, at: (0, m)))
-            args.append(part)
-    width = 0
-    for group in [seconds] + list(arrived):
-        for part in group:
-            specs.append(pl.BlockSpec(part.shape, lambda m, at, nd=part.ndim: (0,) * nd))
-            args.append(part)
-    for part in seconds:
-        width = width + part.shape[-1] * (part.shape[0] if part.ndim == 3 else 1)
-    kernel = partial(weight_kernel, shifts=shifts, count=len(seconds))
-    tile = pl.BlockSpec((size, width), lambda m, at: (m, 0))
-    return call_at(
-        name, kernel, at, (share // size,), specs, args, [(like((share, width), jnp.bfloat16), tile)]
-    )[0]
+        width = seconds[index].shape[1]
+        for start in range(0, width, 512):
+            stop = min(width, start + 512)
+            total = None
+            for rank in range(ranks):
+                ref = seconds[count * rank + index]
+                for which in range(2):
+                    part = matmul_low(firsts[2 * rank + which], ref[places[which], start:stop])
+                    total = part if total is None else total + part
+            if added:
+                total = total + wide(refs[-2][:, at + start : at + stop])
+            out_ref[:, at + start : at + stop] = narrow(total)
+        at = at + width
+
+
+class WeightGrad:
+    def __init__(self, name, own, others, seconds, arrived, core, ctx_rank):
+        self.name = name
+        whole = own[0].shape[1] if isinstance(own, tuple) else own.shape[1]
+        self.ranks = len(others) + 1
+        self.size = whole // self.ranks // 4
+        self.own, self.others = (own, others)
+        self.groups = [list(seconds)] + [list(group) for group in arrived]
+        self.width = sum(part.shape[1] for part in seconds)
+        dp_rank = lax.axis_index("dp")
+        near = ctx_rank ^ 1
+        self.given = jnp.stack([core, dp_rank, near ^ 2, near]).astype(jnp.int32)
+        self.held = jnp.stack([core, dp_rank, ctx_rank ^ 2, ctx_rank]).astype(jnp.int32)
+
+    def part(self, suffix, at, added=None, whole=False):
+        size = self.size
+        half = self.groups[0][0].shape[0] // 2
+        steps = 4 if whole else 2
+        own = list(self.own) if isinstance(self.own, tuple) else [self.own]
+        others = [array for pair in self.others for array in pair]
+        if size % 128 and whole:
+            steps, size = (1, 4 * size)
+            own = [cut(array, at[1], size, 1) for array in own]
+        elif size % 128:
+            steps, size = (1, 2 * size)
+            own = [self.columns(array, 4 * at[1] + at[2], 4 * at[1] + at[3]) for array in own]
+            others = [self.columns(array, at[2], at[3]) for array in others]
+
+        def first_spec(row, from_dp):
+            def place(m, at):
+                if steps == 1:
+                    return (row(at), m)
+                return (row(at), (m if whole else at[2 + m]) + (4 * at[1] if from_dp else 0))
+
+            return pl.BlockSpec((half, size), place)
+
+        if len(own) == 2:
+            specs = 2 * [first_spec(lambda at: 0, True)]
+        else:
+            specs = [first_spec(lambda at: at[0], True), first_spec(lambda at: 1 - at[0], True)]
+            own = 2 * own
+        specs += [first_spec(lambda at: 0, False) for _ in others]
+        args = own + others
+        for group in self.groups:
+            for array in group:
+                specs.append(pl.BlockSpec(array.shape, lambda m, at: (0, 0)))
+                args.append(array)
+        tile = pl.BlockSpec((size, self.width), lambda m, at: (m, 0))
+        if added is not None:
+            specs.append(tile)
+            args.append(added)
+        kernel = partial(
+            weight_kernel, ranks=self.ranks, count=len(self.groups[0]), added=added is not None
+        )
+        out = like((steps * size, self.width), jnp.bfloat16)
+        return call_at(self.name + suffix, kernel, at, (steps,), specs, args, [(out, tile)])[0]
+
+    def columns(self, array, *blocks):
+        return jnp.concatenate([cut(array, block, self.size, 1) for block in blocks], axis=1)
+
+    def whole(self, *awaited):
+        self.made = self.part("_all", after(self.given, *awaited), whole=True)
+        self.total = lax.psum_scatter(self.made, "ctx", scatter_dimension=0, tiled=True)
+        return self.made
+
+    def start(self, *awaited):
+        self.sent = self.part("_given", after(self.given, *awaited))
+        self.near = ctx_partner(self.sent, 1)
+        return self.sent
+
+    def turn(self, *awaited):
+        self.kept = self.part("_held", after(self.held, *awaited), self.near)
+        self.far = ctx_partner(self.kept[: self.size], 2)
+        return self.kept
+
+    def end(self):
+        return wide(self.kept[self.size :]) + wide(self.far)
 
 
 def body(
@@ -794,15 +897,15 @@
     bc_share = 2 * state_width // 4
     heads_query = attn_q.shape[1] // AHEAD_DIM
     ff_local = mlp_down.shape[0]
-    here = jnp.stack([core, lax.axis_index("dp")]).astype(jnp.int32)
-    there = jnp.stack([1 - core, lax.axis_index("dp")]).astype(jnp.int32)
+    here = core.astype(jnp.int32)[None]
+    there = 1 - here
     gain_one = norm1_gain[None]
     gain_two = norm2_gain[None]
 
     input_one = normed(hidden_rows, gain_one)
-    u_matrix = ssm_in[:, 1]
+    in_matrix = ssm_in.reshape(model_width, 2 * inner_local)
     bc_matrix = ssm_bc.reshape(model_width, 2 * state_width)
-    source_rows = matmul_low(input_one, u_matrix).astype(jnp.bfloat16)
+    source_rows = project("project_u", input_one, in_matrix, inner_local, inner_local, jnp.bfloat16)
     bc_rows = matmul_low(input_one, bc_matrix).astype(jnp.bfloat16)
     write_rows = bc_rows[:, :state_width]
     read_rows = bc_rows[:, state_width:]
@@ -829,16 +932,15 @@
     kv_got = [kv_sent] + [moved(kv_sent, "ctx", shift) for shift in range(1, ctx_count)]
     cot_sent = send_columns(cut(after(grad_low, own_state), core, half, 0))
     one_sent = send_columns(cut(one_late, core, half, 0))
-    z_matrix = after(ssm_in, own_state)[:, 0]
     queries = matmul_low(one_late, attn_q).astype(jnp.bfloat16)
-    gate_ssm = matmul_low(one_late, z_matrix)
+    gate_ssm = project("project_z", one_late, in_matrix, 0, inner_local, jnp.float32)
     attend = Attend(tokens, ctx_count * tokens, heads_query)
     rank = ctx_rank.astype(jnp.int32)[None]
     kept = {}
 
     def fill_within(sent):
         kept["within"] = scan.within(source_rows, after(small_rows, own_state), write_rows, read_rows)
-        return (kept["within"], gate_ssm, queries)
+        return (kept["within"], gate_ssm, queries, cot_sent)
 
     def fill_attend(sent):
         mine = jnp.concatenate(kv_got, axis=0)
@@ -849,7 +951,7 @@
             after(rank, sent), queries, kept["key"], kept["value"]
         )
         kept["attended_sent"] = send_rows(kept["attended"])
-        return (kept["attended"],)
+        return (kept["attended"], one_sent)
 
     def fill_act(sent):
         kept["act"] = times_back(after(grad_low, sent), mlp_down)
@@ -862,122 +964,15 @@
         [gated, att] for gated, att in zip(send_rows(gated_rows), kept["attended_sent"], strict=True)
     ]
 
-    terms = [(gated_rows, 0, ssm_out, 0), (attended, 0, attn_out, 0)]
+    terms = [(gated_rows, ssm_out, 0), (attended, attn_out, 0)]
     given = partner(half_share("mix_other", there, terms, False), CORE)
     mix_mine = half_share("mix_own", here, terms, False, given)
     mix_theirs = partner(mix_mine, CHIP)
     gu_matrix = after(mlp_gate_up, mix_mine).reshape(model_width, 2 * ff_local)
     cot_columns = both_halves([after(part, mix_mine) for part in cot_sent])
     one_columns = both_halves([after(part, mix_mine) for part in one_sent])
-    mix_theirs = after(mix_theirs, gu_matrix)
-    middle, two_mine, mix_squares = middle_norm(here, hidden_rows, mix_mine, mix_theirs, gain_two)
-
-    input_two = gather_rows(two_mine, core)
-    activated, grad_gu = expand(input_two, gu_matrix, kept["act"])
-    act_sent = send_rows(activated)
-    two_sent = send_columns(two_mine)
-    gu_sent = send_rows(grad_gu)
-    terms = [(grad_gu, 0, gu_matrix, 0), (grad_gu, 1, gu_matrix, 1)]
-    given = partner(half_share("two_other", there, terms, True), CORE)
-    two_back = half_share("two_own", here, terms, True, given)
-    two_theirs = partner(two_back, CHIP)
-    terms = [(after(activated, two_back), 0, mlp_down, 0)]
-    given = partner(half_share("mlp_other", there, terms, False), CORE)
-    mlp_mine = half_share("mlp_own", here, terms, False, given)
-    down_part = weight_part(
-        "grad_down", after(here, mlp_mine), grad_low, cot_columns, [activated], [[part] for part in act_sent]
-    )
-    grad_down = ctx_sum(down_part)
-    two_theirs = after(two_theirs, down_part)
-    grad_middle, mix_grad_mine, gain_two_sum = norm_grad(
-        "norm_two_back", here, middle, grad_low, two_back, two_theirs, gain_two, (jnp.float32, jnp.bfloat16)
-    )
-
-    grad_mix = gather_rows(mix_grad_mine, core)
-    mix_sent = send_columns(mix_grad_mine)
-    grad_gated = times_back(grad_mix, ssm_out)
-    grad_values = (grad_gated * jax.nn.silu(gate_ssm)).astype(jnp.bfloat16)
-    own_grad = scan.own_state(grad_values, small_rows, read_rows, False)
-    mlp_theirs = partner(after(mlp_mine, own_grad), CHIP)
-    grad_gate_ssm = (grad_gated * ssm_values * silu_slope(gate_ssm)).astype(jnp.bfloat16)
-    grad_attended = times_back(after(grad_mix, own_grad), attn_out).astype(jnp.bfloat16)
-    gate_sent = send_rows(grad_gate_ssm)
-
-    def fill_attend_back(sent):
-        grad_query, grad_key, grad_value = attend.back(
-            after(rank, own_grad), queries, grad_attended, kept["log"], key_rows, value_rows
-        )
-        kept["grad_query"] = grad_query
-        kept["query_sent"] = send_rows(grad_query)
-        own_part = jnp.where(core == 0, grad_key, grad_value)
-        given = partner(jnp.where(core == 0, grad_value, grad_key).astype(jnp.bfloat16), CORE)
-        paired = (own_part + given.astype(jnp.float32)).reshape(ctx_count, tokens, AHEAD_DIM)
-        kept["kv"] = paired[0]
-        kept["kv_sent"] = [
-            moved(paired[shift].astype(jnp.bfloat16), "ctx", -shift) for shift in range(1, ctx_count)
-        ]
-        return (grad_query,)
-
-    def fill_scan_back(sent):
-        kept["scan"] = scan.within_back(
-            source_rows, after(grad_values, sent), small_rows, write_rows, read_rows
-        )
-        return (kept["scan"][0],)
-
-    def fill_weights(sent):
-        kept["gate_up"] = weight_part(
-            "grad_gate_up",
-            after(here, sent),
-            input_two,
-            both_halves(two_sent),
-            [grad_gu],
-            [[part] for part in gu_sent],
-        )
-        kept["outs"] = weight_part(
-            "grad_outs", after(here, sent), grad_mix, both_halves(mix_sent), [gated_rows, attended], outs_sent
-        )
-        return (kept["gate_up"], kept["outs"])
-
-    leaving = chained(own_grad, running[:, -1], False, [fill_attend_back, fill_scan_back, fill_weights])
-    grad_gate_up = ctx_sum(kept["gate_up"])
-    grad_outs = ctx_sum(kept["outs"])
-    grad_written, scan_sums, grad_b, grad_c = kept["scan"]
-    grad_source, steps, grad_b, grad_c = scan.carried_back(
-        source_rows, grad_values, small_rows, scan_sums, grad_written,
-        write_rows, read_rows, entering, leaving, grad_b, grad_c,
-    )
-    source_sent = send_rows(grad_source)
-    grad_bc = jnp.concatenate([grad_b, grad_c], axis=1)
-    bc_sent = partner(cut(grad_bc, 1 - core, 2 * bc_share, 1).astype(jnp.bfloat16), CORE)
-    bc_mine = cut(grad_bc, core, 2 * bc_share, 1) + bc_sent.astype(jnp.float32)
-    bc_given = partner(cut(bc_mine, 1 - chip, bc_share, 1).astype(jnp.bfloat16), CHIP)
-    grad_bc_low = (cut(bc_mine, chip, bc_share, 1) + bc_given.astype(jnp.float32)).astype(jnp.bfloat16)
-    kv_sum = kept["kv"]
-    for part in kept["kv_sent"]:
-        kv_sum = kv_sum + part.astype(jnp.float32)
-    grad_kv_low = kv_sum.astype(jnp.bfloat16)
-    grad_query = kept["grad_query"]
-    kv_columns = cut(attn_kv, chip, AHEAD_DIM, 2)
-    kv_columns = lax.dynamic_index_in_dim(kv_columns, core, 1, keepdims=False)
-    ins_first = weight_part(
-        "grad_ins_first",
-        here,
-        input_one,
-        one_columns,
-        [grad_gate_ssm, grad_query],
-        [[gate, query] for gate, query in zip(gate_sent, kept["query_sent"], strict=True)],
-    )
-    grad_ins_first = ctx_sum(ins_first)
-
-    grad_dt_pre = steps[:, 0:2].reshape(heads_local, tokens) * jax.nn.sigmoid(dt_pre)
-    flow_rows = steps[:, 2:4].reshape(heads_local, tokens)
-    grad_dt_bias = jnp.sum(grad_dt_pre, axis=1)
-    grad_a_log = decay_rate * jnp.sum(dt_rows * flow_rows, axis=1)
-    grad_d_skip = jnp.sum(scan_sums[:, 4, : 2 * head_width].reshape(heads_local, head_width), axis=1)
+    kv_columns = lax.dynamic_index_in_dim(after(kv_pair, mix_mine), core, 1, keepdims=False)
     pad = -heads_local % AHEAD_DIM
-    grad_dt_low = jnp.pad(grad_dt_pre.astype(jnp.bfloat16).T, ((0, 0), (0, pad)))
-    grad_small = jnp.concatenate([grad_kv_low, grad_bc_low, grad_dt_low], axis=1)
-    small_sent = send_rows(grad_small)
     weight_small = jnp.concatenate(
         [
             kv_columns,
@@ -986,82 +981,195 @@
         ],
         axis=1,
     )
+    mix_theirs = after(mix_theirs, gu_matrix, cot_columns, one_columns, weight_small, outs_sent)
+    middle, two_mine, mix_squares = middle_norm(here, hidden_rows, mix_mine, mix_theirs, gain_two)
+
+    two_other = partner(two_mine, CORE)
+    activated, grad_gate, grad_up = expand(here, two_mine, two_other, gu_matrix, kept["act"])
+    act_sent = send_rows(activated)
+    two_sent = send_columns(two_mine)
+    gate_sent = send_rows(grad_gate)
+    up_sent = send_rows(grad_up)
+    terms = [(grad_gate, gu_matrix, 0), (grad_up, gu_matrix, 1)]
+    given = partner(half_share("two_other", there, terms, True), CORE)
+    two_back = half_share("two_own", here, terms, True, given)
+    two_theirs = partner(two_back, CHIP)
+    down = WeightGrad(
+        "grad_down", grad_low, cot_columns, [activated], [[part] for part in act_sent], core, ctx_rank
+    )
+    two_theirs = after(two_theirs, act_sent, two_sent)
+    grad_middle, mix_grad_mine, gain_two_sum = norm_grad(
+        "norm_two_back", here, middle, grad_low, two_back, two_theirs, gain_two, (jnp.float32, jnp.bfloat16)
+    )
+
+    mix_grad_other = partner(mix_grad_mine, CORE)
+    mix_sent = send_columns(mix_grad_mine)
+    down.whole(mix_grad_mine)
+    grad_values, grad_gate_ssm = gated_back(
+        after(here, down.made), mix_grad_mine, mix_grad_other, ssm_out, gate_ssm, ssm_values
+    )
+    own_grad = scan.own_state(grad_values, small_rows, read_rows, False)
+    z_sent = send_rows(grad_gate_ssm)
+    two_pair = (two_mine, two_other)
+    two_columns = both_halves([after(part, mix_grad_mine) for part in two_sent])
+    gate = WeightGrad(
+        "grad_gate", two_pair, two_columns, [grad_gate], [[part] for part in gate_sent], core, ctx_rank
+    )
+    up = WeightGrad(
+        "grad_up", two_pair, two_columns, [grad_up], [[part] for part in up_sent], core, ctx_rank
+    )
+    outs = WeightGrad(
+        "grad_outs",
+        (mix_grad_mine, mix_grad_other),
+        both_halves(mix_sent),
+        [gated_rows, attended],
+        outs_sent,
+        core,
+        ctx_rank,
+    )
+
+    def fill_attend_back(sent):
+        grad_attended = rows_back(after(here, sent), mix_grad_mine, mix_grad_other, attn_out)
+        kept["grads"] = attend.back(rank, queries, grad_attended, kept["log"], key_rows, value_rows)
+        kept["query_sent"] = send_rows(kept["grads"][0])
+        return (kept["grads"][0], gate_sent, two_columns)
+
+    def fill_scan_back(sent):
+        gate.whole(sent)
+        kept["scan"] = scan.within_back(
+            source_rows, after(grad_values, gate.made), small_rows, write_rows, read_rows
+        )
+        return (kept["scan"][0], up_sent)
+
+    def fill_weights(sent):
+        up.whole(sent)
+        return (up.made,)
+
+    leaving = chained(own_grad, running[:, -1], False, [fill_attend_back, fill_scan_back, fill_weights])
+    leaving = after(leaving, down.total)
+    grad_query, grad_key, grad_value = kept["grads"]
+    own_part = jnp.where(core == 0, grad_key, grad_value)
+    given = partner(after(jnp.where(core == 0, grad_value, grad_key).astype(jnp.bfloat16), leaving), CORE)
+    grad_written, scan_sums, grad_b, grad_c = kept["scan"]
+    grad_source, steps, grad_b, grad_c = scan.carried_back(
+        source_rows, grad_values, small_rows, scan_sums, grad_written,
+        write_rows, read_rows, entering, leaving, grad_b, grad_c,
+    )
+    source_sent = send_rows(grad_source)
+    paired = (own_part + given.astype(jnp.float32)).reshape(ctx_count, tokens, AHEAD_DIM)
+    kv_sent_back = [
+        moved(paired[shift].astype(jnp.bfloat16), "ctx", -shift) for shift in range(1, ctx_count)
+    ]
+    grad_bc = jnp.concatenate([grad_b, grad_c], axis=1)
+    bc_sent = partner(cut(grad_bc, 1 - core, 2 * bc_share, 1).astype(jnp.bfloat16), CORE)
+    bc_mine = cut(grad_bc, core, 2 * bc_share, 1) + bc_sent.astype(jnp.float32)
+    bc_given = partner(cut(bc_mine, 1 - chip, bc_share, 1).astype(jnp.bfloat16), CHIP)
+    grad_bc_low = (cut(bc_mine, chip, bc_share, 1) + bc_given.astype(jnp.float32)).astype(jnp.bfloat16)
+    kv_sum = paired[0]
+    for part in kv_sent_back:
+        kv_sum = kv_sum + part.astype(jnp.float32)
+    grad_kv_low = kv_sum.astype(jnp.bfloat16)
+    first = WeightGrad(
+        "grad_first",
+        input_one,
+        one_columns,
+        [grad_gate_ssm, grad_query],
+        [[gate, query] for gate, query in zip(z_sent, kept["query_sent"], strict=True)],
+        core,
+        ctx_rank,
+    )
+    outs.whole(grad_source)
+    first.whole(outs.made)
+
+    grad_dt_pre = steps[:, 0:2].reshape(heads_local, tokens) * jax.nn.sigmoid(dt_pre)
+    flow_rows = steps[:, 2:4].reshape(heads_local, tokens)
+    grad_dt_bias = jnp.sum(grad_dt_pre, axis=1)
+    grad_a_log = decay_rate * jnp.sum(dt_rows * flow_rows, axis=1)
+    grad_d_skip = jnp.sum(scan_sums[:, 4, : 2 * head_width].reshape(heads_local, head_width), axis=1)
+    grad_dt_low = jnp.pad(grad_dt_pre.astype(jnp.bfloat16).T, ((0, 0), (0, pad)))
+    grad_small = jnp.concatenate([grad_kv_low, grad_bc_low, grad_dt_low], axis=1)
+    small_sent = send_rows(grad_small)
     terms = [
-        (grad_gate_ssm, 0, z_matrix, 0),
-        (grad_source, 0, u_matrix, 0),
-        (grad_query, 0, attn_q, 0),
-        (grad_small, 0, weight_small, 0),
+        (grad_gate_ssm, in_matrix, 0),
+        (grad_source, in_matrix, 1),
+        (grad_query, attn_q, 0),
+        (grad_small, weight_small, 0),
     ]
-    given = partner(half_share("one_other", there, terms, True), CORE)
-    one_back = half_share("one_own", here, terms, True, given)
+    given = partner(half_share("one_other", after(there, first.made), terms, True), CORE)
+    one_back = half_share("one_own", after(here, source_sent), terms, True, given)
     one_theirs = partner(one_back, CHIP)
-    ins_small = weight_part(
-        "grad_ins_small", after(here, one_back), input_one, one_columns, [grad_small], [[p] for p in small_sent]
-    )
-    grad_ins_small = ctx_sum(ins_small)
-    ins_source = weight_part(
-        "grad_ins_source", after(here, ins_small), input_one, one_columns, [grad_source], [[p] for p in source_sent]
-    )
-    grad_ins_source = ctx_sum(ins_source)
-    one_theirs = after(one_theirs, ins_source)
+    source = WeightGrad(
+        "grad_source", input_one, one_columns, [grad_source], [[part] for part in source_sent], core, ctx_rank
+    )
+    little = WeightGrad(
+        "grad_little", input_one, one_columns, [grad_small], [[part] for part in small_sent], core, ctx_rank
+    )
+    little.start(one_back)
+    source.start(little.sent)
+    terms = [(activated, mlp_down, 0)]
+    given = partner(half_share("mlp_other", after(there, source.sent), terms, False), CORE)
+    mlp_mine = half_share("mlp_own", here, terms, False, given)
+    mlp_theirs = partner(mlp_mine, CHIP)
+    one_theirs = after(one_theirs, mlp_mine, gate.total)
     hidden_mine, gain_one_sum = norm_grad(
         "norm_one_back", here, hidden_rows, grad_middle, one_back, one_theirs, gain_one, (jnp.bfloat16,)
     )
     grad_hidden = gather_rows(hidden_mine, core)
-
-    mlp_total = mlp_mine.astype(jnp.float32) + mlp_theirs.astype(jnp.float32)
+    little.turn(hidden_mine)
+    source.turn(little.kept)
+    mlp_total = mlp_mine.astype(jnp.float32) + after(mlp_theirs, source.kept).astype(jnp.float32)
     block_out = middle + mlp_total
     output = gather_rows(block_out.astype(jnp.bfloat16), core)
 
-    kv_part = grad_ins_small[:, :AHEAD_DIM]
-    bc_part = grad_ins_small[:, AHEAD_DIM : AHEAD_DIM + bc_share]
-    grad_ssm_dt = grad_ins_small[:, AHEAD_DIM + bc_share : AHEAD_DIM + bc_share + heads_local]
-    share = kv_part.shape[0] // 4
-    blocks = [cut(kv_part, tensor_rank, share, 0)]
-    for stride in range(1, 4):
-        blocks.append(partner(cut(kv_part, tensor_rank ^ stride, share, 0), stride))
-    blocks = jnp.stack(blocks)
-    bc_blocks = jnp.stack([bc_part] + [partner(bc_part, stride) for stride in range(1, 4)])
-
-    def of_rank(pieces, rank):
-        return lax.dynamic_index_in_dim(pieces, tensor_rank ^ rank, 0, keepdims=False)
-
+    grad_little = little.end()
+    held = narrow(grad_little[:, : AHEAD_DIM + bc_share])
+    pieces = jnp.stack([held] + [partner(held, stride) for stride in range(1, 4)])
+
+    def of_rank(rank):
+        return lax.dynamic_index_in_dim(pieces, tensor_rank ^ rank, 0, keepdims=False).astype(jnp.float32)
+
+    by_rank = [of_rank(rank) for rank in range(4)]
+    kv_rows = held.shape[0] // 4
+    kv_parts = [cut(part[:, :AHEAD_DIM], tensor_rank, kv_rows, 0) for part in by_rank]
     grad_attn_kv = jnp.stack(
-        [
-            jnp.concatenate([of_rank(blocks, kind), of_rank(blocks, 2 + kind)], axis=1)
-            for kind in range(2)
-        ],
-        axis=1,
+        [jnp.concatenate([kv_parts[kind], kv_parts[2 + kind]], axis=1) for kind in range(2)], axis=1
     )
     grad_ssm_bc = jnp.concatenate(
-        [of_rank(bc_blocks, 2 * (place % 2) + place // 2) for place in range(4)], axis=1
+        [by_rank[2 * (place % 2) + place // 2][:, AHEAD_DIM:] for place in range(4)], axis=1
     ).reshape(-1, 2, state_width)
-
-    gains = jnp.concatenate([gain_one_sum, gain_two_sum], axis=0).T
-    gains = gains + partner(gains, CORE)
-    gains = scatter_sum(scatter_sum(gains, "dp"), "ctx")
+    grad_ssm_dt = grad_little[:, AHEAD_DIM + bc_share : AHEAD_DIM + bc_share + heads_local]
+
     squares = jnp.stack([jnp.sum(mix_squares), jnp.sum(mlp_total * mlp_total), jnp.sum(block_out * block_out)])
-    squares = squares + partner(squares, CORE)
-    small = jnp.concatenate([grad_dt_bias, grad_a_log, grad_d_skip, squares])
-    small = all_sum(all_sum(small, "dp"), "ctx")
+    halves = jnp.concatenate([gain_one_sum[0], gain_two_sum[0], squares])
+    halves = halves + partner(halves, CORE)
+    sums = jnp.concatenate([halves, grad_dt_bias, grad_a_log, grad_d_skip])
+    sums = jnp.pad(sums, (0, -sums.shape[0] % 1024)).reshape(-1, 128)
+    sums = all_sum(all_sum(sums, "dp"), "ctx").reshape(-1)
+    place = lax.axis_index("dp") * ctx_count + ctx_rank
+    share = model_width // (lax.axis_size("dp") * ctx_count)
+    small = sums[2 * model_width :]
     counted = tokens * model_width * lax.axis_size("dp") * ctx_count
-    branch_rms = jnp.sqrt(small[3 * heads_local :] / counted)
+    grad_down = wide(down.total)
+    grad_gate_up = jnp.stack([wide(gate.total), wide(after(up.total, grad_down))], axis=1)
+    grad_outs = wide(after(outs.total, grad_gate_up))
+    grad_first = wide(after(first.total, grad_outs))
+    branch_rms = jnp.sqrt(small[:3] / counted)
     return (
         output[None],
         grad_hidden[None],
-        gains[:, 0],
-        jnp.stack([grad_ins_first[:, :inner_local], grad_ins_source], axis=1),
+        cut(sums[:model_width], place, share, 0),
+        jnp.stack([grad_first[:, :inner_local], source.end()], axis=1),
         grad_ssm_bc,
         grad_ssm_dt,
-        small[:heads_local],
-        small[heads_local : 2 * heads_local],
-        small[2 * heads_local : 3 * heads_local],
+        small[3 : 3 + heads_local],
+        small[3 + heads_local : 3 + 2 * heads_local],
+        small[3 + 2 * heads_local : 3 + 3 * heads_local],
         grad_outs[:, :inner_local].T,
-        grad_ins_first[:, inner_local:],
+        grad_first[:, inner_local:],
         grad_attn_kv,
         grad_outs[:, inner_local:].T,
-        gains[:, 1],
-        grad_gate_up.reshape(-1, 2, ff_local),
+        cut(sums[model_width : 2 * model_width], place, share, 0),
+        grad_gate_up,
         grad_down.T,
         branch_rms,
     )

time: 614 us -> 565 us (0.920)
  waiting for transfers between devices: 205 us -> 166 us
  local copies, waits for them, and re-layouts: 101 us -> 134 us
  starting transfers between devices: 70.6 us -> 55.1 us
  Pallas kernels: 146 us -> 134 us
  matrix products: 18.3 us -> 9.17 us
  other arithmetic: 47.5 us -> 41.2 us
    reduce_scatter x6 -> x5, waiting for transfers between devices: 64.3 us -> 0.03 us  [whole(): lax.psum_scatter(self.made, 'ctx', scatter_dimension=0, tiled=True)]
    unnamed x188 -> x300, local copies, waits for them, and re-layouts: 57.2 us -> 104 us
    ppermute x28 -> x24, waiting for transfers between devices: 55.9 us -> 26.8 us  [partner(): lax.ppermute(value, 'tensor', [(rank, rank ^ stride) for rank in range(4)])]
    ppermute x0 -> x4, waiting for transfers between devices: none -> 28.1 us  [ctx_partner(): lax.ppermute(value, 'ctx', [(rank, rank ^ stride) for rank in range(4)])]
    ppermute x6, waiting for transfers between devices: 0.02 us -> 21.3 us  [moved(): return lax.ppermute(value, axis, pairs)]
    ppermute x6, waiting for transfers between devices: 0.02 us -> 15.5 us  [chained(): arrived = lax.ppermute(sent, 'ctx', [pair])]
    ppermute x20 -> x17, starting transfers between devices: 34.2 us -> 21.3 us  [shifted(): lax.ppermute(value, axis, [(i, (i + shift) % count) for i in range(count)])]
    ppermute x20 -> x17, waiting for transfers between devices: 84.2 us -> 74.3 us  [shifted(): lax.ppermute(value, axis, [(i, (i + shift) % count) for i in range(count)])]
  transfers between devices with their start and end apart: 66 -> 62, of which waited for: 25 -> 21; matrix products, arithmetic and copies ran while one was open for 18% -> 16% of each run, Pallas kernels for 17% -> 17%
where the time goes in v4:
time: 565 us; the launch traced here: 556 us
  waiting for transfers between devices  166 us (29%)
  local copies, waits for them, and re-layouts  134 us (24%)
  Pallas kernels  134 us (24%)
  starting transfers between devices  55.1 us (10%)
  other arithmetic  41.2 us (7%)
  between operations  16.2 us (3%)
  matrix products  9.17 us (2%)
    unnamed x300, local copies, waits for them, and re-layouts  104 us
    pallas_call x23, Pallas kernels, call_at(): pl.pallas_call(kernel, name=name, grid_spec=pltpu.PrefetchScalarGridSpec(...  87.1 us
    ppermute x17, waiting for transfers between devices, shifted(): lax.ppermute(value, axis, [(i, (i + shift) % count) for i in range(count)])  74.3 us
    pallas_call x11, Pallas kernels, call(): pl.pallas_call(kernel, name=name, grid=grid, in_specs=specs, out_specs=[s...  46.6 us
    ppermute x4, waiting for transfers between devices, ctx_partner(): lax.ppermute(value, 'ctx', [(rank, rank ^ stride) for rank in range(4)])  28.1 us
    ppermute x24, waiting for transfers between devices, partner(): lax.ppermute(value, 'tensor', [(rank, rank ^ stride) for rank in range(4)])  26.8 us
    ppermute x6, waiting for transfers between devices, moved(): return lax.ppermute(value, axis, pairs)  21.3 us
    ppermute x17, starting transfers between devices, shifted(): lax.ppermute(value, axis, [(i, (i + shift) % count) for i in range(count)])  21.3 us
  transfers between devices with their start and end apart: 62, of which 21 were waited for; matrix products, arithmetic and copies ran while one was open for 16% of the time, Pallas kernels for 17%

profile of v4, /device:TPU:0, one launch (start us, length us, event | category | flops | bytes accessed | tf_op | source)
XLA Modules:
  0.0 555.9 jit_solution(7051587473809258549)
XLA Ops:
  10.3 3.7 copy.103
  20.2 4.1 copy.104
  24.3 2.5 project_u.1.u_ref
  30.1 3.3 own_state.2
  35.5 5.6 %collective-permute-start.3 = (bf16[512,128]{1,0:T(8,128)(2,1)}, bf16[512,128]{1,0:T(8,128)(2,1)}, u32[]{:S(2)}, u32[]{:S(2)}) collective-permute-start(bf16[512,128]{1,0:T(8,128)(2,1)} %dynamic-slice_convert_fusion.1), channel_id=1, source_target_pairs={{0,4},{4,8},{8,12},{1,5},{5,9},{9,13},{2,6},{6,10},{10,14},{3,7},{... | collective-permute-start | bytes 393224 | tf_op jit(solution)/shard_map/ppermute | solution.py:34
  41.1 4.5 collective-permute-start.4
  47.5 2.2 collective-permute-start
  53.5 2.8 copy-done.5
  56.3 2.5 project_z.1.z_ref.gate_ref
  59.9 3.2 scan.1.y_ref
  73.2 6.7 %attend.1 = (bf16[512,256]{1,0:T(8,128)(2,1)S(1)}, f32[2,8,512]{2,1,0:T(8,128)S(1)}) custom-call(s32[1]{0:T(128)} %bitcast.7.rank_ref, bf16[512,256]{1,0:T(8,128)(2,1)S(1)} %convolution_convert_fusion.1.q_ref, bf16[2048,128]{1,0:T(8,128)(2,1)S(1)} %get-tuple-element.233.k_ref, bf16[2048,128]{1,0:T(8,128)(2,1)S(1)} %get-tuple-element.232.v_ref), custom_call_target="tpu_custom_call" | custom-call | flops 1 | bytes 1 | tf_op jit(solution)/shard_map/attend/pallas_call | solution.py:383
  82.1 3.7 fusion.30.dact_ref
  90.4 3.0 mix_other.1
  94.0 2.3 collective-permute-done.9.refs_4_
  96.3 3.4 mix_own.1.mine_ref
  107.6 10.4 %copy.107 = bf16[256,8,2,1024]{3,1,2,0:T(8,128)(2,1)} copy(bf16[256,8,2,1024]{3,2,1,0:T(2,128)(2,1)} %bitcast.121) | data formatting | bytes 16777216
  120.9 2.9 fusion.2.refs_7_
  123.8 2.9 collective-permute-done.14.refs_7_
  126.8 2.4 norm_two.1
  131.1 2.7 collective-permute-done.15.other_ref.refs_1_
  133.8 3.5 copy-done.2
  137.3 7.9 %expand.1 = (bf16[512,1024]{1,0:T(8,128)(2,1)}, bf16[512,1024]{1,0:T(8,128)(2,1)S(1)}, bf16[512,1024]{1,0:T(8,128)(2,1)S(1)}) custom-call(s32[1]{0:T(128)} %bitcast.at_ref, bf16[256,2048]{1,0:T(8,128)(2,1)S(1)} %get-tuple-element.101.mine_ref.refs_0_, bf16[256,2048]{1,0:T(8,128)(2,1)S(1)} %collective-permute-done.15.other_ref.refs_1_, ...), custom_call_target="tpu_custom_call" | custom-call | flops 1 | bytes 1 | tf_op jit(solution)/shard_map/expand/pallas_call | solution.py:518
  145.2 3.2 two_other.1
  151.1 4.0 two_own.1.mine_ref
  158.1 27.4 %collective-permute-done.19.refs_2_ = bf16[256,1024]{1,0:T(8,128)(2,1)} collective-permute-done((bf16[256,1024]{1,0:T(8,128)(2,1)}, bf16[256,1024]{1,0:T(8,128)(2,1)}, u32[]{:S(2)}, u32[]{:S(2)}) %collective-permute-start.19) | collective-permute-done | bytes 524320 | tf_op jit(solution)/shard_map/ppermute | solution.py:28
  188.8 3.3 norm_two_back.1
  195.0 5.7 %grad_down_all.1 = bf16[1024,1024]{1,0:T(8,128)(2,1)S(1)} custom-call(s32[4]{0:T(128)S(1)} %pad_add_fusion.at_ref, bf16[512,2048]{1,0:T(8,128)(2,1)S(1)} %bitcast.110, bf16[512,2048]{1,0:T(8,128)(2,1)S(1)} %bitcast.111, bf16[256,1024]{1,0:T(8,128)(2,1)} %collective-permute-done.1.refs_2_, bf16[256,1024]{1,0:T(8,128)(2,1)} %collective-permute-done.11.refs_3_, ...), custom_call_target="tpu_custom_call" | custom-call | flops 1 | bytes 1 | tf_op jit(solution)/shard_map/grad_down_all/pallas_call | solution.py:518
  205.0 2.3 copy-done.8
  211.4 2.9 gated_back.1
  214.3 2.3 own_state.3
  219.3 8.8 %attend_back.1 = (bf16[512,256]{1,0:T(8,128)(2,1)S(1)}, f32[2048,128]{1,0:T(8,128)S(1)}, f32[2048,128]{1,0:T(8,128)S(1)}) custom-call(s32[1]{0:T(128)} %bitcast.7.rank_ref, bf16[512,256]{1,0:T(8,128)(2,1)S(1)} %copy-done.104, bf16[512,256]{1,0:T(8,128)(2,1)S(1)} %attended_back.1.do_ref, f32[2,8,512]{2,1,0:T(8,128)S(1)} %get-tuple-element.112.log_ref, ...), custom_call_target="tpu_custom_call" | custom-call | flops 1 | bytes 1 | tf_op jit(solution)/shard_map/attend_back/pallas_call | solution.py:383
  231.8 4.8 grad_gate_all.1
  243.4 9.5 %scan_back.1 = (f32[512,768]{1,0:T(8,128)S(1)}, f32[6,8,512]{2,1,0:T(8,128)S(1)}, f32[512,256]{1,0:T(8,128)S(1)}, f32[512,256]{1,0:T(8,128)S(1)}) custom-call(bf16[512,768]{1,0:T(8,128)(2,1)S(1)} %project_u.1.u_ref, bf16[512,768]{1,0:T(8,128)(2,1)S(1)} %copy-done.60, f32[6,8,512]{2,1,0:T(8,128)S(1)} %reshape.157.small_ref, bf16[512,256]{1,0:T(8,128)(2,1)S(1)} %copy-done.64, ...), custom_call_target="tpu_custom_call" | custom-call | flops 1 | bytes 1 | tf_op jit(solution)/shard_map/scan_back/pallas_call | solution.py:383
  256.4 7.2 %collective-permute-done.25.refs_5_ = bf16[512,1024]{1,0:T(8,128)(2,1)S(1)} collective-permute-done((bf16[512,1024]{1,0:T(8,128)(2,1)}, bf16[512,1024]{1,0:T(8,128)(2,1)S(1)}, u32[]{:S(2)}, u32[]{:S(2)}) %collective-permute-start.25) | collective-permute-done | bytes 1048608 | tf_op jit(solution)/shard_map/ppermute | solution.py:28
  267.4 4.8 grad_up_all.1
  277.6 13.1 %collective-permute-done.34.refs_2_ = bf16[256,1024]{1,0:T(8,128)(2,1)} collective-permute-done((bf16[256,1024]{1,0:T(8,128)(2,1)}, bf16[256,1024]{1,0:T(8,128)(2,1)}, u32[]{:S(2)}, u32[]{:S(2)}) %collective-permute-start.34) | collective-permute-done | bytes 524320 | tf_op jit(solution)/shard_map/ppermute | solution.py:28
  295.8 15.5 %collective-permute-done.26 = bf16[768,256]{1,0:T(8,128)(2,1)S(1)} collective-permute-done((bf16[768,256]{1,0:T(8,128)(2,1)}, bf16[768,256]{1,0:T(8,128)(2,1)S(1)}, u32[]{:S(2)}, u32[]{:S(2)}) %collective-permute-start.26) | collective-permute-done | bytes 393248 | tf_op jit(solution)/shard_map/ppermute | solution.py:93
  321.6 4.9 carry_back.1
  329.7 5.6 %grad_outs_all.1 = bf16[1024,1024]{1,0:T(8,128)(2,1)S(1)} custom-call(s32[4]{0:T(128)S(1)} %copy-done.119, bf16[256,2048]{1,0:T(8,128)(2,1)S(1)} %copy-done.24, bf16[256,2048]{1,0:T(8,128)(2,1)S(1)} %copy-done.39, bf16[256,1024]{1,0:T(8,128)(2,1)} %collective-permute-done.34.refs_2_, bf16[256,1024]{1,0:T(8,128)(2,1)} %collective-permute-done.35.refs_3_, ...), custom_call_target="tpu_custom_call" | custom-call | flops 1 | bytes 1 | tf_op jit(solution)/shard_map/grad_outs_all/pallas_call | solution.py:518
  337.7 5.3 grad_first_all.1
  359.6 9.5 %collective-permute-done.29 = bf16[512,128]{1,0:T(8,128)(2,1)S(1)} collective-permute-done((bf16[512,128]{1,0:T(8,128)(2,1)S(1)}, bf16[512,128]{1,0:T(8,128)(2,1)S(1)}, u32[]{:S(2)}, u32[]{:S(2)}) %collective-permute-start.29) | collective-permute-done | bytes 131104 | tf_op jit(solution)/shard_map/ppermute | solution.py:34
  369.1 11.8 %collective-permute-done.30 = bf16[512,128]{1,0:T(8,128)(2,1)S(1)} collective-permute-done((bf16[512,128]{1,0:T(8,128)(2,1)S(1)}, bf16[512,128]{1,0:T(8,128)(2,1)S(1)}, u32[]{:S(2)}, u32[]{:S(2)}) %collective-permute-start.30) | collective-permute-done | bytes 131104 | tf_op jit(solution)/shard_map/ppermute | solution.py:34
  381.1 2.8 copy-done.6
  383.9 3.3 one_other.1
  389.4 18.3 %collective-permute-done.27.refs_5_ = bf16[512,768]{1,0:T(8,128)(2,1)S(1)} collective-permute-done((bf16[512,768]{1,0:T(8,128)(2,1)S(1)}, bf16[512,768]{1,0:T(8,128)(2,1)S(1)}, u32[]{:S(2)}, u32[]{:S(2)}) %collective-permute-start.27) | collective-permute-done | bytes 786464 | tf_op jit(solution)/shard_map/ppermute | solution.py:28
  407.7 4.2 one_own.1.mine_ref
  411.9 3.8 collective-permute-done.39.refs_5_
  415.7 2.5 grad_little_given.1
  419.0 3.2 grad_source_given.1
  423.1 3.4 mlp_other.1
  432.4 2.2 copy-done.17
  434.6 3.7 mlp_own.1
  438.3 14.1 %collective-permute-done.42.theirs_ref = bf16[256,2048]{1,0:T(8,128)(2,1)} collective-permute-done((bf16[256,2048]{1,0:T(8,128)(2,1)}, bf16[256,2048]{1,0:T(8,128)(2,1)}, u32[]{:S(2)}, u32[]{:S(2)}) %collective-permute-start.42) | collective-permute-done | bytes 1048608 | tf_op jit(solution)/shard_map/ppermute | solution.py:23
  455.6 3.7 norm_one_back.1
  459.3 2.7 grad_little_held.1
  463.5 2.6 copy.101
  467.4 2.9 copy.100
  470.6 22.6 %collective-permute-done.44.refs_6_ = bf16[512,768]{1,0:T(8,128)(2,1)} collective-permute-done((bf16[512,768]{1,0:T(8,128)(2,1)}, bf16[512,768]{1,0:T(8,128)(2,1)}, u32[]{:S(2)}, u32[]{:S(2)}) %collective-permute-start.44) | collective-permute-done | bytes 786464 | tf_op jit(solution)/shard_map/ppermute | solution.py:72
  493.2 3.3 grad_source_held.1
  501.9 3.7 collective-permute-done.55
  509.9 3.8 multiply_reduce_fusion
  516.4 5.5 collective-permute-done.52
  528.7 3.0 collective-permute-start.51
  540.7 2.4 copy.95
  (515 shorter events, 183.8 us)
Async XLA Ops:
  7.2 304.9 %reduce-scatter.6.cloned.1.call-start = ((), (), s32[]{:S(2)}) async-start(), calls=%async_computation.5 | async-start | bytes 2621440 | tf_op jit(solution)/shard_map/reduce_scatter | solution.py:848
  35.5 30.2 %collective-permute-start.3 = (bf16[512,128]{1,0:T(8,128)(2,1)}, bf16[512,128]{1,0:T(8,128)(2,1)}, u32[]{:S(2)}, u32[]{:S(2)}) collective-permute-start(bf16[512,128]{1,0:T(8,128)(2,1)} %dynamic-slice_convert_fusion.1), channel_id=1, source_target_pairs={{0,4},{4,8},{8,12},{1,5},{5,9},{9,13},{2,6},{6,10},{10,14},{3,7},{... | collective-permute-start | bytes 393224 | tf_op jit(solution)/shard_map/ppermute | solution.py:34
  41.1 25.1 %collective-permute-start.4 = (bf16[512,128]{1,0:T(8,128)(2,1)}, bf16[512,128]{1,0:T(8,128)(2,1)}, u32[]{:S(2)}, u32[]{:S(2)}) collective-permute-start(bf16[512,128]{1,0:T(8,128)(2,1)} %dynamic-slice_convert_fusion.1), channel_id=1, source_target_pairs={{0,8},{4,12},{1,9},{5,13},{2,10},{6,14},{3,11},{7,15},{16,24},{20,... | collective-permute-start | bytes 393224 | tf_op jit(solution)/shard_map/ppermute | solution.py:34
  45.6 20.6 %collective-permute-start.5 = (bf16[512,128]{1,0:T(8,128)(2,1)}, bf16[512,128]{1,0:T(8,128)(2,1)}, u32[]{:S(2)}, u32[]{:S(2)}) collective-permute-start(bf16[512,128]{1,0:T(8,128)(2,1)} %dynamic-slice_convert_fusion.1), channel_id=1, source_target_pairs={{0,12},{1,13},{2,14},{3,15},{16,28},{17,29},{18,30},{19,31}} | collective-permute-start | bytes 393224 | tf_op jit(solution)/shard_map/ppermute | solution.py:34
  47.5 22.0 %collective-permute-start = (bf16[768,256]{1,0:T(8,128)(2,1)}, bf16[768,256]{1,0:T(8,128)(2,1)}, u32[]{:S(2)}, u32[]{:S(2)}) collective-permute-start(bf16[768,256]{1,0:T(8,128)(2,1)} %own_state.2), channel_id=1, source_target_pairs={{0,4},{1,5},{2,6},{3,7},{16,20},{17,21},{18,22},{19,23}} | collective-permute-start | bytes 1179656 | tf_op jit(solution)/shard_map/ppermute | solution.py:93
  51.9 17.6 %collective-permute-start.1 = (bf16[256,1024]{1,0:T(8,128)(2,1)}, bf16[256,1024]{1,0:T(8,128)(2,1)}, u32[]{:S(2)}, u32[]{:S(2)}) collective-permute-start(bf16[256,1024]{1,0:T(8,128)(2,1)} %dynamic_slice.90), channel_id=1, source_target_pairs={{0,16},{16,0},{1,17},{17,1},{2,18},{18,2},{3,19},{19,3},{4,20},{20... | collective-permute-start | bytes 1572872 | tf_op jit(solution)/shard_map/ppermute | solution.py:28
  65.7 14.2 %collective-permute-start.7 = (bf16[256,1024]{1,0:T(8,128)(2,1)}, bf16[256,1024]{1,0:T(8,128)(2,1)S(1)}, u32[]{:S(2)}, u32[]{:S(2)}) collective-permute-start(bf16[256,1024]{1,0:T(8,128)(2,1)} %dynamic_slice.93), channel_id=1, source_target_pairs={{0,16},{16,0},{1,17},{17,1},{2,18},{18,2},{3,19},{19,3},{4,20},{20... | collective-permute-start | bytes 1572872 | tf_op jit(solution)/shard_map/ppermute | solution.py:28
  67.3 4.3 collective-permute-start.6
  71.0 9.0 %collective-permute-start.2 = (bf16[768,256]{1,0:T(8,128)(2,1)S(1)}, bf16[768,256]{1,0:T(8,128)(2,1)S(1)}, u32[]{:S(2)}, u32[]{:S(2)}) collective-permute-start(bf16[768,256]{1,0:T(8,128)(2,1)S(1)} %fusion.5), channel_id=1, source_target_pairs={{4,8},{5,9},{6,10},{7,11},{20,24},{21,25},{22,26},{23,27}} | collective-permute-start | bytes 1179656 | tf_op jit(solution)/shard_map/ppermute | solution.py:93
  81.2 4.6 collective-permute-start.8
  93.5 2.8 collective-permute-start.9
  99.7 27.0 %collective-permute-start.10 = (bf16[256,2048]{1,0:T(8,128)(2,1)}, bf16[256,2048]{1,0:T(8,128)(2,1)}, u32[]{:S(2)}, u32[]{:S(2)}) collective-permute-start(bf16[256,2048]{1,0:T(8,128)(2,1)} %mix_own.1.mine_ref), channel_id=1, source_target_pairs={{0,2},{1,3},{2,0},{3,1},{4,6},{5,7},{6,4},{7,5},{8,10},{9,11},{10,... | collective-permute-start | bytes 3145736 | tf_op jit(solution)/shard_map/ppermute | solution.py:23
  101.2 25.5 %collective-permute-start.13 = (bf16[512,768]{1,0:T(8,128)(2,1)}, bf16[512,768]{1,0:T(8,128)(2,1)}, u32[]{:S(2)}, u32[]{:S(2)}) collective-permute-start(bf16[512,768]{1,0:T(8,128)(2,1)} %get-tuple-element.94.refs_0_.refs_4_), channel_id=1, source_target_pairs={{0,16},{16,0},{1,17},{17,1},{2,18},{18,2},{3,19},{19,3},{4,20},{20... | collective-permute-start | bytes 2359304 | tf_op jit(solution)/shard_map/ppermute | solution.py:28
  102.8 23.9 %collective-permute-start.12 = (bf16[256,1024]{1,0:T(8,128)(2,1)S(1)}, bf16[256,1024]{1,0:T(8,128)(2,1)}, u32[]{:S(2)}, u32[]{:S(2)}) collective-permute-start(bf16[256,1024]{1,0:T(8,128)(2,1)S(1)} %collective-permute-done.7.refs_2_), channel_id=1, source_target_pairs={{0,1},{1,0},{2,3},{3,2},{4,5},{5,4},{6,7},{7,6},{8,9},{9,8},{10,11... | collective-permute-start | bytes 1572872 | tf_op jit(solution)/shard_map/ppermute | solution.py:23
  102.8 23.9 %collective-permute-start.11 = (bf16[256,1024]{1,0:T(8,128)(2,1)}, bf16[256,1024]{1,0:T(8,128)(2,1)}, u32[]{:S(2)}, u32[]{:S(2)}) collective-permute-start(bf16[256,1024]{1,0:T(8,128)(2,1)} %collective-permute-done.1.refs_2_), channel_id=1, source_target_pairs={{0,1},{1,0},{2,3},{3,2},{4,5},{5,4},{6,7},{7,6},{8,9},{9,8},{10,11... | collective-permute-start | bytes 1572872 | tf_op jit(solution)/shard_map/ppermute | solution.py:23
  107.1 19.6 %collective-permute-start.14 = (bf16[512,256]{1,0:T(8,128)(2,1)}, bf16[512,256]{1,0:T(8,128)(2,1)}, u32[]{:S(2)}, u32[]{:S(2)}) collective-permute-start(bf16[512,256]{1,0:T(8,128)(2,1)} %copy-done.87), channel_id=1, source_target_pairs={{0,16},{16,0},{1,17},{17,1},{2,18},{18,2},{3,19},{19,3},{4,20},{20... | collective-permute-start | bytes 786440 | tf_op jit(solution)/shard_map/ppermute | solution.py:28
  131.1 2.7 collective-permute-start.15
  148.4 2.7 collective-permute-start.16
  148.6 37.0 %collective-permute-start.18 = (bf16[512,1024]{1,0:T(8,128)(2,1)}, bf16[512,1024]{1,0:T(8,128)(2,1)}, u32[]{:S(2)}, u32[]{:S(2)}) collective-permute-start(bf16[512,1024]{1,0:T(8,128)(2,1)} %get-tuple-element.102.refs_4_.refs_0_), channel_id=1, source_target_pairs={{0,16},{16,0},{1,17},{17,1},{2,18},{18,2},{3,19},{19,3},{4,20},{20... | collective-permute-start | bytes 3145736 | tf_op jit(solution)/shard_map/ppermute | solution.py:28
  155.1 30.5 %collective-permute-start.17 = (bf16[256,2048]{1,0:T(8,128)(2,1)}, bf16[256,2048]{1,0:T(8,128)(2,1)}, u32[]{:S(2)}, u32[]{:S(2)}) collective-permute-start(bf16[256,2048]{1,0:T(8,128)(2,1)} %two_own.1.mine_ref), channel_id=1, source_target_pairs={{0,2},{1,3},{2,0},{3,1},{4,6},{5,7},{6,4},{7,5},{8,10},{9,11},{10,... | collective-permute-start | bytes 3145736 | tf_op jit(solution)/shard_map/ppermute | solution.py:23
  156.5 29.1 %collective-permute-start.19 = (bf16[256,1024]{1,0:T(8,128)(2,1)}, bf16[256,1024]{1,0:T(8,128)(2,1)}, u32[]{:S(2)}, u32[]{:S(2)}) collective-permute-start(bf16[256,1024]{1,0:T(8,128)(2,1)} %constant_dynamic-slice_fusion.5), channel_id=1, source_target_pairs={{0,16},{16,0},{1,17},{17,1},{2,18},{18,2},{3,19},{19,3},{4,20},{20... | collective-permute-start | bytes 1572872 | tf_op jit(solution)/shard_map/ppermute | solution.py:28
  158.1 36.8 %copy-start.118 = (s32[4]{0:T(128)}, s32[4]{0:T(128)S(1)}, u32[]{:S(2)}) copy-start(s32[4]{0:T(128)S(1)} %pad_add_fusion.at_ref) | copy-start | bytes 52
  202.0 236.2 %reduce-scatter.8.cloned.1.call-start = ((), (), s32[]{:S(2)}) async-start(), calls=%async_computation.6 | async-start | bytes 2621440 | tf_op jit(solution)/shard_map/reduce_scatter | solution.py:848
  202.1 2.9 collective-permute-start.20
  202.2 28.5 %collective-permute-start.22 = (bf16[512,1024]{1,0:T(8,128)(2,1)}, bf16[512,1024]{1,0:T(8,128)(2,1)S(1)}, u32[]{:S(2)}, u32[]{:S(2)}) collective-permute-start(bf16[512,1024]{1,0:T(8,128)(2,1)} %copy-done.34), channel_id=1, source_target_pairs={{0,16},{16,0},{1,17},{17,1},{2,18},{18,2},{3,19},{19,3},{4,20},{20... | collective-permute-start | bytes 3145736 | tf_op jit(solution)/shard_map/ppermute | solution.py:28
  203.8 26.9 %collective-permute-start.23 = (bf16[256,1024]{1,0:T(8,128)(2,1)}, bf16[256,1024]{1,0:T(8,128)(2,1)S(1)}, u32[]{:S(2)}, u32[]{:S(2)}) collective-permute-start(bf16[256,1024]{1,0:T(8,128)(2,1)} %collective-permute-done.19.refs_2_), channel_id=1, source_target_pairs={{0,1},{1,0},{2,3},{3,2},{4,5},{5,4},{6,7},{7,6},{8,9},{9,8},{10,11... | collective-permute-start | bytes 1572872 | tf_op jit(solution)/shard_map/ppermute | solution.py:23
  217.6 13.1 %collective-permute-start.21 = (bf16[768,256]{1,0:T(8,128)(2,1)S(1)}, bf16[768,256]{1,0:T(8,128)(2,1)S(1)}, u32[]{:S(2)}, u32[]{:S(2)}) collective-permute-start(bf16[768,256]{1,0:T(8,128)(2,1)S(1)} %own_state.3), channel_id=1, source_target_pairs={{12,8},{13,9},{14,10},{15,11},{28,24},{29,25},{30,26},{31,27}} | collective-permute-start | bytes 1179656 | tf_op jit(solution)/shard_map/ppermute | solution.py:93
  238.0 228.0 %reduce-scatter.14.cloned.1.call-start = ((), (), s32[]{:S(2)}) async-start(), calls=%async_computation.9 | async-start | bytes 2621440 | tf_op jit(solution)/shard_map/reduce_scatter | solution.py:848
  238.1 25.5 %collective-permute-start.25 = (bf16[512,1024]{1,0:T(8,128)(2,1)}, bf16[512,1024]{1,0:T(8,128)(2,1)S(1)}, u32[]{:S(2)}, u32[]{:S(2)}) collective-permute-start(bf16[512,1024]{1,0:T(8,128)(2,1)} %copy-done.32), channel_id=1, source_target_pairs={{0,16},{16,0},{1,17},{17,1},{2,18},{18,2},{3,19},{19,3},{4,20},{20... | collective-permute-start | bytes 3145736 | tf_op jit(solution)/shard_map/ppermute | solution.py:28
  239.7 23.9 %collective-permute-start.24 = (bf16[768,256]{1,0:T(8,128)(2,1)}, bf16[768,256]{1,0:T(8,128)(2,1)S(1)}, u32[]{:S(2)}, u32[]{:S(2)}) collective-permute-start(bf16[768,256]{1,0:T(8,128)(2,1)} %fusion.7), channel_id=1, source_target_pairs={{8,4},{9,5},{10,6},{11,7},{24,20},{25,21},{26,22},{27,23}} | collective-permute-start | bytes 1179656 | tf_op jit(solution)/shard_map/ppermute | solution.py:93
  273.6 262.9 %reduce-scatter.12.cloned.1.call-start = ((), (), s32[]{:S(2)}) async-start(), calls=%async_computation.8 | async-start | bytes 2621440 | tf_op jit(solution)/shard_map/reduce_scatter | solution.py:848
  275.5 15.2 %collective-permute-start.34 = (bf16[256,1024]{1,0:T(8,128)(2,1)}, bf16[256,1024]{1,0:T(8,128)(2,1)}, u32[]{:S(2)}, u32[]{:S(2)}) collective-permute-start(bf16[256,1024]{1,0:T(8,128)(2,1)} %constant_dynamic-slice_fusion.4), channel_id=1, source_target_pairs={{0,16},{16,0},{1,17},{17,1},{2,18},{18,2},{3,19},{19,3},{4,20},{20... | collective-permute-start | bytes 1572872 | tf_op jit(solution)/shard_map/ppermute | solution.py:28
  277.0 59.7 %collective-permute-start.36 = (bf16[512,768]{1,0:T(8,128)(2,1)}, bf16[512,768]{1,0:T(8,128)(2,1)}, u32[]{:S(2)}, u32[]{:S(2)}) collective-permute-start(bf16[512,768]{1,0:T(8,128)(2,1)} %copy-done.56), channel_id=1, source_target_pairs={{0,16},{16,0},{1,17},{17,1},{2,18},{18,2},{3,19},{19,3},{4,20},{20... | collective-permute-start | bytes 2359304 | tf_op jit(solution)/shard_map/ppermute | solution.py:28
  277.6 33.8 %copy-start.135 = (bf16[768,256]{1,0:T(8,128)(2,1)S(1)}, bf16[768,256]{1,0:T(8,128)(2,1)}, u32[]{:S(2)}) copy-start(bf16[768,256]{1,0:T(8,128)(2,1)} %copy-done.134) | copy-start | bytes 1179652
  290.7 39.0 %collective-permute-start.35 = (bf16[256,1024]{1,0:T(8,128)(2,1)}, bf16[256,1024]{1,0:T(8,128)(2,1)}, u32[]{:S(2)}, u32[]{:S(2)}) collective-permute-start(bf16[256,1024]{1,0:T(8,128)(2,1)} %collective-permute-done.34.refs_2_), channel_id=1, source_target_pairs={{0,1},{1,0},{2,3},{3,2},{4,5},{5,4},{6,7},{7,6},{8,9},{9,8},{10,11... | collective-permute-start | bytes 1572872 | tf_op jit(solution)/shard_map/ppermute | solution.py:23
  290.7 46.0 %collective-permute-start.37 = (bf16[512,256]{1,0:T(8,128)(2,1)}, bf16[512,256]{1,0:T(8,128)(2,1)}, u32[]{:S(2)}, u32[]{:S(2)}) collective-permute-start(bf16[512,256]{1,0:T(8,128)(2,1)} %copy-done.84), channel_id=1, source_target_pairs={{0,16},{16,0},{1,17},{17,1},{2,18},{18,2},{3,19},{19,3},{4,20},{20... | collective-permute-start | bytes 786440 | tf_op jit(solution)/shard_map/ppermute | solution.py:28
  292.2 19.1 %collective-permute-start.26 = (bf16[768,256]{1,0:T(8,128)(2,1)}, bf16[768,256]{1,0:T(8,128)(2,1)S(1)}, u32[]{:S(2)}, u32[]{:S(2)}) collective-permute-start(bf16[768,256]{1,0:T(8,128)(2,1)} %fusion.8), channel_id=1, source_target_pairs={{4,0},{5,1},{6,2},{7,3},{20,16},{21,17},{22,18},{23,19}} | collective-permute-start | bytes 1179656 | tf_op jit(solution)/shard_map/ppermute | solution.py:93
  344.3 9.5 %collective-permute-start.28 = (bf16[2048,128]{1,0:T(8,128)(2,1)}, bf16[2048,128]{1,0:T(8,128)(2,1)}, u32[]{:S(2)}, u32[]{:S(2)}) collective-permute-start(bf16[2048,128]{1,0:T(8,128)(2,1)} %select_convert_fusion), channel_id=1, source_target_pairs={{0,1},{1,0},{2,3},{3,2},{4,5},{5,4},{6,7},{7,6},{8,9},{9,8},{10,11... | collective-permute-start | bytes 1572872 | tf_op jit(solution)/shard_map/ppermute | solution.py:23
  346.4 191.3 %reduce-scatter.10.cloned.1.call-start = ((), (), s32[]{:S(2)}) async-start(), calls=%async_computation.7 | async-start | bytes 2621440 | tf_op jit(solution)/shard_map/reduce_scatter | solution.py:848
  349.0 2.1 collective-permute-start.32
  352.2 7.3 %collective-permute-start.33 = (bf16[512,128]{1,0:T(8,128)(2,1)S(1)}, bf16[512,128]{1,0:T(8,128)(2,1)S(1)}, u32[]{:S(2)}, u32[]{:S(2)}) collective-permute-start(bf16[512,128]{1,0:T(8,128)(2,1)S(1)} %dynamic-slice_convert_fusion.2), channel_id=1, source_target_pairs={{0,2},{1,3},{2,0},{3,1},{4,6},{5,7},{6,4},{7,5},{8,10},{9,11},{10,... | collective-permute-start | bytes 393224 | tf_op jit(solution)/shard_map/ppermute | solution.py:23
  355.2 13.8 %collective-permute-start.29 = (bf16[512,128]{1,0:T(8,128)(2,1)S(1)}, bf16[512,128]{1,0:T(8,128)(2,1)S(1)}, u32[]{:S(2)}, u32[]{:S(2)}) collective-permute-start(bf16[512,128]{1,0:T(8,128)(2,1)S(1)} %get-tuple-element.239), channel_id=1, source_target_pairs={{4,0},{8,4},{12,8},{5,1},{9,5},{13,9},{6,2},{10,6},{14,10},{7,3},{... | collective-permute-start | bytes 393224 | tf_op jit(solution)/shard_map/ppermute | solution.py:34
  356.7 24.2 %collective-permute-start.30 = (bf16[512,128]{1,0:T(8,128)(2,1)S(1)}, bf16[512,128]{1,0:T(8,128)(2,1)S(1)}, u32[]{:S(2)}, u32[]{:S(2)}) collective-permute-start(bf16[512,128]{1,0:T(8,128)(2,1)S(1)} %get-tuple-element.241), channel_id=1, source_target_pairs={{8,0},{12,4},{9,1},{13,5},{10,2},{14,6},{11,3},{15,7},{24,16},{28,... | collective-permute-start | bytes 393224 | tf_op jit(solution)/shard_map/ppermute | solution.py:34
  358.0 22.9 %collective-permute-start.31 = (bf16[512,128]{1,0:T(8,128)(2,1)S(1)}, bf16[512,128]{1,0:T(8,128)(2,1)S(1)}, u32[]{:S(2)}, u32[]{:S(2)}) collective-permute-start(bf16[512,128]{1,0:T(8,128)(2,1)S(1)} %get-tuple-element.240), channel_id=1, source_target_pairs={{12,0},{13,1},{14,2},{15,3},{28,16},{29,17},{30,18},{31,19}} | collective-permute-start | bytes 393224 | tf_op jit(solution)/shard_map/ppermute | solution.py:34
  387.2 20.5 %collective-permute-start.38 = (bf16[256,2048]{1,0:T(8,128)(2,1)S(1)}, bf16[256,2048]{1,0:T(8,128)(2,1)S(1)}, u32[]{:S(2)}, u32[]{:S(2)}) collective-permute-start(bf16[256,2048]{1,0:T(8,128)(2,1)S(1)} %one_other.1), channel_id=1, source_target_pairs={{0,1},{1,0},{2,3},{3,2},{4,5},{5,4},{6,7},{7,6},{8,9},{9,8},{10,11... | collective-permute-start | bytes 3145736 | tf_op jit(solution)/shard_map/ppermute | solution.py:23
  387.3 20.4 %collective-permute-start.27 = (bf16[512,768]{1,0:T(8,128)(2,1)S(1)}, bf16[512,768]{1,0:T(8,128)(2,1)S(1)}, u32[]{:S(2)}, u32[]{:S(2)}) collective-permute-start(bf16[512,768]{1,0:T(8,128)(2,1)S(1)} %copy-done.29), channel_id=1, source_target_pairs={{0,16},{16,0},{1,17},{17,1},{2,18},{18,2},{3,19},{19,3},{4,20},{20... | collective-permute-start | bytes 2359304 | tf_op jit(solution)/shard_map/ppermute | solution.py:28
  388.8 26.9 %collective-permute-start.39 = (bf16[512,384]{1,0:T(8,128)(2,1)S(1)}, bf16[512,384]{1,0:T(8,128)(2,1)S(1)}, u32[]{:S(2)}, u32[]{:S(2)}) collective-permute-start(bf16[512,384]{1,0:T(8,128)(2,1)S(1)} %fusion.10.refs_3_.refs_4_), channel_id=1, source_target_pairs={{0,16},{16,0},{1,17},{17,1},{2,18},{18,2},{3,19},{19,3},{4,20},{20... | collective-permute-start | bytes 1179656 | tf_op jit(solution)/shard_map/ppermute | solution.py:28
  426.5 5.9 %collective-permute-start.40 = (bf16[256,2048]{1,0:T(8,128)(2,1)}, bf16[256,2048]{1,0:T(8,128)(2,1)}, u32[]{:S(2)}, u32[]{:S(2)}) collective-permute-start(bf16[256,2048]{1,0:T(8,128)(2,1)} %mlp_other.1), channel_id=1, source_target_pairs={{0,1},{1,0},{2,3},{3,2},{4,5},{5,4},{6,7},{7,6},{8,9},{9,8},{10,11... | collective-permute-start | bytes 3145736 | tf_op jit(solution)/shard_map/ppermute | solution.py:23
  426.5 25.9 %collective-permute-start.42 = (bf16[256,2048]{1,0:T(8,128)(2,1)}, bf16[256,2048]{1,0:T(8,128)(2,1)}, u32[]{:S(2)}, u32[]{:S(2)}) collective-permute-start(bf16[256,2048]{1,0:T(8,128)(2,1)} %one_own.1.mine_ref), channel_id=1, source_target_pairs={{0,2},{1,3},{2,0},{3,1},{4,6},{5,7},{6,4},{7,5},{8,10},{9,11},{10,... | collective-permute-start | bytes 3145736 | tf_op jit(solution)/shard_map/ppermute | solution.py:23
  426.5 32.8 %collective-permute-start.43 = (bf16[512,384]{1,0:T(8,128)(2,1)}, bf16[512,384]{1,0:T(8,128)(2,1)}, u32[]{:S(2)}, u32[]{:S(2)}) collective-permute-start(bf16[512,384]{1,0:T(8,128)(2,1)} %copy-done.113), channel_id=1, source_target_pairs={{0,4},{4,0},{8,12},{12,8},{1,5},{5,1},{9,13},{13,9},{2,6},{6,2},{1... | collective-permute-start | bytes 1179656 | tf_op jit(solution)/shard_map/ppermute | solution.py:72
  426.6 66.6 %collective-permute-start.44 = (bf16[512,768]{1,0:T(8,128)(2,1)}, bf16[512,768]{1,0:T(8,128)(2,1)}, u32[]{:S(2)}, u32[]{:S(2)}) collective-permute-start(bf16[512,768]{1,0:T(8,128)(2,1)} %copy-done.105), channel_id=1, source_target_pairs={{0,4},{4,0},{8,12},{12,8},{1,5},{5,1},{9,13},{13,9},{2,6},{6,2},{1... | collective-permute-start | bytes 2359304 | tf_op jit(solution)/shard_map/ppermute | solution.py:72
  463.5 34.7 %collective-permute-start.53 = (bf16[256,384]{1,0:T(8,128)(2,1)}, bf16[256,384]{1,0:T(8,128)(2,1)}, u32[]{:S(2)}, u32[]{:S(2)}) collective-permute-start(bf16[256,384]{1,0:T(8,128)(2,1)} %slice.185), channel_id=1, source_target_pairs={{0,8},{4,12},{8,0},{12,4},{1,9},{5,13},{9,1},{13,5},{2,10},{6,14},... | collective-permute-start | bytes 589832 | tf_op jit(solution)/shard_map/ppermute | solution.py:72
  470.3 39.5 %collective-permute-start.41 = (bf16[256,2048]{1,0:T(8,128)(2,1)}, bf16[256,2048]{1,0:T(8,128)(2,1)}, u32[]{:S(2)}, u32[]{:S(2)}) collective-permute-start(bf16[256,2048]{1,0:T(8,128)(2,1)} %mlp_own.1), channel_id=1, source_target_pairs={{0,2},{1,3},{2,0},{3,1},{4,6},{5,7},{6,4},{7,5},{8,10},{9,11},{10,... | collective-permute-start | bytes 3145736 | tf_op jit(solution)/shard_map/ppermute | solution.py:23
  470.6 54.9 %collective-permute-start.46 = (bf16[256,2048]{1,0:T(8,128)(2,1)}, bf16[256,2048]{1,0:T(8,128)(2,1)}, u32[]{:S(2)}, u32[]{:S(2)}) collective-permute-start(bf16[256,2048]{1,0:T(8,128)(2,1)} %get-tuple-element.143), channel_id=1, source_target_pairs={{0,1},{1,0},{2,3},{3,2},{4,5},{5,4},{6,7},{7,6},{8,9},{9,8},{10,11... | collective-permute-start | bytes 3145736 | tf_op jit(solution)/shard_map/ppermute | solution.py:23
  499.2 2.7 collective-permute-start.54
  499.2 6.4 %collective-permute-start.55 = (bf16[256,256]{1,0:T(8,128)(2,1)S(1)}, bf16[256,256]{1,0:T(8,128)(2,1)S(1)}, u32[]{:S(2)}, u32[]{:S(2)}) collective-permute-start(bf16[256,256]{1,0:T(8,128)(2,1)S(1)} %slice.223), channel_id=1, source_target_pairs={{0,2},{1,3},{2,0},{3,1},{4,6},{5,7},{6,4},{7,5},{8,10},{9,11},{10,... | collective-permute-start | bytes 393224 | tf_op jit(solution)/shard_map/ppermute | solution.py:23
  501.0 6.5 %collective-permute-start.56 = (bf16[256,256]{1,0:T(8,128)(2,1)S(1)}, bf16[256,256]{1,0:T(8,128)(2,1)S(1)}, u32[]{:S(2)}, u32[]{:S(2)}) collective-permute-start(bf16[256,256]{1,0:T(8,128)(2,1)S(1)} %slice.223), channel_id=1, source_target_pairs={{0,3},{1,2},{2,1},{3,0},{4,7},{5,6},{6,5},{7,4},{8,11},{9,10},{10,... | collective-permute-start | bytes 393224 | tf_op jit(solution)/shard_map/ppermute | solution.py:23
  501.9 20.0 %collective-permute-start.52 = (bf16[256,768]{1,0:T(8,128)(2,1)}, bf16[256,768]{1,0:T(8,128)(2,1)}, u32[]{:S(2)}, u32[]{:S(2)}) collective-permute-start(bf16[256,768]{1,0:T(8,128)(2,1)} %slice.183), channel_id=1, source_target_pairs={{0,8},{4,12},{8,0},{12,4},{1,9},{5,13},{9,1},{13,5},{2,10},{6,14},... | collective-permute-start | bytes 1179656 | tf_op jit(solution)/shard_map/ppermute | solution.py:72
  515.7 8.2 %collective-permute-start.47 = (f32[4099]{0:T(1024)S(1)}, f32[4099]{0:T(1024)S(1)}, u32[]{:S(2)}, u32[]{:S(2)}) collective-permute-start(f32[4099]{0:T(1024)S(1)} %concatenate.40), channel_id=1, source_target_pairs={{0,1},{1,0},{2,3},{3,2},{4,5},{5,4},{6,7},{7,6},{8,9},{9,8},{10,11... | collective-permute-start | bytes 49196 | tf_op jit(solution)/shard_map/ppermute | solution.py:23
  523.8 21.3 %collective-permute-start.45 = (bf16[256,2048]{1,0:T(8,128)(2,1)}, bf16[256,2048]{1,0:T(8,128)(2,1)}, u32[]{:S(2)}, u32[]{:S(2)}) collective-permute-start(bf16[256,2048]{1,0:T(8,128)(2,1)} %get-tuple-element.227), channel_id=1, source_target_pairs={{0,1},{1,0},{2,3},{3,2},{4,5},{5,4},{6,7},{7,6},{8,9},{9,8},{10,11... | collective-permute-start | bytes 3145736 | tf_op jit(solution)/shard_map/ppermute | solution.py:23
  524.0 3.8 collective-permute-start.48
  527.8 5.7 %collective-permute-start.49 = (f32[40,128]{1,0:T(8,128)S(1)}, f32[40,128]{1,0:T(8,128)S(1)}, u32[]{:S(2)}, u32[]{:S(2)}) collective-permute-start(f32[40,128]{1,0:T(8,128)S(1)} %bitcast.135), channel_id=1, source_target_pairs={{0,4},{4,8},{8,12},{12,0},{1,5},{5,9},{9,13},{13,1},{2,6},{6,10},{... | collective-permute-start | bytes 61448 | tf_op jit(solution)/shard_map/ppermute | solution.py:28
  527.9 5.6 %collective-permute-start.50 = (f32[40,128]{1,0:T(8,128)S(1)}, f32[40,128]{1,0:T(8,128)S(1)}, u32[]{:S(2)}, u32[]{:S(2)}) collective-permute-start(f32[40,128]{1,0:T(8,128)S(1)} %bitcast.136), channel_id=1, source_target_pairs={{0,8},{4,12},{8,0},{12,4},{1,9},{5,13},{9,1},{13,5},{2,10},{6,14},... | collective-permute-start | bytes 61448 | tf_op jit(solution)/shard_map/ppermute | solution.py:28
  528.7 5.3 collective-permute-start.51
  (141 other events, 870.1 us)
Sparse Core Ops, SparseCore 0:
  202.2 57.2 reduce-scatter.5
  261.9 44.0 reduce-scatter.7
  308.2 42.3 reduce-scatter.13
  352.9 50.0 reduce-scatter.11
  430.4 62.5 reduce-scatter.9

commit v5 on v4

--- a/solution.py
+++ b/solution.py
@@ -15,6 +15,7 @@
 EPSILON = 1e-05
 NEG_FILL = -1e30
 VMEM_GRANT = 28 * 1024 * 1024
+WIDE_GRANT = 60 * 1024 * 1024
 
 CORE, CHIP = (1, 2)
 
@@ -66,10 +67,6 @@
 
 def send_rows(value):
     return [shifted(value, "dp", shift) for shift in range(1, lax.axis_size("dp"))]
-
-
-def ctx_partner(value, stride):
-    return lax.ppermute(value, "ctx", [(rank, rank ^ stride) for rank in range(4)])
 
 
 def all_sum(value, axis):
@@ -379,7 +376,7 @@
     dq_ref[...] = narrow((matmul_low(flat_ref[...], grad_score) * factor).T)
 
 
-def call(name, kernel, grid, specs, args, outs, scratch=()):
+def call(name, kernel, grid, specs, args, outs, scratch=(), grant=VMEM_GRANT):
     return pl.pallas_call(
         kernel,
         name=name,
@@ -389,7 +386,7 @@
         out_shape=[out for out, _ in outs],
         scratch_shapes=list(scratch),
         cost_estimate=pl.CostEstimate(flops=1, bytes_accessed=1, transcendentals=0),
-        compiler_params=pltpu.CompilerParams(vmem_limit_bytes=VMEM_GRANT),
+        compiler_params=pltpu.CompilerParams(vmem_limit_bytes=grant),
     )(*args)
 
 
@@ -474,6 +471,7 @@
             [tile, tile, row, row, tile] + 2 * [self.shared] + 2 * [states] + 2 * [self.shared],
             (u, dy, small, sums, dw, b, c, state, grad, db, dc),
             [(self.rows_like(jnp.bfloat16), tile), (self.small_like, row)] + 2 * [(shared, self.shared)],
+            grant=WIDE_GRANT,
         )
 
 
@@ -514,7 +512,7 @@
         )
 
 
-def call_at(name, kernel, scalars, grid, specs, args, outs):
+def call_at(name, kernel, scalars, grid, specs, args, outs, grant=VMEM_GRANT):
     return pl.pallas_call(
         kernel,
         name=name,
@@ -526,7 +524,7 @@
         ),
         out_shape=[out for out, _ in outs],
         cost_estimate=pl.CostEstimate(flops=1, bytes_accessed=1, transcendentals=0),
-        compiler_params=pltpu.CompilerParams(vmem_limit_bytes=VMEM_GRANT),
+        compiler_params=pltpu.CompilerParams(vmem_limit_bytes=grant),
     )(scalars, *args)
 
 
@@ -641,6 +639,7 @@
         ],
         (x, weight),
         [(like((rows, width), kind), pl.BlockSpec((rows, size), lambda j: (0, j)))],
+        grant=VMEM_GRANT,
     )[0]
 
 
@@ -676,6 +675,7 @@
         ],
         (mine, other, weight, weight, dact),
         [(like((rows, width), jnp.bfloat16), tile)] * 3,
+        VMEM_GRANT,
     )
 
 
@@ -706,6 +706,7 @@
         [whole, whole, pl.BlockSpec((size, depth), lambda j, at: (j, 0)), tile, tile],
         (mine, other, weight, gate, y),
         [(like((rows, width), jnp.bfloat16), tile)] * 2,
+        VMEM_GRANT,
     )
 
 
@@ -756,110 +757,75 @@
         specs.append(tile)
         args.append(added)
     kernel = partial(share_kernel, count=len(terms), back=back, added=added is not None)
-    return call_at(
-        name, kernel, at, (width // size,), specs, args, [(like((rows, width), jnp.bfloat16), tile)]
-    )[0]
-
-
-def weight_kernel(at_ref, *refs, ranks, count, added):
+    outs = [(like((rows, width), jnp.bfloat16), tile)]
+    return call_at(name, kernel, at, (width // size,), specs, args, outs, VMEM_GRANT)[0]
+
+
+def weight_kernel(at_ref, *refs, ranks, counts):
     out_ref = refs[-1]
-    firsts = [ref[...].T for ref in refs[: 2 * ranks]]
-    seconds = refs[2 * ranks : 2 * ranks + ranks * count]
-    places = half_places(at_ref, seconds[0].shape[0])
+    refs = list(refs[:-1])
+    firsts = [[refs.pop(0)[...].T for _ in range(2 * ranks)] for _ in counts]
     at = 0
-    for index in range(count):
-        width = seconds[index].shape[1]
-        for start in range(0, width, 512):
-            stop = min(width, start + 512)
-            total = None
-            for rank in range(ranks):
-                ref = seconds[count * rank + index]
-                for which in range(2):
-                    part = matmul_low(firsts[2 * rank + which], ref[places[which], start:stop])
-                    total = part if total is None else total + part
-            if added:
-                total = total + wide(refs[-2][:, at + start : at + stop])
-            out_ref[:, at + start : at + stop] = narrow(total)
-        at = at + width
-
-
-class WeightGrad:
-    def __init__(self, name, own, others, seconds, arrived, core, ctx_rank):
-        self.name = name
-        whole = own[0].shape[1] if isinstance(own, tuple) else own.shape[1]
-        self.ranks = len(others) + 1
-        self.size = whole // self.ranks // 4
-        self.own, self.others = (own, others)
-        self.groups = [list(seconds)] + [list(group) for group in arrived]
-        self.width = sum(part.shape[1] for part in seconds)
-        dp_rank = lax.axis_index("dp")
-        near = ctx_rank ^ 1
-        self.given = jnp.stack([core, dp_rank, near ^ 2, near]).astype(jnp.int32)
-        self.held = jnp.stack([core, dp_rank, ctx_rank ^ 2, ctx_rank]).astype(jnp.int32)
-
-    def part(self, suffix, at, added=None, whole=False):
-        size = self.size
-        half = self.groups[0][0].shape[0] // 2
-        steps = 4 if whole else 2
-        own = list(self.own) if isinstance(self.own, tuple) else [self.own]
-        others = [array for pair in self.others for array in pair]
-        if size % 128 and whole:
-            steps, size = (1, 4 * size)
-            own = [cut(array, at[1], size, 1) for array in own]
-        elif size % 128:
-            steps, size = (1, 2 * size)
-            own = [self.columns(array, 4 * at[1] + at[2], 4 * at[1] + at[3]) for array in own]
-            others = [self.columns(array, at[2], at[3]) for array in others]
-
-        def first_spec(row, from_dp):
-            def place(m, at):
-                if steps == 1:
-                    return (row(at), m)
-                return (row(at), (m if whole else at[2 + m]) + (4 * at[1] if from_dp else 0))
-
-            return pl.BlockSpec((half, size), place)
+    for first, count in zip(firsts, counts, strict=True):
+        seconds = [refs.pop(0) for _ in range(ranks * count)]
+        places = half_places(at_ref, seconds[0].shape[0])
+        for index in range(count):
+            width = seconds[index].shape[1]
+            for start in range(0, width, 512):
+                stop = min(width, start + 512)
+                total = None
+                for rank in range(ranks):
+                    ref = seconds[count * rank + index]
+                    for which in range(2):
+                        part = matmul_low(first[2 * rank + which], ref[places[which], start:stop])
+                        total = part if total is None else total + part
+                out_ref[:, at + start : at + stop] = narrow(total)
+            at = at + width
+
+
+def weight_grad(name, core, sets, *awaited):
+    ranks = lax.axis_size("dp")
+    dp_rank = lax.axis_index("dp")
+    at = after(jnp.stack([core, dp_rank]).astype(jnp.int32), *awaited)
+    specs, args, pieces, counts = ([], [], [], [])
+    width = 0
+    for own, others, seconds, arrived in sets:
+        own = list(own) if isinstance(own, tuple) else [own]
+        others = [array for pair in others for array in pair]
+        groups = [list(seconds)] + [list(group) for group in arrived]
+        half = seconds[0].shape[0] // 2
+        share = own[0].shape[1] // ranks
+        size = min(256, share)
+        steps = share // size
+
+        def spec(row, from_dp, half=half, size=size, steps=steps):
+            return pl.BlockSpec(
+                (half, size), lambda m, at: (row(at), m + (steps * at[1] if from_dp else 0))
+            )
 
         if len(own) == 2:
-            specs = 2 * [first_spec(lambda at: 0, True)]
+            specs += 2 * [spec(lambda at: 0, True)]
         else:
-            specs = [first_spec(lambda at: at[0], True), first_spec(lambda at: 1 - at[0], True)]
+            specs += [spec(lambda at: at[0], True), spec(lambda at: 1 - at[0], True)]
             own = 2 * own
-        specs += [first_spec(lambda at: 0, False) for _ in others]
-        args = own + others
-        for group in self.groups:
-            for array in group:
-                specs.append(pl.BlockSpec(array.shape, lambda m, at: (0, 0)))
-                args.append(array)
-        tile = pl.BlockSpec((size, self.width), lambda m, at: (m, 0))
-        if added is not None:
-            specs.append(tile)
-            args.append(added)
-        kernel = partial(
-            weight_kernel, ranks=self.ranks, count=len(self.groups[0]), added=added is not None
-        )
-        out = like((steps * size, self.width), jnp.bfloat16)
-        return call_at(self.name + suffix, kernel, at, (steps,), specs, args, [(out, tile)])[0]
-
-    def columns(self, array, *blocks):
-        return jnp.concatenate([cut(array, block, self.size, 1) for block in blocks], axis=1)
-
-    def whole(self, *awaited):
-        self.made = self.part("_all", after(self.given, *awaited), whole=True)
-        self.total = lax.psum_scatter(self.made, "ctx", scatter_dimension=0, tiled=True)
-        return self.made
-
-    def start(self, *awaited):
-        self.sent = self.part("_given", after(self.given, *awaited))
-        self.near = ctx_partner(self.sent, 1)
-        return self.sent
-
-    def turn(self, *awaited):
-        self.kept = self.part("_held", after(self.held, *awaited), self.near)
-        self.far = ctx_partner(self.kept[: self.size], 2)
-        return self.kept
-
-    def end(self):
-        return wide(self.kept[self.size :]) + wide(self.far)
+        specs += [spec(lambda at: 0, False) for _ in others]
+        args += own + others
+        for group in groups:
+            pieces += group
+        counts.append(len(seconds))
+        width = width + sum(part.shape[1] for part in seconds)
+    for array in pieces:
+        specs.append(pl.BlockSpec(array.shape, lambda m, at: (0, 0)))
+        args.append(array)
+    kernel = partial(weight_kernel, ranks=ranks, counts=tuple(counts))
+    out = like((share, width), jnp.bfloat16)
+    tile = pl.BlockSpec((size, width), lambda m, at: (m, 0))
+    made = call_at(name, kernel, at, (steps,), specs, args, [(out, tile)])[0]
+    return (made, lax.psum_scatter(made, "ctx", scatter_dimension=0, tiled=True))
+
+
+def listed(*arrived):
+    return [list(group) for group in zip(*arrived, strict=True)]
 
 
 def body(
@@ -994,93 +960,89 @@
     given = partner(half_share("two_other", there, terms, True), CORE)
     two_back = half_share("two_own", here, terms, True, given)
     two_theirs = partner(two_back, CHIP)
-    down = WeightGrad(
-        "grad_down", grad_low, cot_columns, [activated], [[part] for part in act_sent], core, ctx_rank
-    )
-    two_theirs = after(two_theirs, act_sent, two_sent)
+    down_made, down_sum = weight_grad(
+        "grad_down", core, [(grad_low, cot_columns, [activated], listed(act_sent))], two_back
+    )
+    two_theirs = after(two_theirs, down_made, two_sent, gate_sent)
     grad_middle, mix_grad_mine, gain_two_sum = norm_grad(
         "norm_two_back", here, middle, grad_low, two_back, two_theirs, gain_two, (jnp.float32, jnp.bfloat16)
     )
 
     mix_grad_other = partner(mix_grad_mine, CORE)
     mix_sent = send_columns(mix_grad_mine)
-    down.whole(mix_grad_mine)
     grad_values, grad_gate_ssm = gated_back(
-        after(here, down.made), mix_grad_mine, mix_grad_other, ssm_out, gate_ssm, ssm_values
+        here, mix_grad_mine, mix_grad_other, ssm_out, gate_ssm, ssm_values
     )
     own_grad = scan.own_state(grad_values, small_rows, read_rows, False)
     z_sent = send_rows(grad_gate_ssm)
-    two_pair = (two_mine, two_other)
     two_columns = both_halves([after(part, mix_grad_mine) for part in two_sent])
-    gate = WeightGrad(
-        "grad_gate", two_pair, two_columns, [grad_gate], [[part] for part in gate_sent], core, ctx_rank
-    )
-    up = WeightGrad(
-        "grad_up", two_pair, two_columns, [grad_up], [[part] for part in up_sent], core, ctx_rank
-    )
-    outs = WeightGrad(
-        "grad_outs",
-        (mix_grad_mine, mix_grad_other),
-        both_halves(mix_sent),
-        [gated_rows, attended],
-        outs_sent,
-        core,
-        ctx_rank,
-    )
+    mlp_terms = [(activated, mlp_down, 0)]
 
     def fill_attend_back(sent):
-        grad_attended = rows_back(after(here, sent), mix_grad_mine, mix_grad_other, attn_out)
+        kept["mlp_given"] = partner(half_share("mlp_other", after(there, sent), mlp_terms, False), CORE)
+        kept["gate_up"] = weight_grad(
+            "grad_gate_up",
+            core,
+            [((two_mine, two_other), two_columns, [grad_gate, grad_up], listed(gate_sent, up_sent))],
+            sent,
+        )
+        grad_attended = rows_back(after(here, kept["gate_up"][0]), mix_grad_mine, mix_grad_other, attn_out)
         kept["grads"] = attend.back(rank, queries, grad_attended, kept["log"], key_rows, value_rows)
-        kept["query_sent"] = send_rows(kept["grads"][0])
-        return (kept["grads"][0], gate_sent, two_columns)
+        grad_query, grad_key, grad_value = kept["grads"]
+        kept["query_sent"] = send_rows(grad_query)
+        kept["kv_given"] = jnp.where(core == 0, grad_value, grad_key).astype(jnp.bfloat16)
+        return (grad_query, kept["kv_given"], kept["mlp_given"])
 
     def fill_scan_back(sent):
-        gate.whole(sent)
+        given = partner(after(kept["kv_given"], sent), CORE)
         kept["scan"] = scan.within_back(
-            source_rows, after(grad_values, gate.made), small_rows, write_rows, read_rows
+            source_rows, after(grad_values, sent), small_rows, write_rows, read_rows
         )
-        return (kept["scan"][0], up_sent)
+        _, grad_key, grad_value = kept["grads"]
+        own_part = jnp.where(core == 0, grad_key, grad_value)
+        paired = (own_part + given.astype(jnp.float32)).reshape(ctx_count, tokens, AHEAD_DIM)
+        kept["kv"] = [paired[0]] + [paired[shift].astype(jnp.bfloat16) for shift in range(1, ctx_count)]
+        return (kept["scan"][0], kept["kv"], mix_sent, z_sent, kept["query_sent"])
 
     def fill_weights(sent):
-        up.whole(sent)
-        return (up.made,)
+        kept["kv_back"] = [
+            moved(after(part, sent), "ctx", -shift) for shift, part in enumerate(kept["kv"]) if shift
+        ]
+        kept["mlp_mine"] = half_share("mlp_own", after(here, sent), mlp_terms, False, kept["mlp_given"])
+        mix_columns = both_halves([after(part, sent) for part in mix_sent])
+        kept["mixer"] = weight_grad(
+            "grad_mixer",
+            core,
+            [
+                ((mix_grad_mine, mix_grad_other), mix_columns, [gated_rows, attended], outs_sent),
+                (
+                    input_one,
+                    one_columns,
+                    [grad_gate_ssm, kept["grads"][0]],
+                    listed(z_sent, kept["query_sent"]),
+                ),
+            ],
+            kept["mlp_mine"],
+        )
+        return (kept["mixer"][0],)
 
     leaving = chained(own_grad, running[:, -1], False, [fill_attend_back, fill_scan_back, fill_weights])
-    leaving = after(leaving, down.total)
-    grad_query, grad_key, grad_value = kept["grads"]
-    own_part = jnp.where(core == 0, grad_key, grad_value)
-    given = partner(after(jnp.where(core == 0, grad_value, grad_key).astype(jnp.bfloat16), leaving), CORE)
+    grad_query = kept["grads"][0]
     grad_written, scan_sums, grad_b, grad_c = kept["scan"]
     grad_source, steps, grad_b, grad_c = scan.carried_back(
         source_rows, grad_values, small_rows, scan_sums, grad_written,
         write_rows, read_rows, entering, leaving, grad_b, grad_c,
     )
     source_sent = send_rows(grad_source)
-    paired = (own_part + given.astype(jnp.float32)).reshape(ctx_count, tokens, AHEAD_DIM)
-    kv_sent_back = [
-        moved(paired[shift].astype(jnp.bfloat16), "ctx", -shift) for shift in range(1, ctx_count)
-    ]
     grad_bc = jnp.concatenate([grad_b, grad_c], axis=1)
     bc_sent = partner(cut(grad_bc, 1 - core, 2 * bc_share, 1).astype(jnp.bfloat16), CORE)
     bc_mine = cut(grad_bc, core, 2 * bc_share, 1) + bc_sent.astype(jnp.float32)
     bc_given = partner(cut(bc_mine, 1 - chip, bc_share, 1).astype(jnp.bfloat16), CHIP)
     grad_bc_low = (cut(bc_mine, chip, bc_share, 1) + bc_given.astype(jnp.float32)).astype(jnp.bfloat16)
-    kv_sum = paired[0]
-    for part in kv_sent_back:
+    kv_sum = kept["kv"][0]
+    for part in kept["kv_back"]:
         kv_sum = kv_sum + part.astype(jnp.float32)
     grad_kv_low = kv_sum.astype(jnp.bfloat16)
-    first = WeightGrad(
-        "grad_first",
-        input_one,
-        one_columns,
-        [grad_gate_ssm, grad_query],
-        [[gate, query] for gate, query in zip(z_sent, kept["query_sent"], strict=True)],
-        core,
-        ctx_rank,
-    )
-    outs.whole(grad_source)
-    first.whole(outs.made)
-
     grad_dt_pre = steps[:, 0:2].reshape(heads_local, tokens) * jax.nn.sigmoid(dt_pre)
     flow_rows = steps[:, 2:4].reshape(heads_local, tokens)
     grad_dt_bias = jnp.sum(grad_dt_pre, axis=1)
@@ -1095,70 +1057,66 @@
         (grad_query, attn_q, 0),
         (grad_small, weight_small, 0),
     ]
-    given = partner(half_share("one_other", after(there, first.made), terms, True), CORE)
-    one_back = half_share("one_own", after(here, source_sent), terms, True, given)
+    mlp_theirs = partner(after(kept["mlp_mine"], grad_bc_low), CHIP)
+    given = partner(half_share("one_other", after(there, source_sent, down_sum, kept["gate_up"][1]), terms, True), CORE)
+    one_back = half_share("one_own", after(here, mlp_theirs), terms, True, given)
     one_theirs = partner(one_back, CHIP)
-    source = WeightGrad(
-        "grad_source", input_one, one_columns, [grad_source], [[part] for part in source_sent], core, ctx_rank
-    )
-    little = WeightGrad(
-        "grad_little", input_one, one_columns, [grad_small], [[part] for part in small_sent], core, ctx_rank
-    )
-    little.start(one_back)
-    source.start(little.sent)
-    terms = [(activated, mlp_down, 0)]
-    given = partner(half_share("mlp_other", after(there, source.sent), terms, False), CORE)
-    mlp_mine = half_share("mlp_own", here, terms, False, given)
-    mlp_theirs = partner(mlp_mine, CHIP)
-    one_theirs = after(one_theirs, mlp_mine, gate.total)
+    last_made, last_sum = weight_grad(
+        "grad_last",
+        core,
+        [(input_one, one_columns, [grad_source, grad_small], listed(source_sent, small_sent))],
+        one_back,
+    )
+    one_theirs = after(one_theirs, last_made, kept["mixer"][1])
     hidden_mine, gain_one_sum = norm_grad(
         "norm_one_back", here, hidden_rows, grad_middle, one_back, one_theirs, gain_one, (jnp.bfloat16,)
     )
     grad_hidden = gather_rows(hidden_mine, core)
-    little.turn(hidden_mine)
-    source.turn(little.kept)
-    mlp_total = mlp_mine.astype(jnp.float32) + after(mlp_theirs, source.kept).astype(jnp.float32)
+    mlp_total = wide(kept["mlp_mine"]) + wide(after(mlp_theirs, hidden_mine))
     block_out = middle + mlp_total
     output = gather_rows(block_out.astype(jnp.bfloat16), core)
-
-    grad_little = little.end()
-    held = narrow(grad_little[:, : AHEAD_DIM + bc_share])
-    pieces = jnp.stack([held] + [partner(held, stride) for stride in range(1, 4)])
-
-    def of_rank(rank):
-        return lax.dynamic_index_in_dim(pieces, tensor_rank ^ rank, 0, keepdims=False).astype(jnp.float32)
-
-    by_rank = [of_rank(rank) for rank in range(4)]
-    kv_rows = held.shape[0] // 4
-    kv_parts = [cut(part[:, :AHEAD_DIM], tensor_rank, kv_rows, 0) for part in by_rank]
-    grad_attn_kv = jnp.stack(
-        [jnp.concatenate([kv_parts[kind], kv_parts[2 + kind]], axis=1) for kind in range(2)], axis=1
-    )
-    grad_ssm_bc = jnp.concatenate(
-        [by_rank[2 * (place % 2) + place // 2][:, AHEAD_DIM:] for place in range(4)], axis=1
-    ).reshape(-1, 2, state_width)
-    grad_ssm_dt = grad_little[:, AHEAD_DIM + bc_share : AHEAD_DIM + bc_share + heads_local]
-
     squares = jnp.stack([jnp.sum(mix_squares), jnp.sum(mlp_total * mlp_total), jnp.sum(block_out * block_out)])
     halves = jnp.concatenate([gain_one_sum[0], gain_two_sum[0], squares])
     halves = halves + partner(halves, CORE)
     sums = jnp.concatenate([halves, grad_dt_bias, grad_a_log, grad_d_skip])
     sums = jnp.pad(sums, (0, -sums.shape[0] % 1024)).reshape(-1, 128)
     sums = all_sum(all_sum(sums, "dp"), "ctx").reshape(-1)
+
+    grad_last = wide(after(last_sum, kept["mixer"][1], sums))
+    grad_little = grad_last[:, inner_local:]
+    held = narrow(grad_little[:, : AHEAD_DIM + bc_share])
+    pieces = jnp.stack([held] + [partner(held, stride) for stride in range(1, 4)])
+
+    def of_rank(rank):
+        return lax.dynamic_index_in_dim(pieces, tensor_rank ^ rank, 0, keepdims=False).astype(jnp.float32)
+
+    by_rank = [of_rank(rank) for rank in range(4)]
+    kv_rows = held.shape[0] // 4
+    kv_parts = [cut(part[:, :AHEAD_DIM], tensor_rank, kv_rows, 0) for part in by_rank]
+    grad_attn_kv = jnp.stack(
+        [jnp.concatenate([kv_parts[kind], kv_parts[2 + kind]], axis=1) for kind in range(2)], axis=1
+    )
+    grad_ssm_bc = jnp.concatenate(
+        [by_rank[2 * (place % 2) + place // 2][:, AHEAD_DIM:] for place in range(4)], axis=1
+    ).reshape(-1, 2, state_width)
+    grad_ssm_dt = grad_little[:, AHEAD_DIM + bc_share : AHEAD_DIM + bc_share + heads_local]
+
     place = lax.axis_index("dp") * ctx_count + ctx_rank
     share = model_width // (lax.axis_size("dp") * ctx_count)
     small = sums[2 * model_width :]
     counted = tokens * model_width * lax.axis_size("dp") * ctx_count
-    grad_down = wide(down.total)
-    grad_gate_up = jnp.stack([wide(gate.total), wide(after(up.total, grad_down))], axis=1)
-    grad_outs = wide(after(outs.total, grad_gate_up))
-    grad_first = wide(after(first.total, grad_outs))
+    grad_down = wide(down_sum)
+    grad_gate_up = wide(after(kept["gate_up"][1], grad_down)).reshape(-1, 2, ff_local)
+    grad_mixer = wide(after(kept["mixer"][1], grad_gate_up))
+    outs_width = inner_local + heads_query * AHEAD_DIM
+    grad_outs = grad_mixer[:, :outs_width]
+    grad_first = grad_mixer[:, outs_width:]
     branch_rms = jnp.sqrt(small[:3] / counted)
     return (
         output[None],
         grad_hidden[None],
         cut(sums[:model_width], place, share, 0),
-        jnp.stack([grad_first[:, :inner_local], source.end()], axis=1),
+        jnp.stack([grad_first[:, :inner_local], grad_last[:, :inner_local]], axis=1),
         grad_ssm_bc,
         grad_ssm_dt,
         small[3 : 3 + heads_local],

time: 565 us -> 507 us (0.90)
  local copies, waits for them, and re-layouts: 134 us -> 107 us
  Pallas kernels: 134 us -> 118 us
  other arithmetic: 41.2 us -> 31.5 us
  starting transfers between devices: 55.1 us -> 47 us
    ppermute x17, waiting for transfers between devices: 74.3 us -> 112 us  [shifted(): lax.ppermute(value, axis, [(i, (i + shift) % count) for i in range(count)])]
    unnamed x300 -> x239, local copies, waits for them, and re-layouts: 104 us -> 73.3 us
    ppermute x4 -> x0, waiting for transfers between devices: 28.1 us -> none  [ctx_partner(): lax.ppermute(value, 'ctx', [(rank, rank ^ stride) for rank in range(4)])]
    ppermute x6, waiting for transfers between devices: 21.3 us -> 1.81 us  [moved(): return lax.ppermute(value, axis, pairs)]
    pallas_call x23 -> x18, Pallas kernels: 87.1 us -> 68.3 us  [call_at(): pl.pallas_call(kernel, name=name, grid_spec=pltpu.PrefetchScalarGridSpec(...]
    ppermute x6, waiting for transfers between devices: 15.5 us -> 28.2 us  [chained(): arrived = lax.ppermute(sent, 'ctx', [pair])]
    ppermute x24, waiting for transfers between devices: 26.8 us -> 17 us  [partner(): lax.ppermute(value, 'tensor', [(rank, rank ^ stride) for rank in range(4)])]
    reduce_scatter x5 -> x4, waiting for transfers between devices: 0.03 us -> 9.04 us  [weight_grad(): lax.psum_scatter(made, 'ctx', scatter_dimension=0, tiled=True)]
  transfers between devices with their start and end apart: 62 -> 57, of which waited for: 21 -> 24; matrix products, arithmetic and copies ran while one was open for 16% -> 16% of each run, Pallas kernels for 17% -> 17%
where the time goes in v5:
time: 507 us; the launch traced here: 499 us
  waiting for transfers between devices  168 us (33%)
  Pallas kernels  118 us (23%)
  local copies, waits for them, and re-layouts  107 us (21%)
  starting transfers between devices  47 us (9%)
  other arithmetic  31.5 us (6%)
  between operations  16.1 us (3%)
  matrix products  10.4 us (2%)
    ppermute x17, waiting for transfers between devices, shifted(): lax.ppermute(value, axis, [(i, (i + shift) % count) for i in range(count)])  112 us
    unnamed x239, local copies, waits for them, and re-layouts  73.3 us
    pallas_call x18, Pallas kernels, call_at(): pl.pallas_call(kernel, name=name, grid_spec=pltpu.PrefetchScalarGridSpec(...  68.3 us
    pallas_call x11, Pallas kernels, call(): pl.pallas_call(kernel, name=name, grid=grid, in_specs=specs, out_specs=[s...  50.1 us
    ppermute x6, waiting for transfers between devices, chained(): arrived = lax.ppermute(sent, 'ctx', [pair])  28.2 us
    ppermute x24, waiting for transfers between devices, partner(): lax.ppermute(value, 'tensor', [(rank, rank ^ stride) for rank in range(4)])  17 us
    ppermute x17, starting transfers between devices, shifted(): lax.ppermute(value, axis, [(i, (i + shift) % count) for i in range(count)])  16.3 us
    ppermute x6, starting transfers between devices, moved(): return lax.ppermute(value, axis, pairs)  15.9 us
  transfers between devices with their start and end apart: 57, of which 24 were waited for; matrix products, arithmetic and copies ran while one was open for 16% of the time, Pallas kernels for 17%

profile of v5, /device:TPU:0, one launch (start us, length us, event | category | flops | bytes accessed | tf_op | source)
XLA Modules:
  0.0 498.6 jit_solution(8753921248214480220)
XLA Ops:
  9.7 2.0 copy.99
  17.7 2.2 copy.101
  23.8 2.5 project_u.1.u_ref
  26.4 3.3 own_state.2
  29.7 2.0 fusion.26
  32.3 7.6 %collective-permute-start.5 = (bf16[512,128]{1,0:T(8,128)(2,1)}, bf16[512,128]{1,0:T(8,128)(2,1)}, u32[]{:S(2)}, u32[]{:S(2)}) collective-permute-start(bf16[512,128]{1,0:T(8,128)(2,1)} %dynamic-slice_convert_fusion.1), channel_id=1, source_target_pairs={{0,12},{1,13},{2,14},{3,15},{16,28},{17,29},{18,30},{19,31}} | collective-permute-start | bytes 393224 | tf_op jit(solution)/shard_map/ppermute | solution.py:35
  39.9 1.9 collective-permute-start.4
  41.9 2.5 collective-permute-start.3
  44.4 2.2 collective-permute-start
  46.6 2.1 dynamic_slice.90
  50.3 2.8 copy-done.5
  53.1 2.5 project_z.1.z_ref.gate_ref
  56.7 3.2 scan.1.y_ref
  65.6 2.1 convolution_convert_fusion.1.q_ref
  71.3 6.7 %attend.1 = (bf16[512,256]{1,0:T(8,128)(2,1)S(1)}, f32[2,8,512]{2,1,0:T(8,128)S(1)}) custom-call(s32[1]{0:T(128)} %bitcast.7.rank_ref, bf16[512,256]{1,0:T(8,128)(2,1)S(1)} %convolution_convert_fusion.1.q_ref, bf16[2048,128]{1,0:T(8,128)(2,1)S(1)} %get-tuple-element.233.k_ref, bf16[2048,128]{1,0:T(8,128)(2,1)S(1)} %get-tuple-element.232.v_ref), custom_call_target="tpu_custom_call" | custom-call | flops 1 | bytes 1 | tf_op jit(solution)/shard_map/attend/pallas_call | solution.py:380
  80.3 3.7 fusion.27.dact_ref
  85.6 2.0 carry.1
  88.7 3.0 mix_other.1
  92.3 2.3 collective-permute-done.9.refs_4_
  94.6 3.4 mix_own.1.mine_ref
  107.7 2.0 copy.86
  109.7 10.4 %copy.103 = bf16[256,8,2,1024]{3,1,2,0:T(8,128)(2,1)} copy(bf16[256,8,2,1024]{3,2,1,0:T(2,128)(2,1)} %bitcast.116) | data formatting | bytes 16777216
  121.6 3.4 collective-permute-done.14.refs_11_
  125.0 2.4 norm_two.1
  128.8 2.7 collective-permute-done.15.other_ref.refs_1_
  131.4 3.4 copy-done.2
  134.8 7.4 %expand.1 = (bf16[512,1024]{1,0:T(8,128)(2,1)S(1)}, bf16[512,1024]{1,0:T(8,128)(2,1)S(1)}, bf16[512,1024]{1,0:T(8,128)(2,1)S(1)}) custom-call(s32[1]{0:T(128)} %bitcast.at_ref, bf16[256,2048]{1,0:T(8,128)(2,1)S(1)} %get-tuple-element.100.mine_ref.refs_0_, bf16[256,2048]{1,0:T(8,128)(2,1)S(1)} %collective-permute-done.15.other_ref.refs_1_, ...), custom_call_target="tpu_custom_call" | custom-call | flops 1 | bytes 1 | tf_op jit(solution)/shard_map/expand/pallas_call | solution.py:516
  142.3 3.2 two_other.1
  148.3 3.3 two_own.1.mine_ref
  152.6 18.6 %collective-permute-done.18.refs_5_ = bf16[512,1024]{1,0:T(8,128)(2,1)S(1)} collective-permute-done((bf16[512,1024]{1,0:T(8,128)(2,1)S(1)}, bf16[512,1024]{1,0:T(8,128)(2,1)S(1)}, u32[]{:S(2)}, u32[]{:S(2)}) %collective-permute-start.18) | collective-permute-done | bytes 1048608 | tf_op jit(solution)/shard_map/ppermute | solution.py:29
  171.2 5.0 grad_down.1
  181.5 32.4 %collective-permute-done.19.refs_2_ = bf16[256,1024]{1,0:T(8,128)(2,1)S(1)} collective-permute-done((bf16[256,1024]{1,0:T(8,128)(2,1)S(1)}, bf16[256,1024]{1,0:T(8,128)(2,1)S(1)}, u32[]{:S(2)}, u32[]{:S(2)}) %collective-permute-start.19) | collective-permute-done | bytes 524320 | tf_op jit(solution)/shard_map/ppermute | solution.py:29
  225.5 2.9 gated_back.1
  230.3 2.3 own_state.3
  233.4 13.6 %collective-permute-done.24.refs_7_ = bf16[512,1024]{1,0:T(8,128)(2,1)S(1)} collective-permute-done((bf16[512,1024]{1,0:T(8,128)(2,1)S(1)}, bf16[512,1024]{1,0:T(8,128)(2,1)S(1)}, u32[]{:S(2)}, u32[]{:S(2)}) %collective-permute-start.24) | collective-permute-done | bytes 1048608 | tf_op jit(solution)/shard_map/ppermute | solution.py:29
  247.1 6.2 %grad_gate_up.1 = bf16[1024,2048]{1,0:T(8,128)(2,1)S(1)} custom-call(s32[2]{0:T(128)S(1)} %pad_add_fusion.at_ref, bf16[256,2048]{1,0:T(8,128)(2,1)S(1)} %copy-done.51, bf16[256,2048]{1,0:T(8,128)(2,1)S(1)} %copy-done.61, bf16[256,1024]{1,0:T(8,128)(2,1)S(1)} %collective-permute-done.19.refs_2_, bf16[256,1024]{1,0:T(8,128)(2,1)S(1)} %collective-permute-done.23.refs_3_, ...), custom_call_target="tpu_custom_call" | custom-call | flops 1 | bytes 1 | tf_op jit(solution)/shard_map/grad_gate_up/pallas_call | solution.py:516
  253.2 2.0 copy-done.20
  255.3 2.2 copy-done.18
  262.4 8.8 %attend_back.1 = (bf16[512,256]{1,0:T(8,128)(2,1)S(1)}, f32[2048,128]{1,0:T(8,128)S(1)}, f32[2048,128]{1,0:T(8,128)S(1)}) custom-call(s32[1]{0:T(128)} %bitcast.7.rank_ref, bf16[512,256]{1,0:T(8,128)(2,1)S(1)} %copy-done.82, bf16[512,256]{1,0:T(8,128)(2,1)S(1)} %attended_back.1.do_ref, f32[2,8,512]{2,1,0:T(8,128)S(1)} %copy-done.89, ...), custom_call_target="tpu_custom_call" | custom-call | flops 1 | bytes 1 | tf_op jit(solution)/shard_map/attend_back/pallas_call | solution.py:380
  276.6 9.5 %scan_back.1 = (f32[512,768]{1,0:T(8,128)S(1)}, f32[6,8,512]{2,1,0:T(8,128)S(1)}, f32[512,256]{1,0:T(8,128)S(1)}, f32[512,256]{1,0:T(8,128)S(1)}) custom-call(bf16[512,768]{1,0:T(8,128)(2,1)S(1)} %project_u.1.u_ref, bf16[512,768]{1,0:T(8,128)(2,1)S(1)} %copy-done.49, f32[6,8,512]{2,1,0:T(8,128)S(1)} %reshape.167.small_ref, ...), custom_call_target="tpu_custom_call" | custom-call | flops 1 | bytes 1 | tf_op jit(solution)/shard_map/scan_back/pallas_call | solution.py:380
  289.7 2.8 collective-permute-done.30.refs_15_
  292.4 16.1 %collective-permute-done.29.refs_14_ = bf16[512,768]{1,0:T(8,128)(2,1)S(1)} collective-permute-done((bf16[512,768]{1,0:T(8,128)(2,1)S(1)}, bf16[512,768]{1,0:T(8,128)(2,1)S(1)}, u32[]{:S(2)}, u32[]{:S(2)}) %collective-permute-start.29) | collective-permute-done | bytes 786464 | tf_op jit(solution)/shard_map/ppermute | solution.py:29
  309.5 2.6 mlp_own.1
  312.1 7.9 %grad_mixer.1 = bf16[1024,2048]{1,0:T(8,128)(2,1)S(1)} custom-call(s32[2]{0:T(128)S(1)} %pad_add_fusion.at_ref, bf16[256,2048]{1,0:T(8,128)(2,1)S(1)} %copy-done.26, bf16[256,2048]{1,0:T(8,128)(2,1)S(1)} %copy-done.33, bf16[256,1024]{1,0:T(8,128)(2,1)S(1)} %collective-permute-done.28.refs_2_, bf16[256,1024]{1,0:T(8,128)(2,1)S(1)} %collective-permute-done.32.refs_3_, ...), custom_call_target="tpu_custom_call" | custom-call | flops 1 | bytes 1 | tf_op jit(solution)/shard_map/grad_mixer/pallas_call | solution.py:516
  320.0 2.1 copy-done.16
  327.5 28.2 %collective-permute-done.31 = bf16[768,256]{1,0:T(8,128)(2,1)} collective-permute-done((bf16[768,256]{1,0:T(8,128)(2,1)}, bf16[768,256]{1,0:T(8,128)(2,1)}, u32[]{:S(2)}, u32[]{:S(2)}) %collective-permute-start.31) | collective-permute-done | bytes 393248 | tf_op jit(solution)/shard_map/ppermute | solution.py:90
  355.7 2.1 add_add_fusion.grad_ref
  357.8 8.5 %carry_back.1 = (bf16[512,768]{1,0:T(8,128)(2,1)}, f32[6,8,512]{2,1,0:T(8,128)}, f32[512,256]{1,0:T(8,128)}, f32[512,256]{1,0:T(8,128)}) custom-call(bf16[512,768]{1,0:T(8,128)(2,1)} %copy-done.12, bf16[512,768]{1,0:T(8,128)(2,1)} %copy-done.48, f32[6,8,512]{2,1,0:T(8,128)} %copy-done.55, f32[6,8,512]{2,1,0:T(8,128)} %copy-done.85, f32[512,768]{1,0:T(8,128)} %copy-done.80, ...), custom_call_target="tpu_custom_call" | custom-call | flops 1 | bytes 1 | tf_op jit(solution)/shard_map/carry_back/pallas_call | solution.py:380
  376.8 2.9 collective-permute-done.34
  380.1 12.1 %collective-permute-done.39.refs_6_ = bf16[512,768]{1,0:T(8,128)(2,1)} collective-permute-done((bf16[512,768]{1,0:T(8,128)(2,1)}, bf16[512,768]{1,0:T(8,128)(2,1)}, u32[]{:S(2)}, u32[]{:S(2)}) %collective-permute-start.39) | collective-permute-done | bytes 786464 | tf_op jit(solution)/shard_map/ppermute | solution.py:29
  392.3 2.9 copy-done.6
  398.9 3.6 one_other.1
  405.2 4.1 one_own.1.mine_ref
  410.0 10.6 %collective-permute-done.42.refs_7_ = bf16[512,384]{1,0:T(8,128)(2,1)S(1)} collective-permute-done((bf16[512,384]{1,0:T(8,128)(2,1)S(1)}, bf16[512,384]{1,0:T(8,128)(2,1)S(1)}, u32[]{:S(2)}, u32[]{:S(2)}) %collective-permute-start.42) | collective-permute-done | bytes 393248 | tf_op jit(solution)/shard_map/ppermute | solution.py:29
  420.6 5.6 %grad_last.1 = bf16[1024,1152]{1,0:T(8,128)(2,1)S(1)} custom-call(s32[2]{0:T(128)S(1)} %pad_add_fusion.at_ref, bf16[512,2048]{1,0:T(8,128)(2,1)S(1)} %norm_one.1.x_ref.refs_4_.refs_5_.refs_0_.refs_1_, bf16[512,2048]{1,0:T(8,128)(2,1)S(1)} %norm_one.1.x_ref.refs_4_.refs_5_.refs_0_.refs_1_, bf16[256,1024]{1,0:T(8,128)(2,1)S(1)} %copy-done.75, ...), custom_call_target="tpu_custom_call" | custom-call | flops 1 | bytes 1 | tf_op jit(solution)/shard_map/grad_last/pallas_call | solution.py:516
  432.3 2.6 collective-permute-done.41.theirs_ref
  436.5 3.3 norm_one_back.1
  439.9 3.8 multiply_reduce_fusion
  443.7 2.0 concatenate.40
  447.1 4.1 reshape.178
  454.4 2.1 collective-permute-done.46
  460.3 2.3 copy.94
  472.6 7.6 %reduce-scatter.11.cloned.1.call-done = bf16[256,1152]{1,0:T(8,128)(2,1)} async-done(((bf16[1024,1152]{1,0:T(8,128)(2,1)}), bf16[256,1152]{1,0:T(8,128)(2,1)}) %reduce-scatter.11.cloned.1.call-update) | async-done | bytes 589840 | tf_op jit(solution)/shard_map/reduce_scatter | solution.py:824
  486.2 2.4 copy.92
  (433 shorter events, 138.7 us)
Async XLA Ops:
  7.2 372.9 %reduce-scatter.5.cloned.1.call-start = ((), (), s32[]{:S(2)}) async-start(), calls=%async_computation.4 | async-start | bytes 2621440 | tf_op jit(solution)/shard_map/reduce_scatter | solution.py:824
  17.7 258.9 %copy-start.55 = (f32[6,8,512]{2,1,0:T(8,128)}, f32[6,8,512]{2,1,0:T(8,128)S(1)}, u32[]{:S(2)}) copy-start(f32[6,8,512]{2,1,0:T(8,128)S(1)} %reshape.167.small_ref) | copy-start | bytes 294916
  21.2 255.3 %copy-start.38 = (bf16[512,256]{1,0:T(8,128)(2,1)}, bf16[512,256]{1,0:T(8,128)(2,1)S(1)}, u32[]{:S(2)}) copy-start(bf16[512,256]{1,0:T(8,128)(2,1)S(1)} %get-tuple-element.244.c_ref.b_ref) | copy-start | bytes 786436
  21.2 255.3 %copy-start.52 = (bf16[512,256]{1,0:T(8,128)(2,1)}, bf16[512,256]{1,0:T(8,128)(2,1)S(1)}, u32[]{:S(2)}) copy-start(bf16[512,256]{1,0:T(8,128)(2,1)S(1)} %get-tuple-element.245.b_ref) | copy-start | bytes 786436
  26.4 250.2 %copy-start.12 = (bf16[512,768]{1,0:T(8,128)(2,1)}, bf16[512,768]{1,0:T(8,128)(2,1)S(1)}, u32[]{:S(2)}) copy-start(bf16[512,768]{1,0:T(8,128)(2,1)S(1)} %project_u.1.u_ref) | copy-start | bytes 2359300
  32.3 31.5 %collective-permute-start.5 = (bf16[512,128]{1,0:T(8,128)(2,1)}, bf16[512,128]{1,0:T(8,128)(2,1)}, u32[]{:S(2)}, u32[]{:S(2)}) collective-permute-start(bf16[512,128]{1,0:T(8,128)(2,1)} %dynamic-slice_convert_fusion.1), channel_id=1, source_target_pairs={{0,12},{1,13},{2,14},{3,15},{16,28},{17,29},{18,30},{19,31}} | collective-permute-start | bytes 393224 | tf_op jit(solution)/shard_map/ppermute | solution.py:35
  39.9 24.5 %collective-permute-start.4 = (bf16[512,128]{1,0:T(8,128)(2,1)}, bf16[512,128]{1,0:T(8,128)(2,1)}, u32[]{:S(2)}, u32[]{:S(2)}) collective-permute-start(bf16[512,128]{1,0:T(8,128)(2,1)} %dynamic-slice_convert_fusion.1), channel_id=1, source_target_pairs={{0,8},{4,12},{1,9},{5,13},{2,10},{6,14},{3,11},{7,15},{16,24},{20,... | collective-permute-start | bytes 393224 | tf_op jit(solution)/shard_map/ppermute | solution.py:35
  41.9 22.5 %collective-permute-start.3 = (bf16[512,128]{1,0:T(8,128)(2,1)}, bf16[512,128]{1,0:T(8,128)(2,1)}, u32[]{:S(2)}, u32[]{:S(2)}) collective-permute-start(bf16[512,128]{1,0:T(8,128)(2,1)} %dynamic-slice_convert_fusion.1), channel_id=1, source_target_pairs={{0,4},{4,8},{8,12},{1,5},{5,9},{9,13},{2,6},{6,10},{10,14},{3,7},{... | collective-permute-start | bytes 393224 | tf_op jit(solution)/shard_map/ppermute | solution.py:35
  44.4 23.4 %collective-permute-start = (bf16[768,256]{1,0:T(8,128)(2,1)}, bf16[768,256]{1,0:T(8,128)(2,1)}, u32[]{:S(2)}, u32[]{:S(2)}) collective-permute-start(bf16[768,256]{1,0:T(8,128)(2,1)} %own_state.2), channel_id=1, source_target_pairs={{0,4},{1,5},{2,6},{3,7},{16,20},{17,21},{18,22},{19,23}} | collective-permute-start | bytes 1179656 | tf_op jit(solution)/shard_map/ppermute | solution.py:90
  48.8 19.0 %collective-permute-start.1 = (bf16[256,1024]{1,0:T(8,128)(2,1)}, bf16[256,1024]{1,0:T(8,128)(2,1)}, u32[]{:S(2)}, u32[]{:S(2)}) collective-permute-start(bf16[256,1024]{1,0:T(8,128)(2,1)} %dynamic_slice.90), channel_id=1, source_target_pairs={{0,16},{16,0},{1,17},{17,1},{2,18},{18,2},{3,19},{19,3},{4,20},{20... | collective-permute-start | bytes 1572872 | tf_op jit(solution)/shard_map/ppermute | solution.py:29
  63.9 14.2 %collective-permute-start.7 = (bf16[256,1024]{1,0:T(8,128)(2,1)}, bf16[256,1024]{1,0:T(8,128)(2,1)S(1)}, u32[]{:S(2)}, u32[]{:S(2)}) collective-permute-start(bf16[256,1024]{1,0:T(8,128)(2,1)} %dynamic_slice.93), channel_id=1, source_target_pairs={{0,16},{16,0},{1,17},{17,1},{2,18},{18,2},{3,19},{19,3},{4,20},{20... | collective-permute-start | bytes 1572872 | tf_op jit(solution)/shard_map/ppermute | solution.py:29
  65.5 4.3 collective-permute-start.6
  69.2 9.0 %collective-permute-start.2 = (bf16[768,256]{1,0:T(8,128)(2,1)S(1)}, bf16[768,256]{1,0:T(8,128)(2,1)S(1)}, u32[]{:S(2)}, u32[]{:S(2)}) collective-permute-start(bf16[768,256]{1,0:T(8,128)(2,1)S(1)} %fusion.5), channel_id=1, source_target_pairs={{4,8},{5,9},{6,10},{7,11},{20,24},{21,25},{22,26},{23,27}} | collective-permute-start | bytes 1179656 | tf_op jit(solution)/shard_map/ppermute | solution.py:90
  79.6 4.4 collective-permute-start.8
  91.7 2.8 collective-permute-start.9
  98.0 27.0 %collective-permute-start.10 = (bf16[256,2048]{1,0:T(8,128)(2,1)}, bf16[256,2048]{1,0:T(8,128)(2,1)}, u32[]{:S(2)}, u32[]{:S(2)}) collective-permute-start(bf16[256,2048]{1,0:T(8,128)(2,1)} %mix_own.1.mine_ref), channel_id=1, source_target_pairs={{0,2},{1,3},{2,0},{3,1},{4,6},{5,7},{6,4},{7,5},{8,10},{9,11},{10,... | collective-permute-start | bytes 3145736 | tf_op jit(solution)/shard_map/ppermute | solution.py:24
  99.5 25.5 %collective-permute-start.13 = (bf16[512,768]{1,0:T(8,128)(2,1)}, bf16[512,768]{1,0:T(8,128)(2,1)}, u32[]{:S(2)}, u32[]{:S(2)}) collective-permute-start(bf16[512,768]{1,0:T(8,128)(2,1)} %get-tuple-element.93.refs_0_.refs_8_), channel_id=1, source_target_pairs={{0,16},{16,0},{1,17},{17,1},{2,18},{18,2},{3,19},{19,3},{4,20},{20... | collective-permute-start | bytes 2359304 | tf_op jit(solution)/shard_map/ppermute | solution.py:29
  101.0 23.9 %collective-permute-start.11 = (bf16[256,1024]{1,0:T(8,128)(2,1)}, bf16[256,1024]{1,0:T(8,128)(2,1)}, u32[]{:S(2)}, u32[]{:S(2)}) collective-permute-start(bf16[256,1024]{1,0:T(8,128)(2,1)} %collective-permute-done.1.refs_2_), channel_id=1, source_target_pairs={{0,1},{1,0},{2,3},{3,2},{4,5},{5,4},{6,7},{7,6},{8,9},{9,8},{10,11... | collective-permute-start | bytes 1572872 | tf_op jit(solution)/shard_map/ppermute | solution.py:24
  101.0 23.9 %collective-permute-start.12 = (bf16[256,1024]{1,0:T(8,128)(2,1)}, bf16[256,1024]{1,0:T(8,128)(2,1)}, u32[]{:S(2)}, u32[]{:S(2)}) collective-permute-start(bf16[256,1024]{1,0:T(8,128)(2,1)} %copy-done.73), channel_id=1, source_target_pairs={{0,1},{1,0},{2,3},{3,2},{4,5},{5,4},{6,7},{7,6},{8,9},{9,8},{10,11... | collective-permute-start | bytes 1572872 | tf_op jit(solution)/shard_map/ppermute | solution.py:24
  105.3 19.7 %collective-permute-start.14 = (bf16[512,256]{1,0:T(8,128)(2,1)}, bf16[512,256]{1,0:T(8,128)(2,1)}, u32[]{:S(2)}, u32[]{:S(2)}) collective-permute-start(bf16[512,256]{1,0:T(8,128)(2,1)} %copy-done.70), channel_id=1, source_target_pairs={{0,16},{16,0},{1,17},{17,1},{2,18},{18,2},{3,19},{19,3},{4,20},{20... | collective-permute-start | bytes 786440 | tf_op jit(solution)/shard_map/ppermute | solution.py:29
  128.8 2.7 collective-permute-start.15
  142.3 28.9 %copy-start.34 = (bf16[512,1024]{1,0:T(8,128)(2,1)}, bf16[512,1024]{1,0:T(8,128)(2,1)S(1)}, u32[]{:S(2)}) copy-start(bf16[512,1024]{1,0:T(8,128)(2,1)S(1)} %get-tuple-element.104.refs_4_.refs_0_) | copy-start | bytes 3145732
  145.6 2.7 collective-permute-start.16
  145.8 25.4 %collective-permute-start.18 = (bf16[512,1024]{1,0:T(8,128)(2,1)S(1)}, bf16[512,1024]{1,0:T(8,128)(2,1)S(1)}, u32[]{:S(2)}, u32[]{:S(2)}) collective-permute-start(bf16[512,1024]{1,0:T(8,128)(2,1)S(1)} %get-tuple-element.104.refs_4_.refs_0_), channel_id=1, source_target_pairs={{0,16},{16,0},{1,17},{17,1},{2,18},{18,2},{3,19},{19,3},{4,20},{20... | collective-permute-start | bytes 3145736 | tf_op jit(solution)/shard_map/ppermute | solution.py:29
  177.5 214.7 %reduce-scatter.7.cloned.1.call-start = ((), (), s32[]{:S(2)}) async-start(), calls=%async_computation.5 | async-start | bytes 5242880 | tf_op jit(solution)/shard_map/reduce_scatter | solution.py:824
  177.7 36.1 %collective-permute-start.20 = (bf16[512,1024]{1,0:T(8,128)(2,1)}, bf16[512,1024]{1,0:T(8,128)(2,1)S(1)}, u32[]{:S(2)}, u32[]{:S(2)}) collective-permute-start(bf16[512,1024]{1,0:T(8,128)(2,1)} %copy-done.27), channel_id=1, source_target_pairs={{0,16},{16,0},{1,17},{17,1},{2,18},{18,2},{3,19},{19,3},{4,20},{20... | collective-permute-start | bytes 3145736 | tf_op jit(solution)/shard_map/ppermute | solution.py:29
  179.4 34.5 %collective-permute-start.17 = (bf16[256,2048]{1,0:T(8,128)(2,1)}, bf16[256,2048]{1,0:T(8,128)(2,1)S(1)}, u32[]{:S(2)}, u32[]{:S(2)}) collective-permute-start(bf16[256,2048]{1,0:T(8,128)(2,1)} %copy-done.62), channel_id=1, source_target_pairs={{0,2},{1,3},{2,0},{3,1},{4,6},{5,7},{6,4},{7,5},{8,10},{9,11},{10,... | collective-permute-start | bytes 3145736 | tf_op jit(solution)/shard_map/ppermute | solution.py:24
  181.0 32.9 %collective-permute-start.19 = (bf16[256,1024]{1,0:T(8,128)(2,1)S(1)}, bf16[256,1024]{1,0:T(8,128)(2,1)S(1)}, u32[]{:S(2)}, u32[]{:S(2)}) collective-permute-start(bf16[256,1024]{1,0:T(8,128)(2,1)S(1)} %constant_dynamic-slice_fusion.5), channel_id=1, source_target_pairs={{0,16},{16,0},{1,17},{17,1},{2,18},{18,2},{3,19},{19,3},{4,20},{20... | collective-permute-start | bytes 1572872 | tf_op jit(solution)/shard_map/ppermute | solution.py:29
  221.5 2.7 collective-permute-start.21
  221.5 25.6 %collective-permute-start.24 = (bf16[512,1024]{1,0:T(8,128)(2,1)S(1)}, bf16[512,1024]{1,0:T(8,128)(2,1)S(1)}, u32[]{:S(2)}, u32[]{:S(2)}) collective-permute-start(bf16[512,1024]{1,0:T(8,128)(2,1)S(1)} %copy-done.30), channel_id=1, source_target_pairs={{0,16},{16,0},{1,17},{17,1},{2,18},{18,2},{3,19},{19,3},{4,20},{20... | collective-permute-start | bytes 3145736 | tf_op jit(solution)/shard_map/ppermute | solution.py:29
  223.1 24.0 %collective-permute-start.23 = (bf16[256,1024]{1,0:T(8,128)(2,1)S(1)}, bf16[256,1024]{1,0:T(8,128)(2,1)S(1)}, u32[]{:S(2)}, u32[]{:S(2)}) collective-permute-start(bf16[256,1024]{1,0:T(8,128)(2,1)S(1)} %collective-permute-done.19.refs_2_), channel_id=1, source_target_pairs={{0,1},{1,0},{2,3},{3,2},{4,5},{5,4},{6,7},{7,6},{8,9},{9,8},{10,11... | collective-permute-start | bytes 1572872 | tf_op jit(solution)/shard_map/ppermute | solution.py:24
  255.3 177.1 %reduce-scatter.9.cloned.1.call-start = ((), (), s32[]{:S(2)}) async-start(), calls=%async_computation.6 | async-start | bytes 5242880 | tf_op jit(solution)/shard_map/reduce_scatter | solution.py:824
  260.6 10.7 %collective-permute-start.25 = (bf16[256,2048]{1,0:T(8,128)(2,1)S(1)}, bf16[256,2048]{1,0:T(8,128)(2,1)S(1)}, u32[]{:S(2)}, u32[]{:S(2)}) collective-permute-start(bf16[256,2048]{1,0:T(8,128)(2,1)S(1)} %mlp_other.1), channel_id=1, source_target_pairs={{0,1},{1,0},{2,3},{3,2},{4,5},{5,4},{6,7},{7,6},{8,9},{9,8},{10,11... | collective-permute-start | bytes 3145736 | tf_op jit(solution)/shard_map/ppermute | solution.py:24
  260.7 10.6 %collective-permute-start.22 = (bf16[768,256]{1,0:T(8,128)(2,1)S(1)}, bf16[768,256]{1,0:T(8,128)(2,1)S(1)}, u32[]{:S(2)}, u32[]{:S(2)}) collective-permute-start(bf16[768,256]{1,0:T(8,128)(2,1)S(1)} %copy-done.67), channel_id=1, source_target_pairs={{12,8},{13,9},{14,10},{15,11},{28,24},{29,25},{30,26},{31,27}} | collective-permute-start | bytes 1179656 | tf_op jit(solution)/shard_map/ppermute | solution.py:90
  271.1 41.0 %copy-start.68 = (bf16[512,256]{1,0:T(8,128)(2,1)}, bf16[512,256]{1,0:T(8,128)(2,1)S(1)}, u32[]{:S(2)}) copy-start(bf16[512,256]{1,0:T(8,128)(2,1)S(1)} %get-tuple-element.113.refs_13_.refs_2_) | copy-start | bytes 786436
  271.5 16.5 %collective-permute-start.27 = (bf16[2048,128]{1,0:T(8,128)(2,1)S(1)}, bf16[2048,128]{1,0:T(8,128)(2,1)S(1)}, u32[]{:S(2)}, u32[]{:S(2)}) collective-permute-start(bf16[2048,128]{1,0:T(8,128)(2,1)S(1)} %select_convert_fusion), channel_id=1, source_target_pairs={{0,1},{1,0},{2,3},{3,2},{4,5},{5,4},{6,7},{7,6},{8,9},{9,8},{10,11... | collective-permute-start | bytes 1572872 | tf_op jit(solution)/shard_map/ppermute | solution.py:24
  272.0 17.7 %collective-permute-start.28 = (bf16[256,1024]{1,0:T(8,128)(2,1)S(1)}, bf16[256,1024]{1,0:T(8,128)(2,1)S(1)}, u32[]{:S(2)}, u32[]{:S(2)}) collective-permute-start(bf16[256,1024]{1,0:T(8,128)(2,1)S(1)} %constant_dynamic-slice_fusion.4), channel_id=1, source_target_pairs={{0,16},{16,0},{1,17},{17,1},{2,18},{18,2},{3,19},{19,3},{4,20},{20... | collective-permute-start | bytes 1572872 | tf_op jit(solution)/shard_map/ppermute | solution.py:29
  273.6 18.8 %collective-permute-start.30 = (bf16[512,256]{1,0:T(8,128)(2,1)S(1)}, bf16[512,256]{1,0:T(8,128)(2,1)S(1)}, u32[]{:S(2)}, u32[]{:S(2)}) collective-permute-start(bf16[512,256]{1,0:T(8,128)(2,1)S(1)} %get-tuple-element.113.refs_13_.refs_2_), channel_id=1, source_target_pairs={{0,16},{16,0},{1,17},{17,1},{2,18},{18,2},{3,19},{19,3},{4,20},{20... | collective-permute-start | bytes 786440 | tf_op jit(solution)/shard_map/ppermute | solution.py:29
  274.1 34.4 %collective-permute-start.29 = (bf16[512,768]{1,0:T(8,128)(2,1)S(1)}, bf16[512,768]{1,0:T(8,128)(2,1)S(1)}, u32[]{:S(2)}, u32[]{:S(2)}) collective-permute-start(bf16[512,768]{1,0:T(8,128)(2,1)S(1)} %copy-done.44), channel_id=1, source_target_pairs={{0,16},{16,0},{1,17},{17,1},{2,18},{18,2},{3,19},{19,3},{4,20},{20... | collective-permute-start | bytes 2359304 | tf_op jit(solution)/shard_map/ppermute | solution.py:29
  275.6 32.9 %collective-permute-start.26 = (bf16[768,256]{1,0:T(8,128)(2,1)S(1)}, bf16[768,256]{1,0:T(8,128)(2,1)S(1)}, u32[]{:S(2)}, u32[]{:S(2)}) collective-permute-start(bf16[768,256]{1,0:T(8,128)(2,1)S(1)} %fusion.7), channel_id=1, source_target_pairs={{8,4},{9,5},{10,6},{11,7},{24,20},{25,21},{26,22},{27,23}} | collective-permute-start | bytes 1179656 | tf_op jit(solution)/shard_map/ppermute | solution.py:90
  309.5 2.6 collective-permute-start.32
  322.1 33.6 %copy-start.102 = (bf16[768,256]{1,0:T(8,128)(2,1)S(1)}, bf16[768,256]{1,0:T(8,128)(2,1)}, u32[]{:S(2)}) copy-start(bf16[768,256]{1,0:T(8,128)(2,1)} %copy-done.101) | copy-start | bytes 1179652
  322.1 158.1 %reduce-scatter.11.cloned.1.call-start = ((), (), s32[]{:S(2)}) async-start(), calls=%async_computation.7 | async-start | bytes 2949120 | tf_op jit(solution)/shard_map/reduce_scatter | solution.py:824
  322.2 33.5 %collective-permute-start.31 = (bf16[768,256]{1,0:T(8,128)(2,1)}, bf16[768,256]{1,0:T(8,128)(2,1)}, u32[]{:S(2)}, u32[]{:S(2)}) collective-permute-start(bf16[768,256]{1,0:T(8,128)(2,1)} %fusion.8), channel_id=1, source_target_pairs={{4,0},{5,1},{6,2},{7,3},{20,16},{21,17},{22,18},{23,19}} | collective-permute-start | bytes 1179656 | tf_op jit(solution)/shard_map/ppermute | solution.py:90
  323.6 47.5 %collective-permute-start.36 = (bf16[512,128]{1,0:T(8,128)(2,1)}, bf16[512,128]{1,0:T(8,128)(2,1)S(1)}, u32[]{:S(2)}, u32[]{:S(2)}) collective-permute-start(bf16[512,128]{1,0:T(8,128)(2,1)} %get-tuple-element.136), channel_id=1, source_target_pairs={{4,0},{8,4},{12,8},{5,1},{9,5},{13,9},{6,2},{10,6},{14,10},{7,3},{... | collective-permute-start | bytes 393224 | tf_op jit(solution)/shard_map/ppermute | solution.py:35
  324.9 46.3 %collective-permute-start.37 = (bf16[512,128]{1,0:T(8,128)(2,1)}, bf16[512,128]{1,0:T(8,128)(2,1)S(1)}, u32[]{:S(2)}, u32[]{:S(2)}) collective-permute-start(bf16[512,128]{1,0:T(8,128)(2,1)} %get-tuple-element.137), channel_id=1, source_target_pairs={{8,0},{12,4},{9,1},{13,5},{10,2},{14,6},{11,3},{15,7},{24,16},{28,... | collective-permute-start | bytes 393224 | tf_op jit(solution)/shard_map/ppermute | solution.py:35
  326.2 45.0 %collective-permute-start.38 = (bf16[512,128]{1,0:T(8,128)(2,1)}, bf16[512,128]{1,0:T(8,128)(2,1)S(1)}, u32[]{:S(2)}, u32[]{:S(2)}) collective-permute-start(bf16[512,128]{1,0:T(8,128)(2,1)} %get-tuple-element.138), channel_id=1, source_target_pairs={{12,0},{13,1},{14,2},{15,3},{28,16},{29,17},{30,18},{31,19}} | collective-permute-start | bytes 393224 | tf_op jit(solution)/shard_map/ppermute | solution.py:35
  369.4 4.1 collective-permute-start.33
  373.0 19.3 %collective-permute-start.39 = (bf16[512,768]{1,0:T(8,128)(2,1)}, bf16[512,768]{1,0:T(8,128)(2,1)}, u32[]{:S(2)}, u32[]{:S(2)}) collective-permute-start(bf16[512,768]{1,0:T(8,128)(2,1)} %get-tuple-element.135.refs_1_.refs_4_), channel_id=1, source_target_pairs={{0,16},{16,0},{1,17},{17,1},{2,18},{18,2},{3,19},{19,3},{4,20},{20... | collective-permute-start | bytes 2359304 | tf_op jit(solution)/shard_map/ppermute | solution.py:29
  374.7 5.0 %collective-permute-start.34 = (bf16[512,128]{1,0:T(8,128)(2,1)S(1)}, bf16[512,128]{1,0:T(8,128)(2,1)S(1)}, u32[]{:S(2)}, u32[]{:S(2)}) collective-permute-start(bf16[512,128]{1,0:T(8,128)(2,1)S(1)} %dynamic-slice_convert_fusion.2), channel_id=1, source_target_pairs={{0,2},{1,3},{2,0},{3,1},{4,6},{5,7},{6,4},{7,5},{8,10},{9,11},{10,... | collective-permute-start | bytes 393224 | tf_op jit(solution)/shard_map/ppermute | solution.py:24
  379.7 24.0 %collective-permute-start.35 = (bf16[256,2048]{1,0:T(8,128)(2,1)}, bf16[256,2048]{1,0:T(8,128)(2,1)}, u32[]{:S(2)}, u32[]{:S(2)}) collective-permute-start(bf16[256,2048]{1,0:T(8,128)(2,1)} %mlp_own.1), channel_id=1, source_target_pairs={{0,2},{1,3},{2,0},{3,1},{4,6},{5,7},{6,4},{7,5},{8,10},{9,11},{10,... | collective-permute-start | bytes 3145736 | tf_op jit(solution)/shard_map/ppermute | solution.py:24
  402.5 2.7 collective-permute-start.40
  409.4 25.5 %collective-permute-start.41 = (bf16[256,2048]{1,0:T(8,128)(2,1)}, bf16[256,2048]{1,0:T(8,128)(2,1)}, u32[]{:S(2)}, u32[]{:S(2)}) collective-permute-start(bf16[256,2048]{1,0:T(8,128)(2,1)} %one_own.1.mine_ref), channel_id=1, source_target_pairs={{0,2},{1,3},{2,0},{3,1},{4,6},{5,7},{6,4},{7,5},{8,10},{9,11},{10,... | collective-permute-start | bytes 3145736 | tf_op jit(solution)/shard_map/ppermute | solution.py:24
  409.7 10.9 %collective-permute-start.42 = (bf16[512,384]{1,0:T(8,128)(2,1)S(1)}, bf16[512,384]{1,0:T(8,128)(2,1)S(1)}, u32[]{:S(2)}, u32[]{:S(2)}) collective-permute-start(bf16[512,384]{1,0:T(8,128)(2,1)S(1)} %fusion.10.refs_3_.refs_5_), channel_id=1, source_target_pairs={{0,16},{16,0},{1,17},{17,1},{2,18},{18,2},{3,19},{19,3},{4,20},{20... | collective-permute-start | bytes 1179656 | tf_op jit(solution)/shard_map/ppermute | solution.py:29
  445.7 6.9 %collective-permute-start.45 = (f32[4099]{0:T(1024)S(1)}, f32[4099]{0:T(1024)S(1)}, u32[]{:S(2)}, u32[]{:S(2)}) collective-permute-start(f32[4099]{0:T(1024)S(1)} %concatenate.40), channel_id=1, source_target_pairs={{0,1},{1,0},{2,3},{3,2},{4,5},{5,4},{6,7},{7,6},{8,9},{9,8},{10,11... | collective-permute-start | bytes 49196 | tf_op jit(solution)/shard_map/ppermute | solution.py:24
  452.7 3.8 collective-permute-start.46
  456.6 7.4 %collective-permute-start.49 = (f32[40,128]{1,0:T(8,128)S(1)}, f32[40,128]{1,0:T(8,128)S(1)}, u32[]{:S(2)}, u32[]{:S(2)}) collective-permute-start(f32[40,128]{1,0:T(8,128)S(1)} %bitcast.130), channel_id=1, source_target_pairs={{0,12},{4,0},{8,4},{12,8},{1,13},{5,1},{9,5},{13,9},{2,14},{6,2},{... | collective-permute-start | bytes 61448 | tf_op jit(solution)/shard_map/ppermute | solution.py:29
  456.6 7.3 %collective-permute-start.48 = (f32[40,128]{1,0:T(8,128)S(1)}, f32[40,128]{1,0:T(8,128)S(1)}, u32[]{:S(2)}, u32[]{:S(2)}) collective-permute-start(f32[40,128]{1,0:T(8,128)S(1)} %bitcast.131), channel_id=1, source_target_pairs={{0,8},{4,12},{8,0},{12,4},{1,9},{5,13},{9,1},{13,5},{2,10},{6,14},... | collective-permute-start | bytes 61448 | tf_op jit(solution)/shard_map/ppermute | solution.py:29
  457.1 7.0 %collective-permute-start.47 = (f32[40,128]{1,0:T(8,128)S(1)}, f32[40,128]{1,0:T(8,128)S(1)}, u32[]{:S(2)}, u32[]{:S(2)}) collective-permute-start(f32[40,128]{1,0:T(8,128)S(1)} %bitcast.132), channel_id=1, source_target_pairs={{0,4},{4,8},{8,12},{12,0},{1,5},{5,9},{9,13},{13,1},{2,6},{6,10},{... | collective-permute-start | bytes 61448 | tf_op jit(solution)/shard_map/ppermute | solution.py:29
  463.4 7.3 %collective-permute-start.44 = (bf16[256,2048]{1,0:T(8,128)(2,1)S(1)}, bf16[256,2048]{1,0:T(8,128)(2,1)S(1)}, u32[]{:S(2)}, u32[]{:S(2)}) collective-permute-start(bf16[256,2048]{1,0:T(8,128)(2,1)S(1)} %get-tuple-element.143), channel_id=1, source_target_pairs={{0,1},{1,0},{2,3},{3,2},{4,5},{5,4},{6,7},{7,6},{8,9},{9,8},{10,11... | collective-permute-start | bytes 3145736 | tf_op jit(solution)/shard_map/ppermute | solution.py:24
  463.4 4.4 collective-permute-start.43
  482.0 6.6 %collective-permute-start.51 = (bf16[256,256]{1,0:T(8,128)(2,1)S(1)}, bf16[256,256]{1,0:T(8,128)(2,1)S(1)}, u32[]{:S(2)}, u32[]{:S(2)}) collective-permute-start(bf16[256,256]{1,0:T(8,128)(2,1)S(1)} %get-tuple-element.235), channel_id=1, source_target_pairs={{0,2},{1,3},{2,0},{3,1},{4,6},{5,7},{6,4},{7,5},{8,10},{9,11},{10,... | collective-permute-start | bytes 393224 | tf_op jit(solution)/shard_map/ppermute | solution.py:24
  483.6 5.0 %collective-permute-start.50 = (bf16[256,256]{1,0:T(8,128)(2,1)S(1)}, bf16[256,256]{1,0:T(8,128)(2,1)S(1)}, u32[]{:S(2)}, u32[]{:S(2)}) collective-permute-start(bf16[256,256]{1,0:T(8,128)(2,1)S(1)} %get-tuple-element.235), channel_id=1, source_target_pairs={{0,1},{1,0},{2,3},{3,2},{4,5},{5,4},{6,7},{7,6},{8,9},{9,8},{10,11... | collective-permute-start | bytes 393224 | tf_op jit(solution)/shard_map/ppermute | solution.py:24
  483.6 5.8 %collective-permute-start.52 = (bf16[256,256]{1,0:T(8,128)(2,1)S(1)}, bf16[256,256]{1,0:T(8,128)(2,1)S(1)}, u32[]{:S(2)}, u32[]{:S(2)}) collective-permute-start(bf16[256,256]{1,0:T(8,128)(2,1)S(1)} %get-tuple-element.235), channel_id=1, source_target_pairs={{0,3},{1,2},{2,1},{3,0},{4,7},{5,6},{6,5},{7,4},{8,11},{9,10},{10,... | collective-permute-start | bytes 393224 | tf_op jit(solution)/shard_map/ppermute | solution.py:24
  (106 other events, 597.9 us)
Sparse Core Ops, SparseCore 0:
  177.6 49.1 reduce-scatter.4
  255.4 90.2 reduce-scatter.6
  348.0 84.3 reduce-scatter.8
  434.6 45.5 reduce-scatter.10

commit v6 on v5

--- a/solution.py
+++ b/solution.py
@@ -14,7 +14,7 @@
 
 EPSILON = 1e-05
 NEG_FILL = -1e30
-VMEM_GRANT = 28 * 1024 * 1024
+VMEM_GRANT = 24 * 1024 * 1024
 WIDE_GRANT = 60 * 1024 * 1024
 
 CORE, CHIP = (1, 2)
@@ -43,14 +43,14 @@
     return lax.dynamic_slice_in_dim(value, index * size, size, axis)
 
 
-def paired_rows(mine, other, core):
-    first = jnp.where(core == 0, mine, other)
-    second = jnp.where(core == 0, other, mine)
-    return jnp.concatenate([first, second], axis=0)
-
-
-def gather_rows(mine, core):
-    return paired_rows(mine, partner(mine, CORE), core)
+def gather_rows(name, at, mine):
+    rows, width = mine.shape
+    half = pl.BlockSpec((rows, width), lambda i, at: (0, 0))
+    whole = pl.BlockSpec((2 * rows, width), lambda i, at: (0, 0))
+    args = (mine, partner(mine, CORE))
+    outs = [(like((2 * rows, width), mine.dtype), whole)]
+    size = 4 * rows * width * mine.dtype.itemsize
+    return call_at(name, gather_kernel, at, (1,), [half, half], args, outs, moved_bytes=size)[0]
 
 
 def send_columns(rows):
@@ -75,6 +75,15 @@
     total = jnp.zeros_like(value)
     for rank in range(count):
         total = total + lax.dynamic_index_in_dim(pieces, (mine - rank) % count, 0, keepdims=False)
+    return total
+
+
+def scatter_sum(value, axis):
+    count, mine = (lax.axis_size(axis), lax.axis_index(axis))
+    share = value.shape[0] // count
+    total = cut(value, mine, share, 0)
+    for shift in range(1, count):
+        total = total + shifted(cut(value, (mine + shift) % count, share, 0), axis, shift)
     return total
 
 
@@ -512,7 +521,7 @@
         )
 
 
-def call_at(name, kernel, scalars, grid, specs, args, outs, grant=VMEM_GRANT):
+def call_at(name, kernel, scalars, grid, specs, args, outs, grant=VMEM_GRANT, moved_bytes=1):
     return pl.pallas_call(
         kernel,
         name=name,
@@ -523,7 +532,7 @@
             out_specs=[spec for _, spec in outs],
         ),
         out_shape=[out for out, _ in outs],
-        cost_estimate=pl.CostEstimate(flops=1, bytes_accessed=1, transcendentals=0),
+        cost_estimate=pl.CostEstimate(flops=1, bytes_accessed=moved_bytes, transcendentals=0),
         compiler_params=pltpu.CompilerParams(vmem_limit_bytes=grant),
     )(scalars, *args)
 
@@ -677,6 +686,11 @@
         [(like((rows, width), jnp.bfloat16), tile)] * 3,
         VMEM_GRANT,
     )
+
+
+def gather_kernel(at_ref, mine_ref, other_ref, out_ref):
+    for place, half_ref in zip(half_places(at_ref, out_ref.shape[0]), (mine_ref, other_ref), strict=True):
+        out_ref[place, :] = half_ref[...]
 
 
 def gated_back_kernel(
@@ -963,58 +977,59 @@
     down_made, down_sum = weight_grad(
         "grad_down", core, [(grad_low, cot_columns, [activated], listed(act_sent))], two_back
     )
-    two_theirs = after(two_theirs, down_made, two_sent, gate_sent)
+    two_theirs = after(two_theirs, down_made)
     grad_middle, mix_grad_mine, gain_two_sum = norm_grad(
         "norm_two_back", here, middle, grad_low, two_back, two_theirs, gain_two, (jnp.float32, jnp.bfloat16)
     )
 
     mix_grad_other = partner(mix_grad_mine, CORE)
     mix_sent = send_columns(mix_grad_mine)
+    two_pair = (two_mine, two_other)
+    two_columns = both_halves([after(part, two_theirs) for part in two_sent])
+    gate_made, gate_sum = weight_grad(
+        "grad_gate", core, [(two_pair, two_columns, [grad_gate], listed(gate_sent))], mix_grad_mine
+    )
     grad_values, grad_gate_ssm = gated_back(
-        here, mix_grad_mine, mix_grad_other, ssm_out, gate_ssm, ssm_values
+        after(here, gate_made), mix_grad_mine, mix_grad_other, ssm_out, gate_ssm, ssm_values
     )
     own_grad = scan.own_state(grad_values, small_rows, read_rows, False)
     z_sent = send_rows(grad_gate_ssm)
-    two_columns = both_halves([after(part, mix_grad_mine) for part in two_sent])
     mlp_terms = [(activated, mlp_down, 0)]
 
     def fill_attend_back(sent):
         kept["mlp_given"] = partner(half_share("mlp_other", after(there, sent), mlp_terms, False), CORE)
-        kept["gate_up"] = weight_grad(
-            "grad_gate_up",
-            core,
-            [((two_mine, two_other), two_columns, [grad_gate, grad_up], listed(gate_sent, up_sent))],
-            sent,
-        )
-        grad_attended = rows_back(after(here, kept["gate_up"][0]), mix_grad_mine, mix_grad_other, attn_out)
+        grad_attended = rows_back(after(here, sent), mix_grad_mine, mix_grad_other, attn_out)
         kept["grads"] = attend.back(rank, queries, grad_attended, kept["log"], key_rows, value_rows)
         grad_query, grad_key, grad_value = kept["grads"]
         kept["query_sent"] = send_rows(grad_query)
         kept["kv_given"] = jnp.where(core == 0, grad_value, grad_key).astype(jnp.bfloat16)
-        return (grad_query, kept["kv_given"], kept["mlp_given"])
+        return (grad_query, kept["kv_given"], up_sent, kept["mlp_given"])
 
     def fill_scan_back(sent):
         given = partner(after(kept["kv_given"], sent), CORE)
+        kept["up"] = weight_grad(
+            "grad_up", core, [(two_pair, two_columns, [grad_up], listed(up_sent))], sent
+        )
         kept["scan"] = scan.within_back(
-            source_rows, after(grad_values, sent), small_rows, write_rows, read_rows
+            source_rows, after(grad_values, kept["up"][0]), small_rows, write_rows, read_rows
         )
         _, grad_key, grad_value = kept["grads"]
         own_part = jnp.where(core == 0, grad_key, grad_value)
         paired = (own_part + given.astype(jnp.float32)).reshape(ctx_count, tokens, AHEAD_DIM)
         kept["kv"] = [paired[0]] + [paired[shift].astype(jnp.bfloat16) for shift in range(1, ctx_count)]
-        return (kept["scan"][0], kept["kv"], mix_sent, z_sent, kept["query_sent"])
+        kept["mix_columns"] = both_halves([after(part, sent) for part in mix_sent])
+        return (kept["scan"][0], kept["kv"], kept["mix_columns"], z_sent, kept["query_sent"])
 
     def fill_weights(sent):
         kept["kv_back"] = [
             moved(after(part, sent), "ctx", -shift) for shift, part in enumerate(kept["kv"]) if shift
         ]
         kept["mlp_mine"] = half_share("mlp_own", after(here, sent), mlp_terms, False, kept["mlp_given"])
-        mix_columns = both_halves([after(part, sent) for part in mix_sent])
         kept["mixer"] = weight_grad(
             "grad_mixer",
             core,
             [
-                ((mix_grad_mine, mix_grad_other), mix_columns, [gated_rows, attended], outs_sent),
+                ((mix_grad_mine, mix_grad_other), kept["mix_columns"], [gated_rows, attended], outs_sent),
                 (
                     input_one,
                     one_columns,
@@ -1048,17 +1063,20 @@
     grad_dt_bias = jnp.sum(grad_dt_pre, axis=1)
     grad_a_log = decay_rate * jnp.sum(dt_rows * flow_rows, axis=1)
     grad_d_skip = jnp.sum(scan_sums[:, 4, : 2 * head_width].reshape(heads_local, head_width), axis=1)
-    grad_dt_low = jnp.pad(grad_dt_pre.astype(jnp.bfloat16).T, ((0, 0), (0, pad)))
-    grad_small = jnp.concatenate([grad_kv_low, grad_bc_low, grad_dt_low], axis=1)
+    grad_dt_low = grad_dt_pre.astype(jnp.bfloat16)
+    grad_small = jnp.concatenate([grad_kv_low, grad_bc_low], axis=1)
+    grad_dt_all = jnp.concatenate(
+        [grad_small, jnp.pad(grad_dt_low.T, ((0, 0), (0, pad)))], axis=1
+    )
     small_sent = send_rows(grad_small)
     terms = [
         (grad_gate_ssm, in_matrix, 0),
         (grad_source, in_matrix, 1),
         (grad_query, attn_q, 0),
-        (grad_small, weight_small, 0),
+        (grad_dt_all, weight_small, 0),
     ]
     mlp_theirs = partner(after(kept["mlp_mine"], grad_bc_low), CHIP)
-    given = partner(half_share("one_other", after(there, source_sent, down_sum, kept["gate_up"][1]), terms, True), CORE)
+    given = partner(half_share("one_other", after(there, source_sent, down_sum, gate_sum, kept["up"][1]), terms, True), CORE)
     one_back = half_share("one_own", after(here, mlp_theirs), terms, True, given)
     one_theirs = partner(one_back, CHIP)
     last_made, last_sum = weight_grad(
@@ -1071,18 +1089,23 @@
     hidden_mine, gain_one_sum = norm_grad(
         "norm_one_back", here, hidden_rows, grad_middle, one_back, one_theirs, gain_one, (jnp.bfloat16,)
     )
-    grad_hidden = gather_rows(hidden_mine, core)
+    grad_hidden = gather_rows("gather_hidden", here, hidden_mine)
+    step_share = matmul_low(after(grad_dt_low, hidden_mine), input_one).T
+    grad_ssm_dt = scatter_sum(scatter_sum(step_share, "dp"), "ctx")
     mlp_total = wide(kept["mlp_mine"]) + wide(after(mlp_theirs, hidden_mine))
     block_out = middle + mlp_total
-    output = gather_rows(block_out.astype(jnp.bfloat16), core)
+    output = gather_rows("gather_output", here, block_out.astype(jnp.bfloat16))
     squares = jnp.stack([jnp.sum(mix_squares), jnp.sum(mlp_total * mlp_total), jnp.sum(block_out * block_out)])
-    halves = jnp.concatenate([gain_one_sum[0], gain_two_sum[0], squares])
+    def line(*parts):
+        flat = jnp.concatenate(parts)
+        return jnp.pad(flat, (0, model_width - flat.shape[0]))[None]
+
+    halves = jnp.concatenate([gain_one_sum, gain_two_sum, line(squares)], axis=0)
     halves = halves + partner(halves, CORE)
-    sums = jnp.concatenate([halves, grad_dt_bias, grad_a_log, grad_d_skip])
-    sums = jnp.pad(sums, (0, -sums.shape[0] % 1024)).reshape(-1, 128)
-    sums = all_sum(all_sum(sums, "dp"), "ctx").reshape(-1)
-
-    grad_last = wide(after(last_sum, kept["mixer"][1], sums))
+    sums = jnp.concatenate([halves, line(grad_dt_bias, grad_a_log, grad_d_skip)], axis=0)
+    sums = all_sum(all_sum(sums, "dp"), "ctx")
+
+    grad_last = wide(after(last_sum, kept["mixer"][1], sums, grad_ssm_dt, output, grad_hidden))
     grad_little = grad_last[:, inner_local:]
     held = narrow(grad_little[:, : AHEAD_DIM + bc_share])
     pieces = jnp.stack([held] + [partner(held, stride) for stride in range(1, 4)])
@@ -1099,34 +1122,33 @@
     grad_ssm_bc = jnp.concatenate(
         [by_rank[2 * (place % 2) + place // 2][:, AHEAD_DIM:] for place in range(4)], axis=1
     ).reshape(-1, 2, state_width)
-    grad_ssm_dt = grad_little[:, AHEAD_DIM + bc_share : AHEAD_DIM + bc_share + heads_local]
 
     place = lax.axis_index("dp") * ctx_count + ctx_rank
     share = model_width // (lax.axis_size("dp") * ctx_count)
-    small = sums[2 * model_width :]
+    small = sums[3]
     counted = tokens * model_width * lax.axis_size("dp") * ctx_count
     grad_down = wide(down_sum)
-    grad_gate_up = wide(after(kept["gate_up"][1], grad_down)).reshape(-1, 2, ff_local)
+    grad_gate_up = jnp.stack([wide(gate_sum), wide(kept["up"][1])], axis=1)
     grad_mixer = wide(after(kept["mixer"][1], grad_gate_up))
     outs_width = inner_local + heads_query * AHEAD_DIM
     grad_outs = grad_mixer[:, :outs_width]
     grad_first = grad_mixer[:, outs_width:]
-    branch_rms = jnp.sqrt(small[:3] / counted)
+    branch_rms = jnp.sqrt(sums[2, :3] / counted)
     return (
         output[None],
         grad_hidden[None],
-        cut(sums[:model_width], place, share, 0),
+        cut(sums[0], place, share, 0),
         jnp.stack([grad_first[:, :inner_local], grad_last[:, :inner_local]], axis=1),
         grad_ssm_bc,
         grad_ssm_dt,
-        small[3 : 3 + heads_local],
-        small[3 + heads_local : 3 + 2 * heads_local],
-        small[3 + 2 * heads_local : 3 + 3 * heads_local],
+        small[:heads_local],
+        small[heads_local : 2 * heads_local],
+        small[2 * heads_local : 3 * heads_local],
         grad_outs[:, :inner_local].T,
         grad_first[:, inner_local:],
         grad_attn_kv,
         grad_outs[:, inner_local:].T,
-        cut(sums[model_width : 2 * model_width], place, share, 0),
+        cut(sums[1], place, share, 0),
         grad_gate_up,
         grad_down.T,
         branch_rms,

time: 507 us -> 484 us (0.955)
  waiting for transfers between devices: 168 us -> 119 us
  Pallas kernels: 118 us -> 127 us
  starting transfers between devices: 47 us -> 54.3 us
  other arithmetic: 31.5 us -> 38.5 us
    ppermute x17 -> x21, waiting for transfers between devices: 112 us -> 63.2 us  [shifted(): lax.ppermute(value, axis, [(i, (i + shift) % count) for i in range(count)])]
    ppermute x24, waiting for transfers between devices: 17 us -> 36.3 us  [partner(): lax.ppermute(value, 'tensor', [(rank, rank ^ stride) for rank in range(4)])]
    unnamed x239 -> x279, local copies, waits for them, and re-layouts: 73.3 us -> 84.6 us
    ppermute x6, waiting for transfers between devices: 28.2 us -> 18.6 us  [chained(): arrived = lax.ppermute(sent, 'ctx', [pair])]
    pallas_call x18 -> x21, Pallas kernels: 68.3 us -> 77.7 us  [call_at(): pl.pallas_call(kernel, name=name, grid_spec=pltpu.PrefetchScalarGridSpec(...]
    reduce_scatter x4 -> x5, waiting for transfers between devices: 9.04 us -> 0.03 us  [weight_grad(): lax.psum_scatter(made, 'ctx', scatter_dimension=0, tiled=True)]
    ppermute x17 -> x21, starting transfers between devices: 16.3 us -> 20.6 us  [shifted(): lax.ppermute(value, axis, [(i, (i + shift) % count) for i in range(count)])]
  transfers between devices with their start and end apart: 57 -> 62, of which waited for: 24 -> 23; matrix products, arithmetic and copies ran while one was open for 16% -> 18% of each run, Pallas kernels for 17% -> 20%
where the time goes in v6:
time: 484 us; the launch traced here: 476 us
  Pallas kernels  127 us (26%)
  waiting for transfers between devices  119 us (25%)
  local copies, waits for them, and re-layouts  110 us (23%)
  starting transfers between devices  54.3 us (11%)
  other arithmetic  38.5 us (8%)
  between operations  16.2 us (3%)
  matrix products  10.3 us (2%)
    unnamed x279, local copies, waits for them, and re-layouts  84.6 us
    pallas_call x21, Pallas kernels, call_at(): pl.pallas_call(kernel, name=name, grid_spec=pltpu.PrefetchScalarGridSpec(...  77.7 us
    ppermute x21, waiting for transfers between devices, shifted(): lax.ppermute(value, axis, [(i, (i + shift) % count) for i in range(count)])  63.2 us
    pallas_call x11, Pallas kernels, call(): pl.pallas_call(kernel, name=name, grid=grid, in_specs=specs, out_specs=[s...  49.4 us
    ppermute x24, waiting for transfers between devices, partner(): lax.ppermute(value, 'tensor', [(rank, rank ^ stride) for rank in range(4)])  36.3 us
    ppermute x21, starting transfers between devices, shifted(): lax.ppermute(value, axis, [(i, (i + shift) % count) for i in range(count)])  20.6 us
    ppermute x6, waiting for transfers between devices, chained(): arrived = lax.ppermute(sent, 'ctx', [pair])  18.6 us
    ppermute x6, starting transfers between devices, moved(): return lax.ppermute(value, axis, pairs)  15.9 us
  transfers between devices with their start and end apart: 62, of which 23 were waited for; matrix products, arithmetic and copies ran while one was open for 18% of the time, Pallas kernels for 20%

profile of v6, /device:TPU:0, one launch (start us, length us, event | category | flops | bytes accessed | tf_op | source)
XLA Modules:
  0.0 475.5 jit_solution(9678370571380646800)
XLA Ops:
  17.8 4.2 copy.98
  22.0 2.4 project_u.1.u_ref
  27.0 2.6 own_state.2
  33.4 5.6 %collective-permute-start.3 = (bf16[512,128]{1,0:T(8,128)(2,1)}, bf16[512,128]{1,0:T(8,128)(2,1)}, u32[]{:S(2)}, u32[]{:S(2)}) collective-permute-start(bf16[512,128]{1,0:T(8,128)(2,1)} %dynamic-slice_convert_fusion.1), channel_id=1, source_target_pairs={{0,4},{4,8},{8,12},{1,5},{5,9},{9,13},{2,6},{6,10},{10,14},{3,7},{... | collective-permute-start | bytes 393224 | tf_op jit(solution)/shard_map/ppermute | solution.py:35
  38.9 4.5 collective-permute-start.4
  45.4 2.3 collective-permute-start
  47.7 2.1 dynamic_slice.112
  51.4 2.8 copy-done.5
  54.2 2.5 project_z.1.z_ref.gate_ref
  57.8 3.2 scan.1.y_ref
  65.3 2.1 convolution_convert_fusion.1.q_ref
  70.9 6.7 %attend.1 = (bf16[512,256]{1,0:T(8,128)(2,1)S(1)}, f32[2,8,512]{2,1,0:T(8,128)S(1)}) custom-call(s32[1]{0:T(128)} %bitcast.7.rank_ref, bf16[512,256]{1,0:T(8,128)(2,1)S(1)} %convolution_convert_fusion.1.q_ref, bf16[2048,128]{1,0:T(8,128)(2,1)S(1)} %get-tuple-element.233.k_ref, bf16[2048,128]{1,0:T(8,128)(2,1)S(1)} %get-tuple-element.232.v_ref), custom_call_target="tpu_custom_call" | custom-call | flops 1 | bytes 1 | tf_op jit(solution)/shard_map/attend/pallas_call | solution.py:389
  78.7 3.7 fusion.31.dact_ref
  87.0 3.0 mix_other.1
  90.6 2.3 collective-permute-done.9.refs_4_
  92.9 3.4 mix_own.1.mine_ref
  104.1 10.4 %copy.101 = bf16[256,8,2,1024]{3,1,2,0:T(8,128)(2,1)} copy(bf16[256,8,2,1024]{3,2,1,0:T(2,128)(2,1)} %bitcast.120) | data formatting | bytes 16777216
  115.4 2.1 copy.86
  117.5 2.9 fusion.2.refs_7_
  120.4 2.9 collective-permute-done.14.refs_11_
  123.4 2.4 norm_two.1
  127.1 2.7 collective-permute-done.15.other_ref.refs_1_
  129.8 3.5 copy-done.2
  133.3 7.4 %expand.1 = (bf16[512,1024]{1,0:T(8,128)(2,1)S(1)}, bf16[512,1024]{1,0:T(8,128)(2,1)S(1)}, bf16[512,1024]{1,0:T(8,128)(2,1)S(1)}) custom-call(s32[1]{0:T(128)} %bitcast.at_ref, bf16[256,2048]{1,0:T(8,128)(2,1)S(1)} %get-tuple-element.102.mine_ref.refs_0_, bf16[256,2048]{1,0:T(8,128)(2,1)S(1)} %collective-permute-done.15.other_ref.refs_1_, ...), custom_call_target="tpu_custom_call" | custom-call | flops 1 | bytes 1 | tf_op jit(solution)/shard_map/expand/pallas_call | solution.py:525
  140.8 3.2 two_other.1
  146.7 3.3 two_own.1.mine_ref
  151.0 18.6 %collective-permute-done.18.refs_5_ = bf16[512,1024]{1,0:T(8,128)(2,1)S(1)} collective-permute-done((bf16[512,1024]{1,0:T(8,128)(2,1)S(1)}, bf16[512,1024]{1,0:T(8,128)(2,1)S(1)}, u32[]{:S(2)}, u32[]{:S(2)}) %collective-permute-start.18) | collective-permute-done | bytes 1048608 | tf_op jit(solution)/shard_map/ppermute | solution.py:29
  169.6 5.0 %grad_down.1 = bf16[1024,1024]{1,0:T(8,128)(2,1)S(1)} custom-call(s32[2]{0:T(128)S(1)} %pad_add_fusion.at_ref, bf16[512,2048]{1,0:T(8,128)(2,1)S(1)} %bitcast.110, bf16[512,2048]{1,0:T(8,128)(2,1)S(1)} %bitcast.111, bf16[256,1024]{1,0:T(8,128)(2,1)} %collective-permute-done.1.refs_2_, bf16[256,1024]{1,0:T(8,128)(2,1)} %collective-permute-done.11.refs_3_, ...), custom_call_target="tpu_custom_call" | custom-call | flops 1 | bytes 1 | tf_op jit(solution)/shard_map/grad_down/pallas_call | solution.py:525
  180.0 21.1 %collective-permute-done.17.theirs_ref = bf16[256,2048]{1,0:T(8,128)(2,1)S(1)} collective-permute-done((bf16[256,2048]{1,0:T(8,128)(2,1)}, bf16[256,2048]{1,0:T(8,128)(2,1)S(1)}, u32[]{:S(2)}, u32[]{:S(2)}) %collective-permute-start.17) | collective-permute-done | bytes 1048608 | tf_op jit(solution)/shard_map/ppermute | solution.py:24
  209.9 3.6 collective-permute-done.21.refs_5_
  213.6 4.0 grad_gate.1
  222.7 2.3 copy-done.8
  229.0 2.9 gated_back.1
  232.0 2.3 own_state.3
  238.1 8.8 %attend_back.1 = (bf16[512,256]{1,0:T(8,128)(2,1)S(1)}, f32[2048,128]{1,0:T(8,128)S(1)}, f32[2048,128]{1,0:T(8,128)S(1)}) custom-call(s32[1]{0:T(128)} %bitcast.7.rank_ref, bf16[512,256]{1,0:T(8,128)(2,1)S(1)} %copy-done.94, bf16[512,256]{1,0:T(8,128)(2,1)S(1)} %attended_back.1.do_ref, f32[2,8,512]{2,1,0:T(8,128)S(1)} %copy-done.103, ...), custom_call_target="tpu_custom_call" | custom-call | flops 1 | bytes 1 | tf_op jit(solution)/shard_map/attend_back/pallas_call | solution.py:389
  251.2 4.0 grad_up.1
  262.3 10.3 %collective-permute-done.28.refs_2_ = bf16[256,1024]{1,0:T(8,128)(2,1)S(1)} collective-permute-done((bf16[256,1024]{1,0:T(8,128)(2,1)S(1)}, bf16[256,1024]{1,0:T(8,128)(2,1)S(1)}, u32[]{:S(2)}, u32[]{:S(2)}) %collective-permute-start.28) | collective-permute-done | bytes 524320 | tf_op jit(solution)/shard_map/ppermute | solution.py:29
  273.8 9.5 %scan_back.1 = (f32[512,768]{1,0:T(8,128)S(1)}, f32[6,8,512]{2,1,0:T(8,128)S(1)}, f32[512,256]{1,0:T(8,128)S(1)}, f32[512,256]{1,0:T(8,128)S(1)}) custom-call(bf16[512,768]{1,0:T(8,128)(2,1)S(1)} %project_u.1.u_ref, bf16[512,768]{1,0:T(8,128)(2,1)S(1)} %copy-done.55, f32[6,8,512]{2,1,0:T(8,128)S(1)} %reshape.158.small_ref, ...), custom_call_target="tpu_custom_call" | custom-call | flops 1 | bytes 1 | tf_op jit(solution)/shard_map/scan_back/pallas_call | solution.py:389
  287.2 7.1 %collective-permute-done.30.refs_14_ = bf16[512,768]{1,0:T(8,128)(2,1)S(1)} collective-permute-done((bf16[512,768]{1,0:T(8,128)(2,1)}, bf16[512,768]{1,0:T(8,128)(2,1)S(1)}, u32[]{:S(2)}, u32[]{:S(2)}) %collective-permute-start.30) | collective-permute-done | bytes 786464 | tf_op jit(solution)/shard_map/ppermute | solution.py:29
  296.2 2.6 mlp_own.1
  298.9 7.9 %grad_mixer.1 = bf16[1024,2048]{1,0:T(8,128)(2,1)S(1)} custom-call(s32[2]{0:T(128)S(1)} %copy-done.105, bf16[256,2048]{1,0:T(8,128)(2,1)S(1)} %copy-done.26, bf16[256,2048]{1,0:T(8,128)(2,1)S(1)} %copy-done.31, bf16[256,1024]{1,0:T(8,128)(2,1)S(1)} %collective-permute-done.28.refs_2_, bf16[256,1024]{1,0:T(8,128)(2,1)S(1)} %collective-permute-done.29.refs_3_, ...), custom_call_target="tpu_custom_call" | custom-call | flops 1 | bytes 1 | tf_op jit(solution)/shard_map/grad_mixer/pallas_call | solution.py:525
  306.8 2.1 copy-done.16
  314.2 18.6 %collective-permute-done.32 = bf16[768,256]{1,0:T(8,128)(2,1)} collective-permute-done((bf16[768,256]{1,0:T(8,128)(2,1)}, bf16[768,256]{1,0:T(8,128)(2,1)}, u32[]{:S(2)}, u32[]{:S(2)}) %collective-permute-start.32) | collective-permute-done | bytes 393248 | tf_op jit(solution)/shard_map/ppermute | solution.py:99
  334.8 8.5 %carry_back.1 = (bf16[512,768]{1,0:T(8,128)(2,1)}, f32[6,8,512]{2,1,0:T(8,128)}, f32[512,256]{1,0:T(8,128)}, f32[512,256]{1,0:T(8,128)}) custom-call(bf16[512,768]{1,0:T(8,128)(2,1)} %copy-done.12, bf16[512,768]{1,0:T(8,128)(2,1)} %copy-done.54, f32[6,8,512]{2,1,0:T(8,128)} %copy-done.59, f32[6,8,512]{2,1,0:T(8,128)} %copy-done.99, f32[512,768]{1,0:T(8,128)} %copy-done.92, ...), custom_call_target="tpu_custom_call" | custom-call | flops 1 | bytes 1 | tf_op jit(solution)/shard_map/carry_back/pallas_call | solution.py:389
  360.2 9.0 %collective-permute-done.39.refs_6_ = bf16[512,768]{1,0:T(8,128)(2,1)} collective-permute-done((bf16[512,768]{1,0:T(8,128)(2,1)}, bf16[512,768]{1,0:T(8,128)(2,1)}, u32[]{:S(2)}, u32[]{:S(2)}) %collective-permute-start.39) | collective-permute-done | bytes 786464 | tf_op jit(solution)/shard_map/ppermute | solution.py:29
  369.2 2.8 copy-done.6
  374.6 4.4 one_other.1
  379.1 3.8 collective-permute-done.35
  382.9 4.9 %one_own.1.mine_ref = bf16[256,2048]{1,0:T(8,128)(2,1)} custom-call(s32[1]{0:T(128)} %bitcast.at_ref, bf16[512,768]{1,0:T(8,128)(2,1)S(1)} %copy-done.53, bf16[512,768]{1,0:T(8,128)(2,1)} %get-tuple-element.139.refs_1_.refs_4_, bf16[512,256]{1,0:T(8,128)(2,1)S(1)} %copy-done.77, bf16[512,384]{1,0:T(8,128)(2,1)S(1)} %fusion.10.refs_3_, ...), custom_call_target="tpu_custom_call" | custom-call | flops 1 | bytes 1 | tf_op jit(solution)/shard_map/one_own/pallas_call | solution.py:525
  395.2 2.1 convert_bitcast_fusion
  397.3 2.5 copy.95
  401.2 2.9 copy.94
  404.2 5.6 %grad_last.1 = bf16[1024,1024]{1,0:T(8,128)(2,1)S(1)} custom-call(s32[2]{0:T(128)S(1)} %copy-done.106, bf16[512,2048]{1,0:T(8,128)(2,1)S(1)} %norm_one.1.x_ref.refs_4_.refs_5_.refs_0_.refs_1_, bf16[512,2048]{1,0:T(8,128)(2,1)S(1)} %norm_one.1.x_ref.refs_4_.refs_5_.refs_0_.refs_1_, bf16[256,1024]{1,0:T(8,128)(2,1)S(1)} %copy-done.83, ...), custom_call_target="tpu_custom_call" | custom-call | flops 1 | bytes 1 | tf_op jit(solution)/shard_map/grad_last/pallas_call | solution.py:525
  415.5 3.6 norm_one_back.1
  419.1 2.8 multiply_reduce_fusion.1
  429.2 2.3 copy.91
  434.0 3.1 collective-permute-done.46
  437.8 2.2 collective-permute-done.51
  441.7 2.5 collective-permute-start.49
  444.8 2.2 collective-permute-done.47
  447.0 2.4 collective-permute-done.48
  451.2 3.0 gather_hidden.1
  454.2 2.7 gather_output.1
  462.1 2.4 copy.90
  (487 shorter events, 158.7 us)
Async XLA Ops:
  7.2 353.0 %reduce-scatter.6.cloned.1.call-start = ((), (), s32[]{:S(2)}) async-start(), calls=%async_computation.5 | async-start | bytes 2621440 | tf_op jit(solution)/shard_map/reduce_scatter | solution.py:838
  17.7 254.9 %copy-start.59 = (f32[6,8,512]{2,1,0:T(8,128)}, f32[6,8,512]{2,1,0:T(8,128)S(1)}, u32[]{:S(2)}) copy-start(f32[6,8,512]{2,1,0:T(8,128)S(1)} %reshape.158.small_ref) | copy-start | bytes 294916
  24.8 247.8 %copy-start.12 = (bf16[512,768]{1,0:T(8,128)(2,1)}, bf16[512,768]{1,0:T(8,128)(2,1)S(1)}, u32[]{:S(2)}) copy-start(bf16[512,768]{1,0:T(8,128)(2,1)S(1)} %project_u.1.u_ref) | copy-start | bytes 2359300
  33.4 30.2 %collective-permute-start.3 = (bf16[512,128]{1,0:T(8,128)(2,1)}, bf16[512,128]{1,0:T(8,128)(2,1)}, u32[]{:S(2)}, u32[]{:S(2)}) collective-permute-start(bf16[512,128]{1,0:T(8,128)(2,1)} %dynamic-slice_convert_fusion.1), channel_id=1, source_target_pairs={{0,4},{4,8},{8,12},{1,5},{5,9},{9,13},{2,6},{6,10},{10,14},{3,7},{... | collective-permute-start | bytes 393224 | tf_op jit(solution)/shard_map/ppermute | solution.py:35
  38.9 25.1 %collective-permute-start.4 = (bf16[512,128]{1,0:T(8,128)(2,1)}, bf16[512,128]{1,0:T(8,128)(2,1)}, u32[]{:S(2)}, u32[]{:S(2)}) collective-permute-start(bf16[512,128]{1,0:T(8,128)(2,1)} %dynamic-slice_convert_fusion.1), channel_id=1, source_target_pairs={{0,8},{4,12},{1,9},{5,13},{2,10},{6,14},{3,11},{7,15},{16,24},{20,... | collective-permute-start | bytes 393224 | tf_op jit(solution)/shard_map/ppermute | solution.py:35
  43.5 20.6 %collective-permute-start.5 = (bf16[512,128]{1,0:T(8,128)(2,1)}, bf16[512,128]{1,0:T(8,128)(2,1)}, u32[]{:S(2)}, u32[]{:S(2)}) collective-permute-start(bf16[512,128]{1,0:T(8,128)(2,1)} %dynamic-slice_convert_fusion.1), channel_id=1, source_target_pairs={{0,12},{1,13},{2,14},{3,15},{16,28},{17,29},{18,30},{19,31}} | collective-permute-start | bytes 393224 | tf_op jit(solution)/shard_map/ppermute | solution.py:35
  45.4 22.0 %collective-permute-start = (bf16[768,256]{1,0:T(8,128)(2,1)}, bf16[768,256]{1,0:T(8,128)(2,1)}, u32[]{:S(2)}, u32[]{:S(2)}) collective-permute-start(bf16[768,256]{1,0:T(8,128)(2,1)} %copy-done.72), channel_id=1, source_target_pairs={{0,4},{1,5},{2,6},{3,7},{16,20},{17,21},{18,22},{19,23}} | collective-permute-start | bytes 1179656 | tf_op jit(solution)/shard_map/ppermute | solution.py:99
  49.8 17.6 %collective-permute-start.1 = (bf16[256,1024]{1,0:T(8,128)(2,1)}, bf16[256,1024]{1,0:T(8,128)(2,1)}, u32[]{:S(2)}, u32[]{:S(2)}) collective-permute-start(bf16[256,1024]{1,0:T(8,128)(2,1)} %dynamic_slice.112), channel_id=1, source_target_pairs={{0,16},{16,0},{1,17},{17,1},{2,18},{18,2},{3,19},{19,3},{4,20},{20... | collective-permute-start | bytes 1572872 | tf_op jit(solution)/shard_map/ppermute | solution.py:29
  63.6 14.1 %collective-permute-start.7 = (bf16[256,1024]{1,0:T(8,128)(2,1)}, bf16[256,1024]{1,0:T(8,128)(2,1)S(1)}, u32[]{:S(2)}, u32[]{:S(2)}) collective-permute-start(bf16[256,1024]{1,0:T(8,128)(2,1)} %dynamic_slice.115), channel_id=1, source_target_pairs={{0,16},{16,0},{1,17},{17,1},{2,18},{18,2},{3,19},{19,3},{4,20},{20... | collective-permute-start | bytes 1572872 | tf_op jit(solution)/shard_map/ppermute | solution.py:29
  65.2 4.2 collective-permute-start.6
  68.7 9.0 %collective-permute-start.2 = (bf16[768,256]{1,0:T(8,128)(2,1)S(1)}, bf16[768,256]{1,0:T(8,128)(2,1)S(1)}, u32[]{:S(2)}, u32[]{:S(2)}) collective-permute-start(bf16[768,256]{1,0:T(8,128)(2,1)S(1)} %fusion.5), channel_id=1, source_target_pairs={{4,8},{5,9},{6,10},{7,11},{20,24},{21,25},{22,26},{23,27}} | collective-permute-start | bytes 1179656 | tf_op jit(solution)/shard_map/ppermute | solution.py:99
  78.0 4.4 collective-permute-start.8
  90.1 2.8 collective-permute-start.9
  96.3 27.0 %collective-permute-start.10 = (bf16[256,2048]{1,0:T(8,128)(2,1)}, bf16[256,2048]{1,0:T(8,128)(2,1)}, u32[]{:S(2)}, u32[]{:S(2)}) collective-permute-start(bf16[256,2048]{1,0:T(8,128)(2,1)} %mix_own.1.mine_ref), channel_id=1, source_target_pairs={{0,2},{1,3},{2,0},{3,1},{4,6},{5,7},{6,4},{7,5},{8,10},{9,11},{10,... | collective-permute-start | bytes 3145736 | tf_op jit(solution)/shard_map/ppermute | solution.py:24
  97.8 25.5 %collective-permute-start.13 = (bf16[512,768]{1,0:T(8,128)(2,1)}, bf16[512,768]{1,0:T(8,128)(2,1)}, u32[]{:S(2)}, u32[]{:S(2)}) collective-permute-start(bf16[512,768]{1,0:T(8,128)(2,1)} %get-tuple-element.95.refs_0_.refs_8_), channel_id=1, source_target_pairs={{0,16},{16,0},{1,17},{17,1},{2,18},{18,2},{3,19},{19,3},{4,20},{20... | collective-permute-start | bytes 2359304 | tf_op jit(solution)/shard_map/ppermute | solution.py:29
  99.4 23.9 %collective-permute-start.12 = (bf16[256,1024]{1,0:T(8,128)(2,1)}, bf16[256,1024]{1,0:T(8,128)(2,1)}, u32[]{:S(2)}, u32[]{:S(2)}) collective-permute-start(bf16[256,1024]{1,0:T(8,128)(2,1)} %copy-done.81), channel_id=1, source_target_pairs={{0,1},{1,0},{2,3},{3,2},{4,5},{5,4},{6,7},{7,6},{8,9},{9,8},{10,11... | collective-permute-start | bytes 1572872 | tf_op jit(solution)/shard_map/ppermute | solution.py:24
  99.4 23.9 %collective-permute-start.11 = (bf16[256,1024]{1,0:T(8,128)(2,1)}, bf16[256,1024]{1,0:T(8,128)(2,1)}, u32[]{:S(2)}, u32[]{:S(2)}) collective-permute-start(bf16[256,1024]{1,0:T(8,128)(2,1)} %collective-permute-done.1.refs_2_), channel_id=1, source_target_pairs={{0,1},{1,0},{2,3},{3,2},{4,5},{5,4},{6,7},{7,6},{8,9},{9,8},{10,11... | collective-permute-start | bytes 1572872 | tf_op jit(solution)/shard_map/ppermute | solution.py:24
  103.7 19.7 %collective-permute-start.14 = (bf16[512,256]{1,0:T(8,128)(2,1)}, bf16[512,256]{1,0:T(8,128)(2,1)}, u32[]{:S(2)}, u32[]{:S(2)}) collective-permute-start(bf16[512,256]{1,0:T(8,128)(2,1)} %copy-done.78), channel_id=1, source_target_pairs={{0,16},{16,0},{1,17},{17,1},{2,18},{18,2},{3,19},{19,3},{4,20},{20... | collective-permute-start | bytes 786440 | tf_op jit(solution)/shard_map/ppermute | solution.py:29
  127.1 2.7 collective-permute-start.15
  144.0 2.7 collective-permute-start.16
  144.2 25.4 %collective-permute-start.18 = (bf16[512,1024]{1,0:T(8,128)(2,1)S(1)}, bf16[512,1024]{1,0:T(8,128)(2,1)S(1)}, u32[]{:S(2)}, u32[]{:S(2)}) collective-permute-start(bf16[512,1024]{1,0:T(8,128)(2,1)S(1)} %get-tuple-element.106.refs_4_.refs_0_), channel_id=1, source_target_pairs={{0,16},{16,0},{1,17},{17,1},{2,18},{18,2},{3,19},{19,3},{4,20},{20... | collective-permute-start | bytes 3145736 | tf_op jit(solution)/shard_map/ppermute | solution.py:29
  176.0 193.2 %reduce-scatter.8.cloned.1.call-start = ((), (), s32[]{:S(2)}) async-start(), calls=%async_computation.6 | async-start | bytes 2621440 | tf_op jit(solution)/shard_map/reduce_scatter | solution.py:838
  176.2 24.9 %collective-permute-start.17 = (bf16[256,2048]{1,0:T(8,128)(2,1)}, bf16[256,2048]{1,0:T(8,128)(2,1)S(1)}, u32[]{:S(2)}, u32[]{:S(2)}) collective-permute-start(bf16[256,2048]{1,0:T(8,128)(2,1)} %copy-done.64), channel_id=1, source_target_pairs={{0,2},{1,3},{2,0},{3,1},{4,6},{5,7},{6,4},{7,5},{8,10},{9,11},{10,... | collective-permute-start | bytes 3145736 | tf_op jit(solution)/shard_map/ppermute | solution.py:24
  177.9 23.2 %collective-permute-start.19 = (bf16[256,1024]{1,0:T(8,128)(2,1)S(1)}, bf16[256,1024]{1,0:T(8,128)(2,1)S(1)}, u32[]{:S(2)}, u32[]{:S(2)}) collective-permute-start(bf16[256,1024]{1,0:T(8,128)(2,1)S(1)} %constant_dynamic-slice_fusion.11), channel_id=1, source_target_pairs={{0,16},{16,0},{1,17},{17,1},{2,18},{18,2},{3,19},{19,3},{4,20},{20... | collective-permute-start | bytes 1572872 | tf_op jit(solution)/shard_map/ppermute | solution.py:29
  179.5 34.0 %collective-permute-start.21 = (bf16[512,1024]{1,0:T(8,128)(2,1)}, bf16[512,1024]{1,0:T(8,128)(2,1)S(1)}, u32[]{:S(2)}, u32[]{:S(2)}) collective-permute-start(bf16[512,1024]{1,0:T(8,128)(2,1)} %copy-done.37), channel_id=1, source_target_pairs={{0,16},{16,0},{1,17},{17,1},{2,18},{18,2},{3,19},{19,3},{4,20},{20... | collective-permute-start | bytes 3145736 | tf_op jit(solution)/shard_map/ppermute | solution.py:29
  201.1 12.4 %collective-permute-start.20 = (bf16[256,1024]{1,0:T(8,128)(2,1)S(1)}, bf16[256,1024]{1,0:T(8,128)(2,1)S(1)}, u32[]{:S(2)}, u32[]{:S(2)}) collective-permute-start(bf16[256,1024]{1,0:T(8,128)(2,1)S(1)} %collective-permute-done.19.refs_2_), channel_id=1, source_target_pairs={{0,1},{1,0},{2,3},{3,2},{4,5},{5,4},{6,7},{7,6},{8,9},{9,8},{10,11... | collective-permute-start | bytes 1572872 | tf_op jit(solution)/shard_map/ppermute | solution.py:24
  219.7 149.5 %reduce-scatter.10.cloned.1.call-start = ((), (), s32[]{:S(2)}) async-start(), calls=%async_computation.7 | async-start | bytes 2621440 | tf_op jit(solution)/shard_map/reduce_scatter | solution.py:838
  219.8 2.9 collective-permute-start.22
  219.9 28.7 %collective-permute-start.24 = (bf16[512,1024]{1,0:T(8,128)(2,1)}, bf16[512,1024]{1,0:T(8,128)(2,1)S(1)}, u32[]{:S(2)}, u32[]{:S(2)}) collective-permute-start(bf16[512,1024]{1,0:T(8,128)(2,1)} %copy-done.35), channel_id=1, source_target_pairs={{0,16},{16,0},{1,17},{17,1},{2,18},{18,2},{3,19},{19,3},{4,20},{20... | collective-permute-start | bytes 3145736 | tf_op jit(solution)/shard_map/ppermute | solution.py:29
  236.2 12.3 %collective-permute-start.25 = (bf16[256,2048]{1,0:T(8,128)(2,1)S(1)}, bf16[256,2048]{1,0:T(8,128)(2,1)S(1)}, u32[]{:S(2)}, u32[]{:S(2)}) collective-permute-start(bf16[256,2048]{1,0:T(8,128)(2,1)S(1)} %mlp_other.1), channel_id=1, source_target_pairs={{0,1},{1,0},{2,3},{3,2},{4,5},{5,4},{6,7},{7,6},{8,9},{9,8},{10,11... | collective-permute-start | bytes 3145736 | tf_op jit(solution)/shard_map/ppermute | solution.py:24
  236.4 12.1 %collective-permute-start.23 = (bf16[768,256]{1,0:T(8,128)(2,1)S(1)}, bf16[768,256]{1,0:T(8,128)(2,1)S(1)}, u32[]{:S(2)}, u32[]{:S(2)}) collective-permute-start(bf16[768,256]{1,0:T(8,128)(2,1)S(1)} %own_state.3), channel_id=1, source_target_pairs={{12,8},{13,9},{14,10},{15,11},{28,24},{29,25},{30,26},{31,27}} | collective-permute-start | bytes 1179656 | tf_op jit(solution)/shard_map/ppermute | solution.py:99
  256.5 155.5 %reduce-scatter.12.cloned.1.call-start = ((), (), s32[]{:S(2)}) async-start(), calls=%async_computation.8 | async-start | bytes 5242880 | tf_op jit(solution)/shard_map/reduce_scatter | solution.py:838
  257.8 14.8 %collective-permute-start.28 = (bf16[256,1024]{1,0:T(8,128)(2,1)S(1)}, bf16[256,1024]{1,0:T(8,128)(2,1)S(1)}, u32[]{:S(2)}, u32[]{:S(2)}) collective-permute-start(bf16[256,1024]{1,0:T(8,128)(2,1)S(1)} %constant_dynamic-slice_fusion.10), channel_id=1, source_target_pairs={{0,16},{16,0},{1,17},{17,1},{2,18},{18,2},{3,19},{19,3},{4,20},{20... | collective-permute-start | bytes 1572872 | tf_op jit(solution)/shard_map/ppermute | solution.py:29
  259.3 25.9 %collective-permute-start.27 = (bf16[2048,128]{1,0:T(8,128)(2,1)}, bf16[2048,128]{1,0:T(8,128)(2,1)S(1)}, u32[]{:S(2)}, u32[]{:S(2)}) collective-permute-start(bf16[2048,128]{1,0:T(8,128)(2,1)} %select_convert_fusion), channel_id=1, source_target_pairs={{0,1},{1,0},{2,3},{3,2},{4,5},{5,4},{6,7},{7,6},{8,9},{9,8},{10,11... | collective-permute-start | bytes 1572872 | tf_op jit(solution)/shard_map/ppermute | solution.py:24
  259.4 27.9 %collective-permute-start.31 = (bf16[512,256]{1,0:T(8,128)(2,1)}, bf16[512,256]{1,0:T(8,128)(2,1)S(1)}, u32[]{:S(2)}, u32[]{:S(2)}) collective-permute-start(bf16[512,256]{1,0:T(8,128)(2,1)} %copy-done.76), channel_id=1, source_target_pairs={{0,16},{16,0},{1,17},{17,1},{2,18},{18,2},{3,19},{19,3},{4,20},{20... | collective-permute-start | bytes 786440 | tf_op jit(solution)/shard_map/ppermute | solution.py:29
  259.9 34.5 %collective-permute-start.30 = (bf16[512,768]{1,0:T(8,128)(2,1)}, bf16[512,768]{1,0:T(8,128)(2,1)S(1)}, u32[]{:S(2)}, u32[]{:S(2)}) collective-permute-start(bf16[512,768]{1,0:T(8,128)(2,1)} %copy-done.52), channel_id=1, source_target_pairs={{0,16},{16,0},{1,17},{17,1},{2,18},{18,2},{3,19},{19,3},{4,20},{20... | collective-permute-start | bytes 2359304 | tf_op jit(solution)/shard_map/ppermute | solution.py:29
  261.4 33.0 %collective-permute-start.26 = (bf16[768,256]{1,0:T(8,128)(2,1)}, bf16[768,256]{1,0:T(8,128)(2,1)S(1)}, u32[]{:S(2)}, u32[]{:S(2)}) collective-permute-start(bf16[768,256]{1,0:T(8,128)(2,1)} %fusion.7), channel_id=1, source_target_pairs={{8,4},{9,5},{10,6},{11,7},{24,20},{25,21},{26,22},{27,23}} | collective-permute-start | bytes 1179656 | tf_op jit(solution)/shard_map/ppermute | solution.py:99
  272.6 21.8 %collective-permute-start.29 = (bf16[256,1024]{1,0:T(8,128)(2,1)S(1)}, bf16[256,1024]{1,0:T(8,128)(2,1)S(1)}, u32[]{:S(2)}, u32[]{:S(2)}) collective-permute-start(bf16[256,1024]{1,0:T(8,128)(2,1)S(1)} %collective-permute-done.28.refs_2_), channel_id=1, source_target_pairs={{0,1},{1,0},{2,3},{3,2},{4,5},{5,4},{6,7},{7,6},{8,9},{9,8},{10,11... | collective-permute-start | bytes 1572872 | tf_op jit(solution)/shard_map/ppermute | solution.py:24
  308.8 148.1 %reduce-scatter.14.cloned.1.call-start = ((), (), s32[]{:S(2)}) async-start(), calls=%async_computation.9 | async-start | bytes 2621440 | tf_op jit(solution)/shard_map/reduce_scatter | solution.py:838
  308.9 24.0 %collective-permute-start.32 = (bf16[768,256]{1,0:T(8,128)(2,1)}, bf16[768,256]{1,0:T(8,128)(2,1)}, u32[]{:S(2)}, u32[]{:S(2)}) collective-permute-start(bf16[768,256]{1,0:T(8,128)(2,1)} %fusion.8), channel_id=1, source_target_pairs={{4,0},{5,1},{6,2},{7,3},{20,16},{21,17},{22,18},{23,19}} | collective-permute-start | bytes 1179656 | tf_op jit(solution)/shard_map/ppermute | solution.py:99
  310.3 36.9 %collective-permute-start.36 = (bf16[512,128]{1,0:T(8,128)(2,1)}, bf16[512,128]{1,0:T(8,128)(2,1)S(1)}, u32[]{:S(2)}, u32[]{:S(2)}) collective-permute-start(bf16[512,128]{1,0:T(8,128)(2,1)} %get-tuple-element.140), channel_id=1, source_target_pairs={{4,0},{8,4},{12,8},{5,1},{9,5},{13,9},{6,2},{10,6},{14,10},{7,3},{... | collective-permute-start | bytes 393224 | tf_op jit(solution)/shard_map/ppermute | solution.py:35
  311.6 36.2 %collective-permute-start.37 = (bf16[512,128]{1,0:T(8,128)(2,1)}, bf16[512,128]{1,0:T(8,128)(2,1)S(1)}, u32[]{:S(2)}, u32[]{:S(2)}) collective-permute-start(bf16[512,128]{1,0:T(8,128)(2,1)} %get-tuple-element.141), channel_id=1, source_target_pairs={{8,0},{12,4},{9,1},{13,5},{10,2},{14,6},{11,3},{15,7},{24,16},{28,... | collective-permute-start | bytes 393224 | tf_op jit(solution)/shard_map/ppermute | solution.py:35
  312.9 34.9 %collective-permute-start.38 = (bf16[512,128]{1,0:T(8,128)(2,1)}, bf16[512,128]{1,0:T(8,128)(2,1)S(1)}, u32[]{:S(2)}, u32[]{:S(2)}) collective-permute-start(bf16[512,128]{1,0:T(8,128)(2,1)} %get-tuple-element.142), channel_id=1, source_target_pairs={{12,0},{13,1},{14,2},{15,3},{28,16},{29,17},{30,18},{31,19}} | collective-permute-start | bytes 393224 | tf_op jit(solution)/shard_map/ppermute | solution.py:35
  347.2 5.0 %collective-permute-start.33 = (bf16[512,256]{1,0:T(8,128)(2,1)}, bf16[512,256]{1,0:T(8,128)(2,1)}, u32[]{:S(2)}, u32[]{:S(2)}) collective-permute-start(bf16[512,256]{1,0:T(8,128)(2,1)} %dynamic-slice_convert_fusion), channel_id=1, source_target_pairs={{0,1},{1,0},{2,3},{3,2},{4,5},{5,4},{6,7},{7,6},{8,9},{9,8},{10,11... | collective-permute-start | bytes 786440 | tf_op jit(solution)/shard_map/ppermute | solution.py:24
  349.5 19.7 %collective-permute-start.39 = (bf16[512,768]{1,0:T(8,128)(2,1)}, bf16[512,768]{1,0:T(8,128)(2,1)}, u32[]{:S(2)}, u32[]{:S(2)}) collective-permute-start(bf16[512,768]{1,0:T(8,128)(2,1)} %get-tuple-element.139.refs_1_.refs_4_), channel_id=1, source_target_pairs={{0,16},{16,0},{1,17},{17,1},{2,18},{18,2},{3,19},{19,3},{4,20},{20... | collective-permute-start | bytes 2359304 | tf_op jit(solution)/shard_map/ppermute | solution.py:29
  353.5 5.1 %collective-permute-start.34 = (bf16[512,128]{1,0:T(8,128)(2,1)S(1)}, bf16[512,128]{1,0:T(8,128)(2,1)S(1)}, u32[]{:S(2)}, u32[]{:S(2)}) collective-permute-start(bf16[512,128]{1,0:T(8,128)(2,1)S(1)} %dynamic-slice_convert_fusion.2), channel_id=1, source_target_pairs={{0,2},{1,3},{2,0},{3,1},{4,6},{5,7},{6,4},{7,5},{8,10},{9,11},{10,... | collective-permute-start | bytes 393224 | tf_op jit(solution)/shard_map/ppermute | solution.py:24
  358.6 24.3 %collective-permute-start.35 = (bf16[256,2048]{1,0:T(8,128)(2,1)}, bf16[256,2048]{1,0:T(8,128)(2,1)}, u32[]{:S(2)}, u32[]{:S(2)}) collective-permute-start(bf16[256,2048]{1,0:T(8,128)(2,1)} %mlp_own.1), channel_id=1, source_target_pairs={{0,2},{1,3},{2,0},{3,1},{4,6},{5,7},{6,4},{7,5},{8,10},{9,11},{10,... | collective-permute-start | bytes 3145736 | tf_op jit(solution)/shard_map/ppermute | solution.py:24
  379.0 3.9 collective-permute-start.40
  387.8 24.3 %collective-permute-start.41 = (bf16[256,2048]{1,0:T(8,128)(2,1)}, bf16[256,2048]{1,0:T(8,128)(2,1)S(1)}, u32[]{:S(2)}, u32[]{:S(2)}) collective-permute-start(bf16[256,2048]{1,0:T(8,128)(2,1)} %one_own.1.mine_ref), channel_id=1, source_target_pairs={{0,2},{1,3},{2,0},{3,1},{4,6},{5,7},{6,4},{7,5},{8,10},{9,11},{10,... | collective-permute-start | bytes 3145736 | tf_op jit(solution)/shard_map/ppermute | solution.py:24
  394.5 9.7 %collective-permute-start.42 = (bf16[512,256]{1,0:T(8,128)(2,1)S(1)}, bf16[512,256]{1,0:T(8,128)(2,1)}, u32[]{:S(2)}, u32[]{:S(2)}) collective-permute-start(bf16[512,256]{1,0:T(8,128)(2,1)S(1)} %pad_maximum_fusion.4.refs_5_), channel_id=1, source_target_pairs={{0,16},{16,0},{1,17},{17,1},{2,18},{18,2},{3,19},{19,3},{4,20},{20... | collective-permute-start | bytes 786440 | tf_op jit(solution)/shard_map/ppermute | solution.py:29
  419.1 32.1 %collective-permute-start.44 = (bf16[256,2048]{1,0:T(8,128)(2,1)}, bf16[256,2048]{1,0:T(8,128)(2,1)}, u32[]{:S(2)}, u32[]{:S(2)}) collective-permute-start(bf16[256,2048]{1,0:T(8,128)(2,1)} %get-tuple-element.147.mine_ref), channel_id=1, source_target_pairs={{0,1},{1,0},{2,3},{3,2},{4,5},{5,4},{6,7},{7,6},{8,9},{9,8},{10,11... | collective-permute-start | bytes 3145736 | tf_op jit(solution)/shard_map/ppermute | solution.py:24
  424.6 7.7 %collective-permute-start.45 = (f32[3,2048]{1,0:T(4,128)}, f32[3,2048]{1,0:T(4,128)}, u32[]{:S(2)}, u32[]{:S(2)}) collective-permute-start(f32[3,2048]{1,0:T(4,128)} %pad_maximum_fusion.7), channel_id=1, source_target_pairs={{0,1},{1,0},{2,3},{3,2},{4,5},{5,4},{6,7},{7,6},{8,9},{9,8},{10,11... | collective-permute-start | bytes 73736 | tf_op jit(solution)/shard_map/ppermute | solution.py:24
  427.7 6.1 %collective-permute-start.50 = (f32[1024,12]{0,1:T(8,128)S(1)}, f32[1024,12]{0,1:T(8,128)S(1)}, u32[]{:S(2)}, u32[]{:S(2)}) collective-permute-start(f32[1024,12]{0,1:T(8,128)S(1)} %constant_dynamic-slice_fusion.6), channel_id=1, source_target_pairs={{0,16},{16,0},{1,17},{17,1},{2,18},{18,2},{3,19},{19,3},{4,20},{20... | collective-permute-start | bytes 147464 | tf_op jit(solution)/shard_map/ppermute | solution.py:29
  429.1 25.1 %collective-permute-start.43 = (bf16[256,2048]{1,0:T(8,128)(2,1)S(1)}, bf16[256,2048]{1,0:T(8,128)(2,1)}, u32[]{:S(2)}, u32[]{:S(2)}) collective-permute-start(bf16[256,2048]{1,0:T(8,128)(2,1)S(1)} %get-tuple-element.229.mine_ref), channel_id=1, source_target_pairs={{0,1},{1,0},{2,3},{3,2},{4,5},{5,4},{6,7},{7,6},{8,9},{9,8},{10,11... | collective-permute-start | bytes 3145736 | tf_op jit(solution)/shard_map/ppermute | solution.py:24
  433.2 4.0 collective-permute-start.46
  433.9 6.1 %collective-permute-start.51 = (f32[256,12]{0,1:T(8,128)S(1)}, f32[256,12]{0,1:T(8,128)S(1)}, u32[]{:S(2)}, u32[]{:S(2)}) collective-permute-start(f32[256,12]{0,1:T(8,128)S(1)} %get-tuple-element.258), channel_id=1, source_target_pairs={{0,4},{4,8},{8,12},{12,0},{1,5},{5,9},{9,13},{13,1},{2,6},{6,10},{... | collective-permute-start | bytes 36872 | tf_op jit(solution)/shard_map/ppermute | solution.py:29
  434.0 7.5 %collective-permute-start.52 = (f32[256,12]{0,1:T(8,128)S(1)}, f32[256,12]{0,1:T(8,128)S(1)}, u32[]{:S(2)}, u32[]{:S(2)}) collective-permute-start(f32[256,12]{0,1:T(8,128)S(1)} %get-tuple-element.260), channel_id=1, source_target_pairs={{0,8},{4,12},{8,0},{12,4},{1,9},{5,13},{9,1},{13,5},{2,10},{6,14},... | collective-permute-start | bytes 36872 | tf_op jit(solution)/shard_map/ppermute | solution.py:29
  437.2 4.5 collective-permute-start.53
  440.0 7.0 %collective-permute-start.47 = (f32[4,2048]{1,0:T(4,128)S(1)}, f32[4,2048]{1,0:T(4,128)S(1)}, u32[]{:S(2)}, u32[]{:S(2)}) collective-permute-start(f32[4,2048]{1,0:T(4,128)S(1)} %bitcast.134), channel_id=1, source_target_pairs={{0,4},{4,8},{8,12},{12,0},{1,5},{5,9},{9,13},{13,1},{2,6},{6,10},{... | collective-permute-start | bytes 98312 | tf_op jit(solution)/shard_map/ppermute | solution.py:29
  441.4 8.0 %collective-permute-start.48 = (f32[4,2048]{1,0:T(4,128)S(1)}, f32[4,2048]{1,0:T(4,128)S(1)}, u32[]{:S(2)}, u32[]{:S(2)}) collective-permute-start(f32[4,2048]{1,0:T(4,128)S(1)} %bitcast.135), channel_id=1, source_target_pairs={{0,8},{4,12},{8,0},{12,4},{1,9},{5,13},{9,1},{13,5},{2,10},{6,14},... | collective-permute-start | bytes 98312 | tf_op jit(solution)/shard_map/ppermute | solution.py:29
  441.7 7.7 %collective-permute-start.49 = (f32[4,2048]{1,0:T(4,128)S(1)}, f32[4,2048]{1,0:T(4,128)S(1)}, u32[]{:S(2)}, u32[]{:S(2)}) collective-permute-start(f32[4,2048]{1,0:T(4,128)S(1)} %bitcast.136), channel_id=1, source_target_pairs={{0,12},{4,0},{8,4},{12,8},{1,13},{5,1},{9,5},{13,9},{2,14},{6,2},{... | collective-permute-start | bytes 98312 | tf_op jit(solution)/shard_map/ppermute | solution.py:29
  457.8 6.6 %collective-permute-start.54 = (bf16[256,256]{1,0:T(8,128)(2,1)S(1)}, bf16[256,256]{1,0:T(8,128)(2,1)S(1)}, u32[]{:S(2)}, u32[]{:S(2)}) collective-permute-start(bf16[256,256]{1,0:T(8,128)(2,1)S(1)} %get-tuple-element.239), channel_id=1, source_target_pairs={{0,1},{1,0},{2,3},{3,2},{4,5},{5,4},{6,7},{7,6},{8,9},{9,8},{10,11... | collective-permute-start | bytes 393224 | tf_op jit(solution)/shard_map/ppermute | solution.py:24
  457.9 6.5 %collective-permute-start.55 = (bf16[256,256]{1,0:T(8,128)(2,1)S(1)}, bf16[256,256]{1,0:T(8,128)(2,1)S(1)}, u32[]{:S(2)}, u32[]{:S(2)}) collective-permute-start(bf16[256,256]{1,0:T(8,128)(2,1)S(1)} %get-tuple-element.239), channel_id=1, source_target_pairs={{0,2},{1,3},{2,0},{3,1},{4,6},{5,7},{6,4},{7,5},{8,10},{9,11},{10,... | collective-permute-start | bytes 393224 | tf_op jit(solution)/shard_map/ppermute | solution.py:24
  459.4 6.8 %collective-permute-start.56 = (bf16[256,256]{1,0:T(8,128)(2,1)S(1)}, bf16[256,256]{1,0:T(8,128)(2,1)S(1)}, u32[]{:S(2)}, u32[]{:S(2)}) collective-permute-start(bf16[256,256]{1,0:T(8,128)(2,1)S(1)} %get-tuple-element.239), channel_id=1, source_target_pairs={{0,3},{1,2},{2,1},{3,0},{4,7},{5,6},{6,5},{7,4},{8,11},{9,10},{10,... | collective-permute-start | bytes 393224 | tf_op jit(solution)/shard_map/ppermute | solution.py:24
  (131 other events, 1264.9 us)
Sparse Core Ops, SparseCore 0:
  176.1 48.9 reduce-scatter.5
  227.6 51.4 reduce-scatter.7
  281.9 46.0 reduce-scatter.9
  330.3 78.2 reduce-scatter.11
  411.3 44.5 reduce-scatter.13
